TPU v7x, 256 devices: a whole 4x4x8 slice. The times are simulated.
256 devices in a mesh: samp: 16 (over y_lo, x, core), cpg: 16 (over z, y_hi).
Axes of the slice: x: 4, y: 4 (y_hi: 2, y_lo: 2; y = y_hi * 2 + y_lo), z: 8, core: 2. Of those that a mesh axis runs over, the one named last changes fastest.
Arguments:
- responses: bfloat16 [1024, 16384], P('samp', 'cpg'), may hold values from -5 to 5
- weights: bfloat16 [1024, 16384], P('samp', 'cpg'), may hold values from 1 to 8
- phenotype: float32 [16384], P('cpg'), may hold values from -6 to 6
- eigvecs: bfloat16 [16384, 16384], P('cpg', 'samp'), may hold values from -0.046875 to 0.046875
- eigvals: float32 [16384], P('samp'), may hold values from 0.0001 to 1
- positions: int32 [1024], replicated, may hold values from 1 to 307200, as said below
- reaches: int32 [1024], P('cpg'), may hold values from 1 to 8
Outputs:
- smoothed: float32 [1024], P('cpg')
- log_scale: float32 [1024], P('cpg')
Inputs may be any that keep to these rules, and one draw needn't show every extreme that they name: CpG m (from 0) lies at 300 m plus an offset of 1 to 300, so positions strictly increase and consecutive CpGs lie 1 to 599 base pairs apart.
All inputs are finite; a program needn't handle non-finite values.
Results may differ from a plain program's by a relative error of at most 0.0041.
Values may be sent and summed in bfloat16 or wider, within the bound.
No kernel may reach another device: no remote copies, remote signals or barrier semaphores. Data moves between devices by JAX's collectives and lax.ppermute only.
A program may use at most 64 MiB of HBM per device.

v0:
```python
import functools

import jax
import jax.numpy as jnp
from jax import lax
from jax.sharding import Mesh
from jax.sharding import PartitionSpec as P

ITERS = 4
HALO = 8
SAMP = ("samp_0", "samp_1", "samp_2")
CPG = ("cpg_0", "cpg_1")


EPSILON = 1e-06
band_width = 1000.0


def laid_out(parts, dim):
    lengths = list(parts.shape[1:])
    lengths[dim] *= parts.shape[0]
    return jnp.moveaxis(parts, 0, dim).reshape(lengths)


def one_gather(arrays, axis, dims):
    flat = jnp.concatenate([a.reshape(-1) for a in arrays])
    lines, at, gathered = (lax.all_gather(flat, axis), 0, [])
    for a, dim in zip(arrays, dims):
        parts = lines[:, at : at + a.size].reshape(-1, *a.shape)
        gathered.append(laid_out(parts, dim))
        at += a.size
    return tuple(gathered)


def one_axis_at_a_time(value, axes):
    return functools.reduce(lax.psum, axes, value)


def copy_for_each(value, axis):
    peers = lax.axis_size(axis)
    return lax.all_to_all(
        jnp.broadcast_to(value[None], (peers, *value.shape)), axis, 0, 0, tiled=True
    )


def of_everyone(value, axis):
    everything = copy_for_each(value, axis)
    return jnp.sum(everything, axis=0)


def summed_rows(total, axes):
    for axis in axes:
        total = lax.psum_scatter(total, axis, scatter_dimension=0, tiled=True)
    return total


def padded(value, sides, width):
    for axis, dim in sides:
        peers, length = (lax.axis_size(axis), value.shape[dim])
        up = [(i, (i + 1) % peers) for i in range(peers - 1)]
        down = [(j, i) for i, j in up]
        last = lax.slice_in_dim(value, length - width, length, axis=dim)
        leading = lax.slice_in_dim(value, 0, width, axis=dim)
        before = lax.ppermute(last, axis, up)
        after = lax.ppermute(leading, axis, down)
        value = jnp.concatenate([before, value, after], axis=dim)
    return value


def smooth_block(widened, places, present, reaches):
    block_len = reaches.shape[0]
    centre = places[HALO : HALO + block_len]
    total_sum = jnp.zeros((block_len,), jnp.float32)
    norm_sum = jnp.zeros((block_len,), jnp.float32)
    for offset in range(2 * HALO + 1):
        near_scores = widened[offset : offset + block_len]
        near_places = places[offset : offset + block_len]
        within = (abs(offset - HALO) <= reaches).astype(jnp.float32)
        kernel = (
            present[offset : offset + block_len]
            * within
            * jnp.exp(-jnp.abs(near_places - centre) / band_width)
        )
        total_sum = total_sum + kernel * near_scores
        norm_sum = norm_sum + kernel
    return total_sum / norm_sum


def fit_scores(rot_resp, rot_design, eigen_part, sum_axis, fit_total, spread_total, score_total):
    log_scale = jnp.zeros((rot_resp.shape[1 - sum_axis],), jnp.float32)
    for repeat in range(ITERS):
        inverse = 1.0 / (jnp.expand_dims(jnp.exp(log_scale), sum_axis) * eigen_part + 1.0)
        design_over = rot_design * inverse
        crossed_part = jnp.sum(design_over * rot_resp, axis=sum_axis)
        energy_part = jnp.sum(design_over * rot_design, axis=sum_axis)
        leverage = eigen_part * inverse
        traced_part = jnp.sum(leverage + 0.0 * inverse, axis=sum_axis)
        fisher_part = jnp.sum(leverage * leverage, axis=sum_axis)
        crossed, energy, traced, fisher = fit_total(
            (crossed_part, energy_part, traced_part, fisher_part)
        )
        energy = energy + EPSILON
        effect = crossed / energy
        residual = rot_resp - jnp.expand_dims(effect, sum_axis) * rot_design
        spread = spread_total(jnp.sum(leverage * inverse * residual * residual, axis=sum_axis))
        gradient = 0.5 * (spread - traced)
        log_scale = log_scale + jnp.tanh(gradient / (jnp.exp(log_scale) * (0.5 * fisher)))
    inverse = 1.0 / (jnp.expand_dims(jnp.exp(log_scale), sum_axis) * eigen_part + 1.0)
    design_over = rot_design * inverse
    crossed, energy = score_total(
        (
            jnp.sum(design_over * rot_resp, axis=sum_axis),
            jnp.sum(design_over * rot_design, axis=sum_axis),
        )
    )
    return (crossed / jnp.sqrt(energy + EPSILON), log_scale)


def shards(responses, weights, phenotype, eigvecs, eigvals, positions, reaches):
    root_weight = jnp.sqrt(weights.astype(jnp.float32))
    weighted = (root_weight * responses.astype(jnp.float32)).astype(jnp.bfloat16)
    design = (root_weight * phenotype[None, :]).astype(jnp.bfloat16)
    all_resp, all_design = one_gather((weighted, design), SAMP, (0, 0))
    cpg_count = lax.axis_size(CPG)
    block_len = reaches.shape[0]
    total_cpgs = block_len * cpg_count
    base = lax.axis_index(CPG) * block_len

    def fit_block(partials):
        return jax.tree.map(lambda part: one_axis_at_a_time(part, SAMP), partials)

    def spread_block(partial_value):
        return of_everyone(partial_value, SAMP)

    def score_block(partials):
        return jax.tree.map(lambda part: of_everyone(part, SAMP), partials)

    rotated = summed_rows(
        jnp.concatenate(
            [
                jnp.dot(all_resp, eigvecs, preferred_element_type=jnp.float32),
                jnp.dot(all_design, eigvecs, preferred_element_type=jnp.float32),
            ],
            axis=1,
        ),
        CPG,
    )
    comp_width = eigvecs.shape[1]
    scores, log_scale = fit_scores(
        rotated[:, :comp_width],
        rotated[:, comp_width:],
        eigvals[None, :],
        1,
        fit_block,
        spread_block,
        score_block,
    )
    widened = padded(scores, ((CPG, 0),), HALO)
    places = lax.dynamic_slice_in_dim(
        jnp.pad(positions.astype(jnp.float32), HALO), base, block_len + 2 * HALO, 0
    )
    global_index = base - HALO + jnp.arange(block_len + 2 * HALO, dtype=jnp.int32)
    present = ((global_index >= 0) & (global_index < total_cpgs)).astype(jnp.float32)
    smoothed = smooth_block(widened, places, present, reaches)
    return (smoothed, log_scale)


def solution(mesh):
    split = Mesh(
        mesh.devices.reshape(2, 4, 2, 8, 2), ("samp_0", "samp_1", "samp_2", "cpg_0", "cpg_1")
    )
    return jax.shard_map(
        shards,
        mesh=split,
        in_specs=(P(SAMP, CPG), P(SAMP, CPG), P(CPG), P(CPG, SAMP), P(SAMP), P(), P(CPG)),
        out_specs=(P(CPG), P(CPG)),
        check_vma=False,
    )
```

profile of v0, /device:TPU:96, one launch (start us, length us, event | category | flops | bytes accessed | tf_op | source)
XLA Modules:
  0.0 387.5 jit_solution(2524084051933177254)
XLA Ops:
  7.2 1.2 fusion.12
  8.5 0.7 pad_maximum_fusion.1
  9.3 42.4 %all-gather.3.cloned.1.call-done = bf16[2097152]{0:T(1024)(128)(2,1)} async-done(((bf16[131072]{0:T(1024)(128)(2,1)}), bf16[2097152]{0:T(1024)(128)(2,1)}) %all-gather.3.cloned.1.call-update) | async-done | bytes 4194320 | tf_op jit(solution)/shard_map/all_gather | solution.py:27
  51.7 4.7 %reshape.58 = bf16[16,131072]{1,0:T(8,128)(2,1)} reshape(bf16[2097152]{0:T(1024)(128)(2,1)} %all-gather.3.cloned.1.call-done) | data formatting | bytes 8388608 | tf_op jit(solution)/shard_map/all_gather | solution.py:27
  56.3 4.5 %fusion.37 = (bf16[16,65536]{1,0:T(8,128)(2,1)}, bf16[16,65536]{1,0:T(8,128)(2,1)}) fusion(bf16[16,131072]{1,0:T(8,128)(2,1)} %reshape.58), kind=kLoop, calls=%fused_computation.106 | loop fusion | bytes 8388608 | tf_op jit(solution)/shard_map/slice | solution.py:29
  60.8 3.2 reshape_reshape.6
  64.0 3.2 reshape_reshape.7
  67.2 4.1 %fusion.40 = f32[1024,1024]{0,1:T(8,128)S(1)} fusion(bf16[1024,1024]{1,0:T(8,128)(2,1)} %reshape_reshape.6, bf16[1024,1024]{1,0:T(8,128)(2,1)S(1)} %copy-done), kind=kOutput, calls=%fused_computation.109 | convolution fusion | flops 2147483648 | bytes 8388608 | tf_op jit(solution)/shard_map/dot_general | solution.py:141
  71.3 2.4 fusion.41
  73.7 4.1 %pad_maximum_fusion = f32[1024,2048]{0,1:T(8,128)} fusion(f32[1024,1024]{0,1:T(8,128)S(1)} %fusion.41, f32[1024,1024]{0,1:T(8,128)S(1)} %fusion.40), kind=kLoop, calls=%fused_computation | loop fusion | flops 2097152 | bytes 16777216 | tf_op jit(solution)/shard_map/concatenate | solution.py:139
  77.9 94.5 %reduce-scatter.5.cloned.1.call-done = f32[128,2048]{0,1:T(8,128)} async-done(((f32[1024,2048]{0,1:T(8,128)}), f32[128,2048]{0,1:T(8,128)}) %reduce-scatter.5.cloned.1.call-update) | async-done | bytes 1048592 | tf_op jit(solution)/shard_map/reduce_scatter | solution.py:53
  172.4 2.5 copy.15
  175.0 0.6 add_reduce_fusion
  175.6 25.6 %reduce-scatter.7.cloned.1.call-done = f32[64,2048]{1,0:T(8,128)} async-done(((f32[128,2048]{1,0:T(8,128)}), f32[64,2048]{1,0:T(8,128)}) %reduce-scatter.7.cloned.1.call-update) | async-done | bytes 524304
  201.3 1.1 fusion.38
  203.0 0.7 reduce_sum.261
  203.6 0.6 reduce_sum.263
  204.3 4.9 %all-reduce.21 = (f32[64]{0:T(128)S(1)}, f32[64]{0:T(128)S(1)}, f32[64]{0:T(128)S(1)}, f32[64]{0:T(128)S(1)}) all-reduce(f32[64]{0:T(128)S(1)} %reduce_sum.263, f32[64]{0:T(128)S(1)} %get-tuple-element.11, f32[64]{0:T(128)S(1)} %get-tuple-element.10, ...), channel_id=1, replica_groups=mesh['samp_0'=2,'samp_1'=4,'samp_2'=2,'cpg_0'=8,'cpg_1'=2] {'samp_0'}, use_global_device_ids=true, to_apply=%region_17.0 | all-reduce | flops 256 | bytes 2048 | tf_op jit(solution)/shard_map/psum | solution.py:36
  209.2 10.4 %all-reduce.7 = (f32[64]{0:T(128)S(1)}, f32[64]{0:T(128)S(1)}, f32[64]{0:T(128)S(1)}, f32[64]{0:T(128)S(1)}) all-reduce(f32[64]{0:T(128)S(1)} %get-tuple-element.67, f32[64]{0:T(128)S(1)} %get-tuple-element.68, f32[64]{0:T(128)S(1)} %get-tuple-element.69, ...), channel_id=1, replica_groups=mesh['samp_0'=2,'samp_1'=4,'samp_2'=2,'cpg_0'=8,'cpg_1'=2] {'samp_1'}, use_global_device_ids=true, to_apply=%region_18.0 | all-reduce | flops 256 | bytes 2048 | tf_op jit(solution)/shard_map/psum | solution.py:36
  219.6 2.5 all-reduce.14
  222.1 0.2 fusion.8
  222.4 8.6 %all_to_all.36 = f32[16,1,64]{2,1,0:T(1,128)S(1)} all-to-all(f32[16,1,64]{2,1,0:T(1,128)S(1)} %broadcast_in_dim.12), channel_id=1, replica_groups=mesh['samp_0'=2,'samp_1'=4,'samp_2'=2,'cpg_0'=8,'cpg_1'=2] {'samp_0','sa..., dimensions={0} | all-to-all | bytes 8192 | tf_op jit(solution)/shard_map/all_to_all | solution.py:41
  231.0 0.4 multiply_reduce_fusion.6
  231.4 4.9 %all-reduce.20 = (f32[64]{0:T(128)S(1)}, f32[64]{0:T(128)S(1)}) all-reduce(f32[64]{0:T(128)S(1)} %get-tuple-element.9, f32[64]{0:T(128)S(1)} %get-tuple-element.8), channel_id=1, replica_groups=mesh['samp_0'=2,'samp_1'=4,'samp_2'=2,'cpg_0'=8,'cpg_1'=2] {'samp_0'}, use_global_device_ids=true, to_apply=%region_21.0 | all-reduce | flops 128 | bytes 1024 | tf_op jit(solution)/shard_map/psum | solution.py:36
  236.3 8.9 %all-reduce.6 = (f32[64]{0:T(128)S(1)}, f32[64]{0:T(128)S(1)}) all-reduce(f32[64]{0:T(128)S(1)} %get-tuple-element.65, f32[64]{0:T(128)S(1)} %get-tuple-element.66), channel_id=1, replica_groups=mesh['samp_0'=2,'samp_1'=4,'samp_2'=2,'cpg_0'=8,'cpg_1'=2] {'samp_1'}, use_global_device_ids=true, to_apply=%region_22.0 | all-reduce | flops 128 | bytes 1024 | tf_op jit(solution)/shard_map/psum | solution.py:36
  245.2 2.4 all-reduce.13
  247.6 0.3 fusion.9
  247.9 0.6 broadcast_in_dim.13
  248.6 3.5 all-to-all-start.1
  252.1 4.9 %all-reduce.19 = (f32[64]{0:T(128)S(1)}, f32[64]{0:T(128)S(1)}) all-reduce(f32[64]{0:T(128)S(1)} %get-tuple-element.20, f32[64]{0:T(128)S(1)} %get-tuple-element.18), channel_id=1, replica_groups=mesh['samp_0'=2,'samp_1'=4,'samp_2'=2,'cpg_0'=8,'cpg_1'=2] {'samp_0'}, use_global_device_ids=true, to_apply=%region_35.0 | all-reduce | flops 128 | bytes 1024 | tf_op jit(solution)/shard_map/psum | solution.py:36
  257.0 10.7 %all-reduce.5 = (f32[64]{0:T(128)S(1)}, f32[64]{0:T(128)S(1)}) all-reduce(f32[64]{0:T(128)S(1)} %get-tuple-element.63, f32[64]{0:T(128)S(1)} %get-tuple-element.64), channel_id=1, replica_groups=mesh['samp_0'=2,'samp_1'=4,'samp_2'=2,'cpg_0'=8,'cpg_1'=2] {'samp_1'}, use_global_device_ids=true, to_apply=%region_36.0 | all-reduce | flops 128 | bytes 1024 | tf_op jit(solution)/shard_map/psum | solution.py:36
  267.7 2.4 all-reduce.12
  270.2 0.4 multiply_reduce_fusion.4
  270.6 5.1 %all-reduce.18 = (f32[64]{0:T(128)S(1)}, f32[64]{0:T(128)S(1)}) all-reduce(f32[64]{0:T(128)S(1)} %get-tuple-element.7, f32[64]{0:T(128)S(1)} %get-tuple-element.6), channel_id=1, replica_groups=mesh['samp_0'=2,'samp_1'=4,'samp_2'=2,'cpg_0'=8,'cpg_1'=2] {'samp_0'}, use_global_device_ids=true, to_apply=%region_39.0 | all-reduce | flops 128 | bytes 1024 | tf_op jit(solution)/shard_map/psum | solution.py:36
  275.7 7.7 %all-reduce.4 = (f32[64]{0:T(128)S(1)}, f32[64]{0:T(128)S(1)}) all-reduce(f32[64]{0:T(128)S(1)} %get-tuple-element.61, f32[64]{0:T(128)S(1)} %get-tuple-element.62), channel_id=1, replica_groups=mesh['samp_0'=2,'samp_1'=4,'samp_2'=2,'cpg_0'=8,'cpg_1'=2] {'samp_1'}, use_global_device_ids=true, to_apply=%region_40.0 | all-reduce | flops 128 | bytes 1024 | tf_op jit(solution)/shard_map/psum | solution.py:36
  283.4 2.4 all-reduce.11
  285.9 0.3 fusion.10
  286.2 0.6 broadcast_in_dim.14
  286.8 4.4 %all-to-all-start.2 = ((f32[16,1,64]{2,1,0:T(1,128)}), f32[16,1,64]{2,1,0:T(1,128)S(1)}, u32[]{:S(2)}, u32[]{:S(2)}) async-start(f32[16,1,64]{2,1,0:T(1,128)} %broadcast_in_dim.14), calls=%async_computation.3 | async-start | bytes 16384 | tf_op jit(solution)/shard_map/all_to_all | solution.py:41
  291.2 5.0 %all-reduce.17 = (f32[64]{0:T(128)S(1)}, f32[64]{0:T(128)S(1)}) all-reduce(f32[64]{0:T(128)S(1)} %get-tuple-element.17, f32[64]{0:T(128)S(1)} %get-tuple-element.15), channel_id=1, replica_groups=mesh['samp_0'=2,'samp_1'=4,'samp_2'=2,'cpg_0'=8,'cpg_1'=2] {'samp_0'}, use_global_device_ids=true, to_apply=%region_53.0 | all-reduce | flops 128 | bytes 1024 | tf_op jit(solution)/shard_map/psum | solution.py:36
  296.2 10.8 %all-reduce.3 = (f32[64]{0:T(128)S(1)}, f32[64]{0:T(128)S(1)}) all-reduce(f32[64]{0:T(128)S(1)} %get-tuple-element.59, f32[64]{0:T(128)S(1)} %get-tuple-element.60), channel_id=1, replica_groups=mesh['samp_0'=2,'samp_1'=4,'samp_2'=2,'cpg_0'=8,'cpg_1'=2] {'samp_1'}, use_global_device_ids=true, to_apply=%region_54.0 | all-reduce | flops 128 | bytes 1024 | tf_op jit(solution)/shard_map/psum | solution.py:36
  306.9 2.4 all-reduce.10
  309.4 0.4 multiply_reduce_fusion.2
  309.8 4.9 %all-reduce.16 = (f32[64]{0:T(128)S(1)}, f32[64]{0:T(128)S(1)}) all-reduce(f32[64]{0:T(128)S(1)} %get-tuple-element.5, f32[64]{0:T(128)S(1)} %get-tuple-element.4), channel_id=1, replica_groups=mesh['samp_0'=2,'samp_1'=4,'samp_2'=2,'cpg_0'=8,'cpg_1'=2] {'samp_0'}, use_global_device_ids=true, to_apply=%region_57.0 | all-reduce | flops 128 | bytes 1024 | tf_op jit(solution)/shard_map/psum | solution.py:36
  314.7 7.7 %all-reduce.2 = (f32[64]{0:T(128)S(1)}, f32[64]{0:T(128)S(1)}) all-reduce(f32[64]{0:T(128)S(1)} %get-tuple-element.57, f32[64]{0:T(128)S(1)} %get-tuple-element.58), channel_id=1, replica_groups=mesh['samp_0'=2,'samp_1'=4,'samp_2'=2,'cpg_0'=8,'cpg_1'=2] {'samp_1'}, use_global_device_ids=true, to_apply=%region_58.0 | all-reduce | flops 128 | bytes 1024 | tf_op jit(solution)/shard_map/psum | solution.py:36
  322.4 2.4 all-reduce.9
  324.9 0.3 fusion.11
  325.2 0.6 broadcast_in_dim.15
  325.8 4.3 %all-to-all-start.3 = ((f32[16,1,64]{2,1,0:T(1,128)}), f32[16,1,64]{2,1,0:T(1,128)S(1)}, u32[]{:S(2)}, u32[]{:S(2)}) async-start(f32[16,1,64]{2,1,0:T(1,128)} %broadcast_in_dim.15), calls=%async_computation.4 | async-start | bytes 16384 | tf_op jit(solution)/shard_map/all_to_all | solution.py:41
  330.2 5.0 %all-reduce.15 = (f32[64]{0:T(128)S(1)}, f32[64]{0:T(128)S(1)}) all-reduce(f32[64]{0:T(128)S(1)} %get-tuple-element.14, f32[64]{0:T(128)S(1)} %get-tuple-element.12), channel_id=1, replica_groups=mesh['samp_0'=2,'samp_1'=4,'samp_2'=2,'cpg_0'=8,'cpg_1'=2] {'samp_0'}, use_global_device_ids=true, to_apply=%region_71.0 | all-reduce | flops 128 | bytes 1024 | tf_op jit(solution)/shard_map/psum | solution.py:36
  335.1 10.8 %all-reduce.1 = (f32[64]{0:T(128)S(1)}, f32[64]{0:T(128)S(1)}) all-reduce(f32[64]{0:T(128)S(1)} %get-tuple-element.55, f32[64]{0:T(128)S(1)} %get-tuple-element.56), channel_id=1, replica_groups=mesh['samp_0'=2,'samp_1'=4,'samp_2'=2,'cpg_0'=8,'cpg_1'=2] {'samp_1'}, use_global_device_ids=true, to_apply=%region_72.0 | all-reduce | flops 128 | bytes 1024 | tf_op jit(solution)/shard_map/psum | solution.py:36
  345.9 2.4 all-reduce.8
  348.4 0.5 fusion.32
  348.9 0.3 multiply_reduce_fusion
  349.2 0.6 broadcast_in_dim.16
  349.8 3.5 all-to-all-start.4
  353.3 5.8 %all-to-all-done.4 = f32[16,1,64]{2,1,0:T(1,128)S(1)} async-done(((f32[16,1,64]{2,1,0:T(1,128)}), f32[16,1,64]{2,1,0:T(1,128)S(1)}, u32[]{:S(2)}, u32[]{:S(2)}) %all-to-all-start.4) | async-done | bytes 4128 | tf_op jit(solution)/shard_map/all_to_all | solution.py:41
  359.1 0.6 broadcast_in_dim.17
  359.7 3.5 all-to-all-start.5
  363.4 5.7 %all-to-all-done.5 = f32[16,1,64]{2,1,0:T(1,128)S(1)} async-done(((f32[16,1,64]{2,1,0:T(1,128)}), f32[16,1,64]{2,1,0:T(1,128)S(1)}, u32[]{:S(2)}, u32[]{:S(2)}) %all-to-all-start.5) | async-done | bytes 4128 | tf_op jit(solution)/shard_map/all_to_all | solution.py:41
  369.2 3.5 collective-permute-start
  372.7 4.8 %collective-permute-start.1 = (f32[8]{0:T(128)S(1)}, f32[8]{0:T(128)S(1)}, u32[]{:S(2)}, u32[]{:S(2)}) collective-permute-start(f32[8]{0:T(128)S(1)} %get-tuple-element.90), channel_id=1, source_target_pairs={{1,0},{2,1},{3,2},{4,3},{5,4},{6,5},{7,6},{8,7},{9,8},{10,9},{11,1... | collective-permute-start | bytes 104 | tf_op jit(solution)/shard_map/ppermute | solution.py:65
  377.5 2.8 collective-permute-done.1
  380.3 0.6 add_divide_fusion.4
  (45 shorter events, 1.3 us)
Async XLA Ops:
  7.2 60.0 %copy-start = (bf16[1024,1024]{1,0:T(8,128)(2,1)S(1)}, bf16[1024,1024]{1,0:T(8,128)(2,1)}, u32[]{:S(2)}) copy-start(bf16[1024,1024]{1,0:T(8,128)(2,1)} %param.10) | copy-start | bytes 6291460
  7.2 44.5 %all-gather.3.cloned.1.call-start = ((), (), s32[]{:S(2)}) async-start(), calls=%async_computation.9 | async-start | bytes 4456448 | tf_op jit(solution)/shard_map/all_gather | solution.py:27
  9.2 163.2 %reduce-scatter.5.cloned.1.call-start = ((), (), s32[]{:S(2)}) async-start(), calls=%async_computation.8 | async-start | bytes 9437184 | tf_op jit(solution)/shard_map/reduce_scatter | solution.py:53
  67.2 4.1 %copy-start.1 = (bf16[1024,1024]{1,0:T(8,128)(2,1)S(1)}, bf16[1024,1024]{1,0:T(8,128)(2,1)}, u32[]{:S(2)}) copy-start(bf16[1024,1024]{1,0:T(8,128)(2,1)} %reshape_reshape.7) | copy-start | bytes 6291460
  77.8 97.2 %copy-start.2 = (f32[1024]{0:T(1024)S(1)}, f32[1024]{0:T(1024)}, u32[]{:S(2)}) copy-start(f32[1024]{0:T(1024)} %param.11) | copy-start | bytes 12292
  77.8 123.4 %reduce-scatter.7.cloned.1.call-start = ((), (), s32[]{:S(2)}) async-start(), calls=%async_computation.10 | async-start | bytes 1572864
  248.6 21.6 %all-to-all-start.1 = ((f32[16,1,64]{2,1,0:T(1,128)}), f32[16,1,64]{2,1,0:T(1,128)S(1)}, u32[]{:S(2)}, u32[]{:S(2)}) async-start(f32[16,1,64]{2,1,0:T(1,128)} %broadcast_in_dim.13), calls=%async_computation.2 | async-start | bytes 16384 | tf_op jit(solution)/shard_map/all_to_all | solution.py:41
  285.9 67.4 %copy-start.3 = (s32[1024]{0:T(1024)S(1)}, s32[1024]{0:T(1024)}, u32[]{:S(2)}) copy-start(s32[1024]{0:T(1024)} %param.12) | copy-start | bytes 12292
  285.9 94.5 %copy-start.4 = (s32[64]{0:T(128)S(1)}, s32[64]{0:T(128)}, u32[]{:S(2)}) copy-start(s32[64]{0:T(128)} %param.13) | copy-start | bytes 772
  286.8 22.6 %all-to-all-start.2 = ((f32[16,1,64]{2,1,0:T(1,128)}), f32[16,1,64]{2,1,0:T(1,128)S(1)}, u32[]{:S(2)}, u32[]{:S(2)}) async-start(f32[16,1,64]{2,1,0:T(1,128)} %broadcast_in_dim.14), calls=%async_computation.3 | async-start | bytes 16384 | tf_op jit(solution)/shard_map/all_to_all | solution.py:41
  325.8 22.5 %all-to-all-start.3 = ((f32[16,1,64]{2,1,0:T(1,128)}), f32[16,1,64]{2,1,0:T(1,128)S(1)}, u32[]{:S(2)}, u32[]{:S(2)}) async-start(f32[16,1,64]{2,1,0:T(1,128)} %broadcast_in_dim.15), calls=%async_computation.4 | async-start | bytes 16384 | tf_op jit(solution)/shard_map/all_to_all | solution.py:41
  349.8 9.4 %all-to-all-start.4 = ((f32[16,1,64]{2,1,0:T(1,128)}), f32[16,1,64]{2,1,0:T(1,128)S(1)}, u32[]{:S(2)}, u32[]{:S(2)}) async-start(f32[16,1,64]{2,1,0:T(1,128)} %broadcast_in_dim.16), calls=%async_computation.5 | async-start | bytes 16384 | tf_op jit(solution)/shard_map/all_to_all | solution.py:41
  359.7 9.4 %all-to-all-start.5 = ((f32[16,1,64]{2,1,0:T(1,128)}), f32[16,1,64]{2,1,0:T(1,128)S(1)}, u32[]{:S(2)}, u32[]{:S(2)}) async-start(f32[16,1,64]{2,1,0:T(1,128)} %broadcast_in_dim.17), calls=%async_computation.6 | async-start | bytes 16384 | tf_op jit(solution)/shard_map/all_to_all | solution.py:41
  369.2 8.3 %collective-permute-start = (f32[8]{0:T(128)S(1)}, f32[8]{0:T(128)S(1)}, u32[]{:S(2)}, u32[]{:S(2)}) collective-permute-start(f32[8]{0:T(128)S(1)} %get-tuple-element.89), channel_id=1, source_target_pairs={{0,1},{1,2},{2,3},{3,4},{4,5},{5,6},{6,7},{7,8},{8,9},{9,10},{10,1... | collective-permute-start | bytes 104 | tf_op jit(solution)/shard_map/ppermute | solution.py:64
  372.7 7.6 %collective-permute-start.1 = (f32[8]{0:T(128)S(1)}, f32[8]{0:T(128)S(1)}, u32[]{:S(2)}, u32[]{:S(2)}) collective-permute-start(f32[8]{0:T(128)S(1)} %get-tuple-element.90), channel_id=1, source_target_pairs={{1,0},{2,1},{3,2},{4,3},{5,4},{6,5},{7,6},{8,7},{9,8},{10,9},{11,1... | collective-permute-start | bytes 104 | tf_op jit(solution)/shard_map/ppermute | solution.py:65
Sparse Core Ops, SparseCore 0:
  9.9 41.7 all-gather.2
  78.0 94.4 reduce-scatter.4
  175.1 26.1 reduce-scatter.6
where the time goes:
time: 391 us; the launch traced here: 388 us
  waiting for transfers between devices  177 us (45%)
  blocking collectives  128 us (33%)
  starting transfers between devices  27.5 us (7%)
  local copies, waits for them, and re-layouts  24.1 us (6%)
  between operations  14 us (4%)
  other arithmetic  10.8 us (3%)
  matrix products  6.51 us (2%)
    psum x21, blocking collectives, one_axis_at_a_time(): return functools.reduce(lax.psum, axes, value)  119 us
    reduce_scatter x1, waiting for transfers between devices, summed_rows(): total = lax.psum_scatter(total, axis, scatter_dimension=0, tiled=True)  94.5 us
    all_gather x1, waiting for transfers between devices, one_gather(): lines, at, gathered = (lax.all_gather(flat, axis), 0, [])  42.4 us
    unnamed x4, waiting for transfers between devices  25.7 us
    all_to_all x5, starting transfers between devices, copy_for_each(): lax.all_to_all(jnp.broadcast_to(value[None], (peers, *value.shape)), axis...  19.1 us
    all_to_all x5, waiting for transfers between devices, copy_for_each(): lax.all_to_all(jnp.broadcast_to(value[None], (peers, *value.shape)), axis...  11.6 us
    all_to_all x1, blocking collectives, copy_for_each(): lax.all_to_all(jnp.broadcast_to(value[None], (peers, *value.shape)), axis...  8.61 us
  transfers between devices with their start and end apart: 10, of which 6 were waited for; matrix products, arithmetic and copies ran while one was open for 0% of the time, Pallas kernels for 0%

commit v1 on v0

v1 whole, which is shorter than its diff:
```python
import functools

import jax
import jax.numpy as jnp
from jax import lax
from jax.experimental import pallas as pl
from jax.experimental.pallas import tpu as pltpu
from jax.sharding import Mesh
from jax.sharding import PartitionSpec as P

ITERS = 4
HALO = 8
SAMP = ("samp_0", "samp_1", "samp_2")
CPG = ("cpg_0", "cpg_1")
PLANE = ("cpg_1", "samp_0", "samp_1")
LAYER = ("cpg_1", "samp_0", "samp_1", "samp_2")

EPSILON = 1e-06
band_width = 1000.0


def shifted(value, axis, by):
    peers = lax.axis_size(axis)
    return lax.ppermute(value, axis, [(i, (i + by) % peers) for i in range(peers)])


def weigh_kernel(resp_ref, weight_ref, trait_ref, out_ref):
    rows = resp_ref.shape[0]
    trait = trait_ref[...]
    for at in range(0, rows, 16):
        root = jnp.sqrt(weight_ref[at : at + 16, :].astype(jnp.float32))
        weighted = root * resp_ref[at : at + 16, :].astype(jnp.float32)
        design = root * trait
        upper = lax.broadcasted_iota(jnp.int32, (8, root.shape[1]), 0) < 4
        tiles = []
        for half in (0, 8):
            a, b = weighted[half : half + 8], design[half : half + 8]
            tiles.append(jnp.where(upper, a, pltpu.roll(b, 4, 0)))
            tiles.append(jnp.where(upper, pltpu.roll(a, 4, 0), b))
        out_ref[2 * at : 2 * at + 32, :] = jnp.concatenate(tiles, axis=0).astype(jnp.bfloat16)


def weigh(responses, weights, phenotype):
    rows, width = responses.shape
    return pl.pallas_call(
        weigh_kernel,
        out_shape=jax.ShapeDtypeStruct((2 * rows, width), jnp.bfloat16),
    )(responses, weights, phenotype[None, :])


def fit_kernel(sums_ref, values_ref, out_ref, rows_ref, inv_ref):
    sources, width = values_ref.shape
    half = 8 * sources
    step = 512
    starts = [(i, j) for i in range(sources) for j in range(0, width, step)]
    for i in range(0, sources, 2):
        rows_ref[8 * i : 8 * i + 16, :] = sums_ref[8 * i : 8 * i + 16, :].astype(
            jnp.float32
        ) + sums_ref[half + 8 * i : half + 8 * i + 16, :].astype(jnp.float32)

    def total(acc):
        acc = acc.reshape(8, step // 128, 128)
        return jnp.sum(jnp.sum(acc, axis=1), axis=1, keepdims=True)

    def sweep(scale, fit):
        zero = jnp.zeros((8, step), jnp.float32)

        def body(i, accs):
            crossed, energy, traced, fisher = accs
            at = pl.multiple_of(8 * i, 8)
            for j in range(0, width, step):
                own = rows_ref[pl.ds(at, 8), j : j + step]
                lam = jnp.broadcast_to(values_ref[pl.ds(i, 1), j : j + step], (8, step))
                inv = 1.0 / (scale * lam + 1.0)
                over = own * inv
                crossed = crossed + over * pltpu.roll(own, 4, 0)
                energy = energy + over * own
                if fit:
                    lev = lam * inv
                    traced = traced + lev
                    fisher = fisher + lev * lev
                    inv_ref[pl.ds(at, 8), j : j + step] = lev * inv
            return crossed, energy, traced, fisher

        crossed, energy, traced, fisher = lax.fori_loop(0, sources, body, (zero,) * 4)
        crossed, energy = total(crossed), total(energy)
        upper = lax.broadcasted_iota(jnp.int32, (8, 128), 0) < 4
        energy = jnp.broadcast_to(energy, (8, 128))
        energy = jnp.where(upper, pltpu.roll(energy, 4, 0), energy)[:, :1]
        return crossed, energy + EPSILON, total(traced), total(fisher)

    log_scale = jnp.zeros((8, 1), jnp.float32)
    for _ in range(ITERS):
        scale = jnp.exp(log_scale)
        crossed, energy, traced, fisher = sweep(scale, True)
        effect = crossed / energy

        def spread_body(i, acc):
            at = pl.multiple_of(8 * i, 8)
            for j in range(0, width, step):
                own = rows_ref[pl.ds(at, 8), j : j + step]
                residual = own - effect * pltpu.roll(own, 4, 0)
                acc = acc + inv_ref[pl.ds(at, 8), j : j + step] * residual * residual
            return acc

        spread = total(lax.fori_loop(0, sources, spread_body, jnp.zeros((8, step), jnp.float32)))
        gradient = 0.5 * (spread - traced)
        moved = log_scale + jnp.tanh(gradient / (scale * (0.5 * fisher)))
        moved = jnp.broadcast_to(moved, (8, 128))
        upper = lax.broadcasted_iota(jnp.int32, (8, 128), 0) < 4
        log_scale = jnp.where(upper, moved, pltpu.roll(moved, 4, 0))[:, :1]
    crossed, energy, _, _ = sweep(jnp.exp(log_scale), False)
    score = jnp.broadcast_to(crossed / jnp.sqrt(energy), (8, 128))
    upper = lax.broadcasted_iota(jnp.int32, (8, 128), 0) < 4
    out_ref[...] = jnp.where(upper, score, jnp.broadcast_to(log_scale, (8, 128)))


def fit(sums, values):
    rows, width = sums.shape
    return pl.pallas_call(
        fit_kernel,
        out_shape=jax.ShapeDtypeStruct((8, 128), jnp.float32),
        scratch_shapes=[
            pltpu.VMEM((rows // 2, width), jnp.float32),
            pltpu.VMEM((rows // 2, width), jnp.float32),
        ],
    )(sums, values)


def gather_plane(own):
    x, y = "samp_1", "samp_0"
    left = shifted(own, x, 1)
    right = shifted(own, x, -1)
    over = shifted(own, y, 1)
    far = shifted(left, x, 1)
    over_right = shifted(over, x, -1)
    over_left = shifted(left, y, 1)
    over_far = jnp.concatenate(
        [
            shifted(over_left[:48], x, 1),
            shifted(over_right[48:96], x, -1),
            shifted(far[96:], y, 1),
        ],
        axis=0,
    )
    return jnp.stack([own, right, far, left, over, over_right, over_far, over_left])


def smooth_block(widened, places, present, reaches):
    block_len = reaches.shape[0]
    centre = places[HALO : HALO + block_len]
    total_sum = jnp.zeros((block_len,), jnp.float32)
    norm_sum = jnp.zeros((block_len,), jnp.float32)
    for offset in range(2 * HALO + 1):
        near_scores = widened[offset : offset + block_len]
        near_places = places[offset : offset + block_len]
        within = (abs(offset - HALO) <= reaches).astype(jnp.float32)
        kernel = (
            present[offset : offset + block_len]
            * within
            * jnp.exp(-jnp.abs(near_places - centre) / band_width)
        )
        total_sum = total_sum + kernel * near_scores
        norm_sum = norm_sum + kernel
    return total_sum / norm_sum


def shards(responses, weights, phenotype, eigvecs, eigvals, positions, reaches):
    z, x, y = lax.axis_index("cpg_0"), lax.axis_index("samp_1"), lax.axis_index("samp_0")
    layers = lax.axis_size("cpg_0")
    with jax.named_scope("swap_eigvecs"):
        vecs = (eigvecs, shifted(eigvecs, "samp_2", 1))
        values = jnp.concatenate([eigvals, shifted(eigvals, "samp_2", 1)])
    with jax.named_scope("weigh"):
        own = weigh(responses, weights, phenotype)
    with jax.named_scope("gather_rows"):
        blocks = gather_plane(own)
    with jax.named_scope("gather_values"):
        everywhere = lax.all_to_all(
            jnp.broadcast_to(values[None], (8, *values.shape)), ("samp_0", "samp_1"), 0, 0, tiled=True
        )

    def term(ahead, q, lo=0, hi=None):
        dest = lax.rem(z + ahead + layers, layers)
        across, along = dest // 4, lax.rem(dest, 4)
        place = 4 * (across ^ y) + lax.rem(along - x + 4, 4)
        rows = lax.dynamic_index_in_dim(blocks, place, 0, keepdims=False)[lo:hi]
        return jnp.dot(rows, vecs[q], preferred_element_type=jnp.float32)

    with jax.named_scope("sum_layers"):
        far = layers // 2
        rows = own.shape[0]
        cut = rows // 2
        sent = {}
        for q in (0, 1):
            sent[q, 1] = shifted(term(far, q, 0, cut).astype(jnp.bfloat16), "cpg_0", 1)
            sent[q, -1] = shifted(term(far, q, cut, rows).astype(jnp.bfloat16), "cpg_0", -1)
        for ahead in range(far - 1, 0, -1):
            for q in (0, 1):
                for way in (1, -1):
                    got = sent[q, way].astype(jnp.float32)
                    if got.shape[0] < rows:
                        rest = jnp.zeros_like(got)
                        got = jnp.concatenate([got, rest] if way == 1 else [rest, got], axis=0)
                    total = (term(way * ahead, q) + got).astype(jnp.bfloat16)
                    sent[q, way] = shifted(total, "cpg_0", way)
        summed = jnp.concatenate(
            [
                (
                    term(0, q)
                    + sent[q, 1].astype(jnp.float32)
                    + sent[q, -1].astype(jnp.float32)
                ).astype(jnp.bfloat16)
                for q in (0, 1)
            ],
            axis=1,
        )
    with jax.named_scope("to_components"):
        sums = lax.all_to_all(
            summed.reshape(16, rows // 16, -1), PLANE, 0, 0, tiled=True
        ).reshape(rows, -1)
    with jax.named_scope("fit"):
        fitted = fit(sums, everywhere)[:, 0]
    with jax.named_scope("gather_scores"):
        spread_out = lax.all_to_all(
            jnp.broadcast_to(fitted[None], (32, 8)), LAYER, 0, 0, tiled=True
        )
        layer = spread_out.reshape(16, 2, 2, 4).transpose(2, 1, 0, 3).reshape(2, -1)
        scores, scales = layer[0], layer[1]
        up = [(i, i + 1) for i in range(layers - 1)]
        down = [(j, i) for i, j in up]
        before = lax.ppermute(scores[-HALO:], "cpg_0", up)
        after = lax.ppermute(scores[:HALO], "cpg_0", down)
    with jax.named_scope("smooth"):
        block_len = reaches.shape[0]
        high = lax.axis_index("cpg_1")
        widened = lax.dynamic_slice_in_dim(
            jnp.concatenate([before, scores, after]), high * block_len, block_len + 2 * HALO, 0
        )
        log_scale = lax.dynamic_slice_in_dim(scales, high * block_len, block_len, 0)
        base = lax.axis_index(CPG) * block_len
        total_cpgs = block_len * lax.axis_size(CPG)
        places = lax.dynamic_slice_in_dim(
            jnp.pad(positions.astype(jnp.float32), HALO), base, block_len + 2 * HALO, 0
        )
        global_index = base - HALO + jnp.arange(block_len + 2 * HALO, dtype=jnp.int32)
        present = ((global_index >= 0) & (global_index < total_cpgs)).astype(jnp.float32)
        smoothed = smooth_block(widened, places, present, reaches)
    return (smoothed, log_scale)


def solution(mesh):
    split = Mesh(
        mesh.devices.reshape(2, 4, 2, 8, 2), ("samp_0", "samp_1", "samp_2", "cpg_0", "cpg_1")
    )
    return jax.shard_map(
        shards,
        mesh=split,
        in_specs=(P(SAMP, CPG), P(SAMP, CPG), P(CPG), P(CPG, SAMP), P(SAMP), P(), P(CPG)),
        out_specs=(P(CPG), P(CPG)),
        check_vma=False,
    )
```

time: 391 us -> 156 us (0.40)
  blocking collectives: 128 us -> 0 us
  waiting for transfers between devices: 177 us -> 51.6 us
  starting transfers between devices: 27.5 us -> 66.4 us
  between operations: 14 us -> 1.06 us
  local copies, waits for them, and re-layouts: 24.1 us -> 12.3 us
  Pallas kernels: 0 us -> 11 us
  other arithmetic: 10.8 us -> 3.66 us
    psum x21 -> x0, blocking collectives: 119 us -> none  [one_axis_at_a_time(): return functools.reduce(lax.psum, axes, value)]
    reduce_scatter x1 -> x0, waiting for transfers between devices: 94.5 us -> none  [summed_rows(): total = lax.psum_scatter(total, axis, scatter_dimension=0, tiled=True)]
    ppermute x2 -> x29, starting transfers between devices: 8.24 us -> 51.5 us  [the longest x27 45.7 us: shifted(): lax.ppermute(value, axis, [(i, (i + by) % peers) for i in range(peers)])]
    all_gather x1 -> x0, waiting for transfers between devices: 42.4 us -> none  [one_gather(): lines, at, gathered = (lax.all_gather(flat, axis), 0, [])]
    ppermute x2 -> x29, waiting for transfers between devices: 2.8 us -> 34.9 us  [the longest x27 32.9 us: shifted(): lax.ppermute(value, axis, [(i, (i + by) % peers) for i in range(peers)])]
    unnamed x4 -> x0, waiting for transfers between devices: 25.7 us -> none
    pallas_call x0 -> x2, Pallas kernels: none -> 11 us  [the longest x1 9.17 us: fit(): pl.pallas_call(fit_kernel, out_shape=jax.ShapeDtypeStruct((8, 128), jnp.f...]
    all_to_all x1 -> x0, blocking collectives: 8.61 us -> none  [copy_for_each(): lax.all_to_all(jnp.broadcast_to(value[None], (peers, *value.shape)), axis...]
  transfers between devices with their start and end apart: 10 -> 32, of which waited for: 6 -> 17; matrix products, arithmetic and copies ran while one was open for 0% -> 13% of each run, Pallas kernels for 0% -> 0%
where the time goes in v1:
time: 156 us; the launch traced here: 155 us
  starting transfers between devices  66.4 us (43%)
  waiting for transfers between devices  51.6 us (33%)
  local copies, waits for them, and re-layouts  12.3 us (8%)
  Pallas kernels  11 us (7%)
  matrix products  9.24 us (6%)
  other arithmetic  3.66 us (2%)
    ppermute x27, starting transfers between devices, shifted(): lax.ppermute(value, axis, [(i, (i + by) % peers) for i in range(peers)])  45.7 us
    ppermute x27, waiting for transfers between devices, shifted(): lax.ppermute(value, axis, [(i, (i + by) % peers) for i in range(peers)])  32.9 us
    all_to_all x1, waiting for transfers between devices, shards(): lax.all_to_all(summed.reshape(16, rows // 16, -1), PLANE, 0, 0, tiled=True)  9.45 us
    dot_general x18, matrix products, term(): return jnp.dot(rows, vecs[q], preferred_element_type=jnp.float32)  9.24 us
    pallas_call x1, Pallas kernels, fit(): pl.pallas_call(fit_kernel, out_shape=jax.ShapeDtypeStruct((8, 128), jnp.f...  9.17 us
    unnamed x17, local copies, waits for them, and re-layouts  7.83 us
    all_to_all x1, starting transfers between devices, shards(): lax.all_to_all(summed.reshape(16, rows // 16, -1), PLANE, 0, 0, tiled=True)  7.65 us
    all_to_all x1, waiting for transfers between devices, shards(): lax.all_to_all(jnp.broadcast_to(fitted[None], (32, 8)), LAYER, 0, 0, tile...  7.27 us
  transfers between devices with their start and end apart: 32, of which 17 were waited for; matrix products, arithmetic and copies ran while one was open for 13% of the time, Pallas kernels for 0%

profile of v1, /device:TPU:96, one launch (start us, length us, event | category | flops | bytes accessed | tf_op | source)
XLA Modules:
  0.0 155.2 jit_solution(2304928276613585391)
XLA Ops:
  0.6 1.8 %weigh.1 = bf16[128,1024]{1,0:T(8,128)(2,1)} custom-call(bf16[64,1024]{1,0:T(8,128)(2,1)} %resp_ref.1, bf16[64,1024]{1,0:T(8,128)(2,1)} %weight_ref.1, f32[1,1024]{1,0:T(1,128)} %bitcast.94), custom_call_target="tpu_custom_call" | custom-call | tf_op jit(solution)/shard_map/weigh/pallas_call | solution.py:45
  2.5 1.5 collective-permute-start.1
  4.0 1.6 %collective-permute-start.3 = (bf16[128,1024]{1,0:T(8,128)(2,1)}, bf16[128,1024]{1,0:T(8,128)(2,1)S(1)}, u32[]{:S(2)}, u32[]{:S(2)}) collective-permute-start(bf16[128,1024]{1,0:T(8,128)(2,1)} %weigh.1), channel_id=1, source_target_pairs={{0,128},{128,0},{1,129},{129,1},{2,130},{130,2},{3,131},{131,3},{4... | collective-permute-start | bytes 786440 | tf_op jit(solution)/shard_map/gather_rows/ppermute | solution.py:24
  5.5 1.7 %collective-permute-start = (bf16[128,1024]{1,0:T(8,128)(2,1)}, bf16[128,1024]{1,0:T(8,128)(2,1)}, u32[]{:S(2)}, u32[]{:S(2)}) collective-permute-start(bf16[128,1024]{1,0:T(8,128)(2,1)} %weigh.1), channel_id=1, source_target_pairs={{0,96},{32,0},{64,32},{96,64},{1,97},{33,1},{65,33},{97,65},{2,98}... | collective-permute-start | bytes 786440 | tf_op jit(solution)/shard_map/gather_rows/ppermute | solution.py:24
  7.3 0.5 collective-permute-start.26
  7.8 1.7 %bitcast_dynamic-update-slice_fusion.6 = bf16[8,128,1024]{2,1,0:T(8,128)(2,1)} fusion(bf16[128,1024]{1,0:T(8,128)(2,1)} %weigh.1), kind=kLoop, calls=%fused_computation.57 | loop fusion | bytes 524288
  9.4 2.5 %collective-permute-done.1 = bf16[128,1024]{1,0:T(8,128)(2,1)S(1)} collective-permute-done((bf16[128,1024]{1,0:T(8,128)(2,1)}, bf16[128,1024]{1,0:T(8,128)(2,1)S(1)}, u32[]{:S(2)}, u32[]{:S(2)}) %collective-permute-start.1) | collective-permute-done | bytes 262176 | tf_op jit(solution)/shard_map/gather_rows/ppermute | solution.py:24
  12.2 1.6 %collective-permute-start.5 = (bf16[128,1024]{1,0:T(8,128)(2,1)S(1)}, bf16[128,1024]{1,0:T(8,128)(2,1)S(1)}, u32[]{:S(2)}, u32[]{:S(2)}) collective-permute-start(bf16[128,1024]{1,0:T(8,128)(2,1)S(1)} %collective-permute-done.1), channel_id=1, source_target_pairs={{0,128},{128,0},{1,129},{129,1},{2,130},{130,2},{3,131},{131,3},{4... | collective-permute-start | bytes 786440 | tf_op jit(solution)/shard_map/gather_rows/ppermute | solution.py:24
  13.8 3.0 %collective-permute-start.4 = (bf16[128,1024]{1,0:T(8,128)(2,1)S(1)}, bf16[128,1024]{1,0:T(8,128)(2,1)S(1)}, u32[]{:S(2)}, u32[]{:S(2)}) collective-permute-start(bf16[128,1024]{1,0:T(8,128)(2,1)S(1)} %collective-permute-done.3), channel_id=1, source_target_pairs={{0,96},{32,0},{64,32},{96,64},{1,97},{33,1},{65,33},{97,65},{2,98}... | collective-permute-start | bytes 786440 | tf_op jit(solution)/shard_map/gather_rows/ppermute | solution.py:24
  16.8 0.7 pad_maximum_fusion
  17.4 0.7 broadcast_in_dim.17
  18.1 3.3 %all-to-all-start.1 = ((f32[8,1,2048]{2,1,0:T(1,128)}), f32[8,1,2048]{2,1,0:T(1,128)S(1)}, u32[]{:S(2)}, u32[]{:S(2)}) async-start(f32[8,1,2048]{2,1,0:T(1,128)} %broadcast_in_dim.17), calls=%async_computation.1 | async-start | bytes 131072 | tf_op jit(solution)/shard_map/gather_values/all_to_all | solution.py:179
  21.5 1.8 %bitcast_dynamic-update-slice_fusion.5 = bf16[8,128,1024]{2,1,0:T(8,128)(2,1)} fusion(bf16[8,128,1024]{2,1,0:T(8,128)(2,1)} %bitcast_dynamic-update-slice_fusion.6, bf16[128,1024]{1,0:T(8,128)(2,1)} %collective-permute-done), kind=kLoop, calls=%fused_computation.56 | loop fusion | bytes 524288
  23.3 2.0 %collective-permute-start.6 = (bf16[48,1024]{1,0:T(8,128)(2,1)S(1)}, bf16[48,1024]{1,0:T(8,128)(2,1)S(1)}, u32[]{:S(2)}, u32[]{:S(2)}) collective-permute-start(bf16[48,1024]{1,0:T(8,128)(2,1)S(1)} %slice.257), channel_id=1, source_target_pairs={{0,32},{32,64},{64,96},{96,0},{1,33},{33,65},{65,97},{97,1},{2,34}... | collective-permute-start | bytes 294920 | tf_op jit(solution)/shard_map/gather_rows/ppermute | solution.py:24
  25.3 1.6 %collective-permute-start.8 = (bf16[32,1024]{1,0:T(8,128)(2,1)S(1)}, bf16[32,1024]{1,0:T(8,128)(2,1)S(1)}, u32[]{:S(2)}, u32[]{:S(2)}) collective-permute-start(bf16[32,1024]{1,0:T(8,128)(2,1)S(1)} %slice.259), channel_id=1, source_target_pairs={{0,128},{128,0},{1,129},{129,1},{2,130},{130,2},{3,131},{131,3},{4... | collective-permute-start | bytes 196616 | tf_op jit(solution)/shard_map/gather_rows/ppermute | solution.py:24
  26.9 1.8 %collective-permute-start.7 = (bf16[48,1024]{1,0:T(8,128)(2,1)S(1)}, bf16[48,1024]{1,0:T(8,128)(2,1)S(1)}, u32[]{:S(2)}, u32[]{:S(2)}) collective-permute-start(bf16[48,1024]{1,0:T(8,128)(2,1)S(1)} %slice.258), channel_id=1, source_target_pairs={{0,96},{32,0},{64,32},{96,64},{1,97},{33,1},{65,33},{97,65},{2,98}... | collective-permute-start | bytes 294920 | tf_op jit(solution)/shard_map/gather_rows/ppermute | solution.py:24
  28.7 0.7 bitcast_dynamic-update-slice_fusion.4
  29.5 0.7 bitcast_dynamic-update-slice_fusion.3
  30.2 0.7 bitcast_dynamic-update-slice_fusion.2
  30.9 0.7 bitcast_dynamic-update-slice_fusion.1
  31.7 0.7 fusion.16
  32.4 0.7 bitcast_dynamic-update-slice_fusion
  33.1 1.5 convolution_convert_fusion.3
  34.6 3.2 %collective-permute-start.9 = (bf16[64,1024]{1,0:T(8,128)(2,1)S(1)}, bf16[64,1024]{1,0:T(8,128)(2,1)S(1)}, u32[]{:S(2)}, u32[]{:S(2)}) collective-permute-start(bf16[64,1024]{1,0:T(8,128)(2,1)S(1)} %convolution_convert_fusion.3), channel_id=1, source_target_pairs={{0,2},{2,4},{4,6},{6,8},{8,10},{10,12},{12,14},{14,0},{1,3},{3,5},... | collective-permute-start | bytes 393224 | tf_op jit(solution)/shard_map/sum_layers/ppermute | solution.py:24
  37.9 0.5 convolution_convert_fusion.2
  38.4 1.9 %collective-permute-done.9 = bf16[64,1024]{1,0:T(8,128)(2,1)S(1)} collective-permute-done((bf16[64,1024]{1,0:T(8,128)(2,1)S(1)}, bf16[64,1024]{1,0:T(8,128)(2,1)S(1)}, u32[]{:S(2)}, u32[]{:S(2)}) %collective-permute-start.9) | collective-permute-done | bytes 131104 | tf_op jit(solution)/shard_map/sum_layers/ppermute | solution.py:24
  40.8 3.7 %collective-permute-start.10 = (bf16[128,1024]{1,0:T(8,128)(2,1)S(1)}, bf16[128,1024]{1,0:T(8,128)(2,1)S(1)}, u32[]{:S(2)}, u32[]{:S(2)}) collective-permute-start(bf16[128,1024]{1,0:T(8,128)(2,1)S(1)} %fusion.6), channel_id=1, source_target_pairs={{0,2},{2,4},{4,6},{6,8},{8,10},{10,12},{12,14},{14,0},{1,3},{3,5},... | collective-permute-start | bytes 786440 | tf_op jit(solution)/shard_map/sum_layers/ppermute | solution.py:24
  45.3 4.0 %collective-permute-done.10 = bf16[128,1024]{1,0:T(8,128)(2,1)S(1)} collective-permute-done((bf16[128,1024]{1,0:T(8,128)(2,1)S(1)}, bf16[128,1024]{1,0:T(8,128)(2,1)S(1)}, u32[]{:S(2)}, u32[]{:S(2)}) %collective-permute-start.10) | collective-permute-done | bytes 262176 | tf_op jit(solution)/shard_map/sum_layers/ppermute | solution.py:24
  49.8 3.8 %collective-permute-start.11 = (bf16[128,1024]{1,0:T(8,128)(2,1)S(1)}, bf16[128,1024]{1,0:T(8,128)(2,1)S(1)}, u32[]{:S(2)}, u32[]{:S(2)}) collective-permute-start(bf16[128,1024]{1,0:T(8,128)(2,1)S(1)} %fusion.5), channel_id=1, source_target_pairs={{0,2},{2,4},{4,6},{6,8},{8,10},{10,12},{12,14},{14,0},{1,3},{3,5},... | collective-permute-start | bytes 786440 | tf_op jit(solution)/shard_map/sum_layers/ppermute | solution.py:24
  53.6 0.5 collective-permute-done.14
  54.6 4.9 %collective-permute-done.11 = bf16[128,1024]{1,0:T(8,128)(2,1)S(1)} collective-permute-done((bf16[128,1024]{1,0:T(8,128)(2,1)S(1)}, bf16[128,1024]{1,0:T(8,128)(2,1)S(1)}, u32[]{:S(2)}, u32[]{:S(2)}) %collective-permute-start.11) | collective-permute-done | bytes 262176 | tf_op jit(solution)/shard_map/sum_layers/ppermute | solution.py:24
  60.0 3.8 %collective-permute-start.12 = (bf16[128,1024]{1,0:T(8,128)(2,1)S(1)}, bf16[128,1024]{1,0:T(8,128)(2,1)S(1)}, u32[]{:S(2)}, u32[]{:S(2)}) collective-permute-start(bf16[128,1024]{1,0:T(8,128)(2,1)S(1)} %fusion.4), channel_id=1, source_target_pairs={{0,2},{2,4},{4,6},{6,8},{8,10},{10,12},{12,14},{14,0},{1,3},{3,5},... | collective-permute-start | bytes 786440 | tf_op jit(solution)/shard_map/sum_layers/ppermute | solution.py:24
  63.8 0.8 collective-permute-done.15
  65.1 0.5 convolution_convert_fusion.1
  65.6 3.3 %collective-permute-start.18 = (bf16[64,1024]{1,0:T(8,128)(2,1)S(1)}, bf16[64,1024]{1,0:T(8,128)(2,1)S(1)}, u32[]{:S(2)}, u32[]{:S(2)}) collective-permute-start(bf16[64,1024]{1,0:T(8,128)(2,1)S(1)} %convolution_convert_fusion.1), channel_id=1, source_target_pairs={{0,2},{2,4},{4,6},{6,8},{8,10},{10,12},{12,14},{14,0},{1,3},{3,5},... | collective-permute-start | bytes 393224 | tf_op jit(solution)/shard_map/sum_layers/ppermute | solution.py:24
  68.9 0.5 convolution_convert_fusion
  69.5 2.4 %collective-permute-done.18 = bf16[64,1024]{1,0:T(8,128)(2,1)S(1)} collective-permute-done((bf16[64,1024]{1,0:T(8,128)(2,1)S(1)}, bf16[64,1024]{1,0:T(8,128)(2,1)S(1)}, u32[]{:S(2)}, u32[]{:S(2)}) %collective-permute-start.18) | collective-permute-done | bytes 131104 | tf_op jit(solution)/shard_map/sum_layers/ppermute | solution.py:24
  72.3 3.8 %collective-permute-start.19 = (bf16[128,1024]{1,0:T(8,128)(2,1)S(1)}, bf16[128,1024]{1,0:T(8,128)(2,1)S(1)}, u32[]{:S(2)}, u32[]{:S(2)}) collective-permute-start(bf16[128,1024]{1,0:T(8,128)(2,1)S(1)} %fusion.12), channel_id=1, source_target_pairs={{0,2},{2,4},{4,6},{6,8},{8,10},{10,12},{12,14},{14,0},{1,3},{3,5},... | collective-permute-start | bytes 786440 | tf_op jit(solution)/shard_map/sum_layers/ppermute | solution.py:24
  76.1 0.8 collective-permute-done.22
  77.4 3.5 %collective-permute-done.19 = bf16[128,1024]{1,0:T(8,128)(2,1)S(1)} collective-permute-done((bf16[128,1024]{1,0:T(8,128)(2,1)S(1)}, bf16[128,1024]{1,0:T(8,128)(2,1)S(1)}, u32[]{:S(2)}, u32[]{:S(2)}) %collective-permute-start.19) | collective-permute-done | bytes 262176 | tf_op jit(solution)/shard_map/sum_layers/ppermute | solution.py:24
  81.4 3.8 %collective-permute-start.20 = (bf16[128,1024]{1,0:T(8,128)(2,1)S(1)}, bf16[128,1024]{1,0:T(8,128)(2,1)S(1)}, u32[]{:S(2)}, u32[]{:S(2)}) collective-permute-start(bf16[128,1024]{1,0:T(8,128)(2,1)S(1)} %fusion.11), channel_id=1, source_target_pairs={{0,2},{2,4},{4,6},{6,8},{8,10},{10,12},{12,14},{14,0},{1,3},{3,5},... | collective-permute-start | bytes 786440 | tf_op jit(solution)/shard_map/sum_layers/ppermute | solution.py:24
  85.1 1.0 collective-permute-done.23
  86.7 2.6 %collective-permute-done.20 = bf16[128,1024]{1,0:T(8,128)(2,1)S(1)} collective-permute-done((bf16[128,1024]{1,0:T(8,128)(2,1)S(1)}, bf16[128,1024]{1,0:T(8,128)(2,1)S(1)}, u32[]{:S(2)}, u32[]{:S(2)}) %collective-permute-start.20) | collective-permute-done | bytes 262176 | tf_op jit(solution)/shard_map/sum_layers/ppermute | solution.py:24
  89.7 4.0 %collective-permute-start.21 = (bf16[128,1024]{1,0:T(8,128)(2,1)S(1)}, bf16[128,1024]{1,0:T(8,128)(2,1)S(1)}, u32[]{:S(2)}, u32[]{:S(2)}) collective-permute-start(bf16[128,1024]{1,0:T(8,128)(2,1)S(1)} %fusion.10), channel_id=1, source_target_pairs={{0,2},{2,4},{4,6},{6,8},{8,10},{10,12},{12,14},{14,0},{1,3},{3,5},... | collective-permute-start | bytes 786440 | tf_op jit(solution)/shard_map/sum_layers/ppermute | solution.py:24
  93.7 0.8 collective-permute-done.24
  95.6 2.0 %collective-permute-done.21 = bf16[128,1024]{1,0:T(8,128)(2,1)S(1)} collective-permute-done((bf16[128,1024]{1,0:T(8,128)(2,1)S(1)}, bf16[128,1024]{1,0:T(8,128)(2,1)S(1)}, u32[]{:S(2)}, u32[]{:S(2)}) %collective-permute-start.21) | collective-permute-done | bytes 262176 | tf_op jit(solution)/shard_map/sum_layers/ppermute | solution.py:24
  97.6 5.0 %collective-permute-done.25 = bf16[128,1024]{1,0:T(8,128)(2,1)S(1)} collective-permute-done((bf16[128,1024]{1,0:T(8,128)(2,1)S(1)}, bf16[128,1024]{1,0:T(8,128)(2,1)S(1)}, u32[]{:S(2)}, u32[]{:S(2)}) %collective-permute-start.25) | collective-permute-done | bytes 262176 | tf_op jit(solution)/shard_map/sum_layers/ppermute | solution.py:24
  103.1 0.8 maximum_bitcast_fusion
  104.0 7.7 %all-to-all-start = ((bf16[16,8,2048]{2,1,0:T(8,128)(2,1)}), bf16[16,8,2048]{2,1,0:T(8,128)(2,1)S(1)}, u32[]{:S(2)}, u32[]{:S(2)}) async-start(bf16[16,8,2048]{2,1,0:T(8,128)(2,1)} %maximum_bitcast_fusion), calls=%async_computation | async-start | bytes 1048576 | tf_op jit(solution)/shard_map/to_components/all_to_all | solution.py:219
  111.7 0.6 copy.15
  112.3 9.4 %all-to-all-done = bf16[16,8,2048]{2,1,0:T(8,128)(2,1)S(1)} async-done(((bf16[16,8,2048]{2,1,0:T(8,128)(2,1)}), bf16[16,8,2048]{2,1,0:T(8,128)(2,1)S(1)}, u32[]{:S(2)}, u32[]{:S(2)}) %all-to-all-start) | async-done | bytes 524320 | tf_op jit(solution)/shard_map/to_components/all_to_all | solution.py:219
  121.8 0.8 copy-done.2
  122.6 9.2 %fit.1 = f32[8,128]{1,0:T(8,128)} custom-call(bf16[128,2048]{1,0:T(8,128)(2,1)} %bitcast.91, f32[8,2048]{1,0:T(8,128)} %bitcast.92), custom_call_target="tpu_custom_call" | custom-call | tf_op jit(solution)/shard_map/fit/pallas_call | solution.py:120
  131.7 0.8 slice_reduce_fusion
  132.5 0.6 broadcast_in_dim.19
  133.1 3.8 %all-to-all-start.2 = ((f32[32,1,8]{2,1,0:T(1,128)}), f32[32,1,8]{2,1,0:T(1,128)S(1)}, u32[]{:S(2)}, u32[]{:S(2)}) async-start(f32[32,1,8]{2,1,0:T(1,128)} %broadcast_in_dim.19), calls=%async_computation.2 | async-start | bytes 32768 | tf_op jit(solution)/shard_map/gather_scores/all_to_all | solution.py:225
  137.1 7.3 %all-to-all-done.2 = f32[32,1,8]{2,1,0:T(1,128)S(1)} async-done(((f32[32,1,8]{2,1,0:T(1,128)}), f32[32,1,8]{2,1,0:T(1,128)S(1)}, u32[]{:S(2)}, u32[]{:S(2)}) %all-to-all-start.2) | async-done | bytes 1056 | tf_op jit(solution)/shard_map/gather_scores/all_to_all | solution.py:225
  144.3 0.5 broadcast.128
  144.9 0.7 reduce.5
  145.9 1.9 %collective-permute-start.27 = (f32[8]{0:T(128)S(1)}, f32[8]{0:T(128)S(1)}, u32[]{:S(2)}, u32[]{:S(2)}) collective-permute-start(f32[8]{0:T(128)S(1)} %get-tuple-element.4), channel_id=1, source_target_pairs={{0,2},{2,4},{4,6},{6,8},{8,10},{10,12},{12,14},{1,3},{3,5},{5,7},{... | collective-permute-start | bytes 104 | tf_op jit(solution)/shard_map/gather_scores/ppermute | solution.py:232
  147.8 3.9 %collective-permute-start.28 = (f32[8]{0:T(128)S(1)}, f32[8]{0:T(128)S(1)}, u32[]{:S(2)}, u32[]{:S(2)}) collective-permute-start(f32[8]{0:T(128)S(1)} %get-tuple-element.5), channel_id=1, source_target_pairs={{2,0},{4,2},{6,4},{8,6},{10,8},{12,10},{14,12},{3,1},{5,3},{7,5},{... | collective-permute-start | bytes 104 | tf_op jit(solution)/shard_map/gather_scores/ppermute | solution.py:233
  151.8 0.6 dynamic_slice.54
  152.4 2.0 %collective-permute-done.28 = f32[8]{0:T(128)S(1)} collective-permute-done((f32[8]{0:T(128)S(1)}, f32[8]{0:T(128)S(1)}, u32[]{:S(2)}, u32[]{:S(2)}) %collective-permute-start.28) | collective-permute-done | bytes 64 | tf_op jit(solution)/shard_map/gather_scores/ppermute | solution.py:233
  154.6 0.6 add_divide_fusion
  (63 shorter events, 8.2 us)
Async XLA Ops:
  2.5 9.5 %collective-permute-start.1 = (bf16[128,1024]{1,0:T(8,128)(2,1)}, bf16[128,1024]{1,0:T(8,128)(2,1)S(1)}, u32[]{:S(2)}, u32[]{:S(2)}) collective-permute-start(bf16[128,1024]{1,0:T(8,128)(2,1)} %weigh.1), channel_id=1, source_target_pairs={{0,32},{32,64},{64,96},{96,0},{1,33},{33,65},{65,97},{97,1},{2,34}... | collective-permute-start | bytes 786440 | tf_op jit(solution)/shard_map/gather_rows/ppermute | solution.py:24
  4.0 9.8 %collective-permute-start.3 = (bf16[128,1024]{1,0:T(8,128)(2,1)}, bf16[128,1024]{1,0:T(8,128)(2,1)S(1)}, u32[]{:S(2)}, u32[]{:S(2)}) collective-permute-start(bf16[128,1024]{1,0:T(8,128)(2,1)} %weigh.1), channel_id=1, source_target_pairs={{0,128},{128,0},{1,129},{129,1},{2,130},{130,2},{3,131},{131,3},{4... | collective-permute-start | bytes 786440 | tf_op jit(solution)/shard_map/gather_rows/ppermute | solution.py:24
  5.5 15.9 %collective-permute-start = (bf16[128,1024]{1,0:T(8,128)(2,1)}, bf16[128,1024]{1,0:T(8,128)(2,1)}, u32[]{:S(2)}, u32[]{:S(2)}) collective-permute-start(bf16[128,1024]{1,0:T(8,128)(2,1)} %weigh.1), channel_id=1, source_target_pairs={{0,96},{32,0},{64,32},{96,64},{1,97},{33,1},{65,33},{97,65},{2,98}... | collective-permute-start | bytes 786440 | tf_op jit(solution)/shard_map/gather_rows/ppermute | solution.py:24
  7.3 57.8 %collective-permute-start.17 = (bf16[1024,1024]{1,0:T(8,128)(2,1)}, bf16[1024,1024]{1,0:T(8,128)(2,1)S(1)}, u32[]{:S(2)}, u32[]{:S(2)}) collective-permute-start(bf16[1024,1024]{1,0:T(8,128)(2,1)} %param.10), channel_id=1, source_target_pairs={{0,16},{16,0},{1,17},{17,1},{2,18},{18,2},{3,19},{19,3},{4,20},{20... | collective-permute-start | bytes 6291464 | tf_op jit(solution)/shard_map/swap_eigvecs/ppermute | solution.py:24
  7.3 4.9 %collective-permute-start.26 = (f32[1024]{0:T(1024)}, f32[1024]{0:T(1024)S(1)}, u32[]{:S(2)}, u32[]{:S(2)}) collective-permute-start(f32[1024]{0:T(1024)} %param.11), channel_id=1, source_target_pairs={{0,16},{16,0},{1,17},{17,1},{2,18},{18,2},{3,19},{19,3},{4,20},{20... | collective-permute-start | bytes 12296 | tf_op jit(solution)/shard_map/swap_eigvecs/ppermute | solution.py:24
  11.9 13.4 %collective-permute-start.2 = (bf16[128,1024]{1,0:T(8,128)(2,1)S(1)}, bf16[128,1024]{1,0:T(8,128)(2,1)S(1)}, u32[]{:S(2)}, u32[]{:S(2)}) collective-permute-start(bf16[128,1024]{1,0:T(8,128)(2,1)S(1)} %collective-permute-done.1), channel_id=1, source_target_pairs={{0,32},{32,64},{64,96},{96,0},{1,33},{33,65},{65,97},{97,1},{2,34}... | collective-permute-start | bytes 786440 | tf_op jit(solution)/shard_map/gather_rows/ppermute | solution.py:24
  12.2 11.1 %collective-permute-start.5 = (bf16[128,1024]{1,0:T(8,128)(2,1)S(1)}, bf16[128,1024]{1,0:T(8,128)(2,1)S(1)}, u32[]{:S(2)}, u32[]{:S(2)}) collective-permute-start(bf16[128,1024]{1,0:T(8,128)(2,1)S(1)} %collective-permute-done.1), channel_id=1, source_target_pairs={{0,128},{128,0},{1,129},{129,1},{2,130},{130,2},{3,131},{131,3},{4... | collective-permute-start | bytes 786440 | tf_op jit(solution)/shard_map/gather_rows/ppermute | solution.py:24
  13.8 13.1 %collective-permute-start.4 = (bf16[128,1024]{1,0:T(8,128)(2,1)S(1)}, bf16[128,1024]{1,0:T(8,128)(2,1)S(1)}, u32[]{:S(2)}, u32[]{:S(2)}) collective-permute-start(bf16[128,1024]{1,0:T(8,128)(2,1)S(1)} %collective-permute-done.3), channel_id=1, source_target_pairs={{0,96},{32,0},{64,32},{96,64},{1,97},{33,1},{65,33},{97,65},{2,98}... | collective-permute-start | bytes 786440 | tf_op jit(solution)/shard_map/gather_rows/ppermute | solution.py:24
  18.1 85.9 %all-to-all-start.1 = ((f32[8,1,2048]{2,1,0:T(1,128)}), f32[8,1,2048]{2,1,0:T(1,128)S(1)}, u32[]{:S(2)}, u32[]{:S(2)}) async-start(f32[8,1,2048]{2,1,0:T(1,128)} %broadcast_in_dim.17), calls=%async_computation.1 | async-start | bytes 131072 | tf_op jit(solution)/shard_map/gather_values/all_to_all | solution.py:179
  21.5 11.6 %copy-start = (bf16[1024,1024]{1,0:T(8,128)(2,1)S(1)}, bf16[1024,1024]{1,0:T(8,128)(2,1)}, u32[]{:S(2)}) copy-start(bf16[1024,1024]{1,0:T(8,128)(2,1)} %param.10) | copy-start | bytes 6291460
  23.3 8.3 %collective-permute-start.6 = (bf16[48,1024]{1,0:T(8,128)(2,1)S(1)}, bf16[48,1024]{1,0:T(8,128)(2,1)S(1)}, u32[]{:S(2)}, u32[]{:S(2)}) collective-permute-start(bf16[48,1024]{1,0:T(8,128)(2,1)S(1)} %slice.257), channel_id=1, source_target_pairs={{0,32},{32,64},{64,96},{96,0},{1,33},{33,65},{65,97},{97,1},{2,34}... | collective-permute-start | bytes 294920 | tf_op jit(solution)/shard_map/gather_rows/ppermute | solution.py:24
  25.3 6.3 %collective-permute-start.8 = (bf16[32,1024]{1,0:T(8,128)(2,1)S(1)}, bf16[32,1024]{1,0:T(8,128)(2,1)S(1)}, u32[]{:S(2)}, u32[]{:S(2)}) collective-permute-start(bf16[32,1024]{1,0:T(8,128)(2,1)S(1)} %slice.259), channel_id=1, source_target_pairs={{0,128},{128,0},{1,129},{129,1},{2,130},{130,2},{3,131},{131,3},{4... | collective-permute-start | bytes 196616 | tf_op jit(solution)/shard_map/gather_rows/ppermute | solution.py:24
  26.9 4.7 %collective-permute-start.7 = (bf16[48,1024]{1,0:T(8,128)(2,1)S(1)}, bf16[48,1024]{1,0:T(8,128)(2,1)S(1)}, u32[]{:S(2)}, u32[]{:S(2)}) collective-permute-start(bf16[48,1024]{1,0:T(8,128)(2,1)S(1)} %slice.258), channel_id=1, source_target_pairs={{0,96},{32,0},{64,32},{96,64},{1,97},{33,1},{65,33},{97,65},{2,98}... | collective-permute-start | bytes 294920 | tf_op jit(solution)/shard_map/gather_rows/ppermute | solution.py:24
  33.1 4.8 %copy-start.1 = (bf16[8,128,1024]{2,1,0:T(8,128)(2,1)S(1)}, bf16[8,128,1024]{2,1,0:T(8,128)(2,1)}, u32[]{:S(2)}) copy-start(bf16[8,128,1024]{2,1,0:T(8,128)(2,1)} %bitcast_dynamic-update-slice_fusion) | copy-start | bytes 6291460
  34.6 5.7 %collective-permute-start.9 = (bf16[64,1024]{1,0:T(8,128)(2,1)S(1)}, bf16[64,1024]{1,0:T(8,128)(2,1)S(1)}, u32[]{:S(2)}, u32[]{:S(2)}) collective-permute-start(bf16[64,1024]{1,0:T(8,128)(2,1)S(1)} %convolution_convert_fusion.3), channel_id=1, source_target_pairs={{0,2},{2,4},{4,6},{6,8},{8,10},{10,12},{12,14},{14,0},{1,3},{3,5},... | collective-permute-start | bytes 393224 | tf_op jit(solution)/shard_map/sum_layers/ppermute | solution.py:24
  38.3 6.3 %collective-permute-start.13 = (bf16[64,1024]{1,0:T(8,128)(2,1)S(1)}, bf16[64,1024]{1,0:T(8,128)(2,1)S(1)}, u32[]{:S(2)}, u32[]{:S(2)}) collective-permute-start(bf16[64,1024]{1,0:T(8,128)(2,1)S(1)} %convolution_convert_fusion.2), channel_id=1, source_target_pairs={{0,14},{2,0},{4,2},{6,4},{8,6},{10,8},{12,10},{14,12},{1,15},{3,1}... | collective-permute-start | bytes 393224 | tf_op jit(solution)/shard_map/sum_layers/ppermute | solution.py:24
  40.8 8.5 %collective-permute-start.10 = (bf16[128,1024]{1,0:T(8,128)(2,1)S(1)}, bf16[128,1024]{1,0:T(8,128)(2,1)S(1)}, u32[]{:S(2)}, u32[]{:S(2)}) collective-permute-start(bf16[128,1024]{1,0:T(8,128)(2,1)S(1)} %fusion.6), channel_id=1, source_target_pairs={{0,2},{2,4},{4,6},{6,8},{8,10},{10,12},{12,14},{14,0},{1,3},{3,5},... | collective-permute-start | bytes 786440 | tf_op jit(solution)/shard_map/sum_layers/ppermute | solution.py:24
  45.0 9.0 %collective-permute-start.14 = (bf16[128,1024]{1,0:T(8,128)(2,1)S(1)}, bf16[128,1024]{1,0:T(8,128)(2,1)S(1)}, u32[]{:S(2)}, u32[]{:S(2)}) collective-permute-start(bf16[128,1024]{1,0:T(8,128)(2,1)S(1)} %fusion.9), channel_id=1, source_target_pairs={{0,14},{2,0},{4,2},{6,4},{8,6},{10,8},{12,10},{14,12},{1,15},{3,1}... | collective-permute-start | bytes 786440 | tf_op jit(solution)/shard_map/sum_layers/ppermute | solution.py:24
  49.8 9.7 %collective-permute-start.11 = (bf16[128,1024]{1,0:T(8,128)(2,1)S(1)}, bf16[128,1024]{1,0:T(8,128)(2,1)S(1)}, u32[]{:S(2)}, u32[]{:S(2)}) collective-permute-start(bf16[128,1024]{1,0:T(8,128)(2,1)S(1)} %fusion.5), channel_id=1, source_target_pairs={{0,2},{2,4},{4,6},{6,8},{8,10},{10,12},{12,14},{14,0},{1,3},{3,5},... | collective-permute-start | bytes 786440 | tf_op jit(solution)/shard_map/sum_layers/ppermute | solution.py:24
  54.5 10.1 %collective-permute-start.15 = (bf16[128,1024]{1,0:T(8,128)(2,1)S(1)}, bf16[128,1024]{1,0:T(8,128)(2,1)S(1)}, u32[]{:S(2)}, u32[]{:S(2)}) collective-permute-start(bf16[128,1024]{1,0:T(8,128)(2,1)S(1)} %fusion.8), channel_id=1, source_target_pairs={{0,14},{2,0},{4,2},{6,4},{8,6},{10,8},{12,10},{14,12},{1,15},{3,1}... | collective-permute-start | bytes 786440 | tf_op jit(solution)/shard_map/sum_layers/ppermute | solution.py:24
  60.0 35.1 %collective-permute-start.12 = (bf16[128,1024]{1,0:T(8,128)(2,1)S(1)}, bf16[128,1024]{1,0:T(8,128)(2,1)S(1)}, u32[]{:S(2)}, u32[]{:S(2)}) collective-permute-start(bf16[128,1024]{1,0:T(8,128)(2,1)S(1)} %fusion.4), channel_id=1, source_target_pairs={{0,2},{2,4},{4,6},{6,8},{8,10},{10,12},{12,14},{14,0},{1,3},{3,5},... | collective-permute-start | bytes 786440 | tf_op jit(solution)/shard_map/sum_layers/ppermute | solution.py:24
  65.0 30.1 %collective-permute-start.16 = (bf16[128,1024]{1,0:T(8,128)(2,1)S(1)}, bf16[128,1024]{1,0:T(8,128)(2,1)S(1)}, u32[]{:S(2)}, u32[]{:S(2)}) collective-permute-start(bf16[128,1024]{1,0:T(8,128)(2,1)S(1)} %fusion.7), channel_id=1, source_target_pairs={{0,14},{2,0},{4,2},{6,4},{8,6},{10,8},{12,10},{14,12},{1,15},{3,1}... | collective-permute-start | bytes 786440 | tf_op jit(solution)/shard_map/sum_layers/ppermute | solution.py:24
  65.6 6.2 %collective-permute-start.18 = (bf16[64,1024]{1,0:T(8,128)(2,1)S(1)}, bf16[64,1024]{1,0:T(8,128)(2,1)S(1)}, u32[]{:S(2)}, u32[]{:S(2)}) collective-permute-start(bf16[64,1024]{1,0:T(8,128)(2,1)S(1)} %convolution_convert_fusion.1), channel_id=1, source_target_pairs={{0,2},{2,4},{4,6},{6,8},{8,10},{10,12},{12,14},{14,0},{1,3},{3,5},... | collective-permute-start | bytes 393224 | tf_op jit(solution)/shard_map/sum_layers/ppermute | solution.py:24
  69.4 7.5 %collective-permute-start.22 = (bf16[64,1024]{1,0:T(8,128)(2,1)S(1)}, bf16[64,1024]{1,0:T(8,128)(2,1)S(1)}, u32[]{:S(2)}, u32[]{:S(2)}) collective-permute-start(bf16[64,1024]{1,0:T(8,128)(2,1)S(1)} %convolution_convert_fusion), channel_id=1, source_target_pairs={{0,14},{2,0},{4,2},{6,4},{8,6},{10,8},{12,10},{14,12},{1,15},{3,1}... | collective-permute-start | bytes 393224 | tf_op jit(solution)/shard_map/sum_layers/ppermute | solution.py:24
  72.3 8.6 %collective-permute-start.19 = (bf16[128,1024]{1,0:T(8,128)(2,1)S(1)}, bf16[128,1024]{1,0:T(8,128)(2,1)S(1)}, u32[]{:S(2)}, u32[]{:S(2)}) collective-permute-start(bf16[128,1024]{1,0:T(8,128)(2,1)S(1)} %fusion.12), channel_id=1, source_target_pairs={{0,2},{2,4},{4,6},{6,8},{8,10},{10,12},{12,14},{14,0},{1,3},{3,5},... | collective-permute-start | bytes 786440 | tf_op jit(solution)/shard_map/sum_layers/ppermute | solution.py:24
  77.4 8.8 %collective-permute-start.23 = (bf16[128,1024]{1,0:T(8,128)(2,1)S(1)}, bf16[128,1024]{1,0:T(8,128)(2,1)S(1)}, u32[]{:S(2)}, u32[]{:S(2)}) collective-permute-start(bf16[128,1024]{1,0:T(8,128)(2,1)S(1)} %fusion.15), channel_id=1, source_target_pairs={{0,14},{2,0},{4,2},{6,4},{8,6},{10,8},{12,10},{14,12},{1,15},{3,1}... | collective-permute-start | bytes 786440 | tf_op jit(solution)/shard_map/sum_layers/ppermute | solution.py:24
  81.4 7.9 %collective-permute-start.20 = (bf16[128,1024]{1,0:T(8,128)(2,1)S(1)}, bf16[128,1024]{1,0:T(8,128)(2,1)S(1)}, u32[]{:S(2)}, u32[]{:S(2)}) collective-permute-start(bf16[128,1024]{1,0:T(8,128)(2,1)S(1)} %fusion.11), channel_id=1, source_target_pairs={{0,2},{2,4},{4,6},{6,8},{8,10},{10,12},{12,14},{14,0},{1,3},{3,5},... | collective-permute-start | bytes 786440 | tf_op jit(solution)/shard_map/sum_layers/ppermute | solution.py:24
  86.6 7.9 %collective-permute-start.24 = (bf16[128,1024]{1,0:T(8,128)(2,1)S(1)}, bf16[128,1024]{1,0:T(8,128)(2,1)S(1)}, u32[]{:S(2)}, u32[]{:S(2)}) collective-permute-start(bf16[128,1024]{1,0:T(8,128)(2,1)S(1)} %fusion.14), channel_id=1, source_target_pairs={{0,14},{2,0},{4,2},{6,4},{8,6},{10,8},{12,10},{14,12},{1,15},{3,1}... | collective-permute-start | bytes 786440 | tf_op jit(solution)/shard_map/sum_layers/ppermute | solution.py:24
  89.7 7.9 %collective-permute-start.21 = (bf16[128,1024]{1,0:T(8,128)(2,1)S(1)}, bf16[128,1024]{1,0:T(8,128)(2,1)S(1)}, u32[]{:S(2)}, u32[]{:S(2)}) collective-permute-start(bf16[128,1024]{1,0:T(8,128)(2,1)S(1)} %fusion.10), channel_id=1, source_target_pairs={{0,2},{2,4},{4,6},{6,8},{8,10},{10,12},{12,14},{14,0},{1,3},{3,5},... | collective-permute-start | bytes 786440 | tf_op jit(solution)/shard_map/sum_layers/ppermute | solution.py:24
  95.0 7.7 %collective-permute-start.25 = (bf16[128,1024]{1,0:T(8,128)(2,1)S(1)}, bf16[128,1024]{1,0:T(8,128)(2,1)S(1)}, u32[]{:S(2)}, u32[]{:S(2)}) collective-permute-start(bf16[128,1024]{1,0:T(8,128)(2,1)S(1)} %fusion.13), channel_id=1, source_target_pairs={{0,14},{2,0},{4,2},{6,4},{8,6},{10,8},{12,10},{14,12},{1,15},{3,1}... | collective-permute-start | bytes 786440 | tf_op jit(solution)/shard_map/sum_layers/ppermute | solution.py:24
  95.6 16.1 %copy-start.3 = (s32[1024]{0:T(1024)S(1)}, s32[1024]{0:T(1024)}, u32[]{:S(2)}) copy-start(s32[1024]{0:T(1024)} %param.12) | copy-start | bytes 12292
  103.1 51.5 %copy-start.4 = (s32[64]{0:T(128)S(1)}, s32[64]{0:T(128)}, u32[]{:S(2)}) copy-start(s32[64]{0:T(128)} %param.13) | copy-start | bytes 772
  104.0 17.8 %all-to-all-start = ((bf16[16,8,2048]{2,1,0:T(8,128)(2,1)}), bf16[16,8,2048]{2,1,0:T(8,128)(2,1)S(1)}, u32[]{:S(2)}, u32[]{:S(2)}) async-start(bf16[16,8,2048]{2,1,0:T(8,128)(2,1)} %maximum_bitcast_fusion), calls=%async_computation | async-start | bytes 1048576 | tf_op jit(solution)/shard_map/to_components/all_to_all | solution.py:219
  121.8 0.8 copy-start.2
  133.1 11.2 %all-to-all-start.2 = ((f32[32,1,8]{2,1,0:T(1,128)}), f32[32,1,8]{2,1,0:T(1,128)S(1)}, u32[]{:S(2)}, u32[]{:S(2)}) async-start(f32[32,1,8]{2,1,0:T(1,128)} %broadcast_in_dim.19), calls=%async_computation.2 | async-start | bytes 32768 | tf_op jit(solution)/shard_map/gather_scores/all_to_all | solution.py:225
  145.9 6.6 %collective-permute-start.27 = (f32[8]{0:T(128)S(1)}, f32[8]{0:T(128)S(1)}, u32[]{:S(2)}, u32[]{:S(2)}) collective-permute-start(f32[8]{0:T(128)S(1)} %get-tuple-element.4), channel_id=1, source_target_pairs={{0,2},{2,4},{4,6},{6,8},{8,10},{10,12},{12,14},{1,3},{3,5},{5,7},{... | collective-permute-start | bytes 104 | tf_op jit(solution)/shard_map/gather_scores/ppermute | solution.py:232
  147.8 6.6 %collective-permute-start.28 = (f32[8]{0:T(128)S(1)}, f32[8]{0:T(128)S(1)}, u32[]{:S(2)}, u32[]{:S(2)}) collective-permute-start(f32[8]{0:T(128)S(1)} %get-tuple-element.5), channel_id=1, source_target_pairs={{2,0},{4,2},{6,4},{8,6},{10,8},{12,10},{14,12},{3,1},{5,3},{7,5},{... | collective-permute-start | bytes 104 | tf_op jit(solution)/shard_map/gather_scores/ppermute | solution.py:233

commit v2 on v0

v2 whole, which is shorter than its diff:
```python
import functools

import jax
import jax.numpy as jnp
from jax import lax
from jax.experimental import pallas as pl
from jax.experimental.pallas import tpu as pltpu
from jax.sharding import Mesh
from jax.sharding import PartitionSpec as P

ITERS = 4
HALO = 8
SAMP = ("samp_0", "samp_1", "samp_2")
CPG = ("cpg_0", "cpg_1")
PLANE = ("cpg_1", "samp_0", "samp_1")
FLOOR = ("samp_0", "samp_1")
LAYER = ("cpg_1", "samp_0", "samp_1", "samp_2")

EPSILON = 1e-06
band_width = 1000.0


def shifted(value, axis, by):
    peers = lax.axis_size(axis)
    return lax.ppermute(value, axis, [(i, (i + by) % peers) for i in range(peers)])


def fit_kernel(slot_ref, resp_ref, design_ref, values_ref, out_ref, r_ref, d_ref, w_ref):
    half, width = values_ref.shape
    lanes = 512
    for i in range(0, half, 16):
        for given, kept in ((resp_ref, r_ref), (design_ref, d_ref)):
            kept[i : i + 16, :] = given[i : i + 16, :].astype(jnp.float32) + given[
                half + i : half + i + 16, :
            ].astype(jnp.float32)
    blocks = [(i, j) for i in range(0, half, 8) for j in range(0, width, lanes)]

    def total(acc):
        acc = functools.reduce(jnp.add, [acc[:, k : k + 128] for k in range(0, lanes, 128)])
        acc = acc + pltpu.roll(acc, 4, 0)
        return jnp.broadcast_to(jnp.sum(acc, axis=1, keepdims=True), (8, 128))

    def wide(value):
        return jnp.concatenate([value] * (lanes // 128), axis=1)

    def sweep(scale, last):
        zero = jnp.zeros((8, lanes), jnp.float32)
        crossed, energy, traced, fisher = zero, zero, zero, zero
        scale = wide(scale)
        for i, j in blocks:
            at = (slice(i, i + 8), slice(j, j + lanes))
            lam, resp, design = values_ref[at], r_ref[at], d_ref[at]
            v = scale * lam + 1.0
            inv = pl.reciprocal(v, approx=True)
            inv = inv * (2.0 - v * inv)
            over = design * inv
            crossed = crossed + over * resp
            energy = energy + over * design
            if not last:
                lev = lam * inv
                traced = traced + lev
                fisher = fisher + lev * lev
                w_ref[at] = lev * inv
        return total(crossed), total(energy) + EPSILON, traced, fisher

    log_scale = jnp.zeros((8, 128), jnp.float32)
    for _ in range(ITERS):
        scale = jnp.exp(log_scale)
        crossed, energy, traced, fisher = sweep(scale, False)
        effect = wide(crossed / energy)
        spread = jnp.zeros((8, lanes), jnp.float32)
        for i, j in blocks:
            at = (slice(i, i + 8), slice(j, j + lanes))
            residual = r_ref[at] - effect * d_ref[at]
            spread = spread + w_ref[at] * residual * residual
        gradient = 0.5 * (total(spread) - total(traced))
        log_scale = log_scale + jnp.tanh(gradient / (scale * (0.5 * total(fisher))))
    crossed, energy, _, _ = sweep(jnp.exp(log_scale), True)
    score = crossed / jnp.sqrt(energy)
    lane = lax.broadcasted_iota(jnp.int32, (8, 128), 1)
    row = lax.broadcasted_iota(jnp.int32, (8, 128), 0)
    here = (row < 4) & (lane == 4 * slot_ref[0] + row)
    both = [jnp.sum(jnp.where(here, v, 0.0), axis=0, keepdims=True) for v in (score, log_scale)]
    out_ref[...] = jnp.broadcast_to(
        jnp.concatenate(both, axis=1)[None], (out_ref.shape[0], 1, 256)
    )


def fit(slot, resp, design, values):
    rows, width = resp.shape
    vmem = pl.BlockSpec(memory_space=pltpu.VMEM)
    return pl.pallas_call(
        fit_kernel,
        out_shape=jax.ShapeDtypeStruct((32, 1, 256), jnp.float32),
        in_specs=[pl.BlockSpec(memory_space=pltpu.SMEM), vmem, vmem, vmem],
        out_specs=vmem,
        scratch_shapes=[pltpu.VMEM((rows // 2, width), jnp.float32)] * 3,
        compiler_params=pltpu.CompilerParams(vmem_limit_bytes=16 * 1024 * 1024),
    )(slot, resp, design, values)


def smooth_block(widened, places, present, reaches):
    block_len = reaches.shape[0]
    centre = places[HALO : HALO + block_len]
    total_sum = jnp.zeros((block_len,), jnp.float32)
    norm_sum = jnp.zeros((block_len,), jnp.float32)
    for offset in range(2 * HALO + 1):
        near_scores = widened[offset : offset + block_len]
        near_places = places[offset : offset + block_len]
        within = (abs(offset - HALO) <= reaches).astype(jnp.float32)
        kernel = (
            present[offset : offset + block_len]
            * within
            * jnp.exp(-jnp.abs(near_places - centre) / band_width)
        )
        total_sum = total_sum + kernel * near_scores
        norm_sum = norm_sum + kernel
    return total_sum / norm_sum


def copies(value, axes):
    peers = lax.axis_size(axes)
    return lax.all_to_all(
        jnp.broadcast_to(value[None], (peers, *value.shape)), axes, 0, 0, tiled=True
    )


def shards(responses, weights, phenotype, eigvecs, eigvals, positions, reaches):
    z = lax.axis_index("cpg_0")
    layers = lax.axis_size("cpg_0")
    rows = responses.shape[0]
    with jax.named_scope("weigh"):
        root = jnp.sqrt(weights.astype(jnp.float32))
        weighted = (root * responses.astype(jnp.float32)).astype(jnp.bfloat16)
        design = (root * phenotype[None, :]).astype(jnp.bfloat16)
    with jax.named_scope("gather_rows"):
        blocks = [copies(weighted, FLOOR), copies(design, FLOOR)]
    with jax.named_scope("swap_eigvecs"):
        vecs = jnp.concatenate([eigvecs, shifted(eigvecs, "samp_2", 1)], axis=1)
        values = jnp.concatenate([eigvals, shifted(eigvals, "samp_2", 1)])

    def term(t, ahead, lo, hi):
        dest = lax.rem(z + ahead + layers, layers)
        block = lax.dynamic_index_in_dim(blocks[t], dest, 0, keepdims=False)[lo:hi]
        return jnp.dot(block, vecs, preferred_element_type=jnp.float32)

    far = layers // 2
    cut = rows // 2
    sent = {}

    def first(t):
        sent[t, 1] = shifted(term(t, far, 0, cut).astype(jnp.bfloat16), "cpg_0", 1)
        sent[t, -1] = shifted(term(t, far, cut, rows).astype(jnp.bfloat16), "cpg_0", -1)

    def onward(t, ahead):
        for way in (1, -1):
            got = sent[t, way].astype(jnp.float32)
            if got.shape[0] < rows:
                rest = jnp.zeros_like(got)
                got = jnp.concatenate([got, rest] if way == 1 else [rest, got], axis=0)
            total = (term(t, way * ahead, 0, rows) + got).astype(jnp.bfloat16)
            sent[t, way] = shifted(total, "cpg_0", way)

    def exchanged(t):
        total = term(t, 0, 0, rows)
        for way in (1, -1):
            total = total + sent[t, way].astype(jnp.float32)
        return lax.all_to_all(total.astype(jnp.bfloat16), PLANE, 0, 0, tiled=True)

    with jax.named_scope("sum_layers"):
        first(0)
        onward(0, 3)
        first(1)
        onward(0, 2)
        onward(1, 3)
        onward(0, 1)
        onward(1, 2)
        sums = [exchanged(0)]
        onward(1, 1)
        sums.append(exchanged(1))
    with jax.named_scope("gather_values"):
        everywhere = jnp.repeat(copies(values, FLOOR), 4, axis=0)
    with jax.named_scope("fit"):
        slot = lax.axis_index("samp_2") * 16 + lax.axis_index(PLANE)
        fitted = fit(slot.astype(jnp.int32)[None], *sums, everywhere)
    with jax.named_scope("gather_scores"):
        layer = jnp.sum(lax.all_to_all(fitted, LAYER, 0, 0, tiled=True), axis=(0, 1))
        up = [(i, i + 1) for i in range(layers - 1)]
        down = [(j, i) for i, j in up]
        before = lax.ppermute(layer, "cpg_0", up)[2 * rows - HALO : 2 * rows]
        after = lax.ppermute(layer, "cpg_0", down)[:HALO]
        scores, scales = layer[: 2 * rows], layer[2 * rows :]
    with jax.named_scope("smooth"):
        block_len = reaches.shape[0]
        high = lax.axis_index("cpg_1")
        widened = lax.dynamic_slice_in_dim(
            jnp.concatenate([before, scores, after]), high * block_len, block_len + 2 * HALO, 0
        )
        log_scale = lax.dynamic_slice_in_dim(scales, high * block_len, block_len, 0)
        base = lax.axis_index(CPG) * block_len
        total_cpgs = block_len * lax.axis_size(CPG)
        places = lax.dynamic_slice_in_dim(
            jnp.pad(positions.astype(jnp.float32), HALO), base, block_len + 2 * HALO, 0
        )
        global_index = base - HALO + jnp.arange(block_len + 2 * HALO, dtype=jnp.int32)
        present = ((global_index >= 0) & (global_index < total_cpgs)).astype(jnp.float32)
        smoothed = smooth_block(widened, places, present, reaches)
    return (smoothed, log_scale)


def solution(mesh):
    split = Mesh(
        mesh.devices.reshape(2, 4, 2, 8, 2), ("samp_0", "samp_1", "samp_2", "cpg_0", "cpg_1")
    )
    return jax.shard_map(
        shards,
        mesh=split,
        in_specs=(P(SAMP, CPG), P(SAMP, CPG), P(CPG), P(CPG, SAMP), P(SAMP), P(), P(CPG)),
        out_specs=(P(CPG), P(CPG)),
        check_vma=False,
    )
```

time: 391 us -> 148 us (0.38)
  waiting for transfers between devices: 177 us -> 47.8 us
  blocking collectives: 128 us -> 0 us
  starting transfers between devices: 27.5 us -> 61.4 us
  matrix products: 6.51 us -> 22.1 us
  local copies, waits for them, and re-layouts: 24.1 us -> 10.3 us
  between operations: 14 us -> 1.09 us
  other arithmetic: 10.8 us -> 2 us
    psum x21 -> x0, blocking collectives: 119 us -> none  [one_axis_at_a_time(): return functools.reduce(lax.psum, axes, value)]
    reduce_scatter x1 -> x0, waiting for transfers between devices: 94.5 us -> none  [summed_rows(): total = lax.psum_scatter(total, axis, scatter_dimension=0, tiled=True)]
    all_gather x1 -> x0, waiting for transfers between devices: 42.4 us -> none  [one_gather(): lines, at, gathered = (lax.all_gather(flat, axis), 0, [])]
    all_to_all x5 -> x6, waiting for transfers between devices: 11.6 us -> 40.4 us  [the longest x3 19.9 us: copies(): lax.all_to_all(jnp.broadcast_to(value[None], (peers, *value.shape)), axes...]
    ppermute x2 -> x20, starting transfers between devices: 8.24 us -> 34.6 us  [the longest x18 28.8 us: shifted(): lax.ppermute(value, axis, [(i, (i + by) % peers) for i in range(peers)])]
    unnamed x4 -> x0, waiting for transfers between devices: 25.7 us -> none
    dot_general x2 -> x18, matrix products: 6.51 us -> 22.1 us  [term(): return jnp.dot(block, vecs, preferred_element_type=jnp.float32)]
    all_to_all x1 -> x0, blocking collectives: 8.61 us -> none  [copy_for_each(): lax.all_to_all(jnp.broadcast_to(value[None], (peers, *value.shape)), axis...]
  transfers between devices with their start and end apart: 10 -> 26, of which waited for: 6 -> 9; matrix products, arithmetic and copies ran while one was open for 0% -> 22% of each run, Pallas kernels for 0% -> 0%
where the time goes in v2:
time: 148 us; the launch traced here: 147 us
  starting transfers between devices  61.4 us (41%)
  waiting for transfers between devices  47.8 us (32%)
  matrix products  22.1 us (15%)
  local copies, waits for them, and re-layouts  10.3 us (7%)
  Pallas kernels  2.16 us (1%)
  other arithmetic  2 us (1%)
    ppermute x18, starting transfers between devices, shifted(): lax.ppermute(value, axis, [(i, (i + by) % peers) for i in range(peers)])  28.8 us
    dot_general x18, matrix products, term(): return jnp.dot(block, vecs, preferred_element_type=jnp.float32)  22.1 us
    all_to_all x3, waiting for transfers between devices, copies(): lax.all_to_all(jnp.broadcast_to(value[None], (peers, *value.shape)), axes...  19.9 us
    all_to_all x2, waiting for transfers between devices, exchanged(): return lax.all_to_all(total.astype(jnp.bfloat16), PLANE, 0, 0, tiled=True)  13.1 us
    all_to_all x3, starting transfers between devices, copies(): lax.all_to_all(jnp.broadcast_to(value[None], (peers, *value.shape)), axes...  12.2 us
    all_to_all x2, starting transfers between devices, exchanged(): return lax.all_to_all(total.astype(jnp.bfloat16), PLANE, 0, 0, tiled=True)  10.7 us
    all_to_all x1, waiting for transfers between devices, shards(): lax.all_to_all(fitted, LAYER, 0, 0, tiled=True)  7.32 us
    ppermute x18, waiting for transfers between devices, shifted(): lax.ppermute(value, axis, [(i, (i + by) % peers) for i in range(peers)])  5.41 us
  transfers between devices with their start and end apart: 26, of which 9 were waited for; matrix products, arithmetic and copies ran while one was open for 22% of the time, Pallas kernels for 0%

profile of v2, /device:TPU:96, one launch (start us, length us, event | category | flops | bytes accessed | tf_op | source)
XLA Modules:
  0.0 146.8 jit_solution(16980635645657505386)
XLA Ops:
  0.6 0.1 collective-permute-start
  0.7 1.2 multiply_convert_fusion
  2.0 1.1 broadcast_in_dim.12
  3.0 5.3 %all-to-all-start.2 = ((bf16[8,64,1024]{2,1,0:T(8,128)(2,1)}), bf16[8,64,1024]{2,1,0:T(8,128)(2,1)S(1)}, u32[]{:S(2)}, u32[]{:S(2)}) async-start(bf16[8,64,1024]{2,1,0:T(8,128)(2,1)} %broadcast_in_dim.12), calls=%async_computation.2 | async-start | bytes 2097152 | tf_op jit(solution)/shard_map/gather_rows/all_to_all | solution.py:123
  8.4 0.2 collective-permute-start.17
  8.5 1.5 %constant_dynamic-update-slice_fusion.1 = bf16[1024,2048]{1,0:T(8,128)(2,1)} fusion(bf16[1024,1024]{1,0:T(8,128)(2,1)S(1)} %copy-done.2), kind=kLoop, calls=%fused_computation.73 | loop fusion | bytes 4194304
  10.1 14.5 %all-to-all-done.2 = bf16[8,64,1024]{2,1,0:T(8,128)(2,1)S(1)} async-done(((bf16[8,64,1024]{2,1,0:T(8,128)(2,1)}), bf16[8,64,1024]{2,1,0:T(8,128)(2,1)S(1)}, u32[]{:S(2)}, u32[]{:S(2)}) %all-to-all-start.2) | async-done | bytes 1048608 | tf_op jit(solution)/shard_map/gather_rows/all_to_all | solution.py:123
  24.6 1.1 broadcast_in_dim.11
  25.7 3.6 %all-to-all-start = ((bf16[8,64,1024]{2,1,0:T(8,128)(2,1)}), bf16[8,64,1024]{2,1,0:T(8,128)(2,1)S(1)}, u32[]{:S(2)}, u32[]{:S(2)}) async-start(bf16[8,64,1024]{2,1,0:T(8,128)(2,1)} %broadcast_in_dim.11), calls=%async_computation | async-start | bytes 2097152 | tf_op jit(solution)/shard_map/gather_rows/all_to_all | solution.py:123
  29.3 3.2 %constant_dynamic-update-slice_fusion = bf16[1024,2048]{1,0:T(8,128)(2,1)} fusion(bf16[1024,2048]{1,0:T(8,128)(2,1)} %constant_dynamic-update-slice_fusion.1, bf16[1024,1024]{1,0:T(8,128)(2,1)} %collective-permute-done), kind=kLoop, calls=%fused_computation.72 | loop fusion | bytes 4194304 | tf_op jit(solution)/shard_map/swap_eigvecs/concatenate | solution.py:139
  32.4 3.2 %convolution_convert_fusion.1 = bf16[32,2048]{1,0:T(8,128)(2,1)S(1)} fusion(bf16[1024,2048]{1,0:T(8,128)(2,1)} %constant_dynamic-update-slice_fusion, bf16[8,64,1024]{2,1,0:T(8,128)(2,1)S(1)} %all-to-all-done.2, s32[]{:T(128)S(6)} %select_n.49), kind=kOutput, calls=%fused_computation.31 | convolution fusion | flops 134283264 | bytes 4390916 | tf_op jit(solution)/shard_map/sum_layers/dot_general | solution.py:145
  35.6 3.2 %collective-permute-start.9 = (bf16[32,2048]{1,0:T(8,128)(2,1)S(1)}, bf16[32,2048]{1,0:T(8,128)(2,1)S(1)}, u32[]{:S(2)}, u32[]{:S(2)}) collective-permute-start(bf16[32,2048]{1,0:T(8,128)(2,1)S(1)} %convolution_convert_fusion.1), channel_id=1, source_target_pairs={{0,2},{2,4},{4,6},{6,8},{8,10},{10,12},{12,14},{14,0},{1,3},{3,5},... | collective-permute-start | bytes 393224 | tf_op jit(solution)/shard_map/sum_layers/ppermute | solution.py:25
  38.8 0.8 convolution_convert_fusion
  39.7 5.4 %all-to-all-done = bf16[8,64,1024]{2,1,0:T(8,128)(2,1)S(1)} async-done(((bf16[8,64,1024]{2,1,0:T(8,128)(2,1)}), bf16[8,64,1024]{2,1,0:T(8,128)(2,1)S(1)}, u32[]{:S(2)}, u32[]{:S(2)}) %all-to-all-start) | async-done | bytes 1048608 | tf_op jit(solution)/shard_map/gather_rows/all_to_all | solution.py:123
  45.1 0.6 broadcast_in_dim.13
  45.7 3.3 %all-to-all-start.4 = ((f32[8,1,2048]{2,1,0:T(1,128)}), f32[8,1,2048]{2,1,0:T(1,128)S(1)}, u32[]{:S(2)}, u32[]{:S(2)}) async-start(f32[8,1,2048]{2,1,0:T(1,128)} %broadcast_in_dim.13), calls=%async_computation.4 | async-start | bytes 131072 | tf_op jit(solution)/shard_map/gather_values/all_to_all | solution.py:123
  49.1 3.2 %convolution_convert_fusion.3 = bf16[32,2048]{1,0:T(8,128)(2,1)S(1)} fusion(bf16[1024,2048]{1,0:T(8,128)(2,1)} %constant_dynamic-update-slice_fusion, bf16[8,64,1024]{2,1,0:T(8,128)(2,1)S(1)} %all-to-all-done, s32[]{:T(128)S(6)} %select_n.49), kind=kOutput, calls=%fused_computation.33 | convolution fusion | flops 134283264 | bytes 4390916 | tf_op jit(solution)/shard_map/sum_layers/dot_general | solution.py:145
  52.2 3.2 %collective-permute-start.1 = (bf16[32,2048]{1,0:T(8,128)(2,1)S(1)}, bf16[32,2048]{1,0:T(8,128)(2,1)S(1)}, u32[]{:S(2)}, u32[]{:S(2)}) collective-permute-start(bf16[32,2048]{1,0:T(8,128)(2,1)S(1)} %convolution_convert_fusion.3), channel_id=1, source_target_pairs={{0,2},{2,4},{4,6},{6,8},{8,10},{10,12},{12,14},{14,0},{1,3},{3,5},... | collective-permute-start | bytes 393224 | tf_op jit(solution)/shard_map/sum_layers/ppermute | solution.py:25
  55.4 0.8 convolution_convert_fusion.2
  56.3 0.9 fusion.12
  57.2 3.3 %collective-permute-start.10 = (bf16[64,2048]{1,0:T(8,128)(2,1)S(1)}, bf16[64,2048]{1,0:T(8,128)(2,1)S(1)}, u32[]{:S(2)}, u32[]{:S(2)}) collective-permute-start(bf16[64,2048]{1,0:T(8,128)(2,1)S(1)} %fusion.12), channel_id=1, source_target_pairs={{0,2},{2,4},{4,6},{6,8},{8,10},{10,12},{12,14},{14,0},{1,3},{3,5},... | collective-permute-start | bytes 786440 | tf_op jit(solution)/shard_map/sum_layers/ppermute | solution.py:25
  60.5 0.9 fusion.15
  61.3 0.1 collective-permute-start.14
  61.4 0.8 fusion.5
  62.3 3.5 %collective-permute-start.2 = (bf16[64,2048]{1,0:T(8,128)(2,1)S(1)}, bf16[64,2048]{1,0:T(8,128)(2,1)S(1)}, u32[]{:S(2)}, u32[]{:S(2)}) collective-permute-start(bf16[64,2048]{1,0:T(8,128)(2,1)S(1)} %fusion.5), channel_id=1, source_target_pairs={{0,2},{2,4},{4,6},{6,8},{8,10},{10,12},{12,14},{14,0},{1,3},{3,5},... | collective-permute-start | bytes 786440 | tf_op jit(solution)/shard_map/sum_layers/ppermute | solution.py:25
  65.8 0.9 fusion.8
  66.6 0.1 collective-permute-start.6
  66.7 0.8 fusion.11
  67.6 3.3 %collective-permute-start.11 = (bf16[64,2048]{1,0:T(8,128)(2,1)S(1)}, bf16[64,2048]{1,0:T(8,128)(2,1)S(1)}, u32[]{:S(2)}, u32[]{:S(2)}) collective-permute-start(bf16[64,2048]{1,0:T(8,128)(2,1)S(1)} %fusion.11), channel_id=1, source_target_pairs={{0,2},{2,4},{4,6},{6,8},{8,10},{10,12},{12,14},{14,0},{1,3},{3,5},... | collective-permute-start | bytes 786440 | tf_op jit(solution)/shard_map/sum_layers/ppermute | solution.py:25
  70.9 0.8 fusion.14
  71.7 0.1 collective-permute-start.15
  71.8 0.7 collective-permute-done.2
  72.5 0.8 fusion.4
  73.4 3.8 %collective-permute-start.3 = (bf16[64,2048]{1,0:T(8,128)(2,1)S(1)}, bf16[64,2048]{1,0:T(8,128)(2,1)S(1)}, u32[]{:S(2)}, u32[]{:S(2)}) collective-permute-start(bf16[64,2048]{1,0:T(8,128)(2,1)S(1)} %fusion.4), channel_id=1, source_target_pairs={{0,2},{2,4},{4,6},{6,8},{8,10},{10,12},{12,14},{14,0},{1,3},{3,5},... | collective-permute-start | bytes 786440 | tf_op jit(solution)/shard_map/sum_layers/ppermute | solution.py:25
  77.1 0.8 fusion.7
  78.0 0.1 collective-permute-start.7
  78.1 0.8 fusion.10
  79.0 3.8 %collective-permute-start.12 = (bf16[64,2048]{1,0:T(8,128)(2,1)S(1)}, bf16[64,2048]{1,0:T(8,128)(2,1)S(1)}, u32[]{:S(2)}, u32[]{:S(2)}) collective-permute-start(bf16[64,2048]{1,0:T(8,128)(2,1)S(1)} %fusion.10), channel_id=1, source_target_pairs={{0,2},{2,4},{4,6},{6,8},{8,10},{10,12},{12,14},{14,0},{1,3},{3,5},... | collective-permute-start | bytes 786440 | tf_op jit(solution)/shard_map/sum_layers/ppermute | solution.py:25
  82.8 0.8 fusion.13
  83.6 0.1 collective-permute-start.16
  83.7 0.2 collective-permute-done.3
  83.9 0.8 fusion.3
  84.8 3.8 %collective-permute-start.4 = (bf16[64,2048]{1,0:T(8,128)(2,1)S(1)}, bf16[64,2048]{1,0:T(8,128)(2,1)S(1)}, u32[]{:S(2)}, u32[]{:S(2)}) collective-permute-start(bf16[64,2048]{1,0:T(8,128)(2,1)S(1)} %fusion.3), channel_id=1, source_target_pairs={{0,2},{2,4},{4,6},{6,8},{8,10},{10,12},{12,14},{14,0},{1,3},{3,5},... | collective-permute-start | bytes 786440 | tf_op jit(solution)/shard_map/sum_layers/ppermute | solution.py:25
  88.5 0.9 fusion.6
  89.4 0.3 collective-permute-start.8
  89.7 4.4 %collective-permute-done.16 = bf16[64,2048]{1,0:T(8,128)(2,1)S(1)} collective-permute-done((bf16[64,2048]{1,0:T(8,128)(2,1)S(1)}, bf16[64,2048]{1,0:T(8,128)(2,1)S(1)}, u32[]{:S(2)}, u32[]{:S(2)}) %collective-permute-start.16) | collective-permute-done | bytes 262176 | tf_op jit(solution)/shard_map/sum_layers/ppermute | solution.py:25
  94.1 0.9 fusion.9
  95.0 0.8 all_to_all.34
  95.9 7.2 %all-to-all-start.3 = ((bf16[16,4,2048]{2,1,0:T(4,128)(2,1)}), bf16[16,4,2048]{2,1,0:T(4,128)(2,1)S(1)}, u32[]{:S(2)}, u32[]{:S(2)}) async-start(bf16[16,4,2048]{2,1,0:T(4,128)(2,1)} %all_to_all.34), calls=%async_computation.3 | async-start | bytes 524288 | tf_op jit(solution)/shard_map/sum_layers/all_to_all | solution.py:168
  103.1 3.1 %fusion.2 = bf16[64,2048]{1,0:T(8,128)(2,1)S(1)} fusion(bf16[1024,2048]{1,0:T(8,128)(2,1)} %constant_dynamic-update-slice_fusion, bf16[64,2048]{1,0:T(8,128)(2,1)S(1)} %collective-permute-done.8, bf16[64,2048]{1,0:T(8,128)(2,1)S(1)} %collective-permute-done.4, bf16[8,64,1024]{2,1,0:T(8,128)(2,1)S(1)} %all-to-all-done, s32[]{:T(128)S(6)} %select_n.45), kind=kOutput, calls=%fused_computation.16 | convolution fusion | flops 269090816 | bytes 5111812 | tf_op jit(solution)/shard_map/sum_layers/dot_general | solution.py:145
  106.1 0.8 all_to_all.30
  106.9 4.8 %all-to-all-done.3 = bf16[16,4,2048]{2,1,0:T(4,128)(2,1)S(1)} async-done(((bf16[16,4,2048]{2,1,0:T(4,128)(2,1)}), bf16[16,4,2048]{2,1,0:T(4,128)(2,1)S(1)}, u32[]{:S(2)}, u32[]{:S(2)}) %all-to-all-start.3) | async-done | bytes 262176 | tf_op jit(solution)/shard_map/sum_layers/all_to_all | solution.py:168
  111.7 3.5 %all-to-all-start.1 = ((bf16[16,4,2048]{2,1,0:T(4,128)(2,1)}), bf16[16,4,2048]{2,1,0:T(4,128)(2,1)S(1)}, u32[]{:S(2)}, u32[]{:S(2)}) async-start(bf16[16,4,2048]{2,1,0:T(4,128)(2,1)} %all_to_all.30), calls=%async_computation.1 | async-start | bytes 524288 | tf_op jit(solution)/shard_map/sum_layers/all_to_all | solution.py:168
  115.4 0.1 reshape.24.values_ref
  115.6 8.3 %all-to-all-done.1 = bf16[16,4,2048]{2,1,0:T(4,128)(2,1)S(1)} async-done(((bf16[16,4,2048]{2,1,0:T(4,128)(2,1)}), bf16[16,4,2048]{2,1,0:T(4,128)(2,1)S(1)}, u32[]{:S(2)}, u32[]{:S(2)}) %all-to-all-start.1) | async-done | bytes 262176 | tf_op jit(solution)/shard_map/sum_layers/all_to_all | solution.py:168
  124.0 2.2 %fit.1 = f32[32,1,256]{2,1,0:T(1,128)} custom-call(s32[1]{0:T(128)} %bitcast.slot_ref, bf16[64,2048]{1,0:T(8,128)(2,1)S(1)} %all_to_all.32.resp_ref, bf16[64,2048]{1,0:T(8,128)(2,1)S(1)} %all_to_all.36.design_ref, f32[32,2048]{1,0:T(8,128)S(1)} %reshape.24.values_ref), custom_call_target="tpu_custom_call" | custom-call | tf_op jit(solution)/shard_map/fit/pallas_call | solution.py:92
  126.1 3.8 %all-to-all-start.5 = ((f32[32,1,256]{2,1,0:T(1,128)}), f32[32,1,256]{2,1,0:T(1,128)S(1)}, u32[]{:S(2)}, u32[]{:S(2)}) async-start(f32[32,1,256]{2,1,0:T(1,128)} %fit.1), calls=%async_computation.5 | async-start | bytes 65536 | tf_op jit(solution)/shard_map/gather_scores/all_to_all | solution.py:187
  130.0 0.1 pad_dynamic-slice_fusion
  130.1 7.3 %all-to-all-done.5 = f32[32,1,256]{2,1,0:T(1,128)S(1)} async-done(((f32[32,1,256]{2,1,0:T(1,128)}), f32[32,1,256]{2,1,0:T(1,128)S(1)}, u32[]{:S(2)}, u32[]{:S(2)}) %all-to-all-start.5) | async-done | bytes 32800 | tf_op jit(solution)/shard_map/gather_scores/all_to_all | solution.py:187
  137.4 1.9 %collective-permute-start.18 = (f32[256]{0:T(256)S(1)}, f32[256]{0:T(256)S(1)}, u32[]{:S(2)}, u32[]{:S(2)}) collective-permute-start(f32[256]{0:T(256)S(1)} %reduce_sum.9), channel_id=1, source_target_pairs={{0,2},{2,4},{4,6},{6,8},{8,10},{10,12},{12,14},{1,3},{3,5},{5,7},{... | collective-permute-start | bytes 3080 | tf_op jit(solution)/shard_map/gather_scores/ppermute | solution.py:190
  139.4 3.9 %collective-permute-start.19 = (f32[256]{0:T(256)S(1)}, f32[256]{0:T(256)S(1)}, u32[]{:S(2)}, u32[]{:S(2)}) collective-permute-start(f32[256]{0:T(256)S(1)} %reduce_sum.9), channel_id=1, source_target_pairs={{2,0},{4,2},{6,4},{8,6},{10,8},{12,10},{14,12},{3,1},{5,3},{7,5},{... | collective-permute-start | bytes 3080 | tf_op jit(solution)/shard_map/gather_scores/ppermute | solution.py:191
  143.3 0.6 dynamic_slice.78
  144.0 2.1 %collective-permute-done.19 = f32[256]{0:T(256)S(1)} collective-permute-done((f32[256]{0:T(256)S(1)}, f32[256]{0:T(256)S(1)}, u32[]{:S(2)}, u32[]{:S(2)}) %collective-permute-start.19) | collective-permute-done | bytes 1056 | tf_op jit(solution)/shard_map/gather_scores/ppermute | solution.py:191
  146.2 0.6 add_divide_fusion
  (44 shorter events, 0.7 us)
Async XLA Ops:
  0.6 7.9 %copy-start.2 = (bf16[1024,1024]{1,0:T(8,128)(2,1)S(1)}, bf16[1024,1024]{1,0:T(8,128)(2,1)}, u32[]{:S(2)}) copy-start(bf16[1024,1024]{1,0:T(8,128)(2,1)} %param.10) | copy-start | bytes 6291460
  0.6 28.6 %collective-permute-start = (bf16[1024,1024]{1,0:T(8,128)(2,1)}, bf16[1024,1024]{1,0:T(8,128)(2,1)}, u32[]{:S(2)}, u32[]{:S(2)}) collective-permute-start(bf16[1024,1024]{1,0:T(8,128)(2,1)} %param.10), channel_id=1, source_target_pairs={{0,16},{16,0},{1,17},{17,1},{2,18},{18,2},{3,19},{19,3},{4,20},{20... | collective-permute-start | bytes 6291464 | tf_op jit(solution)/shard_map/swap_eigvecs/ppermute | solution.py:25
  3.0 21.5 %all-to-all-start.2 = ((bf16[8,64,1024]{2,1,0:T(8,128)(2,1)}), bf16[8,64,1024]{2,1,0:T(8,128)(2,1)S(1)}, u32[]{:S(2)}, u32[]{:S(2)}) async-start(bf16[8,64,1024]{2,1,0:T(8,128)(2,1)} %broadcast_in_dim.12), calls=%async_computation.2 | async-start | bytes 2097152 | tf_op jit(solution)/shard_map/gather_rows/all_to_all | solution.py:123
  8.4 20.9 %copy-start.4 = (f32[1024]{0:T(1024)S(1)}, f32[1024]{0:T(1024)}, u32[]{:S(2)}) copy-start(f32[1024]{0:T(1024)} %param.11) | copy-start | bytes 12292
  8.4 20.9 %collective-permute-start.17 = (f32[1024]{0:T(1024)}, f32[1024]{0:T(1024)S(1)}, u32[]{:S(2)}, u32[]{:S(2)}) collective-permute-start(f32[1024]{0:T(1024)} %param.11), channel_id=1, source_target_pairs={{0,16},{16,0},{1,17},{17,1},{2,18},{18,2},{3,19},{19,3},{4,20},{20... | collective-permute-start | bytes 12296 | tf_op jit(solution)/shard_map/swap_eigvecs/ppermute | solution.py:25
  25.7 19.4 %all-to-all-start = ((bf16[8,64,1024]{2,1,0:T(8,128)(2,1)}), bf16[8,64,1024]{2,1,0:T(8,128)(2,1)S(1)}, u32[]{:S(2)}, u32[]{:S(2)}) async-start(bf16[8,64,1024]{2,1,0:T(8,128)(2,1)} %broadcast_in_dim.11), calls=%async_computation | async-start | bytes 2097152 | tf_op jit(solution)/shard_map/gather_rows/all_to_all | solution.py:123
  32.4 6.3 %copy-start = (bf16[1024,2048]{1,0:T(8,128)(2,1)S(1)}, bf16[1024,2048]{1,0:T(8,128)(2,1)}, u32[]{:S(2)}) copy-start(bf16[1024,2048]{1,0:T(8,128)(2,1)} %constant_dynamic-update-slice_fusion) | copy-start | bytes 12582916
  35.6 20.7 %collective-permute-start.9 = (bf16[32,2048]{1,0:T(8,128)(2,1)S(1)}, bf16[32,2048]{1,0:T(8,128)(2,1)S(1)}, u32[]{:S(2)}, u32[]{:S(2)}) collective-permute-start(bf16[32,2048]{1,0:T(8,128)(2,1)S(1)} %convolution_convert_fusion.1), channel_id=1, source_target_pairs={{0,2},{2,4},{4,6},{6,8},{8,10},{10,12},{12,14},{14,0},{1,3},{3,5},... | collective-permute-start | bytes 393224 | tf_op jit(solution)/shard_map/sum_layers/ppermute | solution.py:25
  39.6 20.8 %collective-permute-start.13 = (bf16[32,2048]{1,0:T(8,128)(2,1)S(1)}, bf16[32,2048]{1,0:T(8,128)(2,1)S(1)}, u32[]{:S(2)}, u32[]{:S(2)}) collective-permute-start(bf16[32,2048]{1,0:T(8,128)(2,1)S(1)} %convolution_convert_fusion), channel_id=1, source_target_pairs={{0,14},{2,0},{4,2},{6,4},{8,6},{10,8},{12,10},{14,12},{1,15},{3,1}... | collective-permute-start | bytes 393224 | tf_op jit(solution)/shard_map/sum_layers/ppermute | solution.py:25
  45.7 50.2 %all-to-all-start.4 = ((f32[8,1,2048]{2,1,0:T(1,128)}), f32[8,1,2048]{2,1,0:T(1,128)S(1)}, u32[]{:S(2)}, u32[]{:S(2)}) async-start(f32[8,1,2048]{2,1,0:T(1,128)} %broadcast_in_dim.13), calls=%async_computation.4 | async-start | bytes 131072 | tf_op jit(solution)/shard_map/gather_values/all_to_all | solution.py:123
  49.1 6.4 %copy-start.1 = (bf16[1024,2048]{1,0:T(8,128)(2,1)S(1)}, bf16[1024,2048]{1,0:T(8,128)(2,1)}, u32[]{:S(2)}) copy-start(bf16[1024,2048]{1,0:T(8,128)(2,1)} %constant_dynamic-update-slice_fusion) | copy-start | bytes 12582916
  52.2 9.2 %collective-permute-start.1 = (bf16[32,2048]{1,0:T(8,128)(2,1)S(1)}, bf16[32,2048]{1,0:T(8,128)(2,1)S(1)}, u32[]{:S(2)}, u32[]{:S(2)}) collective-permute-start(bf16[32,2048]{1,0:T(8,128)(2,1)S(1)} %convolution_convert_fusion.3), channel_id=1, source_target_pairs={{0,2},{2,4},{4,6},{6,8},{8,10},{10,12},{12,14},{14,0},{1,3},{3,5},... | collective-permute-start | bytes 393224 | tf_op jit(solution)/shard_map/sum_layers/ppermute | solution.py:25
  56.2 9.5 %collective-permute-start.5 = (bf16[32,2048]{1,0:T(8,128)(2,1)S(1)}, bf16[32,2048]{1,0:T(8,128)(2,1)S(1)}, u32[]{:S(2)}, u32[]{:S(2)}) collective-permute-start(bf16[32,2048]{1,0:T(8,128)(2,1)S(1)} %convolution_convert_fusion.2), channel_id=1, source_target_pairs={{0,14},{2,0},{4,2},{6,4},{8,6},{10,8},{12,10},{14,12},{1,15},{3,1}... | collective-permute-start | bytes 393224 | tf_op jit(solution)/shard_map/sum_layers/ppermute | solution.py:25
  57.2 9.5 %collective-permute-start.10 = (bf16[64,2048]{1,0:T(8,128)(2,1)S(1)}, bf16[64,2048]{1,0:T(8,128)(2,1)S(1)}, u32[]{:S(2)}, u32[]{:S(2)}) collective-permute-start(bf16[64,2048]{1,0:T(8,128)(2,1)S(1)} %fusion.12), channel_id=1, source_target_pairs={{0,2},{2,4},{4,6},{6,8},{8,10},{10,12},{12,14},{14,0},{1,3},{3,5},... | collective-permute-start | bytes 786440 | tf_op jit(solution)/shard_map/sum_layers/ppermute | solution.py:25
  61.3 9.5 %collective-permute-start.14 = (bf16[64,2048]{1,0:T(8,128)(2,1)S(1)}, bf16[64,2048]{1,0:T(8,128)(2,1)S(1)}, u32[]{:S(2)}, u32[]{:S(2)}) collective-permute-start(bf16[64,2048]{1,0:T(8,128)(2,1)S(1)} %fusion.15), channel_id=1, source_target_pairs={{0,14},{2,0},{4,2},{6,4},{8,6},{10,8},{12,10},{14,12},{1,15},{3,1}... | collective-permute-start | bytes 786440 | tf_op jit(solution)/shard_map/sum_layers/ppermute | solution.py:25
  62.3 10.2 %collective-permute-start.2 = (bf16[64,2048]{1,0:T(8,128)(2,1)S(1)}, bf16[64,2048]{1,0:T(8,128)(2,1)S(1)}, u32[]{:S(2)}, u32[]{:S(2)}) collective-permute-start(bf16[64,2048]{1,0:T(8,128)(2,1)S(1)} %fusion.5), channel_id=1, source_target_pairs={{0,2},{2,4},{4,6},{6,8},{8,10},{10,12},{12,14},{14,0},{1,3},{3,5},... | collective-permute-start | bytes 786440 | tf_op jit(solution)/shard_map/sum_layers/ppermute | solution.py:25
  66.6 10.5 %collective-permute-start.6 = (bf16[64,2048]{1,0:T(8,128)(2,1)S(1)}, bf16[64,2048]{1,0:T(8,128)(2,1)S(1)}, u32[]{:S(2)}, u32[]{:S(2)}) collective-permute-start(bf16[64,2048]{1,0:T(8,128)(2,1)S(1)} %fusion.8), channel_id=1, source_target_pairs={{0,14},{2,0},{4,2},{6,4},{8,6},{10,8},{12,10},{14,12},{1,15},{3,1}... | collective-permute-start | bytes 786440 | tf_op jit(solution)/shard_map/sum_layers/ppermute | solution.py:25
  67.6 10.6 %collective-permute-start.11 = (bf16[64,2048]{1,0:T(8,128)(2,1)S(1)}, bf16[64,2048]{1,0:T(8,128)(2,1)S(1)}, u32[]{:S(2)}, u32[]{:S(2)}) collective-permute-start(bf16[64,2048]{1,0:T(8,128)(2,1)S(1)} %fusion.11), channel_id=1, source_target_pairs={{0,2},{2,4},{4,6},{6,8},{8,10},{10,12},{12,14},{14,0},{1,3},{3,5},... | collective-permute-start | bytes 786440 | tf_op jit(solution)/shard_map/sum_layers/ppermute | solution.py:25
  71.7 11.0 %collective-permute-start.15 = (bf16[64,2048]{1,0:T(8,128)(2,1)S(1)}, bf16[64,2048]{1,0:T(8,128)(2,1)S(1)}, u32[]{:S(2)}, u32[]{:S(2)}) collective-permute-start(bf16[64,2048]{1,0:T(8,128)(2,1)S(1)} %fusion.14), channel_id=1, source_target_pairs={{0,14},{2,0},{4,2},{6,4},{8,6},{10,8},{12,10},{14,12},{1,15},{3,1}... | collective-permute-start | bytes 786440 | tf_op jit(solution)/shard_map/sum_layers/ppermute | solution.py:25
  73.4 10.5 %collective-permute-start.3 = (bf16[64,2048]{1,0:T(8,128)(2,1)S(1)}, bf16[64,2048]{1,0:T(8,128)(2,1)S(1)}, u32[]{:S(2)}, u32[]{:S(2)}) collective-permute-start(bf16[64,2048]{1,0:T(8,128)(2,1)S(1)} %fusion.4), channel_id=1, source_target_pairs={{0,2},{2,4},{4,6},{6,8},{8,10},{10,12},{12,14},{14,0},{1,3},{3,5},... | collective-permute-start | bytes 786440 | tf_op jit(solution)/shard_map/sum_layers/ppermute | solution.py:25
  78.0 10.5 %collective-permute-start.7 = (bf16[64,2048]{1,0:T(8,128)(2,1)S(1)}, bf16[64,2048]{1,0:T(8,128)(2,1)S(1)}, u32[]{:S(2)}, u32[]{:S(2)}) collective-permute-start(bf16[64,2048]{1,0:T(8,128)(2,1)S(1)} %fusion.7), channel_id=1, source_target_pairs={{0,14},{2,0},{4,2},{6,4},{8,6},{10,8},{12,10},{14,12},{1,15},{3,1}... | collective-permute-start | bytes 786440 | tf_op jit(solution)/shard_map/sum_layers/ppermute | solution.py:25
  79.0 10.7 %collective-permute-start.12 = (bf16[64,2048]{1,0:T(8,128)(2,1)S(1)}, bf16[64,2048]{1,0:T(8,128)(2,1)S(1)}, u32[]{:S(2)}, u32[]{:S(2)}) collective-permute-start(bf16[64,2048]{1,0:T(8,128)(2,1)S(1)} %fusion.10), channel_id=1, source_target_pairs={{0,2},{2,4},{4,6},{6,8},{8,10},{10,12},{12,14},{14,0},{1,3},{3,5},... | collective-permute-start | bytes 786440 | tf_op jit(solution)/shard_map/sum_layers/ppermute | solution.py:25
  83.6 10.5 %collective-permute-start.16 = (bf16[64,2048]{1,0:T(8,128)(2,1)S(1)}, bf16[64,2048]{1,0:T(8,128)(2,1)S(1)}, u32[]{:S(2)}, u32[]{:S(2)}) collective-permute-start(bf16[64,2048]{1,0:T(8,128)(2,1)S(1)} %fusion.13), channel_id=1, source_target_pairs={{0,14},{2,0},{4,2},{6,4},{8,6},{10,8},{12,10},{14,12},{1,15},{3,1}... | collective-permute-start | bytes 786440 | tf_op jit(solution)/shard_map/sum_layers/ppermute | solution.py:25
  84.8 18.3 %collective-permute-start.4 = (bf16[64,2048]{1,0:T(8,128)(2,1)S(1)}, bf16[64,2048]{1,0:T(8,128)(2,1)S(1)}, u32[]{:S(2)}, u32[]{:S(2)}) collective-permute-start(bf16[64,2048]{1,0:T(8,128)(2,1)S(1)} %fusion.3), channel_id=1, source_target_pairs={{0,2},{2,4},{4,6},{6,8},{8,10},{10,12},{12,14},{14,0},{1,3},{3,5},... | collective-permute-start | bytes 786440 | tf_op jit(solution)/shard_map/sum_layers/ppermute | solution.py:25
  89.4 13.7 %collective-permute-start.8 = (bf16[64,2048]{1,0:T(8,128)(2,1)S(1)}, bf16[64,2048]{1,0:T(8,128)(2,1)S(1)}, u32[]{:S(2)}, u32[]{:S(2)}) collective-permute-start(bf16[64,2048]{1,0:T(8,128)(2,1)S(1)} %fusion.6), channel_id=1, source_target_pairs={{0,14},{2,0},{4,2},{6,4},{8,6},{10,8},{12,10},{14,12},{1,15},{3,1}... | collective-permute-start | bytes 786440 | tf_op jit(solution)/shard_map/sum_layers/ppermute | solution.py:25
  95.0 20.2 %copy-start.3 = (s32[1024]{0:T(1024)S(1)}, s32[1024]{0:T(1024)}, u32[]{:S(2)}) copy-start(s32[1024]{0:T(1024)} %param.12) | copy-start | bytes 12292
  95.9 15.9 %all-to-all-start.3 = ((bf16[16,4,2048]{2,1,0:T(4,128)(2,1)}), bf16[16,4,2048]{2,1,0:T(4,128)(2,1)S(1)}, u32[]{:S(2)}, u32[]{:S(2)}) async-start(bf16[16,4,2048]{2,1,0:T(4,128)(2,1)} %all_to_all.34), calls=%async_computation.3 | async-start | bytes 524288 | tf_op jit(solution)/shard_map/sum_layers/all_to_all | solution.py:168
  103.0 43.2 %copy-start.5 = (s32[64]{0:T(128)S(1)}, s32[64]{0:T(128)}, u32[]{:S(2)}) copy-start(s32[64]{0:T(128)} %param.13) | copy-start | bytes 772
  111.7 12.2 %all-to-all-start.1 = ((bf16[16,4,2048]{2,1,0:T(4,128)(2,1)}), bf16[16,4,2048]{2,1,0:T(4,128)(2,1)S(1)}, u32[]{:S(2)}, u32[]{:S(2)}) async-start(bf16[16,4,2048]{2,1,0:T(4,128)(2,1)} %all_to_all.30), calls=%async_computation.1 | async-start | bytes 524288 | tf_op jit(solution)/shard_map/sum_layers/all_to_all | solution.py:168
  126.1 11.2 %all-to-all-start.5 = ((f32[32,1,256]{2,1,0:T(1,128)}), f32[32,1,256]{2,1,0:T(1,128)S(1)}, u32[]{:S(2)}, u32[]{:S(2)}) async-start(f32[32,1,256]{2,1,0:T(1,128)} %fit.1), calls=%async_computation.5 | async-start | bytes 65536 | tf_op jit(solution)/shard_map/gather_scores/all_to_all | solution.py:187
  137.4 6.5 %collective-permute-start.18 = (f32[256]{0:T(256)S(1)}, f32[256]{0:T(256)S(1)}, u32[]{:S(2)}, u32[]{:S(2)}) collective-permute-start(f32[256]{0:T(256)S(1)} %reduce_sum.9), channel_id=1, source_target_pairs={{0,2},{2,4},{4,6},{6,8},{8,10},{10,12},{12,14},{1,3},{3,5},{5,7},{... | collective-permute-start | bytes 3080 | tf_op jit(solution)/shard_map/gather_scores/ppermute | solution.py:190
  139.4 6.7 %collective-permute-start.19 = (f32[256]{0:T(256)S(1)}, f32[256]{0:T(256)S(1)}, u32[]{:S(2)}, u32[]{:S(2)}) collective-permute-start(f32[256]{0:T(256)S(1)} %reduce_sum.9), channel_id=1, source_target_pairs={{2,0},{4,2},{6,4},{8,6},{10,8},{12,10},{14,12},{3,1},{5,3},{7,5},{... | collective-permute-start | bytes 3080 | tf_op jit(solution)/shard_map/gather_scores/ppermute | solution.py:191

commit v3 on v2

--- a/solution.py
+++ b/solution.py
@@ -25,14 +25,41 @@
     return lax.ppermute(value, axis, [(i, (i + by) % peers) for i in range(peers)])
 
 
-def fit_kernel(slot_ref, resp_ref, design_ref, values_ref, out_ref, r_ref, d_ref, w_ref):
+def weigh_kernel(resp_ref, weight_ref, trait_ref, out_ref):
+    rows = resp_ref.shape[0]
+    trait = trait_ref[...]
+    for at in range(0, rows, 16):
+        root = jnp.sqrt(weight_ref[at : at + 16, :].astype(jnp.float32))
+        weighted = root * resp_ref[at : at + 16, :].astype(jnp.float32)
+        design = root * trait
+        upper = lax.broadcasted_iota(jnp.int32, (8, root.shape[1]), 0) < 4
+        tiles = []
+        for half in (0, 8):
+            a, b = weighted[half : half + 8], design[half : half + 8]
+            tiles.append(jnp.where(upper, a, pltpu.roll(b, 4, 0)))
+            tiles.append(jnp.where(upper, pltpu.roll(a, 4, 0), b))
+        out_ref[2 * at : 2 * at + 32, :] = jnp.concatenate(tiles, axis=0).astype(jnp.bfloat16)
+
+
+def weigh(responses, weights, phenotype):
+    rows, width = responses.shape
+    return pl.pallas_call(
+        weigh_kernel,
+        out_shape=jax.ShapeDtypeStruct((2 * rows, width), jnp.bfloat16),
+    )(responses, weights, phenotype[None, :])
+
+
+def fit_kernel(slot_ref, sums_ref, values_ref, out_ref, r_ref, d_ref, w_ref):
     half, width = values_ref.shape
     lanes = 512
-    for i in range(0, half, 16):
-        for given, kept in ((resp_ref, r_ref), (design_ref, d_ref)):
-            kept[i : i + 16, :] = given[i : i + 16, :].astype(jnp.float32) + given[
-                half + i : half + i + 16, :
-            ].astype(jnp.float32)
+    upper = lax.broadcasted_iota(jnp.int32, (8, width), 0) < 4
+    for i in range(0, half, 8):
+        pair = sums_ref[2 * i : 2 * i + 16, :].astype(jnp.float32) + sums_ref[
+            2 * (half + i) : 2 * (half + i) + 16, :
+        ].astype(jnp.float32)
+        a, b = pair[:8], pair[8:]
+        r_ref[i : i + 8, :] = jnp.where(upper, a, pltpu.roll(b, 4, 0))
+        d_ref[i : i + 8, :] = jnp.where(upper, pltpu.roll(a, 4, 0), b)
     blocks = [(i, j) for i in range(0, half, 8) for j in range(0, width, lanes)]
 
     def total(acc):
@@ -86,17 +113,36 @@
     )
 
 
-def fit(slot, resp, design, values):
-    rows, width = resp.shape
+def fit(slot, sums, values):
+    rows, width = values.shape
     vmem = pl.BlockSpec(memory_space=pltpu.VMEM)
     return pl.pallas_call(
         fit_kernel,
         out_shape=jax.ShapeDtypeStruct((32, 1, 256), jnp.float32),
-        in_specs=[pl.BlockSpec(memory_space=pltpu.SMEM), vmem, vmem, vmem],
+        in_specs=[pl.BlockSpec(memory_space=pltpu.SMEM), vmem, vmem],
         out_specs=vmem,
-        scratch_shapes=[pltpu.VMEM((rows // 2, width), jnp.float32)] * 3,
+        scratch_shapes=[pltpu.VMEM((rows, width), jnp.float32)] * 3,
         compiler_params=pltpu.CompilerParams(vmem_limit_bytes=16 * 1024 * 1024),
-    )(slot, resp, design, values)
+    )(slot, sums, values)
+
+
+def gather_plane(own):
+    x, y = "samp_1", "samp_0"
+    left = shifted(own, x, 1)
+    right = shifted(own, x, -1)
+    over = shifted(own, y, 1)
+    far = shifted(left, x, 1)
+    over_right = shifted(over, x, -1)
+    over_left = shifted(left, y, 1)
+    over_far = jnp.concatenate(
+        [
+            shifted(over_left[:48], x, 1),
+            shifted(over_right[48:96], x, -1),
+            shifted(far[96:], y, 1),
+        ],
+        axis=0,
+    )
+    return jnp.stack([own, right, far, left, over, over_right, over_far, over_left])
 
 
 def smooth_block(widened, places, present, reaches):
@@ -126,70 +172,72 @@
 
 
 def shards(responses, weights, phenotype, eigvecs, eigvals, positions, reaches):
-    z = lax.axis_index("cpg_0")
+    z, x, y = lax.axis_index("cpg_0"), lax.axis_index("samp_1"), lax.axis_index("samp_0")
     layers = lax.axis_size("cpg_0")
-    rows = responses.shape[0]
     with jax.named_scope("weigh"):
-        root = jnp.sqrt(weights.astype(jnp.float32))
-        weighted = (root * responses.astype(jnp.float32)).astype(jnp.bfloat16)
-        design = (root * phenotype[None, :]).astype(jnp.bfloat16)
+        own = weigh(responses, weights, phenotype)
     with jax.named_scope("gather_rows"):
-        blocks = [copies(weighted, FLOOR), copies(design, FLOOR)]
+        blocks = gather_plane(own)
     with jax.named_scope("swap_eigvecs"):
-        vecs = jnp.concatenate([eigvecs, shifted(eigvecs, "samp_2", 1)], axis=1)
-        values = jnp.concatenate([eigvals, shifted(eigvals, "samp_2", 1)])
-
-    def term(t, ahead, lo, hi):
+        low = lax.axis_index("samp_2") == 0
+        other = shifted(eigvecs, "samp_2", 1)
+        vecs = (jnp.where(low, eigvecs, other), jnp.where(low, other, eigvecs))
+        other = shifted(eigvals, "samp_2", 1)
+        values = jnp.where(low, jnp.concatenate([eigvals, other]), jnp.concatenate([other, eigvals]))
+    rows = own.shape[0]
+
+    def term(q, ahead, lo, hi):
         dest = lax.rem(z + ahead + layers, layers)
-        block = lax.dynamic_index_in_dim(blocks[t], dest, 0, keepdims=False)[lo:hi]
-        return jnp.dot(block, vecs, preferred_element_type=jnp.float32)
+        across, along = dest // 4, lax.rem(dest, 4)
+        place = 4 * (across ^ y) + lax.rem(along - x + 4, 4)
+        block = lax.dynamic_index_in_dim(blocks, place, 0, keepdims=False)[lo:hi]
+        return jnp.dot(block, vecs[q], preferred_element_type=jnp.float32)
 
     far = layers // 2
     cut = rows // 2
     sent = {}
 
-    def first(t):
-        sent[t, 1] = shifted(term(t, far, 0, cut).astype(jnp.bfloat16), "cpg_0", 1)
-        sent[t, -1] = shifted(term(t, far, cut, rows).astype(jnp.bfloat16), "cpg_0", -1)
-
-    def onward(t, ahead):
+    def first(q):
+        sent[q, 1] = shifted(term(q, far, 0, cut).astype(jnp.bfloat16), "cpg_0", 1)
+        sent[q, -1] = shifted(term(q, far, cut, rows).astype(jnp.bfloat16), "cpg_0", -1)
+
+    def onward(q, ahead):
         for way in (1, -1):
-            got = sent[t, way].astype(jnp.float32)
+            got = sent[q, way].astype(jnp.float32)
             if got.shape[0] < rows:
                 rest = jnp.zeros_like(got)
                 got = jnp.concatenate([got, rest] if way == 1 else [rest, got], axis=0)
-            total = (term(t, way * ahead, 0, rows) + got).astype(jnp.bfloat16)
-            sent[t, way] = shifted(total, "cpg_0", way)
-
-    def exchanged(t):
-        total = term(t, 0, 0, rows)
+            total = (term(q, way * ahead, 0, rows) + got).astype(jnp.bfloat16)
+            sent[q, way] = shifted(total, "cpg_0", way)
+
+    def summed(q):
+        total = term(q, 0, 0, rows)
         for way in (1, -1):
-            total = total + sent[t, way].astype(jnp.float32)
-        return lax.all_to_all(total.astype(jnp.bfloat16), PLANE, 0, 0, tiled=True)
+            total = total + sent[q, way].astype(jnp.float32)
+        return total.astype(jnp.bfloat16)
 
     with jax.named_scope("sum_layers"):
         first(0)
-        onward(0, 3)
         first(1)
-        onward(0, 2)
-        onward(1, 3)
-        onward(0, 1)
-        onward(1, 2)
-        sums = [exchanged(0)]
-        onward(1, 1)
-        sums.append(exchanged(1))
+        for ahead in range(far - 1, 0, -1):
+            onward(0, ahead)
+            onward(1, ahead)
+        whole = jnp.concatenate([summed(0), summed(1)], axis=1)
+    with jax.named_scope("to_components"):
+        sums = lax.all_to_all(whole, PLANE, 0, 0, tiled=True)
     with jax.named_scope("gather_values"):
+        values = values + 0.0 * whole[0, 0].astype(jnp.float32)
         everywhere = jnp.repeat(copies(values, FLOOR), 4, axis=0)
     with jax.named_scope("fit"):
         slot = lax.axis_index("samp_2") * 16 + lax.axis_index(PLANE)
-        fitted = fit(slot.astype(jnp.int32)[None], *sums, everywhere)
+        fitted = fit(slot.astype(jnp.int32)[None], sums, everywhere)
     with jax.named_scope("gather_scores"):
         layer = jnp.sum(lax.all_to_all(fitted, LAYER, 0, 0, tiled=True), axis=(0, 1))
-        up = [(i, i + 1) for i in range(layers - 1)]
-        down = [(j, i) for i, j in up]
-        before = lax.ppermute(layer, "cpg_0", up)[2 * rows - HALO : 2 * rows]
-        after = lax.ppermute(layer, "cpg_0", down)[:HALO]
-        scores, scales = layer[: 2 * rows], layer[2 * rows :]
+        beside = [(2 * i, 2 * i + 2) for i in range(layers - 1)]
+        beside += [(2 * i + 3, 2 * i + 1) for i in range(layers - 1)]
+        other = lax.ppermute(layer, CPG, beside)
+        scores, scales = layer[:rows], layer[rows:]
+        before, after = other[rows - HALO : rows], other[:HALO]
     with jax.named_scope("smooth"):
         block_len = reaches.shape[0]
         high = lax.axis_index("cpg_1")

time: 148 us -> 126 us (0.85)
  matrix products: 22.1 us -> 9.25 us
  waiting for transfers between devices: 47.8 us -> 40.8 us
  local copies, waits for them, and re-layouts: 10.3 us -> 5.7 us
  other arithmetic: 2 us -> 3.92 us
  Pallas kernels: 2.16 us -> 4.01 us
  starting transfers between devices: 61.4 us -> 59.8 us
    all_to_all x3 -> x1, waiting for transfers between devices: 19.9 us -> 4.05 us  [copies(): lax.all_to_all(jnp.broadcast_to(value[None], (peers, *value.shape)), axes...]
    ppermute x18 -> x27, starting transfers between devices: 28.8 us -> 44.2 us  [shifted(): lax.ppermute(value, axis, [(i, (i + by) % peers) for i in range(peers)])]
    dot_general x18, matrix products: 22.1 us -> 9.25 us  [term(): return jnp.dot(block, vecs[q], preferred_element_type=jnp.float32)]
    ppermute x18 -> x27, waiting for transfers between devices: 5.41 us -> 16.6 us  [shifted(): lax.ppermute(value, axis, [(i, (i + by) % peers) for i in range(peers)])]
    all_to_all x3 -> x1, starting transfers between devices: 12.2 us -> 4.87 us  [copies(): lax.all_to_all(jnp.broadcast_to(value[None], (peers, *value.shape)), axes...]
    all_to_all x2 -> x1, starting transfers between devices: 10.7 us -> 4.97 us  [shards(): sums = lax.all_to_all(whole, PLANE, 0, 0, tiled=True)]
    ppermute x2 -> x1, starting transfers between devices: 5.84 us -> 1.92 us  [shards(): other = lax.ppermute(layer, CPG, beside)]
    all_to_all x2 -> x1, waiting for transfers between devices: 13.1 us -> 9.89 us  [shards(): sums = lax.all_to_all(whole, PLANE, 0, 0, tiled=True)]
  transfers between devices with their start and end apart: 26 -> 31, of which waited for: 9 -> 13; matrix products, arithmetic and copies ran while one was open for 22% -> 13% of each run, Pallas kernels for 0% -> 1%
where the time goes in v3:
time: 126 us
  starting transfers between devices  59.8 us (47%)
  waiting for transfers between devices  40.8 us (32%)
  matrix products  9.25 us (7%)
  local copies, waits for them, and re-layouts  5.7 us (5%)
  Pallas kernels  4.01 us (3%)
  other arithmetic  3.92 us (3%)
  between operations  2.09 us (2%)
    ppermute x27, starting transfers between devices, shifted(): lax.ppermute(value, axis, [(i, (i + by) % peers) for i in range(peers)])  44.2 us
    ppermute x27, waiting for transfers between devices, shifted(): lax.ppermute(value, axis, [(i, (i + by) % peers) for i in range(peers)])  16.6 us
    all_to_all x1, waiting for transfers between devices, shards(): sums = lax.all_to_all(whole, PLANE, 0, 0, tiled=True)  9.89 us
    dot_general x18, matrix products, term(): return jnp.dot(block, vecs[q], preferred_element_type=jnp.float32)  9.25 us
    all_to_all x1, waiting for transfers between devices, shards(): lax.all_to_all(fitted, LAYER, 0, 0, tiled=True)  7.32 us
    all_to_all x1, starting transfers between devices, shards(): sums = lax.all_to_all(whole, PLANE, 0, 0, tiled=True)  4.97 us
    all_to_all x1, starting transfers between devices, copies(): lax.all_to_all(jnp.broadcast_to(value[None], (peers, *value.shape)), axes...  4.87 us
    all_to_all x1, waiting for transfers between devices, copies(): lax.all_to_all(jnp.broadcast_to(value[None], (peers, *value.shape)), axes...  4.05 us
  transfers between devices with their start and end apart: 31, of which 13 were waited for; matrix products, arithmetic and copies ran while one was open for 13% of the time, Pallas kernels for 1%

profile of v3, /device:TPU:96, one launch (start us, length us, event | category | flops | bytes accessed | tf_op | source)
XLA Modules:
  0.0 125.6 jit_solution(2581731703635380380)
XLA Ops:
  0.6 0.1 collective-permute-start.9
  0.7 1.8 %weigh.1 = bf16[128,1024]{1,0:T(8,128)(2,1)} custom-call(bf16[64,1024]{1,0:T(8,128)(2,1)} %resp_ref.1, bf16[64,1024]{1,0:T(8,128)(2,1)} %weight_ref.1, f32[1,1024]{1,0:T(1,128)} %bitcast.90), custom_call_target="tpu_custom_call" | custom-call | tf_op jit(solution)/shard_map/weigh/pallas_call | solution.py:46
  2.5 1.5 %collective-permute-start.1 = (bf16[128,1024]{1,0:T(8,128)(2,1)}, bf16[128,1024]{1,0:T(8,128)(2,1)S(1)}, u32[]{:S(2)}, u32[]{:S(2)}) collective-permute-start(bf16[128,1024]{1,0:T(8,128)(2,1)} %weigh.1), channel_id=1, source_target_pairs={{0,32},{32,64},{64,96},{96,0},{1,33},{33,65},{65,97},{97,1},{2,34}... | collective-permute-start | bytes 786440 | tf_op jit(solution)/shard_map/gather_rows/ppermute | solution.py:25
  4.0 1.6 %collective-permute-start.3 = (bf16[128,1024]{1,0:T(8,128)(2,1)}, bf16[128,1024]{1,0:T(8,128)(2,1)S(1)}, u32[]{:S(2)}, u32[]{:S(2)}) collective-permute-start(bf16[128,1024]{1,0:T(8,128)(2,1)} %weigh.1), channel_id=1, source_target_pairs={{0,128},{128,0},{1,129},{129,1},{2,130},{130,2},{3,131},{131,3},{4... | collective-permute-start | bytes 786440 | tf_op jit(solution)/shard_map/gather_rows/ppermute | solution.py:25
  5.6 1.7 %collective-permute-start = (bf16[128,1024]{1,0:T(8,128)(2,1)}, bf16[128,1024]{1,0:T(8,128)(2,1)}, u32[]{:S(2)}, u32[]{:S(2)}) collective-permute-start(bf16[128,1024]{1,0:T(8,128)(2,1)} %weigh.1), channel_id=1, source_target_pairs={{0,96},{32,0},{64,32},{96,64},{1,97},{33,1},{65,33},{97,65},{2,98}... | collective-permute-start | bytes 786440 | tf_op jit(solution)/shard_map/gather_rows/ppermute | solution.py:25
  7.4 5.3 %collective-permute-done.1 = bf16[128,1024]{1,0:T(8,128)(2,1)S(1)} collective-permute-done((bf16[128,1024]{1,0:T(8,128)(2,1)}, bf16[128,1024]{1,0:T(8,128)(2,1)S(1)}, u32[]{:S(2)}, u32[]{:S(2)}) %collective-permute-start.1) | collective-permute-done | bytes 262176 | tf_op jit(solution)/shard_map/gather_rows/ppermute | solution.py:25
  12.7 0.3 collective-permute-start.2
  12.9 1.6 %collective-permute-start.5 = (bf16[128,1024]{1,0:T(8,128)(2,1)S(1)}, bf16[128,1024]{1,0:T(8,128)(2,1)S(1)}, u32[]{:S(2)}, u32[]{:S(2)}) collective-permute-start(bf16[128,1024]{1,0:T(8,128)(2,1)S(1)} %collective-permute-done.1), channel_id=1, source_target_pairs={{0,128},{128,0},{1,129},{129,1},{2,130},{130,2},{3,131},{131,3},{4... | collective-permute-start | bytes 786440 | tf_op jit(solution)/shard_map/gather_rows/ppermute | solution.py:25
  14.5 3.0 %collective-permute-start.4 = (bf16[128,1024]{1,0:T(8,128)(2,1)S(1)}, bf16[128,1024]{1,0:T(8,128)(2,1)S(1)}, u32[]{:S(2)}, u32[]{:S(2)}) collective-permute-start(bf16[128,1024]{1,0:T(8,128)(2,1)S(1)} %collective-permute-done.3), channel_id=1, source_target_pairs={{0,96},{32,0},{64,32},{96,64},{1,97},{33,1},{65,33},{97,65},{2,98}... | collective-permute-start | bytes 786440 | tf_op jit(solution)/shard_map/gather_rows/ppermute | solution.py:25
  17.5 1.0 bitcast_dynamic-update-slice_fusion.6
  18.9 1.1 bitcast_dynamic-update-slice_fusion.5
  20.0 0.7 collective-permute-done.5
  20.7 1.6 %collective-permute-start.6 = (bf16[48,1024]{1,0:T(8,128)(2,1)S(1)}, bf16[48,1024]{1,0:T(8,128)(2,1)S(1)}, u32[]{:S(2)}, u32[]{:S(2)}) collective-permute-start(bf16[48,1024]{1,0:T(8,128)(2,1)S(1)} %slice.255), channel_id=1, source_target_pairs={{0,32},{32,64},{64,96},{96,0},{1,33},{33,65},{65,97},{97,1},{2,34}... | collective-permute-start | bytes 294920 | tf_op jit(solution)/shard_map/gather_rows/ppermute | solution.py:25
  22.3 1.7 %collective-permute-start.8 = (bf16[32,1024]{1,0:T(8,128)(2,1)S(1)}, bf16[32,1024]{1,0:T(8,128)(2,1)S(1)}, u32[]{:S(2)}, u32[]{:S(2)}) collective-permute-start(bf16[32,1024]{1,0:T(8,128)(2,1)S(1)} %slice.257), channel_id=1, source_target_pairs={{0,128},{128,0},{1,129},{129,1},{2,130},{130,2},{3,131},{131,3},{4... | collective-permute-start | bytes 196616 | tf_op jit(solution)/shard_map/gather_rows/ppermute | solution.py:25
  24.0 2.2 %collective-permute-start.7 = (bf16[48,1024]{1,0:T(8,128)(2,1)S(1)}, bf16[48,1024]{1,0:T(8,128)(2,1)S(1)}, u32[]{:S(2)}, u32[]{:S(2)}) collective-permute-start(bf16[48,1024]{1,0:T(8,128)(2,1)S(1)} %slice.256), channel_id=1, source_target_pairs={{0,96},{32,0},{64,32},{96,64},{1,97},{33,1},{65,33},{97,65},{2,98}... | collective-permute-start | bytes 294920 | tf_op jit(solution)/shard_map/gather_rows/ppermute | solution.py:25
  26.2 0.4 collective-permute-done.8
  26.6 2.0 %collective-permute-done.7 = bf16[48,1024]{1,0:T(8,128)(2,1)S(1)} collective-permute-done((bf16[48,1024]{1,0:T(8,128)(2,1)S(1)}, bf16[48,1024]{1,0:T(8,128)(2,1)S(1)}, u32[]{:S(2)}, u32[]{:S(2)}) %collective-permute-start.7) | collective-permute-done | bytes 98336 | tf_op jit(solution)/shard_map/gather_rows/ppermute | solution.py:25
  28.7 1.3 %copy-done = bf16[8,128,1024]{2,1,0:T(8,128)(2,1)} copy-done((bf16[8,128,1024]{2,1,0:T(8,128)(2,1)}, bf16[8,128,1024]{2,1,0:T(8,128)(2,1)S(1)}, u32[]{:S(2)}) %copy-start) | copy-done | bytes 2097176
  30.1 2.3 %broadcast_select_fusion.1 = (bf16[1024,1024]{1,0:T(8,128)(2,1)S(1)}, bf16[1024,1024]{1,0:T(8,128)(2,1)S(1)}) fusion(bf16[1024,1024]{1,0:T(8,128)(2,1)S(1)} %copy-done.2, bf16[1024,1024]{1,0:T(8,128)(2,1)} %collective-permute-done.9, pred[]{:T(512)S(6)} %eq.3), kind=kLoop, calls=%fused_computation.1 | loop fusion | flops 2097152 | bytes 8388609 | tf_op jit(solution)/shard_map/swap_eigvecs/jit(_where)/select_n | solution.py:184
  32.3 0.5 convolution_convert_fusion.3
  32.8 3.2 %collective-permute-start.10 = (bf16[64,1024]{1,0:T(8,128)(2,1)S(1)}, bf16[64,1024]{1,0:T(8,128)(2,1)S(1)}, u32[]{:S(2)}, u32[]{:S(2)}) collective-permute-start(bf16[64,1024]{1,0:T(8,128)(2,1)S(1)} %convolution_convert_fusion.3), channel_id=1, source_target_pairs={{0,2},{2,4},{4,6},{6,8},{8,10},{10,12},{12,14},{14,0},{1,3},{3,5},... | collective-permute-start | bytes 393224 | tf_op jit(solution)/shard_map/sum_layers/ppermute | solution.py:25
  36.0 0.5 convolution_convert_fusion.2
  36.5 0.5 convolution_convert_fusion.1
  37.0 0.5 convolution_convert_fusion
  37.6 3.2 %collective-permute-start.18 = (bf16[64,1024]{1,0:T(8,128)(2,1)S(1)}, bf16[64,1024]{1,0:T(8,128)(2,1)S(1)}, u32[]{:S(2)}, u32[]{:S(2)}) collective-permute-start(bf16[64,1024]{1,0:T(8,128)(2,1)S(1)} %convolution_convert_fusion.1), channel_id=1, source_target_pairs={{0,2},{2,4},{4,6},{6,8},{8,10},{10,12},{12,14},{14,0},{1,3},{3,5},... | collective-permute-start | bytes 393224 | tf_op jit(solution)/shard_map/sum_layers/ppermute | solution.py:25
  40.8 0.5 fusion.6
  41.3 3.3 %collective-permute-start.11 = (bf16[128,1024]{1,0:T(8,128)(2,1)S(1)}, bf16[128,1024]{1,0:T(8,128)(2,1)S(1)}, u32[]{:S(2)}, u32[]{:S(2)}) collective-permute-start(bf16[128,1024]{1,0:T(8,128)(2,1)S(1)} %fusion.6), channel_id=1, source_target_pairs={{0,2},{2,4},{4,6},{6,8},{8,10},{10,12},{12,14},{14,0},{1,3},{3,5},... | collective-permute-start | bytes 786440 | tf_op jit(solution)/shard_map/sum_layers/ppermute | solution.py:25
  44.6 0.5 fusion.9
  45.2 0.5 fusion.12
  45.6 3.3 %collective-permute-start.19 = (bf16[128,1024]{1,0:T(8,128)(2,1)S(1)}, bf16[128,1024]{1,0:T(8,128)(2,1)S(1)}, u32[]{:S(2)}, u32[]{:S(2)}) collective-permute-start(bf16[128,1024]{1,0:T(8,128)(2,1)S(1)} %fusion.12), channel_id=1, source_target_pairs={{0,2},{2,4},{4,6},{6,8},{8,10},{10,12},{12,14},{14,0},{1,3},{3,5},... | collective-permute-start | bytes 786440 | tf_op jit(solution)/shard_map/sum_layers/ppermute | solution.py:25
  49.0 0.5 fusion.15
  49.5 1.9 %collective-permute-done.11 = bf16[128,1024]{1,0:T(8,128)(2,1)S(1)} collective-permute-done((bf16[128,1024]{1,0:T(8,128)(2,1)S(1)}, bf16[128,1024]{1,0:T(8,128)(2,1)S(1)}, u32[]{:S(2)}, u32[]{:S(2)}) %collective-permute-start.11) | collective-permute-done | bytes 262176 | tf_op jit(solution)/shard_map/sum_layers/ppermute | solution.py:25
  51.4 0.4 fusion.5
  51.8 3.8 %collective-permute-start.12 = (bf16[128,1024]{1,0:T(8,128)(2,1)S(1)}, bf16[128,1024]{1,0:T(8,128)(2,1)S(1)}, u32[]{:S(2)}, u32[]{:S(2)}) collective-permute-start(bf16[128,1024]{1,0:T(8,128)(2,1)S(1)} %fusion.5), channel_id=1, source_target_pairs={{0,2},{2,4},{4,6},{6,8},{8,10},{10,12},{12,14},{14,0},{1,3},{3,5},... | collective-permute-start | bytes 786440 | tf_op jit(solution)/shard_map/sum_layers/ppermute | solution.py:25
  55.6 0.5 fusion.8
  56.2 0.8 collective-permute-done.19
  57.0 0.5 fusion.11
  57.5 3.8 %collective-permute-start.20 = (bf16[128,1024]{1,0:T(8,128)(2,1)S(1)}, bf16[128,1024]{1,0:T(8,128)(2,1)S(1)}, u32[]{:S(2)}, u32[]{:S(2)}) collective-permute-start(bf16[128,1024]{1,0:T(8,128)(2,1)S(1)} %fusion.11), channel_id=1, source_target_pairs={{0,2},{2,4},{4,6},{6,8},{8,10},{10,12},{12,14},{14,0},{1,3},{3,5},... | collective-permute-start | bytes 786440 | tf_op jit(solution)/shard_map/sum_layers/ppermute | solution.py:25
  61.2 0.5 fusion.14
  61.8 0.8 collective-permute-done.12
  62.6 0.4 fusion.4
  63.1 3.8 %collective-permute-start.13 = (bf16[128,1024]{1,0:T(8,128)(2,1)S(1)}, bf16[128,1024]{1,0:T(8,128)(2,1)S(1)}, u32[]{:S(2)}, u32[]{:S(2)}) collective-permute-start(bf16[128,1024]{1,0:T(8,128)(2,1)S(1)} %fusion.4), channel_id=1, source_target_pairs={{0,2},{2,4},{4,6},{6,8},{8,10},{10,12},{12,14},{14,0},{1,3},{3,5},... | collective-permute-start | bytes 786440 | tf_op jit(solution)/shard_map/sum_layers/ppermute | solution.py:25
  66.8 0.4 fusion.7
  67.4 0.8 collective-permute-done.20
  68.2 0.5 fusion.10
  68.7 4.0 %collective-permute-start.21 = (bf16[128,1024]{1,0:T(8,128)(2,1)S(1)}, bf16[128,1024]{1,0:T(8,128)(2,1)S(1)}, u32[]{:S(2)}, u32[]{:S(2)}) collective-permute-start(bf16[128,1024]{1,0:T(8,128)(2,1)S(1)} %fusion.10), channel_id=1, source_target_pairs={{0,2},{2,4},{4,6},{6,8},{8,10},{10,12},{12,14},{14,0},{1,3},{3,5},... | collective-permute-start | bytes 786440 | tf_op jit(solution)/shard_map/sum_layers/ppermute | solution.py:25
  72.7 0.5 fusion.13
  73.3 3.8 %collective-permute-done.17 = bf16[128,1024]{1,0:T(8,128)(2,1)S(1)} collective-permute-done((bf16[128,1024]{1,0:T(8,128)(2,1)S(1)}, bf16[128,1024]{1,0:T(8,128)(2,1)S(1)}, u32[]{:S(2)}, u32[]{:S(2)}) %collective-permute-start.17) | collective-permute-done | bytes 262176 | tf_op jit(solution)/shard_map/sum_layers/ppermute | solution.py:25
  77.1 0.5 fusion.2
  77.5 0.5 slice.258
  78.7 0.7 broadcast_in_dim.17
  79.4 4.9 %all-to-all-start.1 = ((f32[8,1,2048]{2,1,0:T(1,128)}), f32[8,1,2048]{2,1,0:T(1,128)S(1)}, u32[]{:S(2)}, u32[]{:S(2)}) async-start(f32[8,1,2048]{2,1,0:T(1,128)} %broadcast_in_dim.17), calls=%async_computation.1 | async-start | bytes 131072 | tf_op jit(solution)/shard_map/gather_values/all_to_all | solution.py:169
  84.3 1.4 %fusion.3 = bf16[128,1024]{1,0:T(8,128)(2,1)S(1)} fusion(bf16[1024,1024]{1,0:T(8,128)(2,1)S(1)} %get-tuple-element.3, bf16[128,1024]{1,0:T(8,128)(2,1)S(1)} %collective-permute-done.25, bf16[128,1024]{1,0:T(8,128)(2,1)S(1)} %collective-permute-done.21, bf16[8,128,1024]{2,1,0:T(8,128)(2,1)} %copy-done, s32[]{:T(128)S(6)} %select_n.106), kind=kOutput, calls=%fused_computation.19 | convolution fusion | flops 269090816 | bytes 3145732 | tf_op jit(solution)/shard_map/sum_layers/dot_general | solution.py:194
  85.7 0.8 maximum_bitcast_fusion
  86.6 4.0 %all-to-all-done.1 = f32[8,1,2048]{2,1,0:T(1,128)S(1)} async-done(((f32[8,1,2048]{2,1,0:T(1,128)}), f32[8,1,2048]{2,1,0:T(1,128)S(1)}, u32[]{:S(2)}, u32[]{:S(2)}) %all-to-all-start.1) | async-done | bytes 65568 | tf_op jit(solution)/shard_map/gather_values/all_to_all | solution.py:169
  90.6 5.0 %all-to-all-start = ((bf16[16,8,2048]{2,1,0:T(8,128)(2,1)}), bf16[16,8,2048]{2,1,0:T(8,128)(2,1)S(1)}, u32[]{:S(2)}, u32[]{:S(2)}) async-start(bf16[16,8,2048]{2,1,0:T(8,128)(2,1)} %maximum_bitcast_fusion), calls=%async_computation | async-start | bytes 1048576 | tf_op jit(solution)/shard_map/to_components/all_to_all | solution.py:227
  95.9 9.9 %all-to-all-done = bf16[16,8,2048]{2,1,0:T(8,128)(2,1)S(1)} async-done(((bf16[16,8,2048]{2,1,0:T(8,128)(2,1)}), bf16[16,8,2048]{2,1,0:T(8,128)(2,1)S(1)}, u32[]{:S(2)}, u32[]{:S(2)}) %all-to-all-start) | async-done | bytes 524320 | tf_op jit(solution)/shard_map/to_components/all_to_all | solution.py:227
  105.7 2.2 %fit.1 = f32[32,1,256]{2,1,0:T(1,128)} custom-call(s32[1]{0:T(128)} %bitcast.slot_ref, bf16[128,2048]{1,0:T(8,128)(2,1)S(1)} %bitcast.88, f32[32,2048]{1,0:T(8,128)S(1)} %reshape.50.values_ref), custom_call_target="tpu_custom_call" | custom-call | tf_op jit(solution)/shard_map/fit/pallas_call | solution.py:119
  107.9 3.8 %all-to-all-start.2 = ((f32[32,1,256]{2,1,0:T(1,128)}), f32[32,1,256]{2,1,0:T(1,128)S(1)}, u32[]{:S(2)}, u32[]{:S(2)}) async-start(f32[32,1,256]{2,1,0:T(1,128)} %fit.1), calls=%async_computation.2 | async-start | bytes 65536 | tf_op jit(solution)/shard_map/gather_scores/all_to_all | solution.py:235
  111.9 7.3 %all-to-all-done.2 = f32[32,1,256]{2,1,0:T(1,128)S(1)} async-done(((f32[32,1,256]{2,1,0:T(1,128)}), f32[32,1,256]{2,1,0:T(1,128)S(1)}, u32[]{:S(2)}, u32[]{:S(2)}) %all-to-all-start.2) | async-done | bytes 32800 | tf_op jit(solution)/shard_map/gather_scores/all_to_all | solution.py:235
  119.2 1.9 %collective-permute-start.27 = (f32[256]{0:T(256)S(1)}, f32[256]{0:T(256)S(1)}, u32[]{:S(2)}, u32[]{:S(2)}) collective-permute-start(f32[256]{0:T(256)S(1)} %reduce_sum.9), channel_id=1, source_target_pairs={{0,2},{2,4},{4,6},{6,8},{8,10},{10,12},{12,14},{3,1},{5,3},{7,5},{... | collective-permute-start | bytes 3080 | tf_op jit(solution)/shard_map/gather_scores/ppermute | solution.py:238
  121.2 0.6 dynamic_slice.54
  121.8 2.9 %collective-permute-done.27 = f32[256]{0:T(256)S(1)} collective-permute-done((f32[256]{0:T(256)S(1)}, f32[256]{0:T(256)S(1)}, u32[]{:S(2)}, u32[]{:S(2)}) %collective-permute-start.27) | collective-permute-done | bytes 1056 | tf_op jit(solution)/shard_map/gather_scores/ppermute | solution.py:238
  124.9 0.6 add_divide_fusion
  (59 shorter events, 1.4 us)
Async XLA Ops:
  0.6 29.4 %collective-permute-start.9 = (bf16[1024,1024]{1,0:T(8,128)(2,1)}, bf16[1024,1024]{1,0:T(8,128)(2,1)}, u32[]{:S(2)}, u32[]{:S(2)}) collective-permute-start(bf16[1024,1024]{1,0:T(8,128)(2,1)} %param.10), channel_id=1, source_target_pairs={{0,16},{16,0},{1,17},{17,1},{2,18},{18,2},{3,19},{19,3},{4,20},{20... | collective-permute-start | bytes 6291464 | tf_op jit(solution)/shard_map/swap_eigvecs/ppermute | solution.py:25
  2.5 10.1 %collective-permute-start.1 = (bf16[128,1024]{1,0:T(8,128)(2,1)}, bf16[128,1024]{1,0:T(8,128)(2,1)S(1)}, u32[]{:S(2)}, u32[]{:S(2)}) collective-permute-start(bf16[128,1024]{1,0:T(8,128)(2,1)} %weigh.1), channel_id=1, source_target_pairs={{0,32},{32,64},{64,96},{96,0},{1,33},{33,65},{65,97},{97,1},{2,34}... | collective-permute-start | bytes 786440 | tf_op jit(solution)/shard_map/gather_rows/ppermute | solution.py:25
  4.0 10.5 %collective-permute-start.3 = (bf16[128,1024]{1,0:T(8,128)(2,1)}, bf16[128,1024]{1,0:T(8,128)(2,1)S(1)}, u32[]{:S(2)}, u32[]{:S(2)}) collective-permute-start(bf16[128,1024]{1,0:T(8,128)(2,1)} %weigh.1), channel_id=1, source_target_pairs={{0,128},{128,0},{1,129},{129,1},{2,130},{130,2},{3,131},{131,3},{4... | collective-permute-start | bytes 786440 | tf_op jit(solution)/shard_map/gather_rows/ppermute | solution.py:25
  5.6 13.2 %collective-permute-start = (bf16[128,1024]{1,0:T(8,128)(2,1)}, bf16[128,1024]{1,0:T(8,128)(2,1)}, u32[]{:S(2)}, u32[]{:S(2)}) collective-permute-start(bf16[128,1024]{1,0:T(8,128)(2,1)} %weigh.1), channel_id=1, source_target_pairs={{0,96},{32,0},{64,32},{96,64},{1,97},{33,1},{65,33},{97,65},{2,98}... | collective-permute-start | bytes 786440 | tf_op jit(solution)/shard_map/gather_rows/ppermute | solution.py:25
  12.7 9.6 %collective-permute-start.2 = (bf16[128,1024]{1,0:T(8,128)(2,1)S(1)}, bf16[128,1024]{1,0:T(8,128)(2,1)S(1)}, u32[]{:S(2)}, u32[]{:S(2)}) collective-permute-start(bf16[128,1024]{1,0:T(8,128)(2,1)S(1)} %collective-permute-done.1), channel_id=1, source_target_pairs={{0,32},{32,64},{64,96},{96,0},{1,33},{33,65},{65,97},{97,1},{2,34}... | collective-permute-start | bytes 786440 | tf_op jit(solution)/shard_map/gather_rows/ppermute | solution.py:25
  12.9 7.7 %collective-permute-start.5 = (bf16[128,1024]{1,0:T(8,128)(2,1)S(1)}, bf16[128,1024]{1,0:T(8,128)(2,1)S(1)}, u32[]{:S(2)}, u32[]{:S(2)}) collective-permute-start(bf16[128,1024]{1,0:T(8,128)(2,1)S(1)} %collective-permute-done.1), channel_id=1, source_target_pairs={{0,128},{128,0},{1,129},{129,1},{2,130},{130,2},{3,131},{131,3},{4... | collective-permute-start | bytes 786440 | tf_op jit(solution)/shard_map/gather_rows/ppermute | solution.py:25
  14.5 9.4 %collective-permute-start.4 = (bf16[128,1024]{1,0:T(8,128)(2,1)S(1)}, bf16[128,1024]{1,0:T(8,128)(2,1)S(1)}, u32[]{:S(2)}, u32[]{:S(2)}) collective-permute-start(bf16[128,1024]{1,0:T(8,128)(2,1)S(1)} %collective-permute-done.3), channel_id=1, source_target_pairs={{0,96},{32,0},{64,32},{96,64},{1,97},{33,1},{65,33},{97,65},{2,98}... | collective-permute-start | bytes 786440 | tf_op jit(solution)/shard_map/gather_rows/ppermute | solution.py:25
  18.8 11.3 %copy-start.2 = (bf16[1024,1024]{1,0:T(8,128)(2,1)S(1)}, bf16[1024,1024]{1,0:T(8,128)(2,1)}, u32[]{:S(2)}) copy-start(bf16[1024,1024]{1,0:T(8,128)(2,1)} %param.10) | copy-start | bytes 6291460
  18.8 59.9 %collective-permute-start.26 = (f32[1024]{0:T(1024)}, f32[1024]{0:T(1024)S(1)}, u32[]{:S(2)}, u32[]{:S(2)}) collective-permute-start(f32[1024]{0:T(1024)} %param.11), channel_id=1, source_target_pairs={{0,16},{16,0},{1,17},{17,1},{2,18},{18,2},{3,19},{19,3},{4,20},{20... | collective-permute-start | bytes 12296 | tf_op jit(solution)/shard_map/swap_eigvecs/ppermute | solution.py:25
  20.7 5.9 %collective-permute-start.6 = (bf16[48,1024]{1,0:T(8,128)(2,1)S(1)}, bf16[48,1024]{1,0:T(8,128)(2,1)S(1)}, u32[]{:S(2)}, u32[]{:S(2)}) collective-permute-start(bf16[48,1024]{1,0:T(8,128)(2,1)S(1)} %slice.255), channel_id=1, source_target_pairs={{0,32},{32,64},{64,96},{96,0},{1,33},{33,65},{65,97},{97,1},{2,34}... | collective-permute-start | bytes 294920 | tf_op jit(solution)/shard_map/gather_rows/ppermute | solution.py:25
  22.3 4.4 %collective-permute-start.8 = (bf16[32,1024]{1,0:T(8,128)(2,1)S(1)}, bf16[32,1024]{1,0:T(8,128)(2,1)S(1)}, u32[]{:S(2)}, u32[]{:S(2)}) collective-permute-start(bf16[32,1024]{1,0:T(8,128)(2,1)S(1)} %slice.257), channel_id=1, source_target_pairs={{0,128},{128,0},{1,129},{129,1},{2,130},{130,2},{3,131},{131,3},{4... | collective-permute-start | bytes 196616 | tf_op jit(solution)/shard_map/gather_rows/ppermute | solution.py:25
  24.0 4.7 %collective-permute-start.7 = (bf16[48,1024]{1,0:T(8,128)(2,1)S(1)}, bf16[48,1024]{1,0:T(8,128)(2,1)S(1)}, u32[]{:S(2)}, u32[]{:S(2)}) collective-permute-start(bf16[48,1024]{1,0:T(8,128)(2,1)S(1)} %slice.256), channel_id=1, source_target_pairs={{0,96},{32,0},{64,32},{96,64},{1,97},{33,1},{65,33},{97,65},{2,98}... | collective-permute-start | bytes 294920 | tf_op jit(solution)/shard_map/gather_rows/ppermute | solution.py:25
  28.7 1.3 %copy-start = (bf16[8,128,1024]{2,1,0:T(8,128)(2,1)}, bf16[8,128,1024]{2,1,0:T(8,128)(2,1)S(1)}, u32[]{:S(2)}) copy-start(bf16[8,128,1024]{2,1,0:T(8,128)(2,1)S(1)} %bitcast_dynamic-update-slice_fusion) | copy-start | bytes 6291460
  30.1 2.3 %copy-start.1 = (bf16[8,128,1024]{2,1,0:T(8,128)(2,1)S(1)}, bf16[8,128,1024]{2,1,0:T(8,128)(2,1)}, u32[]{:S(2)}) copy-start(bf16[8,128,1024]{2,1,0:T(8,128)(2,1)} %copy-done) | copy-start | bytes 6291460
  32.8 8.0 %collective-permute-start.10 = (bf16[64,1024]{1,0:T(8,128)(2,1)S(1)}, bf16[64,1024]{1,0:T(8,128)(2,1)S(1)}, u32[]{:S(2)}, u32[]{:S(2)}) collective-permute-start(bf16[64,1024]{1,0:T(8,128)(2,1)S(1)} %convolution_convert_fusion.3), channel_id=1, source_target_pairs={{0,2},{2,4},{4,6},{6,8},{8,10},{10,12},{12,14},{14,0},{1,3},{3,5},... | collective-permute-start | bytes 393224 | tf_op jit(solution)/shard_map/sum_layers/ppermute | solution.py:25
  37.5 7.1 %collective-permute-start.14 = (bf16[64,1024]{1,0:T(8,128)(2,1)S(1)}, bf16[64,1024]{1,0:T(8,128)(2,1)S(1)}, u32[]{:S(2)}, u32[]{:S(2)}) collective-permute-start(bf16[64,1024]{1,0:T(8,128)(2,1)S(1)} %convolution_convert_fusion.2), channel_id=1, source_target_pairs={{0,14},{2,0},{4,2},{6,4},{8,6},{10,8},{12,10},{14,12},{1,15},{3,1}... | collective-permute-start | bytes 393224 | tf_op jit(solution)/shard_map/sum_layers/ppermute | solution.py:25
  37.6 7.6 %collective-permute-start.18 = (bf16[64,1024]{1,0:T(8,128)(2,1)S(1)}, bf16[64,1024]{1,0:T(8,128)(2,1)S(1)}, u32[]{:S(2)}, u32[]{:S(2)}) collective-permute-start(bf16[64,1024]{1,0:T(8,128)(2,1)S(1)} %convolution_convert_fusion.1), channel_id=1, source_target_pairs={{0,2},{2,4},{4,6},{6,8},{8,10},{10,12},{12,14},{14,0},{1,3},{3,5},... | collective-permute-start | bytes 393224 | tf_op jit(solution)/shard_map/sum_layers/ppermute | solution.py:25
  40.8 8.1 %collective-permute-start.22 = (bf16[64,1024]{1,0:T(8,128)(2,1)S(1)}, bf16[64,1024]{1,0:T(8,128)(2,1)S(1)}, u32[]{:S(2)}, u32[]{:S(2)}) collective-permute-start(bf16[64,1024]{1,0:T(8,128)(2,1)S(1)} %convolution_convert_fusion), channel_id=1, source_target_pairs={{0,14},{2,0},{4,2},{6,4},{8,6},{10,8},{12,10},{14,12},{1,15},{3,1}... | collective-permute-start | bytes 393224 | tf_op jit(solution)/shard_map/sum_layers/ppermute | solution.py:25
  41.3 10.1 %collective-permute-start.11 = (bf16[128,1024]{1,0:T(8,128)(2,1)S(1)}, bf16[128,1024]{1,0:T(8,128)(2,1)S(1)}, u32[]{:S(2)}, u32[]{:S(2)}) collective-permute-start(bf16[128,1024]{1,0:T(8,128)(2,1)S(1)} %fusion.6), channel_id=1, source_target_pairs={{0,2},{2,4},{4,6},{6,8},{8,10},{10,12},{12,14},{14,0},{1,3},{3,5},... | collective-permute-start | bytes 786440 | tf_op jit(solution)/shard_map/sum_layers/ppermute | solution.py:25
  45.1 10.5 %collective-permute-start.15 = (bf16[128,1024]{1,0:T(8,128)(2,1)S(1)}, bf16[128,1024]{1,0:T(8,128)(2,1)S(1)}, u32[]{:S(2)}, u32[]{:S(2)}) collective-permute-start(bf16[128,1024]{1,0:T(8,128)(2,1)S(1)} %fusion.9), channel_id=1, source_target_pairs={{0,14},{2,0},{4,2},{6,4},{8,6},{10,8},{12,10},{14,12},{1,15},{3,1}... | collective-permute-start | bytes 786440 | tf_op jit(solution)/shard_map/sum_layers/ppermute | solution.py:25
  45.6 11.4 %collective-permute-start.19 = (bf16[128,1024]{1,0:T(8,128)(2,1)S(1)}, bf16[128,1024]{1,0:T(8,128)(2,1)S(1)}, u32[]{:S(2)}, u32[]{:S(2)}) collective-permute-start(bf16[128,1024]{1,0:T(8,128)(2,1)S(1)} %fusion.12), channel_id=1, source_target_pairs={{0,2},{2,4},{4,6},{6,8},{8,10},{10,12},{12,14},{14,0},{1,3},{3,5},... | collective-permute-start | bytes 786440 | tf_op jit(solution)/shard_map/sum_layers/ppermute | solution.py:25
  49.4 11.8 %collective-permute-start.23 = (bf16[128,1024]{1,0:T(8,128)(2,1)S(1)}, bf16[128,1024]{1,0:T(8,128)(2,1)S(1)}, u32[]{:S(2)}, u32[]{:S(2)}) collective-permute-start(bf16[128,1024]{1,0:T(8,128)(2,1)S(1)} %fusion.15), channel_id=1, source_target_pairs={{0,14},{2,0},{4,2},{6,4},{8,6},{10,8},{12,10},{14,12},{1,15},{3,1}... | collective-permute-start | bytes 786440 | tf_op jit(solution)/shard_map/sum_layers/ppermute | solution.py:25
  51.8 10.8 %collective-permute-start.12 = (bf16[128,1024]{1,0:T(8,128)(2,1)S(1)}, bf16[128,1024]{1,0:T(8,128)(2,1)S(1)}, u32[]{:S(2)}, u32[]{:S(2)}) collective-permute-start(bf16[128,1024]{1,0:T(8,128)(2,1)S(1)} %fusion.5), channel_id=1, source_target_pairs={{0,2},{2,4},{4,6},{6,8},{8,10},{10,12},{12,14},{14,0},{1,3},{3,5},... | collective-permute-start | bytes 786440 | tf_op jit(solution)/shard_map/sum_layers/ppermute | solution.py:25
  56.1 10.8 %collective-permute-start.16 = (bf16[128,1024]{1,0:T(8,128)(2,1)S(1)}, bf16[128,1024]{1,0:T(8,128)(2,1)S(1)}, u32[]{:S(2)}, u32[]{:S(2)}) collective-permute-start(bf16[128,1024]{1,0:T(8,128)(2,1)S(1)} %fusion.8), channel_id=1, source_target_pairs={{0,14},{2,0},{4,2},{6,4},{8,6},{10,8},{12,10},{14,12},{1,15},{3,1}... | collective-permute-start | bytes 786440 | tf_op jit(solution)/shard_map/sum_layers/ppermute | solution.py:25
  57.5 10.8 %collective-permute-start.20 = (bf16[128,1024]{1,0:T(8,128)(2,1)S(1)}, bf16[128,1024]{1,0:T(8,128)(2,1)S(1)}, u32[]{:S(2)}, u32[]{:S(2)}) collective-permute-start(bf16[128,1024]{1,0:T(8,128)(2,1)S(1)} %fusion.11), channel_id=1, source_target_pairs={{0,2},{2,4},{4,6},{6,8},{8,10},{10,12},{12,14},{14,0},{1,3},{3,5},... | collective-permute-start | bytes 786440 | tf_op jit(solution)/shard_map/sum_layers/ppermute | solution.py:25
  61.7 11.0 %collective-permute-start.24 = (bf16[128,1024]{1,0:T(8,128)(2,1)S(1)}, bf16[128,1024]{1,0:T(8,128)(2,1)S(1)}, u32[]{:S(2)}, u32[]{:S(2)}) collective-permute-start(bf16[128,1024]{1,0:T(8,128)(2,1)S(1)} %fusion.14), channel_id=1, source_target_pairs={{0,14},{2,0},{4,2},{6,4},{8,6},{10,8},{12,10},{14,12},{1,15},{3,1}... | collective-permute-start | bytes 786440 | tf_op jit(solution)/shard_map/sum_layers/ppermute | solution.py:25
  63.1 10.2 %collective-permute-start.13 = (bf16[128,1024]{1,0:T(8,128)(2,1)S(1)}, bf16[128,1024]{1,0:T(8,128)(2,1)S(1)}, u32[]{:S(2)}, u32[]{:S(2)}) collective-permute-start(bf16[128,1024]{1,0:T(8,128)(2,1)S(1)} %fusion.4), channel_id=1, source_target_pairs={{0,2},{2,4},{4,6},{6,8},{8,10},{10,12},{12,14},{14,0},{1,3},{3,5},... | collective-permute-start | bytes 786440 | tf_op jit(solution)/shard_map/sum_layers/ppermute | solution.py:25
  67.3 9.8 %collective-permute-start.17 = (bf16[128,1024]{1,0:T(8,128)(2,1)S(1)}, bf16[128,1024]{1,0:T(8,128)(2,1)S(1)}, u32[]{:S(2)}, u32[]{:S(2)}) collective-permute-start(bf16[128,1024]{1,0:T(8,128)(2,1)S(1)} %fusion.7), channel_id=1, source_target_pairs={{0,14},{2,0},{4,2},{6,4},{8,6},{10,8},{12,10},{14,12},{1,15},{3,1}... | collective-permute-start | bytes 786440 | tf_op jit(solution)/shard_map/sum_layers/ppermute | solution.py:25
  68.7 15.6 %collective-permute-start.21 = (bf16[128,1024]{1,0:T(8,128)(2,1)S(1)}, bf16[128,1024]{1,0:T(8,128)(2,1)S(1)}, u32[]{:S(2)}, u32[]{:S(2)}) collective-permute-start(bf16[128,1024]{1,0:T(8,128)(2,1)S(1)} %fusion.10), channel_id=1, source_target_pairs={{0,2},{2,4},{4,6},{6,8},{8,10},{10,12},{12,14},{14,0},{1,3},{3,5},... | collective-permute-start | bytes 786440 | tf_op jit(solution)/shard_map/sum_layers/ppermute | solution.py:25
  73.1 5.6 %copy-start.3 = (f32[1024]{0:T(1024)S(1)}, f32[1024]{0:T(1024)}, u32[]{:S(2)}) copy-start(f32[1024]{0:T(1024)} %param.11) | copy-start | bytes 12292
  73.2 11.1 %collective-permute-start.25 = (bf16[128,1024]{1,0:T(8,128)(2,1)S(1)}, bf16[128,1024]{1,0:T(8,128)(2,1)S(1)}, u32[]{:S(2)}, u32[]{:S(2)}) collective-permute-start(bf16[128,1024]{1,0:T(8,128)(2,1)S(1)} %fusion.13), channel_id=1, source_target_pairs={{0,14},{2,0},{4,2},{6,4},{8,6},{10,8},{12,10},{14,12},{1,15},{3,1}... | collective-permute-start | bytes 786440 | tf_op jit(solution)/shard_map/sum_layers/ppermute | solution.py:25
  79.4 11.2 %all-to-all-start.1 = ((f32[8,1,2048]{2,1,0:T(1,128)}), f32[8,1,2048]{2,1,0:T(1,128)S(1)}, u32[]{:S(2)}, u32[]{:S(2)}) async-start(f32[8,1,2048]{2,1,0:T(1,128)} %broadcast_in_dim.17), calls=%async_computation.1 | async-start | bytes 131072 | tf_op jit(solution)/shard_map/gather_values/all_to_all | solution.py:169
  84.3 11.3 %copy-start.4 = (s32[1024]{0:T(1024)S(1)}, s32[1024]{0:T(1024)}, u32[]{:S(2)}) copy-start(s32[1024]{0:T(1024)} %param.12) | copy-start | bytes 12292
  85.7 39.2 %copy-start.5 = (s32[64]{0:T(128)S(1)}, s32[64]{0:T(128)}, u32[]{:S(2)}) copy-start(s32[64]{0:T(128)} %param.13) | copy-start | bytes 772
  90.6 15.1 %all-to-all-start = ((bf16[16,8,2048]{2,1,0:T(8,128)(2,1)}), bf16[16,8,2048]{2,1,0:T(8,128)(2,1)S(1)}, u32[]{:S(2)}, u32[]{:S(2)}) async-start(bf16[16,8,2048]{2,1,0:T(8,128)(2,1)} %maximum_bitcast_fusion), calls=%async_computation | async-start | bytes 1048576 | tf_op jit(solution)/shard_map/to_components/all_to_all | solution.py:227
  107.9 11.2 %all-to-all-start.2 = ((f32[32,1,256]{2,1,0:T(1,128)}), f32[32,1,256]{2,1,0:T(1,128)S(1)}, u32[]{:S(2)}, u32[]{:S(2)}) async-start(f32[32,1,256]{2,1,0:T(1,128)} %fit.1), calls=%async_computation.2 | async-start | bytes 65536 | tf_op jit(solution)/shard_map/gather_scores/all_to_all | solution.py:235
  119.2 5.5 %collective-permute-start.27 = (f32[256]{0:T(256)S(1)}, f32[256]{0:T(256)S(1)}, u32[]{:S(2)}, u32[]{:S(2)}) collective-permute-start(f32[256]{0:T(256)S(1)} %reduce_sum.9), channel_id=1, source_target_pairs={{0,2},{2,4},{4,6},{6,8},{8,10},{10,12},{12,14},{3,1},{5,3},{7,5},{... | collective-permute-start | bytes 3080 | tf_op jit(solution)/shard_map/gather_scores/ppermute | solution.py:238

commit v4 on v3

--- a/solution.py
+++ b/solution.py
@@ -179,17 +179,19 @@
     with jax.named_scope("gather_rows"):
         blocks = gather_plane(own)
     with jax.named_scope("swap_eigvecs"):
-        low = lax.axis_index("samp_2") == 0
         other = shifted(eigvecs, "samp_2", 1)
-        vecs = (jnp.where(low, eigvecs, other), jnp.where(low, other, eigvecs))
-        other = shifted(eigvals, "samp_2", 1)
-        values = jnp.where(low, jnp.concatenate([eigvals, other]), jnp.concatenate([other, eigvals]))
+        vecs = (eigvecs, other)
+        ready = (0.0 * other[0, 0].astype(jnp.float32)).astype(jnp.int32)
+    with jax.named_scope("gather_values"):
+        everywhere = copies(eigvals, SAMP).reshape(-1, 2, eigvals.shape[0])
+        everywhere = jnp.where(lax.axis_index("samp_2") == 0, everywhere, everywhere[:, ::-1])
+        everywhere = jnp.repeat(everywhere.reshape(everywhere.shape[0], -1), 4, axis=0)
     rows = own.shape[0]
 
     def term(q, ahead, lo, hi):
         dest = lax.rem(z + ahead + layers, layers)
         across, along = dest // 4, lax.rem(dest, 4)
-        place = 4 * (across ^ y) + lax.rem(along - x + 4, 4)
+        place = 4 * (across ^ y) + lax.rem(along - x + 4, 4) + ready
         block = lax.dynamic_index_in_dim(blocks, place, 0, keepdims=False)[lo:hi]
         return jnp.dot(block, vecs[q], preferred_element_type=jnp.float32)
 
@@ -225,9 +227,6 @@
         whole = jnp.concatenate([summed(0), summed(1)], axis=1)
     with jax.named_scope("to_components"):
         sums = lax.all_to_all(whole, PLANE, 0, 0, tiled=True)
-    with jax.named_scope("gather_values"):
-        values = values + 0.0 * whole[0, 0].astype(jnp.float32)
-        everywhere = jnp.repeat(copies(values, FLOOR), 4, axis=0)
     with jax.named_scope("fit"):
         slot = lax.axis_index("samp_2") * 16 + lax.axis_index(PLANE)
         fitted = fit(slot.astype(jnp.int32)[None], sums, everywhere)

time: 126 us -> 131 us (1.040)
  matrix products: 9.25 us -> 24.6 us
  waiting for transfers between devices: 40.8 us -> 30.6 us
  local copies, waits for them, and re-layouts: 5.7 us -> 11.1 us
  starting transfers between devices: 59.8 us -> 55.4 us
  other arithmetic: 3.92 us -> 2.51 us
    dot_general x18, matrix products: 9.25 us -> 24.6 us  [term(): return jnp.dot(block, vecs[q], preferred_element_type=jnp.float32)]
    ppermute x27 -> x26, starting transfers between devices: 44.2 us -> 36.9 us  [shifted(): lax.ppermute(value, axis, [(i, (i + by) % peers) for i in range(peers)])]
    all_to_all x1, waiting for transfers between devices: 4.05 us -> 0.01 us  [copies(): lax.all_to_all(jnp.broadcast_to(value[None], (peers, *value.shape)), axes...]
    ppermute x1, starting transfers between devices: 1.92 us -> 5.6 us  [shards(): other = lax.ppermute(layer, CPG, beside)]
    ppermute x27 -> x26, waiting for transfers between devices: 16.6 us -> 13.4 us  [shifted(): lax.ppermute(value, axis, [(i, (i + by) % peers) for i in range(peers)])]
    unnamed x19 -> x15, local copies, waits for them, and re-layouts: 3.52 us -> 6.42 us
    select_n x1 -> x0, other arithmetic: 2.28 us -> none  [shards(): vecs = (jnp.where(low, eigvecs, other), jnp.where(low, other, eigvecs))]
    ppermute x1, waiting for transfers between devices: 2.93 us -> 0.67 us  [shards(): other = lax.ppermute(layer, CPG, beside)]
  transfers between devices with their start and end apart: 31 -> 30, of which waited for: 13 -> 12; matrix products, arithmetic and copies ran while one was open for 13% -> 29% of each run, Pallas kernels for 1% -> 1%
where the time goes in v4:
time: 131 us; the launch traced here: 130 us
  starting transfers between devices  55.4 us (42%)
  waiting for transfers between devices  30.6 us (23%)
  matrix products  24.6 us (19%)
  local copies, waits for them, and re-layouts  11.1 us (8%)
  Pallas kernels  4.01 us (3%)
  other arithmetic  2.51 us (2%)
  between operations  1.78 us (1%)
    ppermute x26, starting transfers between devices, shifted(): lax.ppermute(value, axis, [(i, (i + by) % peers) for i in range(peers)])  36.9 us
    dot_general x18, matrix products, term(): return jnp.dot(block, vecs[q], preferred_element_type=jnp.float32)  24.6 us
    ppermute x26, waiting for transfers between devices, shifted(): lax.ppermute(value, axis, [(i, (i + by) % peers) for i in range(peers)])  13.4 us
    all_to_all x1, waiting for transfers between devices, shards(): sums = lax.all_to_all(whole, PLANE, 0, 0, tiled=True)  9.26 us
    all_to_all x1, waiting for transfers between devices, shards(): lax.all_to_all(fitted, LAYER, 0, 0, tiled=True)  7.32 us
    unnamed x15, local copies, waits for them, and re-layouts  6.42 us
    ppermute x1, starting transfers between devices, shards(): other = lax.ppermute(layer, CPG, beside)  5.6 us
    all_to_all x1, starting transfers between devices, shards(): sums = lax.all_to_all(whole, PLANE, 0, 0, tiled=True)  5.52 us
  transfers between devices with their start and end apart: 30, of which 12 were waited for; matrix products, arithmetic and copies ran while one was open for 29% of the time, Pallas kernels for 1%

profile of v4, /device:TPU:96, one launch (start us, length us, event | category | flops | bytes accessed | tf_op | source)
XLA Modules:
  0.0 130.0 jit_solution(7588820458394491090)
XLA Ops:
  0.7 1.8 %weigh.1 = bf16[128,1024]{1,0:T(8,128)(2,1)} custom-call(bf16[64,1024]{1,0:T(8,128)(2,1)} %resp_ref.1, bf16[64,1024]{1,0:T(8,128)(2,1)} %weight_ref.1, f32[1,1024]{1,0:T(1,128)} %bitcast.90), custom_call_target="tpu_custom_call" | custom-call | tf_op jit(solution)/shard_map/weigh/pallas_call | solution.py:46
  2.5 1.5 %collective-permute-start.1 = (bf16[128,1024]{1,0:T(8,128)(2,1)}, bf16[128,1024]{1,0:T(8,128)(2,1)S(1)}, u32[]{:S(2)}, u32[]{:S(2)}) collective-permute-start(bf16[128,1024]{1,0:T(8,128)(2,1)} %weigh.1), channel_id=1, source_target_pairs={{0,32},{32,64},{64,96},{96,0},{1,33},{33,65},{65,97},{97,1},{2,34}... | collective-permute-start | bytes 786440 | tf_op jit(solution)/shard_map/gather_rows/ppermute | solution.py:25
  4.0 1.6 %collective-permute-start.3 = (bf16[128,1024]{1,0:T(8,128)(2,1)}, bf16[128,1024]{1,0:T(8,128)(2,1)S(1)}, u32[]{:S(2)}, u32[]{:S(2)}) collective-permute-start(bf16[128,1024]{1,0:T(8,128)(2,1)} %weigh.1), channel_id=1, source_target_pairs={{0,128},{128,0},{1,129},{129,1},{2,130},{130,2},{3,131},{131,3},{4... | collective-permute-start | bytes 786440 | tf_op jit(solution)/shard_map/gather_rows/ppermute | solution.py:25
  5.6 1.7 %collective-permute-start = (bf16[128,1024]{1,0:T(8,128)(2,1)}, bf16[128,1024]{1,0:T(8,128)(2,1)}, u32[]{:S(2)}, u32[]{:S(2)}) collective-permute-start(bf16[128,1024]{1,0:T(8,128)(2,1)} %weigh.1), channel_id=1, source_target_pairs={{0,96},{32,0},{64,32},{96,64},{1,97},{33,1},{65,33},{97,65},{2,98}... | collective-permute-start | bytes 786440 | tf_op jit(solution)/shard_map/gather_rows/ppermute | solution.py:25
  7.4 1.3 %broadcast_in_dim.17 = f32[16,1,1024]{2,1,0:T(1,128)} broadcast(f32[1024]{0:T(1024)} %param.11), dimensions={2} | broadcast | bytes 69632 | tf_op jit(solution)/shard_map/gather_values/broadcast_in_dim | solution.py:170
  8.7 3.5 %all-to-all-start.1 = ((f32[16,1,1024]{2,1,0:T(1,128)}), f32[16,1,1024]{2,1,0:T(1,128)S(1)}, u32[]{:S(2)}, u32[]{:S(2)}) async-start(f32[16,1,1024]{2,1,0:T(1,128)} %broadcast_in_dim.17), calls=%async_computation.1 | async-start | bytes 131072 | tf_op jit(solution)/shard_map/gather_values/all_to_all | solution.py:169
  12.2 0.5 collective-permute-done.1
  12.7 1.6 %collective-permute-start.5 = (bf16[128,1024]{1,0:T(8,128)(2,1)S(1)}, bf16[128,1024]{1,0:T(8,128)(2,1)S(1)}, u32[]{:S(2)}, u32[]{:S(2)}) collective-permute-start(bf16[128,1024]{1,0:T(8,128)(2,1)S(1)} %collective-permute-done.1), channel_id=1, source_target_pairs={{0,128},{128,0},{1,129},{129,1},{2,130},{130,2},{3,131},{131,3},{4... | collective-permute-start | bytes 786440 | tf_op jit(solution)/shard_map/gather_rows/ppermute | solution.py:25
  14.2 1.4 %collective-permute-start.2 = (bf16[128,1024]{1,0:T(8,128)(2,1)S(1)}, bf16[128,1024]{1,0:T(8,128)(2,1)S(1)}, u32[]{:S(2)}, u32[]{:S(2)}) collective-permute-start(bf16[128,1024]{1,0:T(8,128)(2,1)S(1)} %collective-permute-done.1), channel_id=1, source_target_pairs={{0,32},{32,64},{64,96},{96,0},{1,33},{33,65},{65,97},{97,1},{2,34}... | collective-permute-start | bytes 786440 | tf_op jit(solution)/shard_map/gather_rows/ppermute | solution.py:25
  15.6 1.9 %collective-permute-start.4 = (bf16[128,1024]{1,0:T(8,128)(2,1)S(1)}, bf16[128,1024]{1,0:T(8,128)(2,1)S(1)}, u32[]{:S(2)}, u32[]{:S(2)}) collective-permute-start(bf16[128,1024]{1,0:T(8,128)(2,1)S(1)} %collective-permute-done.3), channel_id=1, source_target_pairs={{0,96},{32,0},{64,32},{96,64},{1,97},{33,1},{65,33},{97,65},{2,98}... | collective-permute-start | bytes 786440 | tf_op jit(solution)/shard_map/gather_rows/ppermute | solution.py:25
  17.5 1.7 %bitcast_dynamic-update-slice_fusion.6 = bf16[8,128,1024]{2,1,0:T(8,128)(2,1)} fusion(bf16[128,1024]{1,0:T(8,128)(2,1)} %weigh.1), kind=kLoop, calls=%fused_computation.57 | loop fusion | bytes 524288
  19.2 1.8 %bitcast_dynamic-update-slice_fusion.5 = bf16[8,128,1024]{2,1,0:T(8,128)(2,1)} fusion(bf16[8,128,1024]{2,1,0:T(8,128)(2,1)} %bitcast_dynamic-update-slice_fusion.6, bf16[128,1024]{1,0:T(8,128)(2,1)} %collective-permute-done), kind=kLoop, calls=%fused_computation.56 | loop fusion | bytes 524288
  21.0 2.4 %collective-permute-done.4 = bf16[128,1024]{1,0:T(8,128)(2,1)S(1)} collective-permute-done((bf16[128,1024]{1,0:T(8,128)(2,1)S(1)}, bf16[128,1024]{1,0:T(8,128)(2,1)S(1)}, u32[]{:S(2)}, u32[]{:S(2)}) %collective-permute-start.4) | collective-permute-done | bytes 262176 | tf_op jit(solution)/shard_map/gather_rows/ppermute | solution.py:25
  23.4 3.0 %collective-permute-start.7 = (bf16[48,1024]{1,0:T(8,128)(2,1)S(1)}, bf16[48,1024]{1,0:T(8,128)(2,1)S(1)}, u32[]{:S(2)}, u32[]{:S(2)}) collective-permute-start(bf16[48,1024]{1,0:T(8,128)(2,1)S(1)} %slice.256), channel_id=1, source_target_pairs={{0,96},{32,0},{64,32},{96,64},{1,97},{33,1},{65,33},{97,65},{2,98}... | collective-permute-start | bytes 294920 | tf_op jit(solution)/shard_map/gather_rows/ppermute | solution.py:25
  26.6 0.5 collective-permute-start.8
  27.1 0.7 bitcast_dynamic-update-slice_fusion.4
  27.8 0.7 bitcast_dynamic-update-slice_fusion.3
  28.5 0.7 bitcast_dynamic-update-slice_fusion.2
  29.2 0.7 bitcast_dynamic-update-slice_fusion.1
  29.9 1.0 collective-permute-done.8
  31.0 1.4 %collective-permute-done.6 = bf16[48,1024]{1,0:T(8,128)(2,1)S(1)} collective-permute-done((bf16[48,1024]{1,0:T(8,128)(2,1)S(1)}, bf16[48,1024]{1,0:T(8,128)(2,1)S(1)}, u32[]{:S(2)}, u32[]{:S(2)}) %collective-permute-start.6) | collective-permute-done | bytes 98336 | tf_op jit(solution)/shard_map/gather_rows/ppermute | solution.py:25
  32.4 0.7 fusion.16
  33.1 0.7 bitcast_dynamic-update-slice_fusion
  33.8 1.2 slice.258
  35.8 1.4 %convolution_convert_fusion.3 = bf16[64,1024]{1,0:T(8,128)(2,1)S(1)} fusion(bf16[1024,1024]{1,0:T(8,128)(2,1)S(1)} %copy-done, bf16[8,128,1024]{2,1,0:T(8,128)(2,1)} %bitcast_dynamic-update-slice_fusion, s32[]{:T(128)S(6)} %select_n.98), kind=kOutput, calls=%fused_computation.33 | convolution fusion | flops 134283264 | bytes 2359300 | tf_op jit(solution)/shard_map/sum_layers/dot_general | solution.py:196
  37.2 1.4 %convolution_convert_fusion.2 = bf16[64,1024]{1,0:T(8,128)(2,1)S(1)} fusion(bf16[1024,1024]{1,0:T(8,128)(2,1)S(1)} %copy-done, bf16[8,128,1024]{2,1,0:T(8,128)(2,1)} %bitcast_dynamic-update-slice_fusion, s32[]{:T(128)S(6)} %select_n.98, s32[]{:T(128)S(6)} %add.489), kind=kOutput, calls=%fused_computation.32 | convolution fusion | flops 134283264 | bytes 2359304 | tf_op jit(solution)/shard_map/sum_layers/dot_general | solution.py:196
  38.6 3.2 %collective-permute-start.10 = (bf16[64,1024]{1,0:T(8,128)(2,1)S(1)}, bf16[64,1024]{1,0:T(8,128)(2,1)S(1)}, u32[]{:S(2)}, u32[]{:S(2)}) collective-permute-start(bf16[64,1024]{1,0:T(8,128)(2,1)S(1)} %convolution_convert_fusion.3), channel_id=1, source_target_pairs={{0,2},{2,4},{4,6},{6,8},{8,10},{10,12},{12,14},{14,0},{1,3},{3,5},... | collective-permute-start | bytes 393224 | tf_op jit(solution)/shard_map/sum_layers/ppermute | solution.py:25
  41.8 2.1 %convolution_convert_fusion = bf16[64,1024]{1,0:T(8,128)(2,1)S(1)} fusion(bf16[1024,1024]{1,0:T(8,128)(2,1)} %collective-permute-done.9, bf16[8,128,1024]{2,1,0:T(8,128)(2,1)} %bitcast_dynamic-update-slice_fusion, s32[]{:T(128)S(6)} %select_n.98, s32[]{:T(128)S(6)} %add.489), kind=kOutput, calls=%fused_computation.30 | convolution fusion | flops 134283264 | bytes 2359304 | tf_op jit(solution)/shard_map/sum_layers/dot_general | solution.py:196
  44.0 2.2 %convolution_convert_fusion.1 = bf16[64,1024]{1,0:T(8,128)(2,1)S(1)} fusion(bf16[1024,1024]{1,0:T(8,128)(2,1)} %collective-permute-done.9, bf16[8,128,1024]{2,1,0:T(8,128)(2,1)} %bitcast_dynamic-update-slice_fusion, s32[]{:T(128)S(6)} %select_n.98), kind=kOutput, calls=%fused_computation.31 | convolution fusion | flops 134283264 | bytes 2359300 | tf_op jit(solution)/shard_map/sum_layers/dot_general | solution.py:196
  46.2 3.3 %collective-permute-start.18 = (bf16[64,1024]{1,0:T(8,128)(2,1)S(1)}, bf16[64,1024]{1,0:T(8,128)(2,1)S(1)}, u32[]{:S(2)}, u32[]{:S(2)}) collective-permute-start(bf16[64,1024]{1,0:T(8,128)(2,1)S(1)} %convolution_convert_fusion.1), channel_id=1, source_target_pairs={{0,2},{2,4},{4,6},{6,8},{8,10},{10,12},{12,14},{14,0},{1,3},{3,5},... | collective-permute-start | bytes 393224 | tf_op jit(solution)/shard_map/sum_layers/ppermute | solution.py:25
  49.5 1.3 %collective-permute-done.22 = bf16[64,1024]{1,0:T(8,128)(2,1)S(1)} collective-permute-done((bf16[64,1024]{1,0:T(8,128)(2,1)S(1)}, bf16[64,1024]{1,0:T(8,128)(2,1)S(1)}, u32[]{:S(2)}, u32[]{:S(2)}) %collective-permute-start.22) | collective-permute-done | bytes 131104 | tf_op jit(solution)/shard_map/sum_layers/ppermute | solution.py:25
  50.8 2.1 %fusion.15 = bf16[128,1024]{1,0:T(8,128)(2,1)S(1)} fusion(bf16[1024,1024]{1,0:T(8,128)(2,1)} %collective-permute-done.9, bf16[64,1024]{1,0:T(8,128)(2,1)S(1)} %collective-permute-done.22, bf16[8,128,1024]{2,1,0:T(8,128)(2,1)} %bitcast_dynamic-update-slice_fusion, s32[]{:T(128)S(6)} %select_n.104), kind=kOutput, calls=%fused_computation.29 | convolution fusion | flops 268828672 | bytes 2752516 | tf_op jit(solution)/shard_map/sum_layers/dot_general | solution.py:196
  53.0 3.6 %collective-permute-done.14 = bf16[64,1024]{1,0:T(8,128)(2,1)S(1)} collective-permute-done((bf16[64,1024]{1,0:T(8,128)(2,1)S(1)}, bf16[64,1024]{1,0:T(8,128)(2,1)S(1)}, u32[]{:S(2)}, u32[]{:S(2)}) %collective-permute-start.14) | collective-permute-done | bytes 131104 | tf_op jit(solution)/shard_map/sum_layers/ppermute | solution.py:25
  56.7 0.4 fusion.9
  57.2 2.0 %fusion.12 = bf16[128,1024]{1,0:T(8,128)(2,1)S(1)} fusion(bf16[1024,1024]{1,0:T(8,128)(2,1)} %collective-permute-done.9, bf16[64,1024]{1,0:T(8,128)(2,1)S(1)} %collective-permute-done.18, bf16[8,128,1024]{2,1,0:T(8,128)(2,1)S(1)} %copy-done.1, s32[]{:T(128)S(6)} %select_n.96), kind=kOutput, calls=%fused_computation.26 | convolution fusion | flops 268828672 | bytes 2752516 | tf_op jit(solution)/shard_map/sum_layers/dot_general | solution.py:196
  59.3 3.3 %collective-permute-start.19 = (bf16[128,1024]{1,0:T(8,128)(2,1)S(1)}, bf16[128,1024]{1,0:T(8,128)(2,1)S(1)}, u32[]{:S(2)}, u32[]{:S(2)}) collective-permute-start(bf16[128,1024]{1,0:T(8,128)(2,1)S(1)} %fusion.12), channel_id=1, source_target_pairs={{0,2},{2,4},{4,6},{6,8},{8,10},{10,12},{12,14},{14,0},{1,3},{3,5},... | collective-permute-start | bytes 786440 | tf_op jit(solution)/shard_map/sum_layers/ppermute | solution.py:25
  63.1 2.0 %fusion.14 = bf16[128,1024]{1,0:T(8,128)(2,1)S(1)} fusion(bf16[1024,1024]{1,0:T(8,128)(2,1)} %collective-permute-done.9, bf16[128,1024]{1,0:T(8,128)(2,1)S(1)} %collective-permute-done.23, bf16[8,128,1024]{2,1,0:T(8,128)(2,1)S(1)} %copy-done.1, s32[]{:T(128)S(6)} %select_n.102), kind=kOutput, calls=%fused_computation.28 | convolution fusion | flops 268828672 | bytes 2883588 | tf_op jit(solution)/shard_map/sum_layers/dot_general | solution.py:196
  65.2 2.1 %collective-permute-start.24 = (bf16[128,1024]{1,0:T(8,128)(2,1)S(1)}, bf16[128,1024]{1,0:T(8,128)(2,1)S(1)}, u32[]{:S(2)}, u32[]{:S(2)}) collective-permute-start(bf16[128,1024]{1,0:T(8,128)(2,1)S(1)} %fusion.14), channel_id=1, source_target_pairs={{0,14},{2,0},{4,2},{6,4},{8,6},{10,8},{12,10},{14,12},{1,15},{3,1}... | collective-permute-start | bytes 786440 | tf_op jit(solution)/shard_map/sum_layers/ppermute | solution.py:25
  67.2 0.4 fusion.8
  67.8 2.0 %fusion.11 = bf16[128,1024]{1,0:T(8,128)(2,1)S(1)} fusion(bf16[1024,1024]{1,0:T(8,128)(2,1)} %collective-permute-done.9, bf16[128,1024]{1,0:T(8,128)(2,1)S(1)} %collective-permute-done.19, bf16[8,128,1024]{2,1,0:T(8,128)(2,1)S(1)} %copy-done.1, s32[]{:T(128)S(6)} %select_n.94), kind=kOutput, calls=%fused_computation.25 | convolution fusion | flops 268828672 | bytes 2883588 | tf_op jit(solution)/shard_map/sum_layers/dot_general | solution.py:196
  69.8 3.3 %collective-permute-start.20 = (bf16[128,1024]{1,0:T(8,128)(2,1)S(1)}, bf16[128,1024]{1,0:T(8,128)(2,1)S(1)}, u32[]{:S(2)}, u32[]{:S(2)}) collective-permute-start(bf16[128,1024]{1,0:T(8,128)(2,1)S(1)} %fusion.11), channel_id=1, source_target_pairs={{0,2},{2,4},{4,6},{6,8},{8,10},{10,12},{12,14},{14,0},{1,3},{3,5},... | collective-permute-start | bytes 786440 | tf_op jit(solution)/shard_map/sum_layers/ppermute | solution.py:25
  73.1 0.4 fusion.5
  73.6 2.5 %collective-permute-start.12 = (bf16[128,1024]{1,0:T(8,128)(2,1)S(1)}, bf16[128,1024]{1,0:T(8,128)(2,1)S(1)}, u32[]{:S(2)}, u32[]{:S(2)}) collective-permute-start(bf16[128,1024]{1,0:T(8,128)(2,1)S(1)} %fusion.5), channel_id=1, source_target_pairs={{0,2},{2,4},{4,6},{6,8},{8,10},{10,12},{12,14},{14,0},{1,3},{3,5},... | collective-permute-start | bytes 786440 | tf_op jit(solution)/shard_map/sum_layers/ppermute | solution.py:25
  76.1 2.0 %fusion.13 = bf16[128,1024]{1,0:T(8,128)(2,1)S(1)} fusion(bf16[1024,1024]{1,0:T(8,128)(2,1)} %collective-permute-done.9, bf16[128,1024]{1,0:T(8,128)(2,1)S(1)} %collective-permute-done.24, bf16[8,128,1024]{2,1,0:T(8,128)(2,1)S(1)} %copy-done.1, s32[]{:T(128)S(6)} %select_n.100), kind=kOutput, calls=%fused_computation.27 | convolution fusion | flops 268828672 | bytes 2883588 | tf_op jit(solution)/shard_map/sum_layers/dot_general | solution.py:196
  78.6 0.4 fusion.7
  79.1 1.0 collective-permute-start.17
  80.1 2.0 %fusion.10 = bf16[128,1024]{1,0:T(8,128)(2,1)S(1)} fusion(bf16[1024,1024]{1,0:T(8,128)(2,1)} %collective-permute-done.9, bf16[128,1024]{1,0:T(8,128)(2,1)S(1)} %collective-permute-done.20, bf16[8,128,1024]{2,1,0:T(8,128)(2,1)S(1)} %copy-done.1, s32[]{:T(128)S(6)} %select_n.92), kind=kOutput, calls=%fused_computation.24 | convolution fusion | flops 268828672 | bytes 2883588 | tf_op jit(solution)/shard_map/sum_layers/dot_general | solution.py:196
  82.2 2.6 %collective-permute-start.21 = (bf16[128,1024]{1,0:T(8,128)(2,1)S(1)}, bf16[128,1024]{1,0:T(8,128)(2,1)S(1)}, u32[]{:S(2)}, u32[]{:S(2)}) collective-permute-start(bf16[128,1024]{1,0:T(8,128)(2,1)S(1)} %fusion.10), channel_id=1, source_target_pairs={{0,2},{2,4},{4,6},{6,8},{8,10},{10,12},{12,14},{14,0},{1,3},{3,5},... | collective-permute-start | bytes 786440 | tf_op jit(solution)/shard_map/sum_layers/ppermute | solution.py:25
  84.7 0.4 fusion.4
  85.2 1.8 %collective-permute-start.13 = (bf16[128,1024]{1,0:T(8,128)(2,1)S(1)}, bf16[128,1024]{1,0:T(8,128)(2,1)S(1)}, u32[]{:S(2)}, u32[]{:S(2)}) collective-permute-start(bf16[128,1024]{1,0:T(8,128)(2,1)S(1)} %fusion.4), channel_id=1, source_target_pairs={{0,2},{2,4},{4,6},{6,8},{8,10},{10,12},{12,14},{14,0},{1,3},{3,5},... | collective-permute-start | bytes 786440 | tf_op jit(solution)/shard_map/sum_layers/ppermute | solution.py:25
  87.0 1.9 %collective-permute-done.21 = bf16[128,1024]{1,0:T(8,128)(2,1)S(1)} collective-permute-done((bf16[128,1024]{1,0:T(8,128)(2,1)S(1)}, bf16[128,1024]{1,0:T(8,128)(2,1)S(1)}, u32[]{:S(2)}, u32[]{:S(2)}) %collective-permute-start.21) | collective-permute-done | bytes 262176 | tf_op jit(solution)/shard_map/sum_layers/ppermute | solution.py:25
  88.9 2.1 %fusion.3 = bf16[128,1024]{1,0:T(8,128)(2,1)S(1)} fusion(bf16[1024,1024]{1,0:T(8,128)(2,1)} %collective-permute-done.9, bf16[128,1024]{1,0:T(8,128)(2,1)S(1)} %collective-permute-done.25, bf16[128,1024]{1,0:T(8,128)(2,1)S(1)} %collective-permute-done.21, bf16[8,128,1024]{2,1,0:T(8,128)(2,1)S(1)} %copy-done.1, s32[]{:T(128)S(6)} %select_n.90), kind=kOutput, calls=%fused_computation.17 | convolution fusion | flops 269090816 | bytes 3145732 | tf_op jit(solution)/shard_map/sum_layers/dot_general | solution.py:196
  91.0 0.7 collective-permute-done.13
  91.7 0.5 fusion.2
  92.2 0.8 maximum_bitcast_fusion
  93.0 5.5 %all-to-all-start = ((bf16[16,8,2048]{2,1,0:T(8,128)(2,1)}), bf16[16,8,2048]{2,1,0:T(8,128)(2,1)S(1)}, u32[]{:S(2)}, u32[]{:S(2)}) async-start(bf16[16,8,2048]{2,1,0:T(8,128)(2,1)} %maximum_bitcast_fusion), calls=%async_computation | async-start | bytes 1048576 | tf_op jit(solution)/shard_map/to_components/all_to_all | solution.py:229
  99.5 9.3 %all-to-all-done = bf16[16,8,2048]{2,1,0:T(8,128)(2,1)S(1)} async-done(((bf16[16,8,2048]{2,1,0:T(8,128)(2,1)}), bf16[16,8,2048]{2,1,0:T(8,128)(2,1)S(1)}, u32[]{:S(2)}, u32[]{:S(2)}) %all-to-all-start) | async-done | bytes 524320 | tf_op jit(solution)/shard_map/to_components/all_to_all | solution.py:229
  108.7 2.2 %fit.1 = f32[32,1,256]{2,1,0:T(1,128)} custom-call(s32[1]{0:T(128)} %bitcast.slot_ref, bf16[128,2048]{1,0:T(8,128)(2,1)S(1)} %bitcast.88, f32[32,2048]{1,0:T(8,128)S(1)} %reshape.30.values_ref), custom_call_target="tpu_custom_call" | custom-call | tf_op jit(solution)/shard_map/fit/pallas_call | solution.py:119
  110.9 3.8 %all-to-all-start.2 = ((f32[32,1,256]{2,1,0:T(1,128)}), f32[32,1,256]{2,1,0:T(1,128)S(1)}, u32[]{:S(2)}, u32[]{:S(2)}) async-start(f32[32,1,256]{2,1,0:T(1,128)} %fit.1), calls=%async_computation.2 | async-start | bytes 65536 | tf_op jit(solution)/shard_map/gather_scores/all_to_all | solution.py:234
  114.8 7.3 %all-to-all-done.2 = f32[32,1,256]{2,1,0:T(1,128)S(1)} async-done(((f32[32,1,256]{2,1,0:T(1,128)}), f32[32,1,256]{2,1,0:T(1,128)S(1)}, u32[]{:S(2)}, u32[]{:S(2)}) %all-to-all-start.2) | async-done | bytes 32800 | tf_op jit(solution)/shard_map/gather_scores/all_to_all | solution.py:234
  122.2 5.6 %collective-permute-start.26 = (f32[256]{0:T(256)S(1)}, f32[256]{0:T(256)S(1)}, u32[]{:S(2)}, u32[]{:S(2)}) collective-permute-start(f32[256]{0:T(256)S(1)} %reduce_sum.9), channel_id=1, source_target_pairs={{0,2},{2,4},{4,6},{6,8},{8,10},{10,12},{12,14},{3,1},{5,3},{7,5},{... | collective-permute-start | bytes 3080 | tf_op jit(solution)/shard_map/gather_scores/ppermute | solution.py:237
  127.8 0.6 dynamic_slice.54
  128.4 0.7 collective-permute-done.26
  129.3 0.6 add_divide_fusion
  (55 shorter events, 2.8 us)
Async XLA Ops:
  0.6 33.2 %collective-permute-start.9 = (bf16[1024,1024]{1,0:T(8,128)(2,1)}, bf16[1024,1024]{1,0:T(8,128)(2,1)}, u32[]{:S(2)}, u32[]{:S(2)}) collective-permute-start(bf16[1024,1024]{1,0:T(8,128)(2,1)} %param.10), channel_id=1, source_target_pairs={{0,16},{16,0},{1,17},{17,1},{2,18},{18,2},{3,19},{19,3},{4,20},{20... | collective-permute-start | bytes 6291464 | tf_op jit(solution)/shard_map/swap_eigvecs/ppermute | solution.py:25
  2.5 10.1 %collective-permute-start.1 = (bf16[128,1024]{1,0:T(8,128)(2,1)}, bf16[128,1024]{1,0:T(8,128)(2,1)S(1)}, u32[]{:S(2)}, u32[]{:S(2)}) collective-permute-start(bf16[128,1024]{1,0:T(8,128)(2,1)} %weigh.1), channel_id=1, source_target_pairs={{0,32},{32,64},{64,96},{96,0},{1,33},{33,65},{65,97},{97,1},{2,34}... | collective-permute-start | bytes 786440 | tf_op jit(solution)/shard_map/gather_rows/ppermute | solution.py:25
  4.0 11.6 %collective-permute-start.3 = (bf16[128,1024]{1,0:T(8,128)(2,1)}, bf16[128,1024]{1,0:T(8,128)(2,1)S(1)}, u32[]{:S(2)}, u32[]{:S(2)}) collective-permute-start(bf16[128,1024]{1,0:T(8,128)(2,1)} %weigh.1), channel_id=1, source_target_pairs={{0,128},{128,0},{1,129},{129,1},{2,130},{130,2},{3,131},{131,3},{4... | collective-permute-start | bytes 786440 | tf_op jit(solution)/shard_map/gather_rows/ppermute | solution.py:25
  5.6 13.6 %collective-permute-start = (bf16[128,1024]{1,0:T(8,128)(2,1)}, bf16[128,1024]{1,0:T(8,128)(2,1)}, u32[]{:S(2)}, u32[]{:S(2)}) collective-permute-start(bf16[128,1024]{1,0:T(8,128)(2,1)} %weigh.1), channel_id=1, source_target_pairs={{0,96},{32,0},{64,32},{96,64},{1,97},{33,1},{65,33},{97,65},{2,98}... | collective-permute-start | bytes 786440 | tf_op jit(solution)/shard_map/gather_rows/ppermute | solution.py:25
  8.7 84.3 %all-to-all-start.1 = ((f32[16,1,1024]{2,1,0:T(1,128)}), f32[16,1,1024]{2,1,0:T(1,128)S(1)}, u32[]{:S(2)}, u32[]{:S(2)}) async-start(f32[16,1,1024]{2,1,0:T(1,128)} %broadcast_in_dim.17), calls=%async_computation.1 | async-start | bytes 131072 | tf_op jit(solution)/shard_map/gather_values/all_to_all | solution.py:169
  12.7 13.8 %collective-permute-start.5 = (bf16[128,1024]{1,0:T(8,128)(2,1)S(1)}, bf16[128,1024]{1,0:T(8,128)(2,1)S(1)}, u32[]{:S(2)}, u32[]{:S(2)}) collective-permute-start(bf16[128,1024]{1,0:T(8,128)(2,1)S(1)} %collective-permute-done.1), channel_id=1, source_target_pairs={{0,128},{128,0},{1,129},{129,1},{2,130},{130,2},{3,131},{131,3},{4... | collective-permute-start | bytes 786440 | tf_op jit(solution)/shard_map/gather_rows/ppermute | solution.py:25
  14.2 12.3 %collective-permute-start.2 = (bf16[128,1024]{1,0:T(8,128)(2,1)S(1)}, bf16[128,1024]{1,0:T(8,128)(2,1)S(1)}, u32[]{:S(2)}, u32[]{:S(2)}) collective-permute-start(bf16[128,1024]{1,0:T(8,128)(2,1)S(1)} %collective-permute-done.1), channel_id=1, source_target_pairs={{0,32},{32,64},{64,96},{96,0},{1,33},{33,65},{65,97},{97,1},{2,34}... | collective-permute-start | bytes 786440 | tf_op jit(solution)/shard_map/gather_rows/ppermute | solution.py:25
  15.6 7.8 %collective-permute-start.4 = (bf16[128,1024]{1,0:T(8,128)(2,1)S(1)}, bf16[128,1024]{1,0:T(8,128)(2,1)S(1)}, u32[]{:S(2)}, u32[]{:S(2)}) collective-permute-start(bf16[128,1024]{1,0:T(8,128)(2,1)S(1)} %collective-permute-done.3), channel_id=1, source_target_pairs={{0,96},{32,0},{64,32},{96,64},{1,97},{33,1},{65,33},{97,65},{2,98}... | collective-permute-start | bytes 786440 | tf_op jit(solution)/shard_map/gather_rows/ppermute | solution.py:25
  19.2 16.6 %copy-start = (bf16[1024,1024]{1,0:T(8,128)(2,1)S(1)}, bf16[1024,1024]{1,0:T(8,128)(2,1)}, u32[]{:S(2)}) copy-start(bf16[1024,1024]{1,0:T(8,128)(2,1)} %param.10) | copy-start | bytes 6291460
  23.4 7.5 %collective-permute-start.7 = (bf16[48,1024]{1,0:T(8,128)(2,1)S(1)}, bf16[48,1024]{1,0:T(8,128)(2,1)S(1)}, u32[]{:S(2)}, u32[]{:S(2)}) collective-permute-start(bf16[48,1024]{1,0:T(8,128)(2,1)S(1)} %slice.256), channel_id=1, source_target_pairs={{0,96},{32,0},{64,32},{96,64},{1,97},{33,1},{65,33},{97,65},{2,98}... | collective-permute-start | bytes 294920 | tf_op jit(solution)/shard_map/gather_rows/ppermute | solution.py:25
  26.5 5.9 %collective-permute-start.6 = (bf16[48,1024]{1,0:T(8,128)(2,1)S(1)}, bf16[48,1024]{1,0:T(8,128)(2,1)S(1)}, u32[]{:S(2)}, u32[]{:S(2)}) collective-permute-start(bf16[48,1024]{1,0:T(8,128)(2,1)S(1)} %slice.255), channel_id=1, source_target_pairs={{0,32},{32,64},{64,96},{96,0},{1,33},{33,65},{65,97},{97,1},{2,34}... | collective-permute-start | bytes 294920 | tf_op jit(solution)/shard_map/gather_rows/ppermute | solution.py:25
  26.6 4.4 %collective-permute-start.8 = (bf16[32,1024]{1,0:T(8,128)(2,1)S(1)}, bf16[32,1024]{1,0:T(8,128)(2,1)S(1)}, u32[]{:S(2)}, u32[]{:S(2)}) collective-permute-start(bf16[32,1024]{1,0:T(8,128)(2,1)S(1)} %slice.257), channel_id=1, source_target_pairs={{0,128},{128,0},{1,129},{129,1},{2,130},{130,2},{3,131},{131,3},{4... | collective-permute-start | bytes 196616 | tf_op jit(solution)/shard_map/gather_rows/ppermute | solution.py:25
  38.6 24.0 %collective-permute-start.10 = (bf16[64,1024]{1,0:T(8,128)(2,1)S(1)}, bf16[64,1024]{1,0:T(8,128)(2,1)S(1)}, u32[]{:S(2)}, u32[]{:S(2)}) collective-permute-start(bf16[64,1024]{1,0:T(8,128)(2,1)S(1)} %convolution_convert_fusion.3), channel_id=1, source_target_pairs={{0,2},{2,4},{4,6},{6,8},{8,10},{10,12},{12,14},{14,0},{1,3},{3,5},... | collective-permute-start | bytes 393224 | tf_op jit(solution)/shard_map/sum_layers/ppermute | solution.py:25
  43.9 6.9 %collective-permute-start.22 = (bf16[64,1024]{1,0:T(8,128)(2,1)S(1)}, bf16[64,1024]{1,0:T(8,128)(2,1)S(1)}, u32[]{:S(2)}, u32[]{:S(2)}) collective-permute-start(bf16[64,1024]{1,0:T(8,128)(2,1)S(1)} %convolution_convert_fusion), channel_id=1, source_target_pairs={{0,14},{2,0},{4,2},{6,4},{8,6},{10,8},{12,10},{14,12},{1,15},{3,1}... | collective-permute-start | bytes 393224 | tf_op jit(solution)/shard_map/sum_layers/ppermute | solution.py:25
  46.2 11.0 %collective-permute-start.18 = (bf16[64,1024]{1,0:T(8,128)(2,1)S(1)}, bf16[64,1024]{1,0:T(8,128)(2,1)S(1)}, u32[]{:S(2)}, u32[]{:S(2)}) collective-permute-start(bf16[64,1024]{1,0:T(8,128)(2,1)S(1)} %convolution_convert_fusion.1), channel_id=1, source_target_pairs={{0,2},{2,4},{4,6},{6,8},{8,10},{10,12},{12,14},{14,0},{1,3},{3,5},... | collective-permute-start | bytes 393224 | tf_op jit(solution)/shard_map/sum_layers/ppermute | solution.py:25
  49.5 7.2 %collective-permute-start.14 = (bf16[64,1024]{1,0:T(8,128)(2,1)S(1)}, bf16[64,1024]{1,0:T(8,128)(2,1)S(1)}, u32[]{:S(2)}, u32[]{:S(2)}) collective-permute-start(bf16[64,1024]{1,0:T(8,128)(2,1)S(1)} %convolution_convert_fusion.2), channel_id=1, source_target_pairs={{0,14},{2,0},{4,2},{6,4},{8,6},{10,8},{12,10},{14,12},{1,15},{3,1}... | collective-permute-start | bytes 393224 | tf_op jit(solution)/shard_map/sum_layers/ppermute | solution.py:25
  49.5 7.2 %copy-start.1 = (bf16[8,128,1024]{2,1,0:T(8,128)(2,1)S(1)}, bf16[8,128,1024]{2,1,0:T(8,128)(2,1)}, u32[]{:S(2)}) copy-start(bf16[8,128,1024]{2,1,0:T(8,128)(2,1)} %bitcast_dynamic-update-slice_fusion) | copy-start | bytes 6291460
  52.9 10.2 %collective-permute-start.23 = (bf16[128,1024]{1,0:T(8,128)(2,1)S(1)}, bf16[128,1024]{1,0:T(8,128)(2,1)S(1)}, u32[]{:S(2)}, u32[]{:S(2)}) collective-permute-start(bf16[128,1024]{1,0:T(8,128)(2,1)S(1)} %fusion.15), channel_id=1, source_target_pairs={{0,14},{2,0},{4,2},{6,4},{8,6},{10,8},{12,10},{14,12},{1,15},{3,1}... | collective-permute-start | bytes 786440 | tf_op jit(solution)/shard_map/sum_layers/ppermute | solution.py:25
  57.1 10.1 %collective-permute-start.15 = (bf16[128,1024]{1,0:T(8,128)(2,1)S(1)}, bf16[128,1024]{1,0:T(8,128)(2,1)S(1)}, u32[]{:S(2)}, u32[]{:S(2)}) collective-permute-start(bf16[128,1024]{1,0:T(8,128)(2,1)S(1)} %fusion.9), channel_id=1, source_target_pairs={{0,14},{2,0},{4,2},{6,4},{8,6},{10,8},{12,10},{14,12},{1,15},{3,1}... | collective-permute-start | bytes 786440 | tf_op jit(solution)/shard_map/sum_layers/ppermute | solution.py:25
  59.3 8.5 %collective-permute-start.19 = (bf16[128,1024]{1,0:T(8,128)(2,1)S(1)}, bf16[128,1024]{1,0:T(8,128)(2,1)S(1)}, u32[]{:S(2)}, u32[]{:S(2)}) collective-permute-start(bf16[128,1024]{1,0:T(8,128)(2,1)S(1)} %fusion.12), channel_id=1, source_target_pairs={{0,2},{2,4},{4,6},{6,8},{8,10},{10,12},{12,14},{14,0},{1,3},{3,5},... | collective-permute-start | bytes 786440 | tf_op jit(solution)/shard_map/sum_layers/ppermute | solution.py:25
  63.0 10.1 %collective-permute-start.11 = (bf16[128,1024]{1,0:T(8,128)(2,1)S(1)}, bf16[128,1024]{1,0:T(8,128)(2,1)S(1)}, u32[]{:S(2)}, u32[]{:S(2)}) collective-permute-start(bf16[128,1024]{1,0:T(8,128)(2,1)S(1)} %fusion.6), channel_id=1, source_target_pairs={{0,2},{2,4},{4,6},{6,8},{8,10},{10,12},{12,14},{14,0},{1,3},{3,5},... | collective-permute-start | bytes 786440 | tf_op jit(solution)/shard_map/sum_layers/ppermute | solution.py:25
  65.2 10.9 %collective-permute-start.24 = (bf16[128,1024]{1,0:T(8,128)(2,1)S(1)}, bf16[128,1024]{1,0:T(8,128)(2,1)S(1)}, u32[]{:S(2)}, u32[]{:S(2)}) collective-permute-start(bf16[128,1024]{1,0:T(8,128)(2,1)S(1)} %fusion.14), channel_id=1, source_target_pairs={{0,14},{2,0},{4,2},{6,4},{8,6},{10,8},{12,10},{14,12},{1,15},{3,1}... | collective-permute-start | bytes 786440 | tf_op jit(solution)/shard_map/sum_layers/ppermute | solution.py:25
  67.7 10.9 %collective-permute-start.16 = (bf16[128,1024]{1,0:T(8,128)(2,1)S(1)}, bf16[128,1024]{1,0:T(8,128)(2,1)S(1)}, u32[]{:S(2)}, u32[]{:S(2)}) collective-permute-start(bf16[128,1024]{1,0:T(8,128)(2,1)S(1)} %fusion.8), channel_id=1, source_target_pairs={{0,14},{2,0},{4,2},{6,4},{8,6},{10,8},{12,10},{14,12},{1,15},{3,1}... | collective-permute-start | bytes 786440 | tf_op jit(solution)/shard_map/sum_layers/ppermute | solution.py:25
  69.8 10.3 %collective-permute-start.20 = (bf16[128,1024]{1,0:T(8,128)(2,1)S(1)}, bf16[128,1024]{1,0:T(8,128)(2,1)S(1)}, u32[]{:S(2)}, u32[]{:S(2)}) collective-permute-start(bf16[128,1024]{1,0:T(8,128)(2,1)S(1)} %fusion.11), channel_id=1, source_target_pairs={{0,2},{2,4},{4,6},{6,8},{8,10},{10,12},{12,14},{14,0},{1,3},{3,5},... | collective-permute-start | bytes 786440 | tf_op jit(solution)/shard_map/sum_layers/ppermute | solution.py:25
  73.6 11.1 %collective-permute-start.12 = (bf16[128,1024]{1,0:T(8,128)(2,1)S(1)}, bf16[128,1024]{1,0:T(8,128)(2,1)S(1)}, u32[]{:S(2)}, u32[]{:S(2)}) collective-permute-start(bf16[128,1024]{1,0:T(8,128)(2,1)S(1)} %fusion.5), channel_id=1, source_target_pairs={{0,2},{2,4},{4,6},{6,8},{8,10},{10,12},{12,14},{14,0},{1,3},{3,5},... | collective-permute-start | bytes 786440 | tf_op jit(solution)/shard_map/sum_layers/ppermute | solution.py:25
  78.1 8.9 %collective-permute-start.25 = (bf16[128,1024]{1,0:T(8,128)(2,1)S(1)}, bf16[128,1024]{1,0:T(8,128)(2,1)S(1)}, u32[]{:S(2)}, u32[]{:S(2)}) collective-permute-start(bf16[128,1024]{1,0:T(8,128)(2,1)S(1)} %fusion.13), channel_id=1, source_target_pairs={{0,14},{2,0},{4,2},{6,4},{8,6},{10,8},{12,10},{14,12},{1,15},{3,1}... | collective-permute-start | bytes 786440 | tf_op jit(solution)/shard_map/sum_layers/ppermute | solution.py:25
  79.1 11.9 %collective-permute-start.17 = (bf16[128,1024]{1,0:T(8,128)(2,1)S(1)}, bf16[128,1024]{1,0:T(8,128)(2,1)S(1)}, u32[]{:S(2)}, u32[]{:S(2)}) collective-permute-start(bf16[128,1024]{1,0:T(8,128)(2,1)S(1)} %fusion.7), channel_id=1, source_target_pairs={{0,14},{2,0},{4,2},{6,4},{8,6},{10,8},{12,10},{14,12},{1,15},{3,1}... | collective-permute-start | bytes 786440 | tf_op jit(solution)/shard_map/sum_layers/ppermute | solution.py:25
  82.2 6.8 %collective-permute-start.21 = (bf16[128,1024]{1,0:T(8,128)(2,1)S(1)}, bf16[128,1024]{1,0:T(8,128)(2,1)S(1)}, u32[]{:S(2)}, u32[]{:S(2)}) collective-permute-start(bf16[128,1024]{1,0:T(8,128)(2,1)S(1)} %fusion.10), channel_id=1, source_target_pairs={{0,2},{2,4},{4,6},{6,8},{8,10},{10,12},{12,14},{14,0},{1,3},{3,5},... | collective-permute-start | bytes 786440 | tf_op jit(solution)/shard_map/sum_layers/ppermute | solution.py:25
  85.2 6.5 %collective-permute-start.13 = (bf16[128,1024]{1,0:T(8,128)(2,1)S(1)}, bf16[128,1024]{1,0:T(8,128)(2,1)S(1)}, u32[]{:S(2)}, u32[]{:S(2)}) collective-permute-start(bf16[128,1024]{1,0:T(8,128)(2,1)S(1)} %fusion.4), channel_id=1, source_target_pairs={{0,2},{2,4},{4,6},{6,8},{8,10},{10,12},{12,14},{14,0},{1,3},{3,5},... | collective-permute-start | bytes 786440 | tf_op jit(solution)/shard_map/sum_layers/ppermute | solution.py:25
  91.0 7.6 %copy-start.2 = (s32[1024]{0:T(1024)S(1)}, s32[1024]{0:T(1024)}, u32[]{:S(2)}) copy-start(s32[1024]{0:T(1024)} %param.12) | copy-start | bytes 12292
  92.2 37.1 %copy-start.3 = (s32[64]{0:T(128)S(1)}, s32[64]{0:T(128)}, u32[]{:S(2)}) copy-start(s32[64]{0:T(128)} %param.13) | copy-start | bytes 772
  93.0 15.7 %all-to-all-start = ((bf16[16,8,2048]{2,1,0:T(8,128)(2,1)}), bf16[16,8,2048]{2,1,0:T(8,128)(2,1)S(1)}, u32[]{:S(2)}, u32[]{:S(2)}) async-start(bf16[16,8,2048]{2,1,0:T(8,128)(2,1)} %maximum_bitcast_fusion), calls=%async_computation | async-start | bytes 1048576 | tf_op jit(solution)/shard_map/to_components/all_to_all | solution.py:229
  110.9 11.3 %all-to-all-start.2 = ((f32[32,1,256]{2,1,0:T(1,128)}), f32[32,1,256]{2,1,0:T(1,128)S(1)}, u32[]{:S(2)}, u32[]{:S(2)}) async-start(f32[32,1,256]{2,1,0:T(1,128)} %fit.1), calls=%async_computation.2 | async-start | bytes 65536 | tf_op jit(solution)/shard_map/gather_scores/all_to_all | solution.py:234
  122.2 6.9 %collective-permute-start.26 = (f32[256]{0:T(256)S(1)}, f32[256]{0:T(256)S(1)}, u32[]{:S(2)}, u32[]{:S(2)}) collective-permute-start(f32[256]{0:T(256)S(1)} %reduce_sum.9), channel_id=1, source_target_pairs={{0,2},{2,4},{4,6},{6,8},{8,10},{10,12},{12,14},{3,1},{5,3},{7,5},{... | collective-permute-start | bytes 3080 | tf_op jit(solution)/shard_map/gather_scores/ppermute | solution.py:237

commit v5 on v4

--- a/solution.py
+++ b/solution.py
@@ -126,7 +126,7 @@
     )(slot, sums, values)
 
 
-def gather_plane(own):
+def gather_plane(own, other):
     x, y = "samp_1", "samp_0"
     left = shifted(own, x, 1)
     right = shifted(own, x, -1)
@@ -142,6 +142,7 @@
         ],
         axis=0,
     )
+    over_far = over_far + 0 * other[: own.shape[0]]
     return jnp.stack([own, right, far, left, over, over_right, over_far, over_left])
 
 
@@ -174,24 +175,24 @@
 def shards(responses, weights, phenotype, eigvecs, eigvals, positions, reaches):
     z, x, y = lax.axis_index("cpg_0"), lax.axis_index("samp_1"), lax.axis_index("samp_0")
     layers = lax.axis_size("cpg_0")
+    with jax.named_scope("swap_eigvecs"):
+        other = shifted(eigvecs, "samp_2", 1)
     with jax.named_scope("weigh"):
         own = weigh(responses, weights, phenotype)
     with jax.named_scope("gather_rows"):
-        blocks = gather_plane(own)
-    with jax.named_scope("swap_eigvecs"):
-        other = shifted(eigvecs, "samp_2", 1)
-        vecs = (eigvecs, other)
-        ready = (0.0 * other[0, 0].astype(jnp.float32)).astype(jnp.int32)
+        blocks = gather_plane(own, other)
     with jax.named_scope("gather_values"):
         everywhere = copies(eigvals, SAMP).reshape(-1, 2, eigvals.shape[0])
         everywhere = jnp.where(lax.axis_index("samp_2") == 0, everywhere, everywhere[:, ::-1])
         everywhere = jnp.repeat(everywhere.reshape(everywhere.shape[0], -1), 4, axis=0)
+    other = other + 0 * (blocks[6, :1] + everywhere[:1, : other.shape[1]].astype(other.dtype))
+    vecs = (eigvecs, other)
     rows = own.shape[0]
 
     def term(q, ahead, lo, hi):
         dest = lax.rem(z + ahead + layers, layers)
         across, along = dest // 4, lax.rem(dest, 4)
-        place = 4 * (across ^ y) + lax.rem(along - x + 4, 4) + ready
+        place = 4 * (across ^ y) + lax.rem(along - x + 4, 4)
         block = lax.dynamic_index_in_dim(blocks, place, 0, keepdims=False)[lo:hi]
         return jnp.dot(block, vecs[q], preferred_element_type=jnp.float32)
 

time: 131 us -> 132 us (level)
  waiting for transfers between devices: 30.6 us -> 36.4 us
  local copies, waits for them, and re-layouts: 11.1 us -> 6.72 us
  matrix products: 24.6 us -> 22.6 us
  starting transfers between devices: 55.4 us -> 57.3 us
    all_to_all x1, waiting for transfers between devices: 0.01 us -> 4.8 us  [copies(): lax.all_to_all(jnp.broadcast_to(value[None], (peers, *value.shape)), axes...]
    ppermute x26, starting transfers between devices: 36.9 us -> 40.7 us  [shifted(): lax.ppermute(value, axis, [(i, (i + by) % peers) for i in range(peers)])]
    ppermute x1, starting transfers between devices: 5.6 us -> 1.92 us  [shards(): other = lax.ppermute(layer, CPG, beside)]
    unnamed x15 -> x13, local copies, waits for them, and re-layouts: 6.42 us -> 3.96 us
    ppermute x1, waiting for transfers between devices: 0.67 us -> 2.93 us  [shards(): other = lax.ppermute(layer, CPG, beside)]
    ppermute x26, waiting for transfers between devices: 13.4 us -> 11.3 us  [shifted(): lax.ppermute(value, axis, [(i, (i + by) % peers) for i in range(peers)])]
    dot_general x18, matrix products: 24.6 us -> 22.6 us  [term(): return jnp.dot(block, vecs[q], preferred_element_type=jnp.float32)]
    all_to_all x1, starting transfers between devices: 5.52 us -> 7.36 us  [shards(): sums = lax.all_to_all(whole, PLANE, 0, 0, tiled=True)]
  transfers between devices with their start and end apart: 30 -> 30, of which waited for: 12 -> 10; matrix products, arithmetic and copies ran while one was open for 29% -> 20% of each run, Pallas kernels for 1% -> 1%
where the time goes in v5:
time: 132 us; the launch traced here: 131 us
  starting transfers between devices  57.3 us (43%)
  waiting for transfers between devices  36.4 us (28%)
  matrix products  22.6 us (17%)
  local copies, waits for them, and re-layouts  6.72 us (5%)
  Pallas kernels  4.03 us (3%)
  other arithmetic  2.9 us (2%)
  between operations  1.45 us (1%)
    ppermute x26, starting transfers between devices, shifted(): lax.ppermute(value, axis, [(i, (i + by) % peers) for i in range(peers)])  40.7 us
    dot_general x18, matrix products, term(): return jnp.dot(block, vecs[q], preferred_element_type=jnp.float32)  22.6 us
    ppermute x26, waiting for transfers between devices, shifted(): lax.ppermute(value, axis, [(i, (i + by) % peers) for i in range(peers)])  11.3 us
    all_to_all x1, waiting for transfers between devices, shards(): sums = lax.all_to_all(whole, PLANE, 0, 0, tiled=True)  10.1 us
    all_to_all x1, starting transfers between devices, shards(): sums = lax.all_to_all(whole, PLANE, 0, 0, tiled=True)  7.36 us
    all_to_all x1, waiting for transfers between devices, shards(): lax.all_to_all(fitted, LAYER, 0, 0, tiled=True)  7.32 us
    all_to_all x1, waiting for transfers between devices, copies(): lax.all_to_all(jnp.broadcast_to(value[None], (peers, *value.shape)), axes...  4.8 us
    unnamed x13, local copies, waits for them, and re-layouts  3.96 us
  transfers between devices with their start and end apart: 30, of which 10 were waited for; matrix products, arithmetic and copies ran while one was open for 20% of the time, Pallas kernels for 1%

profile of v5, /device:TPU:96, one launch (start us, length us, event | category | flops | bytes accessed | tf_op | source)
XLA Modules:
  0.0 131.4 jit_solution(12137648166249237279)
XLA Ops:
  0.6 0.1 collective-permute-start.9
  0.7 1.8 %weigh.1 = bf16[128,1024]{1,0:T(8,128)(2,1)} custom-call(bf16[64,1024]{1,0:T(8,128)(2,1)} %resp_ref.1, bf16[64,1024]{1,0:T(8,128)(2,1)} %weight_ref.1, f32[1,1024]{1,0:T(1,128)} %bitcast.85), custom_call_target="tpu_custom_call" | custom-call | tf_op jit(solution)/shard_map/weigh/pallas_call | solution.py:46
  2.6 1.5 %collective-permute-start.1 = (bf16[128,1024]{1,0:T(8,128)(2,1)}, bf16[128,1024]{1,0:T(8,128)(2,1)}, u32[]{:S(2)}, u32[]{:S(2)}) collective-permute-start(bf16[128,1024]{1,0:T(8,128)(2,1)} %weigh.1), channel_id=1, source_target_pairs={{0,32},{32,64},{64,96},{96,0},{1,33},{33,65},{65,97},{97,1},{2,34}... | collective-permute-start | bytes 786440 | tf_op jit(solution)/shard_map/gather_rows/ppermute | solution.py:25
  4.1 1.6 %collective-permute-start.3 = (bf16[128,1024]{1,0:T(8,128)(2,1)}, bf16[128,1024]{1,0:T(8,128)(2,1)}, u32[]{:S(2)}, u32[]{:S(2)}) collective-permute-start(bf16[128,1024]{1,0:T(8,128)(2,1)} %weigh.1), channel_id=1, source_target_pairs={{0,128},{128,0},{1,129},{129,1},{2,130},{130,2},{3,131},{131,3},{4... | collective-permute-start | bytes 786440 | tf_op jit(solution)/shard_map/gather_rows/ppermute | solution.py:25
  5.6 1.7 %collective-permute-start = (bf16[128,1024]{1,0:T(8,128)(2,1)}, bf16[128,1024]{1,0:T(8,128)(2,1)}, u32[]{:S(2)}, u32[]{:S(2)}) collective-permute-start(bf16[128,1024]{1,0:T(8,128)(2,1)} %weigh.1), channel_id=1, source_target_pairs={{0,96},{32,0},{64,32},{96,64},{1,97},{33,1},{65,33},{97,65},{2,98}... | collective-permute-start | bytes 786440 | tf_op jit(solution)/shard_map/gather_rows/ppermute | solution.py:25
  7.4 1.3 %broadcast_in_dim.17 = f32[16,1,1024]{2,1,0:T(1,128)} broadcast(f32[1024]{0:T(1024)} %param.11), dimensions={2} | broadcast | bytes 69632 | tf_op jit(solution)/shard_map/gather_values/broadcast_in_dim | solution.py:171
  8.7 3.5 %all-to-all-start = ((f32[16,1,1024]{2,1,0:T(1,128)}), f32[16,1,1024]{2,1,0:T(1,128)S(1)}, u32[]{:S(2)}, u32[]{:S(2)}) async-start(f32[16,1,1024]{2,1,0:T(1,128)} %broadcast_in_dim.17), calls=%async_computation | async-start | bytes 131072 | tf_op jit(solution)/shard_map/gather_values/all_to_all | solution.py:170
  12.2 1.0 bitcast_dynamic-update-slice_fusion.6
  13.5 4.8 %all-to-all-done = f32[16,1,1024]{2,1,0:T(1,128)S(1)} async-done(((f32[16,1,1024]{2,1,0:T(1,128)}), f32[16,1,1024]{2,1,0:T(1,128)S(1)}, u32[]{:S(2)}, u32[]{:S(2)}) %all-to-all-start) | async-done | bytes 65568 | tf_op jit(solution)/shard_map/gather_values/all_to_all | solution.py:170
  18.3 0.2 reduce
  18.5 0.4 rev.3
  18.9 0.7 collective-permute-start.2
  19.5 0.7 collective-permute-start.5
  20.2 2.7 %collective-permute-start.4 = (bf16[128,1024]{1,0:T(8,128)(2,1)}, bf16[128,1024]{1,0:T(8,128)(2,1)S(1)}, u32[]{:S(2)}, u32[]{:S(2)}) collective-permute-start(bf16[128,1024]{1,0:T(8,128)(2,1)} %collective-permute-done.3), channel_id=1, source_target_pairs={{0,96},{32,0},{64,32},{96,64},{1,97},{33,1},{65,33},{97,65},{2,98}... | collective-permute-start | bytes 786440 | tf_op jit(solution)/shard_map/gather_rows/ppermute | solution.py:25
  23.1 1.0 bitcast_dynamic-update-slice_fusion.5
  24.1 3.7 %collective-permute-done.5 = bf16[128,1024]{1,0:T(8,128)(2,1)S(1)} collective-permute-done((bf16[128,1024]{1,0:T(8,128)(2,1)}, bf16[128,1024]{1,0:T(8,128)(2,1)S(1)}, u32[]{:S(2)}, u32[]{:S(2)}) %collective-permute-start.5) | collective-permute-done | bytes 262176 | tf_op jit(solution)/shard_map/gather_rows/ppermute | solution.py:25
  27.8 0.7 collective-permute-start.6
  28.5 0.2 collective-permute-done.2
  28.7 0.7 collective-permute-start.8
  29.4 2.7 %collective-permute-start.7 = (bf16[48,1024]{1,0:T(8,128)(2,1)S(1)}, bf16[48,1024]{1,0:T(8,128)(2,1)S(1)}, u32[]{:S(2)}, u32[]{:S(2)}) collective-permute-start(bf16[48,1024]{1,0:T(8,128)(2,1)S(1)} %slice.265), channel_id=1, source_target_pairs={{0,96},{32,0},{64,32},{96,64},{1,97},{33,1},{65,33},{97,65},{2,98}... | collective-permute-start | bytes 294920 | tf_op jit(solution)/shard_map/gather_rows/ppermute | solution.py:25
  32.1 1.0 bitcast_dynamic-update-slice_fusion.3
  33.1 1.0 bitcast_dynamic-update-slice_fusion.2
  34.1 0.2 collective-permute-done.7
  34.3 1.0 constant_dynamic-update-slice_fusion
  35.4 0.5 convolution_convert_fusion.3
  35.9 3.2 %collective-permute-start.10 = (bf16[64,1024]{1,0:T(8,128)(2,1)S(1)}, bf16[64,1024]{1,0:T(8,128)(2,1)S(1)}, u32[]{:S(2)}, u32[]{:S(2)}) collective-permute-start(bf16[64,1024]{1,0:T(8,128)(2,1)S(1)} %convolution_convert_fusion.3), channel_id=1, source_target_pairs={{0,2},{2,4},{4,6},{6,8},{8,10},{10,12},{12,14},{14,0},{1,3},{3,5},... | collective-permute-start | bytes 393224 | tf_op jit(solution)/shard_map/sum_layers/ppermute | solution.py:25
  39.1 0.5 convolution_convert_fusion.2
  39.7 2.1 %convolution_convert_fusion.1 = bf16[64,1024]{1,0:T(8,128)(2,1)S(1)} fusion(bf16[8,128,1024]{2,1,0:T(8,128)(2,1)S(1)} %bitcast_dynamic-update-slice_fusion, s32[]{:T(128)S(6)} %select_n.98, bf16[1024,1024]{1,0:T(8,128)(2,1)} %collective-permute-done.9, bf16[1024]{0:T(1024)(128)(2,1)S(1)} %fusion.48), kind=kOutput, calls=%fused_computation.31 | convolution fusion | flops 135331840 | bytes 2361348 | tf_op jit(solution)/shard_map/sum_layers/dot_general | solution.py:197
  41.8 3.3 %collective-permute-start.18 = (bf16[64,1024]{1,0:T(8,128)(2,1)S(1)}, bf16[64,1024]{1,0:T(8,128)(2,1)S(1)}, u32[]{:S(2)}, u32[]{:S(2)}) collective-permute-start(bf16[64,1024]{1,0:T(8,128)(2,1)S(1)} %convolution_convert_fusion.1), channel_id=1, source_target_pairs={{0,2},{2,4},{4,6},{6,8},{8,10},{10,12},{12,14},{14,0},{1,3},{3,5},... | collective-permute-start | bytes 393224 | tf_op jit(solution)/shard_map/sum_layers/ppermute | solution.py:25
  45.1 2.1 %convolution_convert_fusion = bf16[64,1024]{1,0:T(8,128)(2,1)S(1)} fusion(bf16[8,128,1024]{2,1,0:T(8,128)(2,1)S(1)} %bitcast_dynamic-update-slice_fusion, s32[]{:T(128)S(6)} %select_n.98, s32[]{:T(128)S(6)} %add.469, bf16[1024,1024]{1,0:T(8,128)(2,1)} %collective-permute-done.9, bf16[1024]{0:T(1024)(128)(2,1)S(1)} %fusion.48), kind=kOutput, calls=%fused_computation.30 | convolution fusion | flops 135331840 | bytes 2361352 | tf_op jit(solution)/shard_map/sum_layers/dot_general | solution.py:197
  47.1 0.3 collective-permute-start.22
  47.4 0.4 fusion.6
  47.9 3.3 %collective-permute-start.11 = (bf16[128,1024]{1,0:T(8,128)(2,1)S(1)}, bf16[128,1024]{1,0:T(8,128)(2,1)S(1)}, u32[]{:S(2)}, u32[]{:S(2)}) collective-permute-start(bf16[128,1024]{1,0:T(8,128)(2,1)S(1)} %fusion.6), channel_id=1, source_target_pairs={{0,2},{2,4},{4,6},{6,8},{8,10},{10,12},{12,14},{14,0},{1,3},{3,5},... | collective-permute-start | bytes 786440 | tf_op jit(solution)/shard_map/sum_layers/ppermute | solution.py:25
  51.2 0.4 fusion.9
  51.7 2.1 %fusion.12 = bf16[128,1024]{1,0:T(8,128)(2,1)S(1)} fusion(bf16[64,1024]{1,0:T(8,128)(2,1)S(1)} %collective-permute-done.18, bf16[8,128,1024]{2,1,0:T(8,128)(2,1)S(1)} %bitcast_dynamic-update-slice_fusion, s32[]{:T(128)S(6)} %select_n.96, bf16[1024,1024]{1,0:T(8,128)(2,1)} %collective-permute-done.9, bf16[1024]{0:T(1024)(128)(2,1)S(1)} %fusion.48), kind=kOutput, calls=%fused_computation.26 | convolution fusion | flops 269877248 | bytes 2754564 | tf_op jit(solution)/shard_map/sum_layers/dot_general | solution.py:197
  53.8 3.3 %collective-permute-start.19 = (bf16[128,1024]{1,0:T(8,128)(2,1)S(1)}, bf16[128,1024]{1,0:T(8,128)(2,1)S(1)}, u32[]{:S(2)}, u32[]{:S(2)}) collective-permute-start(bf16[128,1024]{1,0:T(8,128)(2,1)S(1)} %fusion.12), channel_id=1, source_target_pairs={{0,2},{2,4},{4,6},{6,8},{8,10},{10,12},{12,14},{14,0},{1,3},{3,5},... | collective-permute-start | bytes 786440 | tf_op jit(solution)/shard_map/sum_layers/ppermute | solution.py:25
  57.1 2.0 %fusion.15 = bf16[128,1024]{1,0:T(8,128)(2,1)S(1)} fusion(bf16[64,1024]{1,0:T(8,128)(2,1)S(1)} %collective-permute-done.22, bf16[8,128,1024]{2,1,0:T(8,128)(2,1)S(1)} %bitcast_dynamic-update-slice_fusion, s32[]{:T(128)S(6)} %select_n.104, bf16[1024,1024]{1,0:T(8,128)(2,1)} %collective-permute-done.9, bf16[1024]{0:T(1024)(128)(2,1)S(1)} %fusion.48), kind=kOutput, calls=%fused_computation.29 | convolution fusion | flops 269877248 | bytes 2754564 | tf_op jit(solution)/shard_map/sum_layers/dot_general | solution.py:197
  59.2 0.4 fusion.5
  59.7 3.3 %collective-permute-start.12 = (bf16[128,1024]{1,0:T(8,128)(2,1)S(1)}, bf16[128,1024]{1,0:T(8,128)(2,1)S(1)}, u32[]{:S(2)}, u32[]{:S(2)}) collective-permute-start(bf16[128,1024]{1,0:T(8,128)(2,1)S(1)} %fusion.5), channel_id=1, source_target_pairs={{0,2},{2,4},{4,6},{6,8},{8,10},{10,12},{12,14},{14,0},{1,3},{3,5},... | collective-permute-start | bytes 786440 | tf_op jit(solution)/shard_map/sum_layers/ppermute | solution.py:25
  63.0 0.4 fusion.8
  63.5 2.1 %fusion.11 = bf16[128,1024]{1,0:T(8,128)(2,1)S(1)} fusion(bf16[128,1024]{1,0:T(8,128)(2,1)S(1)} %collective-permute-done.19, bf16[8,128,1024]{2,1,0:T(8,128)(2,1)S(1)} %bitcast_dynamic-update-slice_fusion, s32[]{:T(128)S(6)} %select_n.94, bf16[1024,1024]{1,0:T(8,128)(2,1)} %collective-permute-done.9, bf16[1024]{0:T(1024)(128)(2,1)S(1)} %fusion.48), kind=kOutput, calls=%fused_computation.25 | convolution fusion | flops 269877248 | bytes 2885636 | tf_op jit(solution)/shard_map/sum_layers/dot_general | solution.py:197
  65.6 3.3 %collective-permute-start.20 = (bf16[128,1024]{1,0:T(8,128)(2,1)S(1)}, bf16[128,1024]{1,0:T(8,128)(2,1)S(1)}, u32[]{:S(2)}, u32[]{:S(2)}) collective-permute-start(bf16[128,1024]{1,0:T(8,128)(2,1)S(1)} %fusion.11), channel_id=1, source_target_pairs={{0,2},{2,4},{4,6},{6,8},{8,10},{10,12},{12,14},{14,0},{1,3},{3,5},... | collective-permute-start | bytes 786440 | tf_op jit(solution)/shard_map/sum_layers/ppermute | solution.py:25
  68.9 2.0 %fusion.14 = bf16[128,1024]{1,0:T(8,128)(2,1)S(1)} fusion(bf16[128,1024]{1,0:T(8,128)(2,1)S(1)} %collective-permute-done.23, bf16[8,128,1024]{2,1,0:T(8,128)(2,1)S(1)} %bitcast_dynamic-update-slice_fusion, s32[]{:T(128)S(6)} %select_n.102, bf16[1024,1024]{1,0:T(8,128)(2,1)} %collective-permute-done.9, bf16[1024]{0:T(1024)(128)(2,1)S(1)} %fusion.48), kind=kOutput, calls=%fused_computation.28 | convolution fusion | flops 269877248 | bytes 2885636 | tf_op jit(solution)/shard_map/sum_layers/dot_general | solution.py:197
  71.0 0.4 fusion.4
  71.5 3.3 %collective-permute-start.13 = (bf16[128,1024]{1,0:T(8,128)(2,1)S(1)}, bf16[128,1024]{1,0:T(8,128)(2,1)S(1)}, u32[]{:S(2)}, u32[]{:S(2)}) collective-permute-start(bf16[128,1024]{1,0:T(8,128)(2,1)S(1)} %fusion.4), channel_id=1, source_target_pairs={{0,2},{2,4},{4,6},{6,8},{8,10},{10,12},{12,14},{14,0},{1,3},{3,5},... | collective-permute-start | bytes 786440 | tf_op jit(solution)/shard_map/sum_layers/ppermute | solution.py:25
  74.8 0.4 fusion.7
  75.4 2.1 %fusion.10 = bf16[128,1024]{1,0:T(8,128)(2,1)S(1)} fusion(bf16[128,1024]{1,0:T(8,128)(2,1)S(1)} %collective-permute-done.20, bf16[8,128,1024]{2,1,0:T(8,128)(2,1)S(1)} %bitcast_dynamic-update-slice_fusion, s32[]{:T(128)S(6)} %select_n.92, bf16[1024,1024]{1,0:T(8,128)(2,1)} %collective-permute-done.9, bf16[1024]{0:T(1024)(128)(2,1)S(1)} %fusion.48), kind=kOutput, calls=%fused_computation.24 | convolution fusion | flops 269877248 | bytes 2885636 | tf_op jit(solution)/shard_map/sum_layers/dot_general | solution.py:197
  77.4 4.0 %collective-permute-start.21 = (bf16[128,1024]{1,0:T(8,128)(2,1)S(1)}, bf16[128,1024]{1,0:T(8,128)(2,1)S(1)}, u32[]{:S(2)}, u32[]{:S(2)}) collective-permute-start(bf16[128,1024]{1,0:T(8,128)(2,1)S(1)} %fusion.10), channel_id=1, source_target_pairs={{0,2},{2,4},{4,6},{6,8},{8,10},{10,12},{12,14},{14,0},{1,3},{3,5},... | collective-permute-start | bytes 786440 | tf_op jit(solution)/shard_map/sum_layers/ppermute | solution.py:25
  81.4 2.0 %fusion.13 = bf16[128,1024]{1,0:T(8,128)(2,1)S(1)} fusion(bf16[128,1024]{1,0:T(8,128)(2,1)S(1)} %collective-permute-done.24, bf16[8,128,1024]{2,1,0:T(8,128)(2,1)S(1)} %bitcast_dynamic-update-slice_fusion, s32[]{:T(128)S(6)} %select_n.100, bf16[1024,1024]{1,0:T(8,128)(2,1)} %collective-permute-done.9, bf16[1024]{0:T(1024)(128)(2,1)S(1)} %fusion.48), kind=kOutput, calls=%fused_computation.27 | convolution fusion | flops 269877248 | bytes 2885636 | tf_op jit(solution)/shard_map/sum_layers/dot_general | solution.py:197
  83.5 1.1 collective-permute-done.17
  84.6 0.5 fusion.2
  85.1 0.2 collective-permute-done.21
  85.3 5.8 %collective-permute-done.25 = bf16[128,1024]{1,0:T(8,128)(2,1)S(1)} collective-permute-done((bf16[128,1024]{1,0:T(8,128)(2,1)S(1)}, bf16[128,1024]{1,0:T(8,128)(2,1)S(1)}, u32[]{:S(2)}, u32[]{:S(2)}) %collective-permute-start.25) | collective-permute-done | bytes 262176 | tf_op jit(solution)/shard_map/sum_layers/ppermute | solution.py:25
  91.1 2.1 %fusion.3 = bf16[128,1024]{1,0:T(8,128)(2,1)S(1)} fusion(bf16[128,1024]{1,0:T(8,128)(2,1)S(1)} %collective-permute-done.25, bf16[128,1024]{1,0:T(8,128)(2,1)S(1)} %collective-permute-done.21, bf16[8,128,1024]{2,1,0:T(8,128)(2,1)S(1)} %bitcast_dynamic-update-slice_fusion, s32[]{:T(128)S(6)} %select_n.90, bf16[1024,1024]{1,0:T(8,128)(2,1)} %collective-permute-done.9, ...), kind=kOutput, calls=%fused_computation.17 | convolution fusion | flops 270139392 | bytes 3147780 | tf_op jit(solution)/shard_map/sum_layers/dot_general | solution.py:197
  93.2 0.9 maximum_bitcast_fusion
  94.1 7.4 %all-to-all-start.1 = ((bf16[16,8,2048]{2,1,0:T(8,128)(2,1)}), bf16[16,8,2048]{2,1,0:T(8,128)(2,1)S(1)}, u32[]{:S(2)}, u32[]{:S(2)}) async-start(bf16[16,8,2048]{2,1,0:T(8,128)(2,1)} %maximum_bitcast_fusion), calls=%async_computation.1 | async-start | bytes 1048576 | tf_op jit(solution)/shard_map/to_components/all_to_all | solution.py:230
  101.5 10.1 %all-to-all-done.1 = bf16[16,8,2048]{2,1,0:T(8,128)(2,1)S(1)} async-done(((bf16[16,8,2048]{2,1,0:T(8,128)(2,1)}), bf16[16,8,2048]{2,1,0:T(8,128)(2,1)S(1)}, u32[]{:S(2)}, u32[]{:S(2)}) %all-to-all-start.1) | async-done | bytes 524320 | tf_op jit(solution)/shard_map/to_components/all_to_all | solution.py:230
  111.6 2.2 %fit.1 = f32[32,1,256]{2,1,0:T(1,128)} custom-call(s32[1]{0:T(128)} %bitcast.slot_ref, bf16[128,2048]{1,0:T(8,128)(2,1)S(1)} %bitcast.83, f32[32,2048]{1,0:T(8,128)S(1)} %reshape.26.values_ref), custom_call_target="tpu_custom_call" | custom-call | tf_op jit(solution)/shard_map/fit/pallas_call | solution.py:119
  113.8 3.8 %all-to-all-start.2 = ((f32[32,1,256]{2,1,0:T(1,128)}), f32[32,1,256]{2,1,0:T(1,128)S(1)}, u32[]{:S(2)}, u32[]{:S(2)}) async-start(f32[32,1,256]{2,1,0:T(1,128)} %fit.1), calls=%async_computation.2 | async-start | bytes 65536 | tf_op jit(solution)/shard_map/gather_scores/all_to_all | solution.py:235
  117.7 7.3 %all-to-all-done.2 = f32[32,1,256]{2,1,0:T(1,128)S(1)} async-done(((f32[32,1,256]{2,1,0:T(1,128)}), f32[32,1,256]{2,1,0:T(1,128)S(1)}, u32[]{:S(2)}, u32[]{:S(2)}) %all-to-all-start.2) | async-done | bytes 32800 | tf_op jit(solution)/shard_map/gather_scores/all_to_all | solution.py:235
  125.1 1.9 %collective-permute-start.26 = (f32[256]{0:T(256)S(1)}, f32[256]{0:T(256)S(1)}, u32[]{:S(2)}, u32[]{:S(2)}) collective-permute-start(f32[256]{0:T(256)S(1)} %reduce_sum.9), channel_id=1, source_target_pairs={{0,2},{2,4},{4,6},{6,8},{8,10},{10,12},{12,14},{3,1},{5,3},{7,5},{... | collective-permute-start | bytes 3080 | tf_op jit(solution)/shard_map/gather_scores/ppermute | solution.py:238
  127.0 0.6 dynamic_slice.54
  127.6 2.9 %collective-permute-done.26 = f32[256]{0:T(256)S(1)} collective-permute-done((f32[256]{0:T(256)S(1)}, f32[256]{0:T(256)S(1)}, u32[]{:S(2)}, u32[]{:S(2)}) %collective-permute-start.26) | collective-permute-done | bytes 1056 | tf_op jit(solution)/shard_map/gather_scores/ppermute | solution.py:238
  130.7 0.6 add_divide_fusion
  (53 shorter events, 1.4 us)
Async XLA Ops:
  0.6 33.7 %collective-permute-start.9 = (bf16[1024,1024]{1,0:T(8,128)(2,1)}, bf16[1024,1024]{1,0:T(8,128)(2,1)}, u32[]{:S(2)}, u32[]{:S(2)}) collective-permute-start(bf16[1024,1024]{1,0:T(8,128)(2,1)} %param.10), channel_id=1, source_target_pairs={{0,16},{16,0},{1,17},{17,1},{2,18},{18,2},{3,19},{19,3},{4,20},{20... | collective-permute-start | bytes 6291464 | tf_op jit(solution)/shard_map/swap_eigvecs/ppermute | solution.py:25
  2.6 16.3 %collective-permute-start.1 = (bf16[128,1024]{1,0:T(8,128)(2,1)}, bf16[128,1024]{1,0:T(8,128)(2,1)}, u32[]{:S(2)}, u32[]{:S(2)}) collective-permute-start(bf16[128,1024]{1,0:T(8,128)(2,1)} %weigh.1), channel_id=1, source_target_pairs={{0,32},{32,64},{64,96},{96,0},{1,33},{33,65},{65,97},{97,1},{2,34}... | collective-permute-start | bytes 786440 | tf_op jit(solution)/shard_map/gather_rows/ppermute | solution.py:25
  4.1 16.1 %collective-permute-start.3 = (bf16[128,1024]{1,0:T(8,128)(2,1)}, bf16[128,1024]{1,0:T(8,128)(2,1)}, u32[]{:S(2)}, u32[]{:S(2)}) collective-permute-start(bf16[128,1024]{1,0:T(8,128)(2,1)} %weigh.1), channel_id=1, source_target_pairs={{0,128},{128,0},{1,129},{129,1},{2,130},{130,2},{3,131},{131,3},{4... | collective-permute-start | bytes 786440 | tf_op jit(solution)/shard_map/gather_rows/ppermute | solution.py:25
  5.6 17.4 %collective-permute-start = (bf16[128,1024]{1,0:T(8,128)(2,1)}, bf16[128,1024]{1,0:T(8,128)(2,1)}, u32[]{:S(2)}, u32[]{:S(2)}) collective-permute-start(bf16[128,1024]{1,0:T(8,128)(2,1)} %weigh.1), channel_id=1, source_target_pairs={{0,96},{32,0},{64,32},{96,64},{1,97},{33,1},{65,33},{97,65},{2,98}... | collective-permute-start | bytes 786440 | tf_op jit(solution)/shard_map/gather_rows/ppermute | solution.py:25
  8.7 9.6 %all-to-all-start = ((f32[16,1,1024]{2,1,0:T(1,128)}), f32[16,1,1024]{2,1,0:T(1,128)S(1)}, u32[]{:S(2)}, u32[]{:S(2)}) async-start(f32[16,1,1024]{2,1,0:T(1,128)} %broadcast_in_dim.17), calls=%async_computation | async-start | bytes 131072 | tf_op jit(solution)/shard_map/gather_values/all_to_all | solution.py:170
  18.9 9.8 %collective-permute-start.2 = (bf16[128,1024]{1,0:T(8,128)(2,1)}, bf16[128,1024]{1,0:T(8,128)(2,1)S(1)}, u32[]{:S(2)}, u32[]{:S(2)}) collective-permute-start(bf16[128,1024]{1,0:T(8,128)(2,1)} %collective-permute-done.1), channel_id=1, source_target_pairs={{0,32},{32,64},{64,96},{96,0},{1,33},{33,65},{65,97},{97,1},{2,34}... | collective-permute-start | bytes 786440 | tf_op jit(solution)/shard_map/gather_rows/ppermute | solution.py:25
  19.5 8.3 %collective-permute-start.5 = (bf16[128,1024]{1,0:T(8,128)(2,1)}, bf16[128,1024]{1,0:T(8,128)(2,1)S(1)}, u32[]{:S(2)}, u32[]{:S(2)}) collective-permute-start(bf16[128,1024]{1,0:T(8,128)(2,1)} %collective-permute-done.1), channel_id=1, source_target_pairs={{0,128},{128,0},{1,129},{129,1},{2,130},{130,2},{3,131},{131,3},{4... | collective-permute-start | bytes 786440 | tf_op jit(solution)/shard_map/gather_rows/ppermute | solution.py:25
  20.2 9.2 %collective-permute-start.4 = (bf16[128,1024]{1,0:T(8,128)(2,1)}, bf16[128,1024]{1,0:T(8,128)(2,1)S(1)}, u32[]{:S(2)}, u32[]{:S(2)}) collective-permute-start(bf16[128,1024]{1,0:T(8,128)(2,1)} %collective-permute-done.3), channel_id=1, source_target_pairs={{0,96},{32,0},{64,32},{96,64},{1,97},{33,1},{65,33},{97,65},{2,98}... | collective-permute-start | bytes 786440 | tf_op jit(solution)/shard_map/gather_rows/ppermute | solution.py:25
  24.1 11.4 %copy-start = (bf16[1024,1024]{1,0:T(8,128)(2,1)S(1)}, bf16[1024,1024]{1,0:T(8,128)(2,1)}, u32[]{:S(2)}) copy-start(bf16[1024,1024]{1,0:T(8,128)(2,1)} %param.10) | copy-start | bytes 6291460
  27.8 6.3 %collective-permute-start.6 = (bf16[48,1024]{1,0:T(8,128)(2,1)S(1)}, bf16[48,1024]{1,0:T(8,128)(2,1)S(1)}, u32[]{:S(2)}, u32[]{:S(2)}) collective-permute-start(bf16[48,1024]{1,0:T(8,128)(2,1)S(1)} %slice.264), channel_id=1, source_target_pairs={{0,32},{32,64},{64,96},{96,0},{1,33},{33,65},{65,97},{97,1},{2,34}... | collective-permute-start | bytes 294920 | tf_op jit(solution)/shard_map/gather_rows/ppermute | solution.py:25
  28.7 5.4 %collective-permute-start.8 = (bf16[32,1024]{1,0:T(8,128)(2,1)S(1)}, bf16[32,1024]{1,0:T(8,128)(2,1)S(1)}, u32[]{:S(2)}, u32[]{:S(2)}) collective-permute-start(bf16[32,1024]{1,0:T(8,128)(2,1)S(1)} %slice.266), channel_id=1, source_target_pairs={{0,128},{128,0},{1,129},{129,1},{2,130},{130,2},{3,131},{131,3},{4... | collective-permute-start | bytes 196616 | tf_op jit(solution)/shard_map/gather_rows/ppermute | solution.py:25
  29.4 5.0 %collective-permute-start.7 = (bf16[48,1024]{1,0:T(8,128)(2,1)S(1)}, bf16[48,1024]{1,0:T(8,128)(2,1)S(1)}, u32[]{:S(2)}, u32[]{:S(2)}) collective-permute-start(bf16[48,1024]{1,0:T(8,128)(2,1)S(1)} %slice.265), channel_id=1, source_target_pairs={{0,96},{32,0},{64,32},{96,64},{1,97},{33,1},{65,33},{97,65},{2,98}... | collective-permute-start | bytes 294920 | tf_op jit(solution)/shard_map/gather_rows/ppermute | solution.py:25
  35.9 11.5 %collective-permute-start.10 = (bf16[64,1024]{1,0:T(8,128)(2,1)S(1)}, bf16[64,1024]{1,0:T(8,128)(2,1)S(1)}, u32[]{:S(2)}, u32[]{:S(2)}) collective-permute-start(bf16[64,1024]{1,0:T(8,128)(2,1)S(1)} %convolution_convert_fusion.3), channel_id=1, source_target_pairs={{0,2},{2,4},{4,6},{6,8},{8,10},{10,12},{12,14},{14,0},{1,3},{3,5},... | collective-permute-start | bytes 393224 | tf_op jit(solution)/shard_map/sum_layers/ppermute | solution.py:25
  39.6 11.6 %collective-permute-start.14 = (bf16[64,1024]{1,0:T(8,128)(2,1)S(1)}, bf16[64,1024]{1,0:T(8,128)(2,1)S(1)}, u32[]{:S(2)}, u32[]{:S(2)}) collective-permute-start(bf16[64,1024]{1,0:T(8,128)(2,1)S(1)} %convolution_convert_fusion.2), channel_id=1, source_target_pairs={{0,14},{2,0},{4,2},{6,4},{8,6},{10,8},{12,10},{14,12},{1,15},{3,1}... | collective-permute-start | bytes 393224 | tf_op jit(solution)/shard_map/sum_layers/ppermute | solution.py:25
  41.8 9.9 %collective-permute-start.18 = (bf16[64,1024]{1,0:T(8,128)(2,1)S(1)}, bf16[64,1024]{1,0:T(8,128)(2,1)S(1)}, u32[]{:S(2)}, u32[]{:S(2)}) collective-permute-start(bf16[64,1024]{1,0:T(8,128)(2,1)S(1)} %convolution_convert_fusion.1), channel_id=1, source_target_pairs={{0,2},{2,4},{4,6},{6,8},{8,10},{10,12},{12,14},{14,0},{1,3},{3,5},... | collective-permute-start | bytes 393224 | tf_op jit(solution)/shard_map/sum_layers/ppermute | solution.py:25
  47.1 9.9 %collective-permute-start.22 = (bf16[64,1024]{1,0:T(8,128)(2,1)S(1)}, bf16[64,1024]{1,0:T(8,128)(2,1)S(1)}, u32[]{:S(2)}, u32[]{:S(2)}) collective-permute-start(bf16[64,1024]{1,0:T(8,128)(2,1)S(1)} %convolution_convert_fusion), channel_id=1, source_target_pairs={{0,14},{2,0},{4,2},{6,4},{8,6},{10,8},{12,10},{14,12},{1,15},{3,1}... | collective-permute-start | bytes 393224 | tf_op jit(solution)/shard_map/sum_layers/ppermute | solution.py:25
  47.9 11.3 %collective-permute-start.11 = (bf16[128,1024]{1,0:T(8,128)(2,1)S(1)}, bf16[128,1024]{1,0:T(8,128)(2,1)S(1)}, u32[]{:S(2)}, u32[]{:S(2)}) collective-permute-start(bf16[128,1024]{1,0:T(8,128)(2,1)S(1)} %fusion.6), channel_id=1, source_target_pairs={{0,2},{2,4},{4,6},{6,8},{8,10},{10,12},{12,14},{14,0},{1,3},{3,5},... | collective-permute-start | bytes 786440 | tf_op jit(solution)/shard_map/sum_layers/ppermute | solution.py:25
  51.6 11.3 %collective-permute-start.15 = (bf16[128,1024]{1,0:T(8,128)(2,1)S(1)}, bf16[128,1024]{1,0:T(8,128)(2,1)S(1)}, u32[]{:S(2)}, u32[]{:S(2)}) collective-permute-start(bf16[128,1024]{1,0:T(8,128)(2,1)S(1)} %fusion.9), channel_id=1, source_target_pairs={{0,14},{2,0},{4,2},{6,4},{8,6},{10,8},{12,10},{14,12},{1,15},{3,1}... | collective-permute-start | bytes 786440 | tf_op jit(solution)/shard_map/sum_layers/ppermute | solution.py:25
  53.8 9.7 %collective-permute-start.19 = (bf16[128,1024]{1,0:T(8,128)(2,1)S(1)}, bf16[128,1024]{1,0:T(8,128)(2,1)S(1)}, u32[]{:S(2)}, u32[]{:S(2)}) collective-permute-start(bf16[128,1024]{1,0:T(8,128)(2,1)S(1)} %fusion.12), channel_id=1, source_target_pairs={{0,2},{2,4},{4,6},{6,8},{8,10},{10,12},{12,14},{14,0},{1,3},{3,5},... | collective-permute-start | bytes 786440 | tf_op jit(solution)/shard_map/sum_layers/ppermute | solution.py:25
  59.1 9.8 %collective-permute-start.23 = (bf16[128,1024]{1,0:T(8,128)(2,1)S(1)}, bf16[128,1024]{1,0:T(8,128)(2,1)S(1)}, u32[]{:S(2)}, u32[]{:S(2)}) collective-permute-start(bf16[128,1024]{1,0:T(8,128)(2,1)S(1)} %fusion.15), channel_id=1, source_target_pairs={{0,14},{2,0},{4,2},{6,4},{8,6},{10,8},{12,10},{14,12},{1,15},{3,1}... | collective-permute-start | bytes 786440 | tf_op jit(solution)/shard_map/sum_layers/ppermute | solution.py:25
  59.7 11.4 %collective-permute-start.12 = (bf16[128,1024]{1,0:T(8,128)(2,1)S(1)}, bf16[128,1024]{1,0:T(8,128)(2,1)S(1)}, u32[]{:S(2)}, u32[]{:S(2)}) collective-permute-start(bf16[128,1024]{1,0:T(8,128)(2,1)S(1)} %fusion.5), channel_id=1, source_target_pairs={{0,2},{2,4},{4,6},{6,8},{8,10},{10,12},{12,14},{14,0},{1,3},{3,5},... | collective-permute-start | bytes 786440 | tf_op jit(solution)/shard_map/sum_layers/ppermute | solution.py:25
  63.4 11.4 %collective-permute-start.16 = (bf16[128,1024]{1,0:T(8,128)(2,1)S(1)}, bf16[128,1024]{1,0:T(8,128)(2,1)S(1)}, u32[]{:S(2)}, u32[]{:S(2)}) collective-permute-start(bf16[128,1024]{1,0:T(8,128)(2,1)S(1)} %fusion.8), channel_id=1, source_target_pairs={{0,14},{2,0},{4,2},{6,4},{8,6},{10,8},{12,10},{14,12},{1,15},{3,1}... | collective-permute-start | bytes 786440 | tf_op jit(solution)/shard_map/sum_layers/ppermute | solution.py:25
  65.6 9.7 %collective-permute-start.20 = (bf16[128,1024]{1,0:T(8,128)(2,1)S(1)}, bf16[128,1024]{1,0:T(8,128)(2,1)S(1)}, u32[]{:S(2)}, u32[]{:S(2)}) collective-permute-start(bf16[128,1024]{1,0:T(8,128)(2,1)S(1)} %fusion.11), channel_id=1, source_target_pairs={{0,2},{2,4},{4,6},{6,8},{8,10},{10,12},{12,14},{14,0},{1,3},{3,5},... | collective-permute-start | bytes 786440 | tf_op jit(solution)/shard_map/sum_layers/ppermute | solution.py:25
  70.9 10.4 %collective-permute-start.24 = (bf16[128,1024]{1,0:T(8,128)(2,1)S(1)}, bf16[128,1024]{1,0:T(8,128)(2,1)S(1)}, u32[]{:S(2)}, u32[]{:S(2)}) collective-permute-start(bf16[128,1024]{1,0:T(8,128)(2,1)S(1)} %fusion.14), channel_id=1, source_target_pairs={{0,14},{2,0},{4,2},{6,4},{8,6},{10,8},{12,10},{14,12},{1,15},{3,1}... | collective-permute-start | bytes 786440 | tf_op jit(solution)/shard_map/sum_layers/ppermute | solution.py:25
  71.5 12.0 %collective-permute-start.13 = (bf16[128,1024]{1,0:T(8,128)(2,1)S(1)}, bf16[128,1024]{1,0:T(8,128)(2,1)S(1)}, u32[]{:S(2)}, u32[]{:S(2)}) collective-permute-start(bf16[128,1024]{1,0:T(8,128)(2,1)S(1)} %fusion.4), channel_id=1, source_target_pairs={{0,2},{2,4},{4,6},{6,8},{8,10},{10,12},{12,14},{14,0},{1,3},{3,5},... | collective-permute-start | bytes 786440 | tf_op jit(solution)/shard_map/sum_layers/ppermute | solution.py:25
  75.3 9.4 %collective-permute-start.17 = (bf16[128,1024]{1,0:T(8,128)(2,1)S(1)}, bf16[128,1024]{1,0:T(8,128)(2,1)S(1)}, u32[]{:S(2)}, u32[]{:S(2)}) collective-permute-start(bf16[128,1024]{1,0:T(8,128)(2,1)S(1)} %fusion.7), channel_id=1, source_target_pairs={{0,14},{2,0},{4,2},{6,4},{8,6},{10,8},{12,10},{14,12},{1,15},{3,1}... | collective-permute-start | bytes 786440 | tf_op jit(solution)/shard_map/sum_layers/ppermute | solution.py:25
  77.4 7.9 %collective-permute-start.21 = (bf16[128,1024]{1,0:T(8,128)(2,1)S(1)}, bf16[128,1024]{1,0:T(8,128)(2,1)S(1)}, u32[]{:S(2)}, u32[]{:S(2)}) collective-permute-start(bf16[128,1024]{1,0:T(8,128)(2,1)S(1)} %fusion.10), channel_id=1, source_target_pairs={{0,2},{2,4},{4,6},{6,8},{8,10},{10,12},{12,14},{14,0},{1,3},{3,5},... | collective-permute-start | bytes 786440 | tf_op jit(solution)/shard_map/sum_layers/ppermute | solution.py:25
  83.4 7.7 %collective-permute-start.25 = (bf16[128,1024]{1,0:T(8,128)(2,1)S(1)}, bf16[128,1024]{1,0:T(8,128)(2,1)S(1)}, u32[]{:S(2)}, u32[]{:S(2)}) collective-permute-start(bf16[128,1024]{1,0:T(8,128)(2,1)S(1)} %fusion.13), channel_id=1, source_target_pairs={{0,14},{2,0},{4,2},{6,4},{8,6},{10,8},{12,10},{14,12},{1,15},{3,1}... | collective-permute-start | bytes 786440 | tf_op jit(solution)/shard_map/sum_layers/ppermute | solution.py:25
  93.2 8.3 %copy-start.1 = (s32[1024]{0:T(1024)S(1)}, s32[1024]{0:T(1024)}, u32[]{:S(2)}) copy-start(s32[1024]{0:T(1024)} %param.12) | copy-start | bytes 12292
  93.2 37.5 %copy-start.2 = (s32[64]{0:T(128)S(1)}, s32[64]{0:T(128)}, u32[]{:S(2)}) copy-start(s32[64]{0:T(128)} %param.13) | copy-start | bytes 772
  94.1 17.5 %all-to-all-start.1 = ((bf16[16,8,2048]{2,1,0:T(8,128)(2,1)}), bf16[16,8,2048]{2,1,0:T(8,128)(2,1)S(1)}, u32[]{:S(2)}, u32[]{:S(2)}) async-start(bf16[16,8,2048]{2,1,0:T(8,128)(2,1)} %maximum_bitcast_fusion), calls=%async_computation.1 | async-start | bytes 1048576 | tf_op jit(solution)/shard_map/to_components/all_to_all | solution.py:230
  113.8 11.2 %all-to-all-start.2 = ((f32[32,1,256]{2,1,0:T(1,128)}), f32[32,1,256]{2,1,0:T(1,128)S(1)}, u32[]{:S(2)}, u32[]{:S(2)}) async-start(f32[32,1,256]{2,1,0:T(1,128)} %fit.1), calls=%async_computation.2 | async-start | bytes 65536 | tf_op jit(solution)/shard_map/gather_scores/all_to_all | solution.py:235
  125.1 5.5 %collective-permute-start.26 = (f32[256]{0:T(256)S(1)}, f32[256]{0:T(256)S(1)}, u32[]{:S(2)}, u32[]{:S(2)}) collective-permute-start(f32[256]{0:T(256)S(1)} %reduce_sum.9), channel_id=1, source_target_pairs={{0,2},{2,4},{4,6},{6,8},{8,10},{10,12},{12,14},{3,1},{5,3},{7,5},{... | collective-permute-start | bytes 3080 | tf_op jit(solution)/shard_map/gather_scores/ppermute | solution.py:238

commit v6 on v4

--- a/solution.py
+++ b/solution.py
@@ -47,6 +47,45 @@
         weigh_kernel,
         out_shape=jax.ShapeDtypeStruct((2 * rows, width), jnp.bfloat16),
     )(responses, weights, phenotype[None, :])
+
+
+def open_kernel(place_ref, blocks_ref, own_ref, other_ref, *refs):
+    outs, nears, (block_ref, block_sem, near_sems) = refs[:4], refs[4:6], refs[6:]
+    fetch = pltpu.make_async_copy(blocks_ref.at[place_ref[0]], block_ref, block_sem)
+    copies = [
+        pltpu.make_async_copy(given, near, near_sems.at[q])
+        for q, (given, near) in enumerate(zip((own_ref, other_ref), nears))
+    ]
+    fetch.start()
+    for copy in copies:
+        copy.start()
+    fetch.wait()
+    cut = outs[0].shape[0]
+    for q, copy in enumerate(copies):
+        copy.wait()
+        total = jnp.dot(block_ref[...], nears[q][...], preferred_element_type=jnp.float32)
+        outs[2 * q][...] = total[:cut].astype(jnp.bfloat16)
+        outs[2 * q + 1][...] = total[cut:].astype(jnp.bfloat16)
+
+
+def open_sums(place, blocks, own, other):
+    _, rows, width = blocks.shape
+    columns = own.shape[1]
+    anywhere = pl.BlockSpec(memory_space=pl.ANY)
+    vmem = pl.BlockSpec(memory_space=pltpu.VMEM)
+    return pl.pallas_call(
+        open_kernel,
+        out_shape=[jax.ShapeDtypeStruct((rows // 2, columns), jnp.bfloat16)] * 4
+        + [pltpu.VMEM(own.shape, own.dtype)] * 2,
+        in_specs=[pl.BlockSpec(memory_space=pltpu.SMEM), anywhere, anywhere, anywhere],
+        out_specs=[vmem] * 6,
+        scratch_shapes=[
+            pltpu.VMEM((rows, width), jnp.bfloat16),
+            pltpu.SemaphoreType.DMA,
+            pltpu.SemaphoreType.DMA((2,)),
+        ],
+        compiler_params=pltpu.CompilerParams(vmem_limit_bytes=24 * 1024 * 1024),
+    )(place, blocks, own, other)
 
 
 def fit_kernel(slot_ref, sums_ref, values_ref, out_ref, r_ref, d_ref, w_ref):
@@ -180,28 +219,23 @@
         blocks = gather_plane(own)
     with jax.named_scope("swap_eigvecs"):
         other = shifted(eigvecs, "samp_2", 1)
-        vecs = (eigvecs, other)
-        ready = (0.0 * other[0, 0].astype(jnp.float32)).astype(jnp.int32)
     with jax.named_scope("gather_values"):
         everywhere = copies(eigvals, SAMP).reshape(-1, 2, eigvals.shape[0])
         everywhere = jnp.where(lax.axis_index("samp_2") == 0, everywhere, everywhere[:, ::-1])
         everywhere = jnp.repeat(everywhere.reshape(everywhere.shape[0], -1), 4, axis=0)
     rows = own.shape[0]
 
-    def term(q, ahead, lo, hi):
+    def place(ahead):
         dest = lax.rem(z + ahead + layers, layers)
         across, along = dest // 4, lax.rem(dest, 4)
-        place = 4 * (across ^ y) + lax.rem(along - x + 4, 4) + ready
-        block = lax.dynamic_index_in_dim(blocks, place, 0, keepdims=False)[lo:hi]
+        return 4 * (across ^ y) + lax.rem(along - x + 4, 4)
+
+    def term(q, ahead):
+        block = lax.dynamic_index_in_dim(blocks, place(ahead), 0, keepdims=False)
         return jnp.dot(block, vecs[q], preferred_element_type=jnp.float32)
 
     far = layers // 2
-    cut = rows // 2
     sent = {}
-
-    def first(q):
-        sent[q, 1] = shifted(term(q, far, 0, cut).astype(jnp.bfloat16), "cpg_0", 1)
-        sent[q, -1] = shifted(term(q, far, cut, rows).astype(jnp.bfloat16), "cpg_0", -1)
 
     def onward(q, ahead):
         for way in (1, -1):
@@ -209,18 +243,21 @@
             if got.shape[0] < rows:
                 rest = jnp.zeros_like(got)
                 got = jnp.concatenate([got, rest] if way == 1 else [rest, got], axis=0)
-            total = (term(q, way * ahead, 0, rows) + got).astype(jnp.bfloat16)
+            total = (term(q, way * ahead) + got).astype(jnp.bfloat16)
             sent[q, way] = shifted(total, "cpg_0", way)
 
     def summed(q):
-        total = term(q, 0, 0, rows)
+        total = term(q, 0)
         for way in (1, -1):
             total = total + sent[q, way].astype(jnp.float32)
         return total.astype(jnp.bfloat16)
 
     with jax.named_scope("sum_layers"):
-        first(0)
-        first(1)
+        *halves, near_own, near_other = open_sums(place(far)[None], blocks, eigvecs, other)
+        vecs = (near_own, near_other)
+        for q in (0, 1):
+            for at, way in enumerate((1, -1)):
+                sent[q, way] = shifted(halves[2 * q + at], "cpg_0", way)
         for ahead in range(far - 1, 0, -1):
             onward(0, ahead)
             onward(1, ahead)

time: 131 us -> 130 us (level)
  matrix products: 24.6 us -> 9.06 us
  waiting for transfers between devices: 30.6 us -> 41.4 us
  starting transfers between devices: 55.4 us -> 60.8 us
  local copies, waits for them, and re-layouts: 11.1 us -> 8.54 us
  Pallas kernels: 4.01 us -> 6.24 us
    dot_general x18 -> x14, matrix products: 24.6 us -> 9.06 us  [term(): return jnp.dot(block, vecs[q], preferred_element_type=jnp.float32)]
    ppermute x26, waiting for transfers between devices: 13.4 us -> 22 us  [shifted(): lax.ppermute(value, axis, [(i, (i + by) % peers) for i in range(peers)])]
    ppermute x26, starting transfers between devices: 36.9 us -> 43.3 us  [shifted(): lax.ppermute(value, axis, [(i, (i + by) % peers) for i in range(peers)])]
    ppermute x1, starting transfers between devices: 5.6 us -> 1.92 us  [shards(): other = lax.ppermute(layer, CPG, beside)]
    ppermute x1, waiting for transfers between devices: 0.67 us -> 2.93 us  [shards(): other = lax.ppermute(layer, CPG, beside)]
    pallas_call x0 -> x1, Pallas kernels: none -> 2.23 us  [open_sums(): pl.pallas_call(open_kernel, out_shape=[jax.ShapeDtypeStruct((rows // 2, c...]
    all_to_all x1, starting transfers between devices: 5.52 us -> 7.07 us  [shards(): sums = lax.all_to_all(whole, PLANE, 0, 0, tiled=True)]
    unnamed x15 -> x25, local copies, waits for them, and re-layouts: 6.42 us -> 6.48 us
  transfers between devices with their start and end apart: 30 -> 30, of which waited for: 12 -> 14; matrix products, arithmetic and copies ran while one was open for 29% -> 11% of each run, Pallas kernels for 1% -> 1%
where the time goes in v6:
time: 130 us; the launch traced here: 129 us
  starting transfers between devices  60.8 us (47%)
  waiting for transfers between devices  41.4 us (32%)
  matrix products  9.06 us (7%)
  local copies, waits for them, and re-layouts  8.54 us (7%)
  Pallas kernels  6.24 us (5%)
  other arithmetic  1.82 us (1%)
  between operations  1.46 us (1%)
    ppermute x26, starting transfers between devices, shifted(): lax.ppermute(value, axis, [(i, (i + by) % peers) for i in range(peers)])  43.3 us
    ppermute x26, waiting for transfers between devices, shifted(): lax.ppermute(value, axis, [(i, (i + by) % peers) for i in range(peers)])  22 us
    all_to_all x1, waiting for transfers between devices, shards(): sums = lax.all_to_all(whole, PLANE, 0, 0, tiled=True)  9.21 us
    dot_general x14, matrix products, term(): return jnp.dot(block, vecs[q], preferred_element_type=jnp.float32)  9.06 us
    all_to_all x1, waiting for transfers between devices, shards(): lax.all_to_all(fitted, LAYER, 0, 0, tiled=True)  7.32 us
    all_to_all x1, starting transfers between devices, shards(): sums = lax.all_to_all(whole, PLANE, 0, 0, tiled=True)  7.07 us
    unnamed x25, local copies, waits for them, and re-layouts  6.48 us
    all_to_all x1, starting transfers between devices, copies(): lax.all_to_all(jnp.broadcast_to(value[None], (peers, *value.shape)), axes...  4.69 us
  transfers between devices with their start and end apart: 30, of which 14 were waited for; matrix products, arithmetic and copies ran while one was open for 11% of the time, Pallas kernels for 1%

profile of v6, /device:TPU:96, one launch (start us, length us, event | category | flops | bytes accessed | tf_op | source)
XLA Modules:
  0.0 129.4 jit_solution(13578986134233082999)
XLA Ops:
  0.6 0.1 collective-permute-start.9
  0.7 1.8 %weigh.1 = bf16[128,1024]{1,0:T(8,128)(2,1)} custom-call(bf16[64,1024]{1,0:T(8,128)(2,1)} %resp_ref.1, bf16[64,1024]{1,0:T(8,128)(2,1)} %weight_ref.1, f32[1,1024]{1,0:T(1,128)} %bitcast.78), custom_call_target="tpu_custom_call" | custom-call | tf_op jit(solution)/shard_map/weigh/pallas_call | solution.py:46
  2.5 1.5 %collective-permute-start.1 = (bf16[128,1024]{1,0:T(8,128)(2,1)}, bf16[128,1024]{1,0:T(8,128)(2,1)S(1)}, u32[]{:S(2)}, u32[]{:S(2)}) collective-permute-start(bf16[128,1024]{1,0:T(8,128)(2,1)} %weigh.1), channel_id=1, source_target_pairs={{0,32},{32,64},{64,96},{96,0},{1,33},{33,65},{65,97},{97,1},{2,34}... | collective-permute-start | bytes 786440 | tf_op jit(solution)/shard_map/gather_rows/ppermute | solution.py:25
  4.0 1.6 %collective-permute-start.3 = (bf16[128,1024]{1,0:T(8,128)(2,1)}, bf16[128,1024]{1,0:T(8,128)(2,1)S(1)}, u32[]{:S(2)}, u32[]{:S(2)}) collective-permute-start(bf16[128,1024]{1,0:T(8,128)(2,1)} %weigh.1), channel_id=1, source_target_pairs={{0,128},{128,0},{1,129},{129,1},{2,130},{130,2},{3,131},{131,3},{4... | collective-permute-start | bytes 786440 | tf_op jit(solution)/shard_map/gather_rows/ppermute | solution.py:25
  5.6 1.7 %collective-permute-start = (bf16[128,1024]{1,0:T(8,128)(2,1)}, bf16[128,1024]{1,0:T(8,128)(2,1)}, u32[]{:S(2)}, u32[]{:S(2)}) collective-permute-start(bf16[128,1024]{1,0:T(8,128)(2,1)} %weigh.1), channel_id=1, source_target_pairs={{0,96},{32,0},{64,32},{96,64},{1,97},{33,1},{65,33},{97,65},{2,98}... | collective-permute-start | bytes 786440 | tf_op jit(solution)/shard_map/gather_rows/ppermute | solution.py:25
  7.4 5.3 %collective-permute-done.1 = bf16[128,1024]{1,0:T(8,128)(2,1)S(1)} collective-permute-done((bf16[128,1024]{1,0:T(8,128)(2,1)}, bf16[128,1024]{1,0:T(8,128)(2,1)S(1)}, u32[]{:S(2)}, u32[]{:S(2)}) %collective-permute-start.1) | collective-permute-done | bytes 262176 | tf_op jit(solution)/shard_map/gather_rows/ppermute | solution.py:25
  12.7 0.3 collective-permute-start.2
  13.0 1.6 %collective-permute-start.5 = (bf16[128,1024]{1,0:T(8,128)(2,1)S(1)}, bf16[128,1024]{1,0:T(8,128)(2,1)S(1)}, u32[]{:S(2)}, u32[]{:S(2)}) collective-permute-start(bf16[128,1024]{1,0:T(8,128)(2,1)S(1)} %collective-permute-done.1), channel_id=1, source_target_pairs={{0,128},{128,0},{1,129},{129,1},{2,130},{130,2},{3,131},{131,3},{4... | collective-permute-start | bytes 786440 | tf_op jit(solution)/shard_map/gather_rows/ppermute | solution.py:25
  14.5 3.0 %collective-permute-start.4 = (bf16[128,1024]{1,0:T(8,128)(2,1)S(1)}, bf16[128,1024]{1,0:T(8,128)(2,1)S(1)}, u32[]{:S(2)}, u32[]{:S(2)}) collective-permute-start(bf16[128,1024]{1,0:T(8,128)(2,1)S(1)} %collective-permute-done.3), channel_id=1, source_target_pairs={{0,96},{32,0},{64,32},{96,64},{1,97},{33,1},{65,33},{97,65},{2,98}... | collective-permute-start | bytes 786440 | tf_op jit(solution)/shard_map/gather_rows/ppermute | solution.py:25
  17.5 1.0 bitcast_dynamic-update-slice_fusion.6
  18.5 1.1 bitcast_dynamic-update-slice_fusion.5
  19.6 1.1 collective-permute-done.5
  20.7 1.6 %collective-permute-start.6 = (bf16[48,1024]{1,0:T(8,128)(2,1)S(1)}, bf16[48,1024]{1,0:T(8,128)(2,1)S(1)}, u32[]{:S(2)}, u32[]{:S(2)}) collective-permute-start(bf16[48,1024]{1,0:T(8,128)(2,1)S(1)} %slice.233), channel_id=1, source_target_pairs={{0,32},{32,64},{64,96},{96,0},{1,33},{33,65},{65,97},{97,1},{2,34}... | collective-permute-start | bytes 294920 | tf_op jit(solution)/shard_map/gather_rows/ppermute | solution.py:25
  22.3 1.7 %collective-permute-start.8 = (bf16[32,1024]{1,0:T(8,128)(2,1)S(1)}, bf16[32,1024]{1,0:T(8,128)(2,1)S(1)}, u32[]{:S(2)}, u32[]{:S(2)}) collective-permute-start(bf16[32,1024]{1,0:T(8,128)(2,1)S(1)} %slice.235), channel_id=1, source_target_pairs={{0,128},{128,0},{1,129},{129,1},{2,130},{130,2},{3,131},{131,3},{4... | collective-permute-start | bytes 196616 | tf_op jit(solution)/shard_map/gather_rows/ppermute | solution.py:25
  24.0 2.2 %collective-permute-start.7 = (bf16[48,1024]{1,0:T(8,128)(2,1)S(1)}, bf16[48,1024]{1,0:T(8,128)(2,1)S(1)}, u32[]{:S(2)}, u32[]{:S(2)}) collective-permute-start(bf16[48,1024]{1,0:T(8,128)(2,1)S(1)} %slice.234), channel_id=1, source_target_pairs={{0,96},{32,0},{64,32},{96,64},{1,97},{33,1},{65,33},{97,65},{2,98}... | collective-permute-start | bytes 294920 | tf_op jit(solution)/shard_map/gather_rows/ppermute | solution.py:25
  26.2 0.4 collective-permute-done.8
  26.6 2.0 %collective-permute-done.7 = bf16[48,1024]{1,0:T(8,128)(2,1)S(1)} collective-permute-done((bf16[48,1024]{1,0:T(8,128)(2,1)S(1)}, bf16[48,1024]{1,0:T(8,128)(2,1)S(1)}, u32[]{:S(2)}, u32[]{:S(2)}) %collective-permute-start.7) | collective-permute-done | bytes 98336 | tf_op jit(solution)/shard_map/gather_rows/ppermute | solution.py:25
  28.7 1.3 %copy-done.2 = bf16[8,128,1024]{2,1,0:T(8,128)(2,1)} copy-done((bf16[8,128,1024]{2,1,0:T(8,128)(2,1)}, bf16[8,128,1024]{2,1,0:T(8,128)(2,1)S(1)}, u32[]{:S(2)}) %copy-start.2) | copy-done | bytes 2097176
  30.0 1.6 %copy-done.3 = bf16[8,128,1024]{2,1,0:T(8,128)(2,1)S(1)} copy-done((bf16[8,128,1024]{2,1,0:T(8,128)(2,1)S(1)}, bf16[8,128,1024]{2,1,0:T(8,128)(2,1)}, u32[]{:S(2)}) %copy-start.3) | copy-done | bytes 2097176
  31.6 2.2 %sum_layers.1 = (bf16[64,1024]{1,0:T(8,128)(2,1)S(1)}, bf16[64,1024]{1,0:T(8,128)(2,1)S(1)}, bf16[64,1024]{1,0:T(8,128)(2,1)S(1)}, bf16[64,1024]{1,0:T(8,128)(2,...) custom-call(s32[1]{0:T(128)} %bitcast.11.place_ref, bf16[8,128,1024]{2,1,0:T(8,128)(2,1)S(1)} %copy-done.3, ...), custom_call_target="tpu_custom_call" | custom-call | tf_op jit(solution)/shard_map/sum_layers/pallas_call | solution.py:76
  33.9 1.4 %copy-done = bf16[1024,1024]{1,0:T(8,128)(2,1)} copy-done((bf16[1024,1024]{1,0:T(8,128)(2,1)}, bf16[1024,1024]{1,0:T(8,128)(2,1)S(1)}, u32[]{:S(2)}) %copy-start) | copy-done | bytes 2097176
  35.2 3.1 %collective-permute-start.10 = (bf16[64,1024]{1,0:T(8,128)(2,1)S(1)}, bf16[64,1024]{1,0:T(8,128)(2,1)S(1)}, u32[]{:S(2)}, u32[]{:S(2)}) collective-permute-start(bf16[64,1024]{1,0:T(8,128)(2,1)S(1)} %get-tuple-element.9), channel_id=1, source_target_pairs={{0,2},{2,4},{4,6},{6,8},{8,10},{10,12},{12,14},{14,0},{1,3},{3,5},... | collective-permute-start | bytes 393224 | tf_op jit(solution)/shard_map/sum_layers/ppermute | solution.py:25
  38.4 0.6 broadcast_in_dim.21
  39.0 4.7 %all-to-all-start.1 = ((f32[16,1,1024]{2,1,0:T(1,128)}), f32[16,1,1024]{2,1,0:T(1,128)S(1)}, u32[]{:S(2)}, u32[]{:S(2)}) async-start(f32[16,1,1024]{2,1,0:T(1,128)} %broadcast_in_dim.21), calls=%async_computation.1 | async-start | bytes 131072 | tf_op jit(solution)/shard_map/gather_values/all_to_all | solution.py:208
  44.1 3.2 %collective-permute-start.18 = (bf16[64,1024]{1,0:T(8,128)(2,1)S(1)}, bf16[64,1024]{1,0:T(8,128)(2,1)S(1)}, u32[]{:S(2)}, u32[]{:S(2)}) collective-permute-start(bf16[64,1024]{1,0:T(8,128)(2,1)S(1)} %get-tuple-element.12), channel_id=1, source_target_pairs={{0,2},{2,4},{4,6},{6,8},{8,10},{10,12},{12,14},{14,0},{1,3},{3,5},... | collective-permute-start | bytes 393224 | tf_op jit(solution)/shard_map/sum_layers/ppermute | solution.py:25
  47.3 2.3 %fusion.6 = bf16[128,1024]{1,0:T(8,128)(2,1)S(1)} fusion(bf16[1024,1024]{1,0:T(8,128)(2,1)} %copy-done, bf16[64,1024]{1,0:T(8,128)(2,1)S(1)} %collective-permute-done.10, bf16[8,128,1024]{2,1,0:T(8,128)(2,1)} %copy-done.2, s32[]{:T(128)S(6)} %select_n.88), kind=kOutput, calls=%fused_computation.20 | convolution fusion | flops 268828672 | bytes 2752516 | tf_op jit(solution)/shard_map/sum_layers/dot_general | solution.py:235
  49.6 3.5 %collective-permute-start.11 = (bf16[128,1024]{1,0:T(8,128)(2,1)S(1)}, bf16[128,1024]{1,0:T(8,128)(2,1)S(1)}, u32[]{:S(2)}, u32[]{:S(2)}) collective-permute-start(bf16[128,1024]{1,0:T(8,128)(2,1)S(1)} %fusion.6), channel_id=1, source_target_pairs={{0,2},{2,4},{4,6},{6,8},{8,10},{10,12},{12,14},{14,0},{1,3},{3,5},... | collective-permute-start | bytes 786440 | tf_op jit(solution)/shard_map/sum_layers/ppermute | solution.py:25
  53.1 1.4 %fusion.9 = bf16[128,1024]{1,0:T(8,128)(2,1)S(1)} fusion(bf16[1024,1024]{1,0:T(8,128)(2,1)S(1)} %copy-done.1, bf16[64,1024]{1,0:T(8,128)(2,1)S(1)} %collective-permute-done.14, bf16[8,128,1024]{2,1,0:T(8,128)(2,1)} %copy-done.2, s32[]{:T(128)S(6)} %select_n.94), kind=kOutput, calls=%fused_computation.23 | convolution fusion | flops 268828672 | bytes 2752516 | tf_op jit(solution)/shard_map/sum_layers/dot_general | solution.py:235
  54.6 0.4 fusion.12
  55.1 3.3 %collective-permute-start.19 = (bf16[128,1024]{1,0:T(8,128)(2,1)S(1)}, bf16[128,1024]{1,0:T(8,128)(2,1)S(1)}, u32[]{:S(2)}, u32[]{:S(2)}) collective-permute-start(bf16[128,1024]{1,0:T(8,128)(2,1)S(1)} %fusion.12), channel_id=1, source_target_pairs={{0,2},{2,4},{4,6},{6,8},{8,10},{10,12},{12,14},{14,0},{1,3},{3,5},... | collective-permute-start | bytes 786440 | tf_op jit(solution)/shard_map/sum_layers/ppermute | solution.py:25
  58.3 0.4 fusion.15
  59.0 0.4 fusion.5
  59.4 3.8 %collective-permute-start.12 = (bf16[128,1024]{1,0:T(8,128)(2,1)S(1)}, bf16[128,1024]{1,0:T(8,128)(2,1)S(1)}, u32[]{:S(2)}, u32[]{:S(2)}) collective-permute-start(bf16[128,1024]{1,0:T(8,128)(2,1)S(1)} %fusion.5), channel_id=1, source_target_pairs={{0,2},{2,4},{4,6},{6,8},{8,10},{10,12},{12,14},{14,0},{1,3},{3,5},... | collective-permute-start | bytes 786440 | tf_op jit(solution)/shard_map/sum_layers/ppermute | solution.py:25
  63.2 1.6 %collective-permute-done.15 = bf16[128,1024]{1,0:T(8,128)(2,1)S(1)} collective-permute-done((bf16[128,1024]{1,0:T(8,128)(2,1)S(1)}, bf16[128,1024]{1,0:T(8,128)(2,1)S(1)}, u32[]{:S(2)}, u32[]{:S(2)}) %collective-permute-start.15) | collective-permute-done | bytes 262176 | tf_op jit(solution)/shard_map/sum_layers/ppermute | solution.py:25
  64.8 0.4 fusion.8
  65.4 0.4 fusion.11
  65.8 3.5 %collective-permute-start.20 = (bf16[128,1024]{1,0:T(8,128)(2,1)S(1)}, bf16[128,1024]{1,0:T(8,128)(2,1)S(1)}, u32[]{:S(2)}, u32[]{:S(2)}) collective-permute-start(bf16[128,1024]{1,0:T(8,128)(2,1)S(1)} %fusion.11), channel_id=1, source_target_pairs={{0,2},{2,4},{4,6},{6,8},{8,10},{10,12},{12,14},{14,0},{1,3},{3,5},... | collective-permute-start | bytes 786440 | tf_op jit(solution)/shard_map/sum_layers/ppermute | solution.py:25
  69.3 1.1 collective-permute-done.23
  70.4 0.4 fusion.14
  71.0 0.4 fusion.4
  71.4 3.5 %collective-permute-start.13 = (bf16[128,1024]{1,0:T(8,128)(2,1)S(1)}, bf16[128,1024]{1,0:T(8,128)(2,1)S(1)}, u32[]{:S(2)}, u32[]{:S(2)}) collective-permute-start(bf16[128,1024]{1,0:T(8,128)(2,1)S(1)} %fusion.4), channel_id=1, source_target_pairs={{0,2},{2,4},{4,6},{6,8},{8,10},{10,12},{12,14},{14,0},{1,3},{3,5},... | collective-permute-start | bytes 786440 | tf_op jit(solution)/shard_map/sum_layers/ppermute | solution.py:25
  74.9 1.1 collective-permute-done.16
  76.0 0.4 fusion.7
  76.6 0.5 fusion.10
  77.1 3.5 %collective-permute-start.21 = (bf16[128,1024]{1,0:T(8,128)(2,1)S(1)}, bf16[128,1024]{1,0:T(8,128)(2,1)S(1)}, u32[]{:S(2)}, u32[]{:S(2)}) collective-permute-start(bf16[128,1024]{1,0:T(8,128)(2,1)S(1)} %fusion.10), channel_id=1, source_target_pairs={{0,2},{2,4},{4,6},{6,8},{8,10},{10,12},{12,14},{14,0},{1,3},{3,5},... | collective-permute-start | bytes 786440 | tf_op jit(solution)/shard_map/sum_layers/ppermute | solution.py:25
  80.6 1.1 collective-permute-done.24
  81.7 0.4 fusion.13
  82.1 0.3 collective-permute-start.25
  82.4 4.8 %collective-permute-done.17 = bf16[128,1024]{1,0:T(8,128)(2,1)S(1)} collective-permute-done((bf16[128,1024]{1,0:T(8,128)(2,1)S(1)}, bf16[128,1024]{1,0:T(8,128)(2,1)S(1)}, u32[]{:S(2)}, u32[]{:S(2)}) %collective-permute-start.17) | collective-permute-done | bytes 262176 | tf_op jit(solution)/shard_map/sum_layers/ppermute | solution.py:25
  87.3 0.5 fusion.2
  87.8 3.3 %collective-permute-done.25 = bf16[128,1024]{1,0:T(8,128)(2,1)S(1)} collective-permute-done((bf16[128,1024]{1,0:T(8,128)(2,1)S(1)}, bf16[128,1024]{1,0:T(8,128)(2,1)S(1)}, u32[]{:S(2)}, u32[]{:S(2)}) %collective-permute-start.25) | collective-permute-done | bytes 262176 | tf_op jit(solution)/shard_map/sum_layers/ppermute | solution.py:25
  91.1 0.5 fusion.3
  91.6 0.8 maximum_bitcast_fusion
  92.4 7.1 %all-to-all-start = ((bf16[16,8,2048]{2,1,0:T(8,128)(2,1)}), bf16[16,8,2048]{2,1,0:T(8,128)(2,1)S(1)}, u32[]{:S(2)}, u32[]{:S(2)}) async-start(bf16[16,8,2048]{2,1,0:T(8,128)(2,1)} %maximum_bitcast_fusion), calls=%async_computation | async-start | bytes 1048576 | tf_op jit(solution)/shard_map/to_components/all_to_all | solution.py:266
  99.6 0.2 reduce
  99.8 0.4 rev.3
  100.4 9.2 %all-to-all-done = bf16[16,8,2048]{2,1,0:T(8,128)(2,1)S(1)} async-done(((bf16[16,8,2048]{2,1,0:T(8,128)(2,1)}), bf16[16,8,2048]{2,1,0:T(8,128)(2,1)S(1)}, u32[]{:S(2)}, u32[]{:S(2)}) %all-to-all-start) | async-done | bytes 524320 | tf_op jit(solution)/shard_map/to_components/all_to_all | solution.py:266
  109.6 2.2 %fit.1 = f32[32,1,256]{2,1,0:T(1,128)} custom-call(s32[1]{0:T(128)} %bitcast.slot_ref, bf16[128,2048]{1,0:T(8,128)(2,1)S(1)} %bitcast.76, f32[32,2048]{1,0:T(8,128)S(1)} %reshape.24.values_ref), custom_call_target="tpu_custom_call" | custom-call | tf_op jit(solution)/shard_map/fit/pallas_call | solution.py:158
  111.8 3.8 %all-to-all-start.2 = ((f32[32,1,256]{2,1,0:T(1,128)}), f32[32,1,256]{2,1,0:T(1,128)S(1)}, u32[]{:S(2)}, u32[]{:S(2)}) async-start(f32[32,1,256]{2,1,0:T(1,128)} %fit.1), calls=%async_computation.2 | async-start | bytes 65536 | tf_op jit(solution)/shard_map/gather_scores/all_to_all | solution.py:271
  115.7 7.3 %all-to-all-done.2 = f32[32,1,256]{2,1,0:T(1,128)S(1)} async-done(((f32[32,1,256]{2,1,0:T(1,128)}), f32[32,1,256]{2,1,0:T(1,128)S(1)}, u32[]{:S(2)}, u32[]{:S(2)}) %all-to-all-start.2) | async-done | bytes 32800 | tf_op jit(solution)/shard_map/gather_scores/all_to_all | solution.py:271
  123.0 1.9 %collective-permute-start.26 = (f32[256]{0:T(256)S(1)}, f32[256]{0:T(256)S(1)}, u32[]{:S(2)}, u32[]{:S(2)}) collective-permute-start(f32[256]{0:T(256)S(1)} %reduce_sum.9), channel_id=1, source_target_pairs={{0,2},{2,4},{4,6},{6,8},{8,10},{10,12},{12,14},{3,1},{5,3},{7,5},{... | collective-permute-start | bytes 3080 | tf_op jit(solution)/shard_map/gather_scores/ppermute | solution.py:274
  125.0 0.6 dynamic_slice.47
  125.6 2.9 %collective-permute-done.26 = f32[256]{0:T(256)S(1)} collective-permute-done((f32[256]{0:T(256)S(1)}, f32[256]{0:T(256)S(1)}, u32[]{:S(2)}, u32[]{:S(2)}) %collective-permute-start.26) | collective-permute-done | bytes 1056 | tf_op jit(solution)/shard_map/gather_scores/ppermute | solution.py:274
  128.7 0.6 add_divide_fusion
  (61 shorter events, 1.4 us)
Async XLA Ops:
  0.6 29.4 %collective-permute-start.9 = (bf16[1024,1024]{1,0:T(8,128)(2,1)}, bf16[1024,1024]{1,0:T(8,128)(2,1)}, u32[]{:S(2)}, u32[]{:S(2)}) collective-permute-start(bf16[1024,1024]{1,0:T(8,128)(2,1)} %own_ref.1), channel_id=1, source_target_pairs={{0,16},{16,0},{1,17},{17,1},{2,18},{18,2},{3,19},{19,3},{4,20},{20... | collective-permute-start | bytes 6291464 | tf_op jit(solution)/shard_map/swap_eigvecs/ppermute | solution.py:25
  2.5 10.1 %collective-permute-start.1 = (bf16[128,1024]{1,0:T(8,128)(2,1)}, bf16[128,1024]{1,0:T(8,128)(2,1)S(1)}, u32[]{:S(2)}, u32[]{:S(2)}) collective-permute-start(bf16[128,1024]{1,0:T(8,128)(2,1)} %weigh.1), channel_id=1, source_target_pairs={{0,32},{32,64},{64,96},{96,0},{1,33},{33,65},{65,97},{97,1},{2,34}... | collective-permute-start | bytes 786440 | tf_op jit(solution)/shard_map/gather_rows/ppermute | solution.py:25
  4.0 10.5 %collective-permute-start.3 = (bf16[128,1024]{1,0:T(8,128)(2,1)}, bf16[128,1024]{1,0:T(8,128)(2,1)S(1)}, u32[]{:S(2)}, u32[]{:S(2)}) collective-permute-start(bf16[128,1024]{1,0:T(8,128)(2,1)} %weigh.1), channel_id=1, source_target_pairs={{0,128},{128,0},{1,129},{129,1},{2,130},{130,2},{3,131},{131,3},{4... | collective-permute-start | bytes 786440 | tf_op jit(solution)/shard_map/gather_rows/ppermute | solution.py:25
  5.6 12.9 %collective-permute-start = (bf16[128,1024]{1,0:T(8,128)(2,1)}, bf16[128,1024]{1,0:T(8,128)(2,1)}, u32[]{:S(2)}, u32[]{:S(2)}) collective-permute-start(bf16[128,1024]{1,0:T(8,128)(2,1)} %weigh.1), channel_id=1, source_target_pairs={{0,96},{32,0},{64,32},{96,64},{1,97},{33,1},{65,33},{97,65},{2,98}... | collective-permute-start | bytes 786440 | tf_op jit(solution)/shard_map/gather_rows/ppermute | solution.py:25
  12.7 9.6 %collective-permute-start.2 = (bf16[128,1024]{1,0:T(8,128)(2,1)S(1)}, bf16[128,1024]{1,0:T(8,128)(2,1)S(1)}, u32[]{:S(2)}, u32[]{:S(2)}) collective-permute-start(bf16[128,1024]{1,0:T(8,128)(2,1)S(1)} %collective-permute-done.1), channel_id=1, source_target_pairs={{0,32},{32,64},{64,96},{96,0},{1,33},{33,65},{65,97},{97,1},{2,34}... | collective-permute-start | bytes 786440 | tf_op jit(solution)/shard_map/gather_rows/ppermute | solution.py:25
  13.0 7.7 %collective-permute-start.5 = (bf16[128,1024]{1,0:T(8,128)(2,1)S(1)}, bf16[128,1024]{1,0:T(8,128)(2,1)S(1)}, u32[]{:S(2)}, u32[]{:S(2)}) collective-permute-start(bf16[128,1024]{1,0:T(8,128)(2,1)S(1)} %collective-permute-done.1), channel_id=1, source_target_pairs={{0,128},{128,0},{1,129},{129,1},{2,130},{130,2},{3,131},{131,3},{4... | collective-permute-start | bytes 786440 | tf_op jit(solution)/shard_map/gather_rows/ppermute | solution.py:25
  14.5 9.4 %collective-permute-start.4 = (bf16[128,1024]{1,0:T(8,128)(2,1)S(1)}, bf16[128,1024]{1,0:T(8,128)(2,1)S(1)}, u32[]{:S(2)}, u32[]{:S(2)}) collective-permute-start(bf16[128,1024]{1,0:T(8,128)(2,1)S(1)} %collective-permute-done.3), channel_id=1, source_target_pairs={{0,96},{32,0},{64,32},{96,64},{1,97},{33,1},{65,33},{97,65},{2,98}... | collective-permute-start | bytes 786440 | tf_op jit(solution)/shard_map/gather_rows/ppermute | solution.py:25
  18.5 11.5 %copy-start.5 = (bf16[1024,1024]{1,0:T(8,128)(2,1)S(1)}, bf16[1024,1024]{1,0:T(8,128)(2,1)}, u32[]{:S(2)}) copy-start(bf16[1024,1024]{1,0:T(8,128)(2,1)} %own_ref.1) | copy-start | bytes 6291460
  20.7 5.9 %collective-permute-start.6 = (bf16[48,1024]{1,0:T(8,128)(2,1)S(1)}, bf16[48,1024]{1,0:T(8,128)(2,1)S(1)}, u32[]{:S(2)}, u32[]{:S(2)}) collective-permute-start(bf16[48,1024]{1,0:T(8,128)(2,1)S(1)} %slice.233), channel_id=1, source_target_pairs={{0,32},{32,64},{64,96},{96,0},{1,33},{33,65},{65,97},{97,1},{2,34}... | collective-permute-start | bytes 294920 | tf_op jit(solution)/shard_map/gather_rows/ppermute | solution.py:25
  22.3 4.4 %collective-permute-start.8 = (bf16[32,1024]{1,0:T(8,128)(2,1)S(1)}, bf16[32,1024]{1,0:T(8,128)(2,1)S(1)}, u32[]{:S(2)}, u32[]{:S(2)}) collective-permute-start(bf16[32,1024]{1,0:T(8,128)(2,1)S(1)} %slice.235), channel_id=1, source_target_pairs={{0,128},{128,0},{1,129},{129,1},{2,130},{130,2},{3,131},{131,3},{4... | collective-permute-start | bytes 196616 | tf_op jit(solution)/shard_map/gather_rows/ppermute | solution.py:25
  24.0 4.7 %collective-permute-start.7 = (bf16[48,1024]{1,0:T(8,128)(2,1)S(1)}, bf16[48,1024]{1,0:T(8,128)(2,1)S(1)}, u32[]{:S(2)}, u32[]{:S(2)}) collective-permute-start(bf16[48,1024]{1,0:T(8,128)(2,1)S(1)} %slice.234), channel_id=1, source_target_pairs={{0,96},{32,0},{64,32},{96,64},{1,97},{33,1},{65,33},{97,65},{2,98}... | collective-permute-start | bytes 294920 | tf_op jit(solution)/shard_map/gather_rows/ppermute | solution.py:25
  28.7 1.3 %copy-start.2 = (bf16[8,128,1024]{2,1,0:T(8,128)(2,1)}, bf16[8,128,1024]{2,1,0:T(8,128)(2,1)S(1)}, u32[]{:S(2)}) copy-start(bf16[8,128,1024]{2,1,0:T(8,128)(2,1)S(1)} %bitcast_dynamic-update-slice_fusion.blocks_ref) | copy-start | bytes 6291460
  30.0 1.6 %copy-start.3 = (bf16[8,128,1024]{2,1,0:T(8,128)(2,1)S(1)}, bf16[8,128,1024]{2,1,0:T(8,128)(2,1)}, u32[]{:S(2)}) copy-start(bf16[8,128,1024]{2,1,0:T(8,128)(2,1)} %copy-done.2) | copy-start | bytes 6291460
  31.6 6.7 %copy-start.6 = (f32[1024]{0:T(1024)S(1)}, f32[1024]{0:T(1024)}, u32[]{:S(2)}) copy-start(f32[1024]{0:T(1024)} %param.11) | copy-start | bytes 12292
  33.9 1.4 %copy-start = (bf16[1024,1024]{1,0:T(8,128)(2,1)}, bf16[1024,1024]{1,0:T(8,128)(2,1)S(1)}, u32[]{:S(2)}) copy-start(bf16[1024,1024]{1,0:T(8,128)(2,1)S(1)} %get-tuple-element.8) | copy-start | bytes 6291460
  35.2 12.1 %collective-permute-start.10 = (bf16[64,1024]{1,0:T(8,128)(2,1)S(1)}, bf16[64,1024]{1,0:T(8,128)(2,1)S(1)}, u32[]{:S(2)}, u32[]{:S(2)}) collective-permute-start(bf16[64,1024]{1,0:T(8,128)(2,1)S(1)} %get-tuple-element.9), channel_id=1, source_target_pairs={{0,2},{2,4},{4,6},{6,8},{8,10},{10,12},{12,14},{14,0},{1,3},{3,5},... | collective-permute-start | bytes 393224 | tf_op jit(solution)/shard_map/sum_layers/ppermute | solution.py:25
  39.0 53.4 %all-to-all-start.1 = ((f32[16,1,1024]{2,1,0:T(1,128)}), f32[16,1,1024]{2,1,0:T(1,128)S(1)}, u32[]{:S(2)}, u32[]{:S(2)}) async-start(f32[16,1,1024]{2,1,0:T(1,128)} %broadcast_in_dim.21), calls=%async_computation.1 | async-start | bytes 131072 | tf_op jit(solution)/shard_map/gather_values/all_to_all | solution.py:208
  44.0 9.1 %copy-start.1 = (bf16[1024,1024]{1,0:T(8,128)(2,1)S(1)}, bf16[1024,1024]{1,0:T(8,128)(2,1)}, u32[]{:S(2)}) copy-start(bf16[1024,1024]{1,0:T(8,128)(2,1)} %copy-done) | copy-start | bytes 6291460
  44.0 9.1 %collective-permute-start.14 = (bf16[64,1024]{1,0:T(8,128)(2,1)S(1)}, bf16[64,1024]{1,0:T(8,128)(2,1)S(1)}, u32[]{:S(2)}, u32[]{:S(2)}) collective-permute-start(bf16[64,1024]{1,0:T(8,128)(2,1)S(1)} %get-tuple-element.10), channel_id=1, source_target_pairs={{0,14},{2,0},{4,2},{6,4},{8,6},{10,8},{12,10},{14,12},{1,15},{3,1}... | collective-permute-start | bytes 393224 | tf_op jit(solution)/shard_map/sum_layers/ppermute | solution.py:25
  44.1 10.5 %collective-permute-start.18 = (bf16[64,1024]{1,0:T(8,128)(2,1)S(1)}, bf16[64,1024]{1,0:T(8,128)(2,1)S(1)}, u32[]{:S(2)}, u32[]{:S(2)}) collective-permute-start(bf16[64,1024]{1,0:T(8,128)(2,1)S(1)} %get-tuple-element.12), channel_id=1, source_target_pairs={{0,2},{2,4},{4,6},{6,8},{8,10},{10,12},{12,14},{14,0},{1,3},{3,5},... | collective-permute-start | bytes 393224 | tf_op jit(solution)/shard_map/sum_layers/ppermute | solution.py:25
  47.3 11.0 %collective-permute-start.22 = (bf16[64,1024]{1,0:T(8,128)(2,1)S(1)}, bf16[64,1024]{1,0:T(8,128)(2,1)S(1)}, u32[]{:S(2)}, u32[]{:S(2)}) collective-permute-start(bf16[64,1024]{1,0:T(8,128)(2,1)S(1)} %get-tuple-element.13), channel_id=1, source_target_pairs={{0,14},{2,0},{4,2},{6,4},{8,6},{10,8},{12,10},{14,12},{1,15},{3,1}... | collective-permute-start | bytes 393224 | tf_op jit(solution)/shard_map/sum_layers/ppermute | solution.py:25
  47.3 7.3 %copy-start.4 = (bf16[8,128,1024]{2,1,0:T(8,128)(2,1)S(1)}, bf16[8,128,1024]{2,1,0:T(8,128)(2,1)}, u32[]{:S(2)}) copy-start(bf16[8,128,1024]{2,1,0:T(8,128)(2,1)} %copy-done.2) | copy-start | bytes 6291460
  49.6 9.4 %collective-permute-start.11 = (bf16[128,1024]{1,0:T(8,128)(2,1)S(1)}, bf16[128,1024]{1,0:T(8,128)(2,1)S(1)}, u32[]{:S(2)}, u32[]{:S(2)}) collective-permute-start(bf16[128,1024]{1,0:T(8,128)(2,1)S(1)} %fusion.6), channel_id=1, source_target_pairs={{0,2},{2,4},{4,6},{6,8},{8,10},{10,12},{12,14},{14,0},{1,3},{3,5},... | collective-permute-start | bytes 786440 | tf_op jit(solution)/shard_map/sum_layers/ppermute | solution.py:25
  54.5 10.3 %collective-permute-start.15 = (bf16[128,1024]{1,0:T(8,128)(2,1)S(1)}, bf16[128,1024]{1,0:T(8,128)(2,1)S(1)}, u32[]{:S(2)}, u32[]{:S(2)}) collective-permute-start(bf16[128,1024]{1,0:T(8,128)(2,1)S(1)} %fusion.9), channel_id=1, source_target_pairs={{0,14},{2,0},{4,2},{6,4},{8,6},{10,8},{12,10},{14,12},{1,15},{3,1}... | collective-permute-start | bytes 786440 | tf_op jit(solution)/shard_map/sum_layers/ppermute | solution.py:25
  55.1 10.3 %collective-permute-start.19 = (bf16[128,1024]{1,0:T(8,128)(2,1)S(1)}, bf16[128,1024]{1,0:T(8,128)(2,1)S(1)}, u32[]{:S(2)}, u32[]{:S(2)}) collective-permute-start(bf16[128,1024]{1,0:T(8,128)(2,1)S(1)} %fusion.12), channel_id=1, source_target_pairs={{0,2},{2,4},{4,6},{6,8},{8,10},{10,12},{12,14},{14,0},{1,3},{3,5},... | collective-permute-start | bytes 786440 | tf_op jit(solution)/shard_map/sum_layers/ppermute | solution.py:25
  58.8 11.6 %collective-permute-start.23 = (bf16[128,1024]{1,0:T(8,128)(2,1)S(1)}, bf16[128,1024]{1,0:T(8,128)(2,1)S(1)}, u32[]{:S(2)}, u32[]{:S(2)}) collective-permute-start(bf16[128,1024]{1,0:T(8,128)(2,1)S(1)} %fusion.15), channel_id=1, source_target_pairs={{0,14},{2,0},{4,2},{6,4},{8,6},{10,8},{12,10},{14,12},{1,15},{3,1}... | collective-permute-start | bytes 786440 | tf_op jit(solution)/shard_map/sum_layers/ppermute | solution.py:25
  59.4 11.6 %collective-permute-start.12 = (bf16[128,1024]{1,0:T(8,128)(2,1)S(1)}, bf16[128,1024]{1,0:T(8,128)(2,1)S(1)}, u32[]{:S(2)}, u32[]{:S(2)}) collective-permute-start(bf16[128,1024]{1,0:T(8,128)(2,1)S(1)} %fusion.5), channel_id=1, source_target_pairs={{0,2},{2,4},{4,6},{6,8},{8,10},{10,12},{12,14},{14,0},{1,3},{3,5},... | collective-permute-start | bytes 786440 | tf_op jit(solution)/shard_map/sum_layers/ppermute | solution.py:25
  65.3 10.8 %collective-permute-start.16 = (bf16[128,1024]{1,0:T(8,128)(2,1)S(1)}, bf16[128,1024]{1,0:T(8,128)(2,1)S(1)}, u32[]{:S(2)}, u32[]{:S(2)}) collective-permute-start(bf16[128,1024]{1,0:T(8,128)(2,1)S(1)} %fusion.8), channel_id=1, source_target_pairs={{0,14},{2,0},{4,2},{6,4},{8,6},{10,8},{12,10},{14,12},{1,15},{3,1}... | collective-permute-start | bytes 786440 | tf_op jit(solution)/shard_map/sum_layers/ppermute | solution.py:25
  65.8 10.8 %collective-permute-start.20 = (bf16[128,1024]{1,0:T(8,128)(2,1)S(1)}, bf16[128,1024]{1,0:T(8,128)(2,1)S(1)}, u32[]{:S(2)}, u32[]{:S(2)}) collective-permute-start(bf16[128,1024]{1,0:T(8,128)(2,1)S(1)} %fusion.11), channel_id=1, source_target_pairs={{0,2},{2,4},{4,6},{6,8},{8,10},{10,12},{12,14},{14,0},{1,3},{3,5},... | collective-permute-start | bytes 786440 | tf_op jit(solution)/shard_map/sum_layers/ppermute | solution.py:25
  70.9 10.8 %collective-permute-start.24 = (bf16[128,1024]{1,0:T(8,128)(2,1)S(1)}, bf16[128,1024]{1,0:T(8,128)(2,1)S(1)}, u32[]{:S(2)}, u32[]{:S(2)}) collective-permute-start(bf16[128,1024]{1,0:T(8,128)(2,1)S(1)} %fusion.14), channel_id=1, source_target_pairs={{0,14},{2,0},{4,2},{6,4},{8,6},{10,8},{12,10},{14,12},{1,15},{3,1}... | collective-permute-start | bytes 786440 | tf_op jit(solution)/shard_map/sum_layers/ppermute | solution.py:25
  71.4 11.0 %collective-permute-start.13 = (bf16[128,1024]{1,0:T(8,128)(2,1)S(1)}, bf16[128,1024]{1,0:T(8,128)(2,1)S(1)}, u32[]{:S(2)}, u32[]{:S(2)}) collective-permute-start(bf16[128,1024]{1,0:T(8,128)(2,1)S(1)} %fusion.4), channel_id=1, source_target_pairs={{0,2},{2,4},{4,6},{6,8},{8,10},{10,12},{12,14},{14,0},{1,3},{3,5},... | collective-permute-start | bytes 786440 | tf_op jit(solution)/shard_map/sum_layers/ppermute | solution.py:25
  76.5 10.8 %collective-permute-start.17 = (bf16[128,1024]{1,0:T(8,128)(2,1)S(1)}, bf16[128,1024]{1,0:T(8,128)(2,1)S(1)}, u32[]{:S(2)}, u32[]{:S(2)}) collective-permute-start(bf16[128,1024]{1,0:T(8,128)(2,1)S(1)} %fusion.7), channel_id=1, source_target_pairs={{0,14},{2,0},{4,2},{6,4},{8,6},{10,8},{12,10},{14,12},{1,15},{3,1}... | collective-permute-start | bytes 786440 | tf_op jit(solution)/shard_map/sum_layers/ppermute | solution.py:25
  77.1 10.7 %collective-permute-start.21 = (bf16[128,1024]{1,0:T(8,128)(2,1)S(1)}, bf16[128,1024]{1,0:T(8,128)(2,1)S(1)}, u32[]{:S(2)}, u32[]{:S(2)}) collective-permute-start(bf16[128,1024]{1,0:T(8,128)(2,1)S(1)} %fusion.10), channel_id=1, source_target_pairs={{0,2},{2,4},{4,6},{6,8},{8,10},{10,12},{12,14},{14,0},{1,3},{3,5},... | collective-permute-start | bytes 786440 | tf_op jit(solution)/shard_map/sum_layers/ppermute | solution.py:25
  82.1 9.0 %collective-permute-start.25 = (bf16[128,1024]{1,0:T(8,128)(2,1)S(1)}, bf16[128,1024]{1,0:T(8,128)(2,1)S(1)}, u32[]{:S(2)}, u32[]{:S(2)}) collective-permute-start(bf16[128,1024]{1,0:T(8,128)(2,1)S(1)} %fusion.13), channel_id=1, source_target_pairs={{0,14},{2,0},{4,2},{6,4},{8,6},{10,8},{12,10},{14,12},{1,15},{3,1}... | collective-permute-start | bytes 786440 | tf_op jit(solution)/shard_map/sum_layers/ppermute | solution.py:25
  87.8 11.8 %copy-start.7 = (s32[1024]{0:T(1024)S(1)}, s32[1024]{0:T(1024)}, u32[]{:S(2)}) copy-start(s32[1024]{0:T(1024)} %param.12) | copy-start | bytes 12292
  91.6 37.2 %copy-start.8 = (s32[64]{0:T(128)S(1)}, s32[64]{0:T(128)}, u32[]{:S(2)}) copy-start(s32[64]{0:T(128)} %param.13) | copy-start | bytes 772
  92.4 17.2 %all-to-all-start = ((bf16[16,8,2048]{2,1,0:T(8,128)(2,1)}), bf16[16,8,2048]{2,1,0:T(8,128)(2,1)S(1)}, u32[]{:S(2)}, u32[]{:S(2)}) async-start(bf16[16,8,2048]{2,1,0:T(8,128)(2,1)} %maximum_bitcast_fusion), calls=%async_computation | async-start | bytes 1048576 | tf_op jit(solution)/shard_map/to_components/all_to_all | solution.py:266
  111.8 11.2 %all-to-all-start.2 = ((f32[32,1,256]{2,1,0:T(1,128)}), f32[32,1,256]{2,1,0:T(1,128)S(1)}, u32[]{:S(2)}, u32[]{:S(2)}) async-start(f32[32,1,256]{2,1,0:T(1,128)} %fit.1), calls=%async_computation.2 | async-start | bytes 65536 | tf_op jit(solution)/shard_map/gather_scores/all_to_all | solution.py:271
  123.0 5.5 %collective-permute-start.26 = (f32[256]{0:T(256)S(1)}, f32[256]{0:T(256)S(1)}, u32[]{:S(2)}, u32[]{:S(2)}) collective-permute-start(f32[256]{0:T(256)S(1)} %reduce_sum.9), channel_id=1, source_target_pairs={{0,2},{2,4},{4,6},{6,8},{8,10},{10,12},{12,14},{3,1},{5,3},{7,5},{... | collective-permute-start | bytes 3080 | tf_op jit(solution)/shard_map/gather_scores/ppermute | solution.py:274

commit v7 on v6

--- a/solution.py
+++ b/solution.py
@@ -49,7 +49,7 @@
     )(responses, weights, phenotype[None, :])
 
 
-def open_kernel(place_ref, blocks_ref, own_ref, other_ref, *refs):
+def open_kernel(place_ref, blocks_ref, own_ref, other_ref, done_ref, *refs):
     outs, nears, (block_ref, block_sem, near_sems) = refs[:4], refs[4:6], refs[6:]
     fetch = pltpu.make_async_copy(blocks_ref.at[place_ref[0]], block_ref, block_sem)
     copies = [
@@ -68,7 +68,7 @@
         outs[2 * q + 1][...] = total[cut:].astype(jnp.bfloat16)
 
 
-def open_sums(place, blocks, own, other):
+def open_sums(place, blocks, own, other, done):
     _, rows, width = blocks.shape
     columns = own.shape[1]
     anywhere = pl.BlockSpec(memory_space=pl.ANY)
@@ -77,7 +77,7 @@
         open_kernel,
         out_shape=[jax.ShapeDtypeStruct((rows // 2, columns), jnp.bfloat16)] * 4
         + [pltpu.VMEM(own.shape, own.dtype)] * 2,
-        in_specs=[pl.BlockSpec(memory_space=pltpu.SMEM), anywhere, anywhere, anywhere],
+        in_specs=[pl.BlockSpec(memory_space=pltpu.SMEM), anywhere, anywhere, anywhere, anywhere],
         out_specs=[vmem] * 6,
         scratch_shapes=[
             pltpu.VMEM((rows, width), jnp.bfloat16),
@@ -85,7 +85,7 @@
             pltpu.SemaphoreType.DMA((2,)),
         ],
         compiler_params=pltpu.CompilerParams(vmem_limit_bytes=24 * 1024 * 1024),
-    )(place, blocks, own, other)
+    )(place, blocks, pltpu.with_memory_space_constraint(own, pltpu.HBM), other, done)
 
 
 def fit_kernel(slot_ref, sums_ref, values_ref, out_ref, r_ref, d_ref, w_ref):
@@ -220,7 +220,8 @@
     with jax.named_scope("swap_eigvecs"):
         other = shifted(eigvecs, "samp_2", 1)
     with jax.named_scope("gather_values"):
-        everywhere = copies(eigvals, SAMP).reshape(-1, 2, eigvals.shape[0])
+        raw = copies(eigvals, SAMP)
+        everywhere = raw.reshape(-1, 2, eigvals.shape[0])
         everywhere = jnp.where(lax.axis_index("samp_2") == 0, everywhere, everywhere[:, ::-1])
         everywhere = jnp.repeat(everywhere.reshape(everywhere.shape[0], -1), 4, axis=0)
     rows = own.shape[0]
@@ -253,7 +254,9 @@
         return total.astype(jnp.bfloat16)
 
     with jax.named_scope("sum_layers"):
-        *halves, near_own, near_other = open_sums(place(far)[None], blocks, eigvecs, other)
+        *halves, near_own, near_other = open_sums(
+            place(far)[None], blocks, eigvecs, other, raw
+        )
         vecs = (near_own, near_other)
         for q in (0, 1):
             for at, way in enumerate((1, -1)):

time: 130 us -> 125 us (0.962)
  waiting for transfers between devices: 41.4 us -> 36.9 us
    ppermute x26, waiting for transfers between devices: 22 us -> 17.3 us  [shifted(): lax.ppermute(value, axis, [(i, (i + by) % peers) for i in range(peers)])]
    unnamed x25 -> x22, local copies, waits for them, and re-layouts: 6.48 us -> 6.34 us
  transfers between devices with their start and end apart: 30 -> 30, of which waited for: 14 -> 15; matrix products, arithmetic and copies ran while one was open for 11% -> 11% of each run, Pallas kernels for 1% -> 1%
where the time goes in v7:
time: 125 us
  starting transfers between devices  59.9 us (48%)
  waiting for transfers between devices  36.9 us (30%)
  local copies, waits for them, and re-layouts  9.09 us (7%)
  matrix products  9.05 us (7%)
  Pallas kernels  6.73 us (5%)
  other arithmetic  1.82 us (1%)
    ppermute x26, starting transfers between devices, shifted(): lax.ppermute(value, axis, [(i, (i + by) % peers) for i in range(peers)])  43.7 us
    ppermute x26, waiting for transfers between devices, shifted(): lax.ppermute(value, axis, [(i, (i + by) % peers) for i in range(peers)])  17.3 us
    all_to_all x1, waiting for transfers between devices, shards(): sums = lax.all_to_all(whole, PLANE, 0, 0, tiled=True)  9.26 us
    dot_general x14, matrix products, term(): return jnp.dot(block, vecs[q], preferred_element_type=jnp.float32)  9.05 us
    all_to_all x1, waiting for transfers between devices, shards(): lax.all_to_all(fitted, LAYER, 0, 0, tiled=True)  7.32 us
    all_to_all x1, starting transfers between devices, shards(): sums = lax.all_to_all(whole, PLANE, 0, 0, tiled=True)  6.94 us
    unnamed x22, local copies, waits for them, and re-layouts  6.34 us
    all_to_all x1, starting transfers between devices, shards(): lax.all_to_all(fitted, LAYER, 0, 0, tiled=True)  3.83 us
  transfers between devices with their start and end apart: 30, of which 15 were waited for; matrix products, arithmetic and copies ran while one was open for 11% of the time, Pallas kernels for 1%

profile of v7, /device:TPU:96, one launch (start us, length us, event | category | flops | bytes accessed | tf_op | source)
XLA Modules:
  0.0 124.6 jit_solution(8930537798390240045)
XLA Ops:
  0.7 1.8 %weigh.1 = bf16[128,1024]{1,0:T(8,128)(2,1)} custom-call(bf16[64,1024]{1,0:T(8,128)(2,1)} %resp_ref.1, bf16[64,1024]{1,0:T(8,128)(2,1)} %weight_ref.1, f32[1,1024]{1,0:T(1,128)} %bitcast.82), custom_call_target="tpu_custom_call" | custom-call | tf_op jit(solution)/shard_map/weigh/pallas_call | solution.py:46
  2.5 1.5 %collective-permute-start.1 = (bf16[128,1024]{1,0:T(8,128)(2,1)}, bf16[128,1024]{1,0:T(8,128)(2,1)S(1)}, u32[]{:S(2)}, u32[]{:S(2)}) collective-permute-start(bf16[128,1024]{1,0:T(8,128)(2,1)} %weigh.1), channel_id=1, source_target_pairs={{0,32},{32,64},{64,96},{96,0},{1,33},{33,65},{65,97},{97,1},{2,34}... | collective-permute-start | bytes 786440 | tf_op jit(solution)/shard_map/gather_rows/ppermute | solution.py:25
  4.0 1.6 %collective-permute-start.3 = (bf16[128,1024]{1,0:T(8,128)(2,1)}, bf16[128,1024]{1,0:T(8,128)(2,1)S(1)}, u32[]{:S(2)}, u32[]{:S(2)}) collective-permute-start(bf16[128,1024]{1,0:T(8,128)(2,1)} %weigh.1), channel_id=1, source_target_pairs={{0,128},{128,0},{1,129},{129,1},{2,130},{130,2},{3,131},{131,3},{4... | collective-permute-start | bytes 786440 | tf_op jit(solution)/shard_map/gather_rows/ppermute | solution.py:25
  5.6 1.7 %collective-permute-start = (bf16[128,1024]{1,0:T(8,128)(2,1)}, bf16[128,1024]{1,0:T(8,128)(2,1)}, u32[]{:S(2)}, u32[]{:S(2)}) collective-permute-start(bf16[128,1024]{1,0:T(8,128)(2,1)} %weigh.1), channel_id=1, source_target_pairs={{0,96},{32,0},{64,32},{96,64},{1,97},{33,1},{65,33},{97,65},{2,98}... | collective-permute-start | bytes 786440 | tf_op jit(solution)/shard_map/gather_rows/ppermute | solution.py:25
  7.4 1.3 %broadcast_in_dim.21 = f32[16,1,1024]{2,1,0:T(1,128)} broadcast(f32[1024]{0:T(1024)} %param.11), dimensions={2} | broadcast | bytes 69632 | tf_op jit(solution)/shard_map/gather_values/broadcast_in_dim | solution.py:209
  8.7 3.5 %all-to-all-start = ((f32[16,1,1024]{2,1,0:T(1,128)}), f32[16,1,1024]{2,1,0:T(1,128)S(1)}, u32[]{:S(2)}, u32[]{:S(2)}) async-start(f32[16,1,1024]{2,1,0:T(1,128)} %broadcast_in_dim.21), calls=%async_computation | async-start | bytes 131072 | tf_op jit(solution)/shard_map/gather_values/all_to_all | solution.py:208
  12.2 0.5 collective-permute-done.1
  12.7 1.4 %collective-permute-start.2 = (bf16[128,1024]{1,0:T(8,128)(2,1)S(1)}, bf16[128,1024]{1,0:T(8,128)(2,1)S(1)}, u32[]{:S(2)}, u32[]{:S(2)}) collective-permute-start(bf16[128,1024]{1,0:T(8,128)(2,1)S(1)} %collective-permute-done.1), channel_id=1, source_target_pairs={{0,32},{32,64},{64,96},{96,0},{1,33},{33,65},{65,97},{97,1},{2,34}... | collective-permute-start | bytes 786440 | tf_op jit(solution)/shard_map/gather_rows/ppermute | solution.py:25
  14.1 1.5 %collective-permute-start.5 = (bf16[128,1024]{1,0:T(8,128)(2,1)S(1)}, bf16[128,1024]{1,0:T(8,128)(2,1)S(1)}, u32[]{:S(2)}, u32[]{:S(2)}) collective-permute-start(bf16[128,1024]{1,0:T(8,128)(2,1)S(1)} %collective-permute-done.1), channel_id=1, source_target_pairs={{0,128},{128,0},{1,129},{129,1},{2,130},{130,2},{3,131},{131,3},{4... | collective-permute-start | bytes 786440 | tf_op jit(solution)/shard_map/gather_rows/ppermute | solution.py:25
  15.6 1.9 %collective-permute-start.4 = (bf16[128,1024]{1,0:T(8,128)(2,1)S(1)}, bf16[128,1024]{1,0:T(8,128)(2,1)S(1)}, u32[]{:S(2)}, u32[]{:S(2)}) collective-permute-start(bf16[128,1024]{1,0:T(8,128)(2,1)S(1)} %collective-permute-done.3), channel_id=1, source_target_pairs={{0,96},{32,0},{64,32},{96,64},{1,97},{33,1},{65,33},{97,65},{2,98}... | collective-permute-start | bytes 786440 | tf_op jit(solution)/shard_map/gather_rows/ppermute | solution.py:25
  17.5 1.0 bitcast_dynamic-update-slice_fusion.6
  18.5 1.0 bitcast_dynamic-update-slice_fusion.5
  19.5 3.1 %collective-permute-done.5 = bf16[128,1024]{1,0:T(8,128)(2,1)S(1)} collective-permute-done((bf16[128,1024]{1,0:T(8,128)(2,1)S(1)}, bf16[128,1024]{1,0:T(8,128)(2,1)S(1)}, u32[]{:S(2)}, u32[]{:S(2)}) %collective-permute-start.5) | collective-permute-done | bytes 262176 | tf_op jit(solution)/shard_map/gather_rows/ppermute | solution.py:25
  22.6 1.4 %collective-permute-start.6 = (bf16[48,1024]{1,0:T(8,128)(2,1)S(1)}, bf16[48,1024]{1,0:T(8,128)(2,1)S(1)}, u32[]{:S(2)}, u32[]{:S(2)}) collective-permute-start(bf16[48,1024]{1,0:T(8,128)(2,1)S(1)} %slice.233), channel_id=1, source_target_pairs={{0,32},{32,64},{64,96},{96,0},{1,33},{33,65},{65,97},{97,1},{2,34}... | collective-permute-start | bytes 294920 | tf_op jit(solution)/shard_map/gather_rows/ppermute | solution.py:25
  24.0 1.3 %collective-permute-start.8 = (bf16[32,1024]{1,0:T(8,128)(2,1)S(1)}, bf16[32,1024]{1,0:T(8,128)(2,1)S(1)}, u32[]{:S(2)}, u32[]{:S(2)}) collective-permute-start(bf16[32,1024]{1,0:T(8,128)(2,1)S(1)} %slice.235), channel_id=1, source_target_pairs={{0,128},{128,0},{1,129},{129,1},{2,130},{130,2},{3,131},{131,3},{4... | collective-permute-start | bytes 196616 | tf_op jit(solution)/shard_map/gather_rows/ppermute | solution.py:25
  25.4 2.1 %collective-permute-start.7 = (bf16[48,1024]{1,0:T(8,128)(2,1)S(1)}, bf16[48,1024]{1,0:T(8,128)(2,1)S(1)}, u32[]{:S(2)}, u32[]{:S(2)}) collective-permute-start(bf16[48,1024]{1,0:T(8,128)(2,1)S(1)} %slice.234), channel_id=1, source_target_pairs={{0,96},{32,0},{64,32},{96,64},{1,97},{33,1},{65,33},{97,65},{2,98}... | collective-permute-start | bytes 294920 | tf_op jit(solution)/shard_map/gather_rows/ppermute | solution.py:25
  27.6 0.8 collective-permute-done.8
  28.4 0.2 collective-permute-done.6
  28.5 1.5 %collective-permute-done.7 = bf16[48,1024]{1,0:T(8,128)(2,1)S(1)} collective-permute-done((bf16[48,1024]{1,0:T(8,128)(2,1)S(1)}, bf16[48,1024]{1,0:T(8,128)(2,1)S(1)}, u32[]{:S(2)}, u32[]{:S(2)}) %collective-permute-start.7) | collective-permute-done | bytes 98336 | tf_op jit(solution)/shard_map/gather_rows/ppermute | solution.py:25
  30.1 1.3 %copy-done.2 = bf16[8,128,1024]{2,1,0:T(8,128)(2,1)} copy-done((bf16[8,128,1024]{2,1,0:T(8,128)(2,1)}, bf16[8,128,1024]{2,1,0:T(8,128)(2,1)S(1)}, u32[]{:S(2)}) %copy-start.2) | copy-done | bytes 2097176
  31.5 1.6 %copy-done.3 = bf16[8,128,1024]{2,1,0:T(8,128)(2,1)S(1)} copy-done((bf16[8,128,1024]{2,1,0:T(8,128)(2,1)S(1)}, bf16[8,128,1024]{2,1,0:T(8,128)(2,1)}, u32[]{:S(2)}) %copy-start.3) | copy-done | bytes 2097176
  33.0 2.7 %sum_layers.1 = (bf16[64,1024]{1,0:T(8,128)(2,1)S(1)}, bf16[64,1024]{1,0:T(8,128)(2,1)S(1)}, bf16[64,1024]{1,0:T(8,128)(2,1)S(1)}, bf16[64,1024]{1,0:T(8,128)(2,...) custom-call(s32[1]{0:T(128)} %bitcast.11.place_ref, bf16[8,128,1024]{2,1,0:T(8,128)(2,1)S(1)} %copy-done.3, ...), custom_call_target="tpu_custom_call" | custom-call | tf_op jit(solution)/shard_map/sum_layers/pallas_call | solution.py:76
  35.8 1.3 %copy-done = bf16[1024,1024]{1,0:T(8,128)(2,1)} copy-done((bf16[1024,1024]{1,0:T(8,128)(2,1)}, bf16[1024,1024]{1,0:T(8,128)(2,1)S(1)}, u32[]{:S(2)}) %copy-start) | copy-done | bytes 2097176
  37.1 3.1 %collective-permute-start.10 = (bf16[64,1024]{1,0:T(8,128)(2,1)S(1)}, bf16[64,1024]{1,0:T(8,128)(2,1)S(1)}, u32[]{:S(2)}, u32[]{:S(2)}) collective-permute-start(bf16[64,1024]{1,0:T(8,128)(2,1)S(1)} %get-tuple-element.9), channel_id=1, source_target_pairs={{0,2},{2,4},{4,6},{6,8},{8,10},{10,12},{12,14},{14,0},{1,3},{3,5},... | collective-permute-start | bytes 393224 | tf_op jit(solution)/shard_map/sum_layers/ppermute | solution.py:25
  40.3 3.2 %collective-permute-start.18 = (bf16[64,1024]{1,0:T(8,128)(2,1)S(1)}, bf16[64,1024]{1,0:T(8,128)(2,1)S(1)}, u32[]{:S(2)}, u32[]{:S(2)}) collective-permute-start(bf16[64,1024]{1,0:T(8,128)(2,1)S(1)} %get-tuple-element.12), channel_id=1, source_target_pairs={{0,2},{2,4},{4,6},{6,8},{8,10},{10,12},{12,14},{14,0},{1,3},{3,5},... | collective-permute-start | bytes 393224 | tf_op jit(solution)/shard_map/sum_layers/ppermute | solution.py:25
  43.5 2.3 %fusion.6 = bf16[128,1024]{1,0:T(8,128)(2,1)S(1)} fusion(bf16[1024,1024]{1,0:T(8,128)(2,1)} %copy-done, bf16[64,1024]{1,0:T(8,128)(2,1)S(1)} %collective-permute-done.10, bf16[8,128,1024]{2,1,0:T(8,128)(2,1)} %copy-done.2, s32[]{:T(128)S(6)} %select_n.88), kind=kOutput, calls=%fused_computation.20 | convolution fusion | flops 268828672 | bytes 2752516 | tf_op jit(solution)/shard_map/sum_layers/dot_general | solution.py:236
  45.8 3.9 %collective-permute-start.11 = (bf16[128,1024]{1,0:T(8,128)(2,1)S(1)}, bf16[128,1024]{1,0:T(8,128)(2,1)S(1)}, u32[]{:S(2)}, u32[]{:S(2)}) collective-permute-start(bf16[128,1024]{1,0:T(8,128)(2,1)S(1)} %fusion.6), channel_id=1, source_target_pairs={{0,2},{2,4},{4,6},{6,8},{8,10},{10,12},{12,14},{14,0},{1,3},{3,5},... | collective-permute-start | bytes 786440 | tf_op jit(solution)/shard_map/sum_layers/ppermute | solution.py:25
  49.7 1.4 %fusion.9 = bf16[128,1024]{1,0:T(8,128)(2,1)S(1)} fusion(bf16[1024,1024]{1,0:T(8,128)(2,1)S(1)} %copy-done.1, bf16[64,1024]{1,0:T(8,128)(2,1)S(1)} %collective-permute-done.14, bf16[8,128,1024]{2,1,0:T(8,128)(2,1)} %copy-done.2, s32[]{:T(128)S(6)} %select_n.94), kind=kOutput, calls=%fused_computation.23 | convolution fusion | flops 268828672 | bytes 2752516 | tf_op jit(solution)/shard_map/sum_layers/dot_general | solution.py:236
  51.2 0.4 fusion.12
  51.6 3.3 %collective-permute-start.19 = (bf16[128,1024]{1,0:T(8,128)(2,1)S(1)}, bf16[128,1024]{1,0:T(8,128)(2,1)S(1)}, u32[]{:S(2)}, u32[]{:S(2)}) collective-permute-start(bf16[128,1024]{1,0:T(8,128)(2,1)S(1)} %fusion.12), channel_id=1, source_target_pairs={{0,2},{2,4},{4,6},{6,8},{8,10},{10,12},{12,14},{14,0},{1,3},{3,5},... | collective-permute-start | bytes 786440 | tf_op jit(solution)/shard_map/sum_layers/ppermute | solution.py:25
  54.9 0.4 fusion.15
  55.5 0.9 collective-permute-done.11
  56.4 0.4 fusion.5
  56.8 3.8 %collective-permute-start.12 = (bf16[128,1024]{1,0:T(8,128)(2,1)S(1)}, bf16[128,1024]{1,0:T(8,128)(2,1)S(1)}, u32[]{:S(2)}, u32[]{:S(2)}) collective-permute-start(bf16[128,1024]{1,0:T(8,128)(2,1)S(1)} %fusion.5), channel_id=1, source_target_pairs={{0,2},{2,4},{4,6},{6,8},{8,10},{10,12},{12,14},{14,0},{1,3},{3,5},... | collective-permute-start | bytes 786440 | tf_op jit(solution)/shard_map/sum_layers/ppermute | solution.py:25
  60.6 1.0 collective-permute-done.15
  61.6 0.4 fusion.8
  62.2 0.4 fusion.11
  62.6 3.6 %collective-permute-start.20 = (bf16[128,1024]{1,0:T(8,128)(2,1)S(1)}, bf16[128,1024]{1,0:T(8,128)(2,1)S(1)}, u32[]{:S(2)}, u32[]{:S(2)}) collective-permute-start(bf16[128,1024]{1,0:T(8,128)(2,1)S(1)} %fusion.11), channel_id=1, source_target_pairs={{0,2},{2,4},{4,6},{6,8},{8,10},{10,12},{12,14},{14,0},{1,3},{3,5},... | collective-permute-start | bytes 786440 | tf_op jit(solution)/shard_map/sum_layers/ppermute | solution.py:25
  66.2 0.8 collective-permute-done.23
  67.0 0.4 fusion.14
  67.6 0.4 fusion.4
  68.1 3.8 %collective-permute-start.13 = (bf16[128,1024]{1,0:T(8,128)(2,1)S(1)}, bf16[128,1024]{1,0:T(8,128)(2,1)S(1)}, u32[]{:S(2)}, u32[]{:S(2)}) collective-permute-start(bf16[128,1024]{1,0:T(8,128)(2,1)S(1)} %fusion.4), channel_id=1, source_target_pairs={{0,2},{2,4},{4,6},{6,8},{8,10},{10,12},{12,14},{14,0},{1,3},{3,5},... | collective-permute-start | bytes 786440 | tf_op jit(solution)/shard_map/sum_layers/ppermute | solution.py:25
  71.8 0.8 collective-permute-done.16
  72.7 0.4 fusion.7
  73.2 0.4 fusion.10
  73.7 3.8 %collective-permute-start.21 = (bf16[128,1024]{1,0:T(8,128)(2,1)S(1)}, bf16[128,1024]{1,0:T(8,128)(2,1)S(1)}, u32[]{:S(2)}, u32[]{:S(2)}) collective-permute-start(bf16[128,1024]{1,0:T(8,128)(2,1)S(1)} %fusion.10), channel_id=1, source_target_pairs={{0,2},{2,4},{4,6},{6,8},{8,10},{10,12},{12,14},{14,0},{1,3},{3,5},... | collective-permute-start | bytes 786440 | tf_op jit(solution)/shard_map/sum_layers/ppermute | solution.py:25
  77.5 0.6 collective-permute-done.24
  78.1 0.4 fusion.13
  78.5 0.3 collective-permute-start.25
  78.8 3.8 %collective-permute-done.17 = bf16[128,1024]{1,0:T(8,128)(2,1)S(1)} collective-permute-done((bf16[128,1024]{1,0:T(8,128)(2,1)S(1)}, bf16[128,1024]{1,0:T(8,128)(2,1)S(1)}, u32[]{:S(2)}, u32[]{:S(2)}) %collective-permute-start.17) | collective-permute-done | bytes 262176 | tf_op jit(solution)/shard_map/sum_layers/ppermute | solution.py:25
  82.6 0.5 fusion.2
  83.1 3.3 %collective-permute-done.25 = bf16[128,1024]{1,0:T(8,128)(2,1)S(1)} collective-permute-done((bf16[128,1024]{1,0:T(8,128)(2,1)S(1)}, bf16[128,1024]{1,0:T(8,128)(2,1)S(1)}, u32[]{:S(2)}, u32[]{:S(2)}) %collective-permute-start.25) | collective-permute-done | bytes 262176 | tf_op jit(solution)/shard_map/sum_layers/ppermute | solution.py:25
  86.4 0.5 fusion.3
  86.9 0.8 maximum_bitcast_fusion
  87.7 6.9 %all-to-all-start.1 = ((bf16[16,8,2048]{2,1,0:T(8,128)(2,1)}), bf16[16,8,2048]{2,1,0:T(8,128)(2,1)S(1)}, u32[]{:S(2)}, u32[]{:S(2)}) async-start(bf16[16,8,2048]{2,1,0:T(8,128)(2,1)} %maximum_bitcast_fusion), calls=%async_computation.1 | async-start | bytes 1048576 | tf_op jit(solution)/shard_map/to_components/all_to_all | solution.py:269
  94.9 0.4 rev.3
  95.5 9.3 %all-to-all-done.1 = bf16[16,8,2048]{2,1,0:T(8,128)(2,1)S(1)} async-done(((bf16[16,8,2048]{2,1,0:T(8,128)(2,1)}), bf16[16,8,2048]{2,1,0:T(8,128)(2,1)S(1)}, u32[]{:S(2)}, u32[]{:S(2)}) %all-to-all-start.1) | async-done | bytes 524320 | tf_op jit(solution)/shard_map/to_components/all_to_all | solution.py:269
  104.8 2.2 %fit.1 = f32[32,1,256]{2,1,0:T(1,128)} custom-call(s32[1]{0:T(128)} %bitcast.slot_ref, bf16[128,2048]{1,0:T(8,128)(2,1)S(1)} %bitcast.79, f32[32,2048]{1,0:T(8,128)S(1)} %reshape.24.values_ref), custom_call_target="tpu_custom_call" | custom-call | tf_op jit(solution)/shard_map/fit/pallas_call | solution.py:158
  107.0 3.8 %all-to-all-start.2 = ((f32[32,1,256]{2,1,0:T(1,128)}), f32[32,1,256]{2,1,0:T(1,128)S(1)}, u32[]{:S(2)}, u32[]{:S(2)}) async-start(f32[32,1,256]{2,1,0:T(1,128)} %fit.1), calls=%async_computation.2 | async-start | bytes 65536 | tf_op jit(solution)/shard_map/gather_scores/all_to_all | solution.py:274
  110.9 7.3 %all-to-all-done.2 = f32[32,1,256]{2,1,0:T(1,128)S(1)} async-done(((f32[32,1,256]{2,1,0:T(1,128)}), f32[32,1,256]{2,1,0:T(1,128)S(1)}, u32[]{:S(2)}, u32[]{:S(2)}) %all-to-all-start.2) | async-done | bytes 32800 | tf_op jit(solution)/shard_map/gather_scores/all_to_all | solution.py:274
  118.3 1.9 %collective-permute-start.26 = (f32[256]{0:T(256)S(1)}, f32[256]{0:T(256)S(1)}, u32[]{:S(2)}, u32[]{:S(2)}) collective-permute-start(f32[256]{0:T(256)S(1)} %reduce_sum.9), channel_id=1, source_target_pairs={{0,2},{2,4},{4,6},{6,8},{8,10},{10,12},{12,14},{3,1},{5,3},{7,5},{... | collective-permute-start | bytes 3080 | tf_op jit(solution)/shard_map/gather_scores/ppermute | solution.py:277
  120.2 0.6 dynamic_slice.47
  120.8 2.9 %collective-permute-done.26 = f32[256]{0:T(256)S(1)} collective-permute-done((f32[256]{0:T(256)S(1)}, f32[256]{0:T(256)S(1)}, u32[]{:S(2)}, u32[]{:S(2)}) %collective-permute-start.26) | collective-permute-done | bytes 1056 | tf_op jit(solution)/shard_map/gather_scores/ppermute | solution.py:277
  124.0 0.6 add_divide_fusion
  (58 shorter events, 1.5 us)
Async XLA Ops:
  0.6 30.8 %collective-permute-start.9 = (bf16[1024,1024]{1,0:T(8,128)(2,1)}, bf16[1024,1024]{1,0:T(8,128)(2,1)}, u32[]{:S(2)}, u32[]{:S(2)}) collective-permute-start(bf16[1024,1024]{1,0:T(8,128)(2,1)} %own_ref.1), channel_id=1, source_target_pairs={{0,16},{16,0},{1,17},{17,1},{2,18},{18,2},{3,19},{19,3},{4,20},{20... | collective-permute-start | bytes 6291464 | tf_op jit(solution)/shard_map/swap_eigvecs/ppermute | solution.py:25
  2.5 10.1 %collective-permute-start.1 = (bf16[128,1024]{1,0:T(8,128)(2,1)}, bf16[128,1024]{1,0:T(8,128)(2,1)S(1)}, u32[]{:S(2)}, u32[]{:S(2)}) collective-permute-start(bf16[128,1024]{1,0:T(8,128)(2,1)} %weigh.1), channel_id=1, source_target_pairs={{0,32},{32,64},{64,96},{96,0},{1,33},{33,65},{65,97},{97,1},{2,34}... | collective-permute-start | bytes 786440 | tf_op jit(solution)/shard_map/gather_rows/ppermute | solution.py:25
  4.0 11.6 %collective-permute-start.3 = (bf16[128,1024]{1,0:T(8,128)(2,1)}, bf16[128,1024]{1,0:T(8,128)(2,1)S(1)}, u32[]{:S(2)}, u32[]{:S(2)}) collective-permute-start(bf16[128,1024]{1,0:T(8,128)(2,1)} %weigh.1), channel_id=1, source_target_pairs={{0,128},{128,0},{1,129},{129,1},{2,130},{130,2},{3,131},{131,3},{4... | collective-permute-start | bytes 786440 | tf_op jit(solution)/shard_map/gather_rows/ppermute | solution.py:25
  5.6 12.9 %collective-permute-start = (bf16[128,1024]{1,0:T(8,128)(2,1)}, bf16[128,1024]{1,0:T(8,128)(2,1)}, u32[]{:S(2)}, u32[]{:S(2)}) collective-permute-start(bf16[128,1024]{1,0:T(8,128)(2,1)} %weigh.1), channel_id=1, source_target_pairs={{0,96},{32,0},{64,32},{96,64},{1,97},{33,1},{65,33},{97,65},{2,98}... | collective-permute-start | bytes 786440 | tf_op jit(solution)/shard_map/gather_rows/ppermute | solution.py:25
  8.7 9.8 %all-to-all-start = ((f32[16,1,1024]{2,1,0:T(1,128)}), f32[16,1,1024]{2,1,0:T(1,128)S(1)}, u32[]{:S(2)}, u32[]{:S(2)}) async-start(f32[16,1,1024]{2,1,0:T(1,128)} %broadcast_in_dim.21), calls=%async_computation | async-start | bytes 131072 | tf_op jit(solution)/shard_map/gather_values/all_to_all | solution.py:208
  12.7 11.3 %collective-permute-start.2 = (bf16[128,1024]{1,0:T(8,128)(2,1)S(1)}, bf16[128,1024]{1,0:T(8,128)(2,1)S(1)}, u32[]{:S(2)}, u32[]{:S(2)}) collective-permute-start(bf16[128,1024]{1,0:T(8,128)(2,1)S(1)} %collective-permute-done.1), channel_id=1, source_target_pairs={{0,32},{32,64},{64,96},{96,0},{1,33},{33,65},{65,97},{97,1},{2,34}... | collective-permute-start | bytes 786440 | tf_op jit(solution)/shard_map/gather_rows/ppermute | solution.py:25
  14.1 8.5 %collective-permute-start.5 = (bf16[128,1024]{1,0:T(8,128)(2,1)S(1)}, bf16[128,1024]{1,0:T(8,128)(2,1)S(1)}, u32[]{:S(2)}, u32[]{:S(2)}) collective-permute-start(bf16[128,1024]{1,0:T(8,128)(2,1)S(1)} %collective-permute-done.1), channel_id=1, source_target_pairs={{0,128},{128,0},{1,129},{129,1},{2,130},{130,2},{3,131},{131,3},{4... | collective-permute-start | bytes 786440 | tf_op jit(solution)/shard_map/gather_rows/ppermute | solution.py:25
  15.6 9.7 %collective-permute-start.4 = (bf16[128,1024]{1,0:T(8,128)(2,1)S(1)}, bf16[128,1024]{1,0:T(8,128)(2,1)S(1)}, u32[]{:S(2)}, u32[]{:S(2)}) collective-permute-start(bf16[128,1024]{1,0:T(8,128)(2,1)S(1)} %collective-permute-done.3), channel_id=1, source_target_pairs={{0,96},{32,0},{64,32},{96,64},{1,97},{33,1},{65,33},{97,65},{2,98}... | collective-permute-start | bytes 786440 | tf_op jit(solution)/shard_map/gather_rows/ppermute | solution.py:25
  22.6 5.9 %collective-permute-start.6 = (bf16[48,1024]{1,0:T(8,128)(2,1)S(1)}, bf16[48,1024]{1,0:T(8,128)(2,1)S(1)}, u32[]{:S(2)}, u32[]{:S(2)}) collective-permute-start(bf16[48,1024]{1,0:T(8,128)(2,1)S(1)} %slice.233), channel_id=1, source_target_pairs={{0,32},{32,64},{64,96},{96,0},{1,33},{33,65},{65,97},{97,1},{2,34}... | collective-permute-start | bytes 294920 | tf_op jit(solution)/shard_map/gather_rows/ppermute | solution.py:25
  24.0 4.4 %collective-permute-start.8 = (bf16[32,1024]{1,0:T(8,128)(2,1)S(1)}, bf16[32,1024]{1,0:T(8,128)(2,1)S(1)}, u32[]{:S(2)}, u32[]{:S(2)}) collective-permute-start(bf16[32,1024]{1,0:T(8,128)(2,1)S(1)} %slice.235), channel_id=1, source_target_pairs={{0,128},{128,0},{1,129},{129,1},{2,130},{130,2},{3,131},{131,3},{4... | collective-permute-start | bytes 196616 | tf_op jit(solution)/shard_map/gather_rows/ppermute | solution.py:25
  25.4 4.7 %collective-permute-start.7 = (bf16[48,1024]{1,0:T(8,128)(2,1)S(1)}, bf16[48,1024]{1,0:T(8,128)(2,1)S(1)}, u32[]{:S(2)}, u32[]{:S(2)}) collective-permute-start(bf16[48,1024]{1,0:T(8,128)(2,1)S(1)} %slice.234), channel_id=1, source_target_pairs={{0,96},{32,0},{64,32},{96,64},{1,97},{33,1},{65,33},{97,65},{2,98}... | collective-permute-start | bytes 294920 | tf_op jit(solution)/shard_map/gather_rows/ppermute | solution.py:25
  30.1 1.3 %copy-start.2 = (bf16[8,128,1024]{2,1,0:T(8,128)(2,1)}, bf16[8,128,1024]{2,1,0:T(8,128)(2,1)S(1)}, u32[]{:S(2)}) copy-start(bf16[8,128,1024]{2,1,0:T(8,128)(2,1)S(1)} %bitcast_dynamic-update-slice_fusion.blocks_ref) | copy-start | bytes 6291460
  31.5 1.6 %copy-start.3 = (bf16[8,128,1024]{2,1,0:T(8,128)(2,1)S(1)}, bf16[8,128,1024]{2,1,0:T(8,128)(2,1)}, u32[]{:S(2)}) copy-start(bf16[8,128,1024]{2,1,0:T(8,128)(2,1)} %copy-done.2) | copy-start | bytes 6291460
  35.8 1.4 %copy-start = (bf16[1024,1024]{1,0:T(8,128)(2,1)}, bf16[1024,1024]{1,0:T(8,128)(2,1)S(1)}, u32[]{:S(2)}) copy-start(bf16[1024,1024]{1,0:T(8,128)(2,1)S(1)} %get-tuple-element.8) | copy-start | bytes 6291460
  37.1 6.4 %collective-permute-start.10 = (bf16[64,1024]{1,0:T(8,128)(2,1)S(1)}, bf16[64,1024]{1,0:T(8,128)(2,1)S(1)}, u32[]{:S(2)}, u32[]{:S(2)}) collective-permute-start(bf16[64,1024]{1,0:T(8,128)(2,1)S(1)} %get-tuple-element.9), channel_id=1, source_target_pairs={{0,2},{2,4},{4,6},{6,8},{8,10},{10,12},{12,14},{14,0},{1,3},{3,5},... | collective-permute-start | bytes 393224 | tf_op jit(solution)/shard_map/sum_layers/ppermute | solution.py:25
  40.3 9.4 %copy-start.1 = (bf16[1024,1024]{1,0:T(8,128)(2,1)S(1)}, bf16[1024,1024]{1,0:T(8,128)(2,1)}, u32[]{:S(2)}) copy-start(bf16[1024,1024]{1,0:T(8,128)(2,1)} %copy-done) | copy-start | bytes 6291460
  40.3 9.4 %collective-permute-start.14 = (bf16[64,1024]{1,0:T(8,128)(2,1)S(1)}, bf16[64,1024]{1,0:T(8,128)(2,1)S(1)}, u32[]{:S(2)}, u32[]{:S(2)}) collective-permute-start(bf16[64,1024]{1,0:T(8,128)(2,1)S(1)} %get-tuple-element.10), channel_id=1, source_target_pairs={{0,14},{2,0},{4,2},{6,4},{8,6},{10,8},{12,10},{14,12},{1,15},{3,1}... | collective-permute-start | bytes 393224 | tf_op jit(solution)/shard_map/sum_layers/ppermute | solution.py:25
  40.3 10.9 %collective-permute-start.18 = (bf16[64,1024]{1,0:T(8,128)(2,1)S(1)}, bf16[64,1024]{1,0:T(8,128)(2,1)S(1)}, u32[]{:S(2)}, u32[]{:S(2)}) collective-permute-start(bf16[64,1024]{1,0:T(8,128)(2,1)S(1)} %get-tuple-element.12), channel_id=1, source_target_pairs={{0,2},{2,4},{4,6},{6,8},{8,10},{10,12},{12,14},{14,0},{1,3},{3,5},... | collective-permute-start | bytes 393224 | tf_op jit(solution)/shard_map/sum_layers/ppermute | solution.py:25
  43.5 11.4 %collective-permute-start.22 = (bf16[64,1024]{1,0:T(8,128)(2,1)S(1)}, bf16[64,1024]{1,0:T(8,128)(2,1)S(1)}, u32[]{:S(2)}, u32[]{:S(2)}) collective-permute-start(bf16[64,1024]{1,0:T(8,128)(2,1)S(1)} %get-tuple-element.13), channel_id=1, source_target_pairs={{0,14},{2,0},{4,2},{6,4},{8,6},{10,8},{12,10},{14,12},{1,15},{3,1}... | collective-permute-start | bytes 393224 | tf_op jit(solution)/shard_map/sum_layers/ppermute | solution.py:25
  43.5 7.7 %copy-start.4 = (bf16[8,128,1024]{2,1,0:T(8,128)(2,1)S(1)}, bf16[8,128,1024]{2,1,0:T(8,128)(2,1)}, u32[]{:S(2)}) copy-start(bf16[8,128,1024]{2,1,0:T(8,128)(2,1)} %copy-done.2) | copy-start | bytes 6291460
  45.8 10.6 %collective-permute-start.11 = (bf16[128,1024]{1,0:T(8,128)(2,1)S(1)}, bf16[128,1024]{1,0:T(8,128)(2,1)S(1)}, u32[]{:S(2)}, u32[]{:S(2)}) collective-permute-start(bf16[128,1024]{1,0:T(8,128)(2,1)S(1)} %fusion.6), channel_id=1, source_target_pairs={{0,2},{2,4},{4,6},{6,8},{8,10},{10,12},{12,14},{14,0},{1,3},{3,5},... | collective-permute-start | bytes 786440 | tf_op jit(solution)/shard_map/sum_layers/ppermute | solution.py:25
  51.1 10.5 %collective-permute-start.15 = (bf16[128,1024]{1,0:T(8,128)(2,1)S(1)}, bf16[128,1024]{1,0:T(8,128)(2,1)S(1)}, u32[]{:S(2)}, u32[]{:S(2)}) collective-permute-start(bf16[128,1024]{1,0:T(8,128)(2,1)S(1)} %fusion.9), channel_id=1, source_target_pairs={{0,14},{2,0},{4,2},{6,4},{8,6},{10,8},{12,10},{14,12},{1,15},{3,1}... | collective-permute-start | bytes 786440 | tf_op jit(solution)/shard_map/sum_layers/ppermute | solution.py:25
  51.6 10.5 %collective-permute-start.19 = (bf16[128,1024]{1,0:T(8,128)(2,1)S(1)}, bf16[128,1024]{1,0:T(8,128)(2,1)S(1)}, u32[]{:S(2)}, u32[]{:S(2)}) collective-permute-start(bf16[128,1024]{1,0:T(8,128)(2,1)S(1)} %fusion.12), channel_id=1, source_target_pairs={{0,2},{2,4},{4,6},{6,8},{8,10},{10,12},{12,14},{14,0},{1,3},{3,5},... | collective-permute-start | bytes 786440 | tf_op jit(solution)/shard_map/sum_layers/ppermute | solution.py:25
  55.4 11.6 %collective-permute-start.23 = (bf16[128,1024]{1,0:T(8,128)(2,1)S(1)}, bf16[128,1024]{1,0:T(8,128)(2,1)S(1)}, u32[]{:S(2)}, u32[]{:S(2)}) collective-permute-start(bf16[128,1024]{1,0:T(8,128)(2,1)S(1)} %fusion.15), channel_id=1, source_target_pairs={{0,14},{2,0},{4,2},{6,4},{8,6},{10,8},{12,10},{14,12},{1,15},{3,1}... | collective-permute-start | bytes 786440 | tf_op jit(solution)/shard_map/sum_layers/ppermute | solution.py:25
  56.8 10.8 %collective-permute-start.12 = (bf16[128,1024]{1,0:T(8,128)(2,1)S(1)}, bf16[128,1024]{1,0:T(8,128)(2,1)S(1)}, u32[]{:S(2)}, u32[]{:S(2)}) collective-permute-start(bf16[128,1024]{1,0:T(8,128)(2,1)S(1)} %fusion.5), channel_id=1, source_target_pairs={{0,2},{2,4},{4,6},{6,8},{8,10},{10,12},{12,14},{14,0},{1,3},{3,5},... | collective-permute-start | bytes 786440 | tf_op jit(solution)/shard_map/sum_layers/ppermute | solution.py:25
  62.1 10.6 %collective-permute-start.16 = (bf16[128,1024]{1,0:T(8,128)(2,1)S(1)}, bf16[128,1024]{1,0:T(8,128)(2,1)S(1)}, u32[]{:S(2)}, u32[]{:S(2)}) collective-permute-start(bf16[128,1024]{1,0:T(8,128)(2,1)S(1)} %fusion.8), channel_id=1, source_target_pairs={{0,14},{2,0},{4,2},{6,4},{8,6},{10,8},{12,10},{14,12},{1,15},{3,1}... | collective-permute-start | bytes 786440 | tf_op jit(solution)/shard_map/sum_layers/ppermute | solution.py:25
  62.6 10.6 %collective-permute-start.20 = (bf16[128,1024]{1,0:T(8,128)(2,1)S(1)}, bf16[128,1024]{1,0:T(8,128)(2,1)S(1)}, u32[]{:S(2)}, u32[]{:S(2)}) collective-permute-start(bf16[128,1024]{1,0:T(8,128)(2,1)S(1)} %fusion.11), channel_id=1, source_target_pairs={{0,2},{2,4},{4,6},{6,8},{8,10},{10,12},{12,14},{14,0},{1,3},{3,5},... | collective-permute-start | bytes 786440 | tf_op jit(solution)/shard_map/sum_layers/ppermute | solution.py:25
  67.5 10.6 %collective-permute-start.24 = (bf16[128,1024]{1,0:T(8,128)(2,1)S(1)}, bf16[128,1024]{1,0:T(8,128)(2,1)S(1)}, u32[]{:S(2)}, u32[]{:S(2)}) collective-permute-start(bf16[128,1024]{1,0:T(8,128)(2,1)S(1)} %fusion.14), channel_id=1, source_target_pairs={{0,14},{2,0},{4,2},{6,4},{8,6},{10,8},{12,10},{14,12},{1,15},{3,1}... | collective-permute-start | bytes 786440 | tf_op jit(solution)/shard_map/sum_layers/ppermute | solution.py:25
  68.1 10.8 %collective-permute-start.13 = (bf16[128,1024]{1,0:T(8,128)(2,1)S(1)}, bf16[128,1024]{1,0:T(8,128)(2,1)S(1)}, u32[]{:S(2)}, u32[]{:S(2)}) collective-permute-start(bf16[128,1024]{1,0:T(8,128)(2,1)S(1)} %fusion.4), channel_id=1, source_target_pairs={{0,2},{2,4},{4,6},{6,8},{8,10},{10,12},{12,14},{14,0},{1,3},{3,5},... | collective-permute-start | bytes 786440 | tf_op jit(solution)/shard_map/sum_layers/ppermute | solution.py:25
  73.1 9.5 %collective-permute-start.17 = (bf16[128,1024]{1,0:T(8,128)(2,1)S(1)}, bf16[128,1024]{1,0:T(8,128)(2,1)S(1)}, u32[]{:S(2)}, u32[]{:S(2)}) collective-permute-start(bf16[128,1024]{1,0:T(8,128)(2,1)S(1)} %fusion.7), channel_id=1, source_target_pairs={{0,14},{2,0},{4,2},{6,4},{8,6},{10,8},{12,10},{14,12},{1,15},{3,1}... | collective-permute-start | bytes 786440 | tf_op jit(solution)/shard_map/sum_layers/ppermute | solution.py:25
  73.7 9.4 %collective-permute-start.21 = (bf16[128,1024]{1,0:T(8,128)(2,1)S(1)}, bf16[128,1024]{1,0:T(8,128)(2,1)S(1)}, u32[]{:S(2)}, u32[]{:S(2)}) collective-permute-start(bf16[128,1024]{1,0:T(8,128)(2,1)S(1)} %fusion.10), channel_id=1, source_target_pairs={{0,2},{2,4},{4,6},{6,8},{8,10},{10,12},{12,14},{14,0},{1,3},{3,5},... | collective-permute-start | bytes 786440 | tf_op jit(solution)/shard_map/sum_layers/ppermute | solution.py:25
  78.5 7.9 %collective-permute-start.25 = (bf16[128,1024]{1,0:T(8,128)(2,1)S(1)}, bf16[128,1024]{1,0:T(8,128)(2,1)S(1)}, u32[]{:S(2)}, u32[]{:S(2)}) collective-permute-start(bf16[128,1024]{1,0:T(8,128)(2,1)S(1)} %fusion.13), channel_id=1, source_target_pairs={{0,14},{2,0},{4,2},{6,4},{8,6},{10,8},{12,10},{14,12},{1,15},{3,1}... | collective-permute-start | bytes 786440 | tf_op jit(solution)/shard_map/sum_layers/ppermute | solution.py:25
  83.1 11.6 %copy-start.5 = (s32[1024]{0:T(1024)S(1)}, s32[1024]{0:T(1024)}, u32[]{:S(2)}) copy-start(s32[1024]{0:T(1024)} %param.12) | copy-start | bytes 12292
  86.9 37.1 %copy-start.6 = (s32[64]{0:T(128)S(1)}, s32[64]{0:T(128)}, u32[]{:S(2)}) copy-start(s32[64]{0:T(128)} %param.13) | copy-start | bytes 772
  87.7 17.1 %all-to-all-start.1 = ((bf16[16,8,2048]{2,1,0:T(8,128)(2,1)}), bf16[16,8,2048]{2,1,0:T(8,128)(2,1)S(1)}, u32[]{:S(2)}, u32[]{:S(2)}) async-start(bf16[16,8,2048]{2,1,0:T(8,128)(2,1)} %maximum_bitcast_fusion), calls=%async_computation.1 | async-start | bytes 1048576 | tf_op jit(solution)/shard_map/to_components/all_to_all | solution.py:269
  107.0 11.2 %all-to-all-start.2 = ((f32[32,1,256]{2,1,0:T(1,128)}), f32[32,1,256]{2,1,0:T(1,128)S(1)}, u32[]{:S(2)}, u32[]{:S(2)}) async-start(f32[32,1,256]{2,1,0:T(1,128)} %fit.1), calls=%async_computation.2 | async-start | bytes 65536 | tf_op jit(solution)/shard_map/gather_scores/all_to_all | solution.py:274
  118.3 5.5 %collective-permute-start.26 = (f32[256]{0:T(256)S(1)}, f32[256]{0:T(256)S(1)}, u32[]{:S(2)}, u32[]{:S(2)}) collective-permute-start(f32[256]{0:T(256)S(1)} %reduce_sum.9), channel_id=1, source_target_pairs={{0,2},{2,4},{4,6},{6,8},{8,10},{10,12},{12,14},{3,1},{5,3},{7,5},{... | collective-permute-start | bytes 3080 | tf_op jit(solution)/shard_map/gather_scores/ppermute | solution.py:277

commit v8 on v5

--- a/solution.py
+++ b/solution.py
@@ -177,6 +177,7 @@
     layers = lax.axis_size("cpg_0")
     with jax.named_scope("swap_eigvecs"):
         other = shifted(eigvecs, "samp_2", 1)
+        vecs = (eigvecs, other)
     with jax.named_scope("weigh"):
         own = weigh(responses, weights, phenotype)
     with jax.named_scope("gather_rows"):
@@ -185,8 +186,6 @@
         everywhere = copies(eigvals, SAMP).reshape(-1, 2, eigvals.shape[0])
         everywhere = jnp.where(lax.axis_index("samp_2") == 0, everywhere, everywhere[:, ::-1])
         everywhere = jnp.repeat(everywhere.reshape(everywhere.shape[0], -1), 4, axis=0)
-    other = other + 0 * (blocks[6, :1] + everywhere[:1, : other.shape[1]].astype(other.dtype))
-    vecs = (eigvecs, other)
     rows = own.shape[0]
 
     def term(q, ahead, lo, hi):

time: 132 us -> 120 us (0.909)
  matrix products: 22.6 us -> 9.25 us
  waiting for transfers between devices: 36.4 us -> 33.3 us
  local copies, waits for them, and re-layouts: 6.72 us -> 9.74 us
  starting transfers between devices: 57.3 us -> 59.7 us
    dot_general x18, matrix products: 22.6 us -> 9.25 us  [term(): return jnp.dot(block, vecs[q], preferred_element_type=jnp.float32)]
    all_to_all x1, waiting for transfers between devices: 4.8 us -> 0.01 us  [copies(): lax.all_to_all(jnp.broadcast_to(value[None], (peers, *value.shape)), axes...]
    ppermute x26, starting transfers between devices: 40.7 us -> 43.8 us  [shifted(): lax.ppermute(value, axis, [(i, (i + by) % peers) for i in range(peers)])]
    ppermute x26, waiting for transfers between devices: 11.3 us -> 13.8 us  [shifted(): lax.ppermute(value, axis, [(i, (i + by) % peers) for i in range(peers)])]
    unnamed x13 -> x15, local copies, waits for them, and re-layouts: 3.96 us -> 6.27 us
  transfers between devices with their start and end apart: 30 -> 30, of which waited for: 10 -> 15; matrix products, arithmetic and copies ran while one was open for 20% -> 17% of each run, Pallas kernels for 1% -> 2%
where the time goes in v8:
time: 120 us
  starting transfers between devices  59.7 us (50%)
  waiting for transfers between devices  33.3 us (28%)
  local copies, waits for them, and re-layouts  9.74 us (8%)
  matrix products  9.25 us (8%)
  Pallas kernels  4.03 us (3%)
  other arithmetic  2.62 us (2%)
    ppermute x26, starting transfers between devices, shifted(): lax.ppermute(value, axis, [(i, (i + by) % peers) for i in range(peers)])  43.8 us
    ppermute x26, waiting for transfers between devices, shifted(): lax.ppermute(value, axis, [(i, (i + by) % peers) for i in range(peers)])  13.8 us
    all_to_all x1, waiting for transfers between devices, shards(): sums = lax.all_to_all(whole, PLANE, 0, 0, tiled=True)  9.26 us
    dot_general x18, matrix products, term(): return jnp.dot(block, vecs[q], preferred_element_type=jnp.float32)  9.25 us
    all_to_all x1, waiting for transfers between devices, shards(): lax.all_to_all(fitted, LAYER, 0, 0, tiled=True)  7.32 us
    all_to_all x1, starting transfers between devices, shards(): sums = lax.all_to_all(whole, PLANE, 0, 0, tiled=True)  6.68 us
    unnamed x15, local copies, waits for them, and re-layouts  6.27 us
    all_to_all x1, starting transfers between devices, shards(): lax.all_to_all(fitted, LAYER, 0, 0, tiled=True)  3.84 us
  transfers between devices with their start and end apart: 30, of which 15 were waited for; matrix products, arithmetic and copies ran while one was open for 17% of the time, Pallas kernels for 2%

profile of v8, /device:TPU:96, one launch (start us, length us, event | category | flops | bytes accessed | tf_op | source)
XLA Modules:
  0.0 119.7 jit_solution(3149825010693695148)
XLA Ops:
  0.7 1.8 %weigh.1 = bf16[128,1024]{1,0:T(8,128)(2,1)} custom-call(bf16[64,1024]{1,0:T(8,128)(2,1)} %resp_ref.1, bf16[64,1024]{1,0:T(8,128)(2,1)} %weight_ref.1, f32[1,1024]{1,0:T(1,128)} %bitcast.89), custom_call_target="tpu_custom_call" | custom-call | tf_op jit(solution)/shard_map/weigh/pallas_call | solution.py:46
  2.6 1.5 %collective-permute-start.1 = (bf16[128,1024]{1,0:T(8,128)(2,1)}, bf16[128,1024]{1,0:T(8,128)(2,1)S(1)}, u32[]{:S(2)}, u32[]{:S(2)}) collective-permute-start(bf16[128,1024]{1,0:T(8,128)(2,1)} %weigh.1), channel_id=1, source_target_pairs={{0,32},{32,64},{64,96},{96,0},{1,33},{33,65},{65,97},{97,1},{2,34}... | collective-permute-start | bytes 786440 | tf_op jit(solution)/shard_map/gather_rows/ppermute | solution.py:25
  4.1 1.6 %collective-permute-start.3 = (bf16[128,1024]{1,0:T(8,128)(2,1)}, bf16[128,1024]{1,0:T(8,128)(2,1)S(1)}, u32[]{:S(2)}, u32[]{:S(2)}) collective-permute-start(bf16[128,1024]{1,0:T(8,128)(2,1)} %weigh.1), channel_id=1, source_target_pairs={{0,128},{128,0},{1,129},{129,1},{2,130},{130,2},{3,131},{131,3},{4... | collective-permute-start | bytes 786440 | tf_op jit(solution)/shard_map/gather_rows/ppermute | solution.py:25
  5.6 1.7 %collective-permute-start = (bf16[128,1024]{1,0:T(8,128)(2,1)}, bf16[128,1024]{1,0:T(8,128)(2,1)}, u32[]{:S(2)}, u32[]{:S(2)}) collective-permute-start(bf16[128,1024]{1,0:T(8,128)(2,1)} %weigh.1), channel_id=1, source_target_pairs={{0,96},{32,0},{64,32},{96,64},{1,97},{33,1},{65,33},{97,65},{2,98}... | collective-permute-start | bytes 786440 | tf_op jit(solution)/shard_map/gather_rows/ppermute | solution.py:25
  7.4 1.3 %broadcast_in_dim.17 = f32[16,1,1024]{2,1,0:T(1,128)} broadcast(f32[1024]{0:T(1024)} %param.11), dimensions={2} | broadcast | bytes 69632 | tf_op jit(solution)/shard_map/gather_values/broadcast_in_dim | solution.py:171
  8.7 3.5 %all-to-all-start.1 = ((f32[16,1,1024]{2,1,0:T(1,128)}), f32[16,1,1024]{2,1,0:T(1,128)S(1)}, u32[]{:S(2)}, u32[]{:S(2)}) async-start(f32[16,1,1024]{2,1,0:T(1,128)} %broadcast_in_dim.17), calls=%async_computation.1 | async-start | bytes 131072 | tf_op jit(solution)/shard_map/gather_values/all_to_all | solution.py:170
  12.2 0.5 collective-permute-done.1
  12.7 1.4 %collective-permute-start.2 = (bf16[128,1024]{1,0:T(8,128)(2,1)S(1)}, bf16[128,1024]{1,0:T(8,128)(2,1)S(1)}, u32[]{:S(2)}, u32[]{:S(2)}) collective-permute-start(bf16[128,1024]{1,0:T(8,128)(2,1)S(1)} %collective-permute-done.1), channel_id=1, source_target_pairs={{0,32},{32,64},{64,96},{96,0},{1,33},{33,65},{65,97},{97,1},{2,34}... | collective-permute-start | bytes 786440 | tf_op jit(solution)/shard_map/gather_rows/ppermute | solution.py:25
  14.1 1.5 %collective-permute-start.5 = (bf16[128,1024]{1,0:T(8,128)(2,1)S(1)}, bf16[128,1024]{1,0:T(8,128)(2,1)S(1)}, u32[]{:S(2)}, u32[]{:S(2)}) collective-permute-start(bf16[128,1024]{1,0:T(8,128)(2,1)S(1)} %collective-permute-done.1), channel_id=1, source_target_pairs={{0,128},{128,0},{1,129},{129,1},{2,130},{130,2},{3,131},{131,3},{4... | collective-permute-start | bytes 786440 | tf_op jit(solution)/shard_map/gather_rows/ppermute | solution.py:25
  15.6 1.9 %collective-permute-start.4 = (bf16[128,1024]{1,0:T(8,128)(2,1)S(1)}, bf16[128,1024]{1,0:T(8,128)(2,1)S(1)}, u32[]{:S(2)}, u32[]{:S(2)}) collective-permute-start(bf16[128,1024]{1,0:T(8,128)(2,1)S(1)} %collective-permute-done.3), channel_id=1, source_target_pairs={{0,96},{32,0},{64,32},{96,64},{1,97},{33,1},{65,33},{97,65},{2,98}... | collective-permute-start | bytes 786440 | tf_op jit(solution)/shard_map/gather_rows/ppermute | solution.py:25
  17.5 1.7 %bitcast_dynamic-update-slice_fusion.6 = bf16[8,128,1024]{2,1,0:T(8,128)(2,1)} fusion(bf16[128,1024]{1,0:T(8,128)(2,1)} %weigh.1), kind=kLoop, calls=%fused_computation.59 | loop fusion | bytes 524288
  19.2 1.7 %bitcast_dynamic-update-slice_fusion.5 = bf16[8,128,1024]{2,1,0:T(8,128)(2,1)} fusion(bf16[8,128,1024]{2,1,0:T(8,128)(2,1)} %bitcast_dynamic-update-slice_fusion.6, bf16[128,1024]{1,0:T(8,128)(2,1)} %collective-permute-done), kind=kLoop, calls=%fused_computation.58 | loop fusion | bytes 524288
  20.8 1.8 %collective-permute-done.5 = bf16[128,1024]{1,0:T(8,128)(2,1)S(1)} collective-permute-done((bf16[128,1024]{1,0:T(8,128)(2,1)S(1)}, bf16[128,1024]{1,0:T(8,128)(2,1)S(1)}, u32[]{:S(2)}, u32[]{:S(2)}) %collective-permute-start.5) | collective-permute-done | bytes 262176 | tf_op jit(solution)/shard_map/gather_rows/ppermute | solution.py:25
  22.6 1.4 %collective-permute-start.6 = (bf16[48,1024]{1,0:T(8,128)(2,1)S(1)}, bf16[48,1024]{1,0:T(8,128)(2,1)S(1)}, u32[]{:S(2)}, u32[]{:S(2)}) collective-permute-start(bf16[48,1024]{1,0:T(8,128)(2,1)S(1)} %slice.255), channel_id=1, source_target_pairs={{0,32},{32,64},{64,96},{96,0},{1,33},{33,65},{65,97},{97,1},{2,34}... | collective-permute-start | bytes 294920 | tf_op jit(solution)/shard_map/gather_rows/ppermute | solution.py:25
  24.0 1.3 %collective-permute-start.8 = (bf16[32,1024]{1,0:T(8,128)(2,1)S(1)}, bf16[32,1024]{1,0:T(8,128)(2,1)S(1)}, u32[]{:S(2)}, u32[]{:S(2)}) collective-permute-start(bf16[32,1024]{1,0:T(8,128)(2,1)S(1)} %slice.257), channel_id=1, source_target_pairs={{0,128},{128,0},{1,129},{129,1},{2,130},{130,2},{3,131},{131,3},{4... | collective-permute-start | bytes 196616 | tf_op jit(solution)/shard_map/gather_rows/ppermute | solution.py:25
  25.4 2.1 %collective-permute-start.7 = (bf16[48,1024]{1,0:T(8,128)(2,1)S(1)}, bf16[48,1024]{1,0:T(8,128)(2,1)S(1)}, u32[]{:S(2)}, u32[]{:S(2)}) collective-permute-start(bf16[48,1024]{1,0:T(8,128)(2,1)S(1)} %slice.256), channel_id=1, source_target_pairs={{0,96},{32,0},{64,32},{96,64},{1,97},{33,1},{65,33},{97,65},{2,98}... | collective-permute-start | bytes 294920 | tf_op jit(solution)/shard_map/gather_rows/ppermute | solution.py:25
  27.5 0.7 bitcast_dynamic-update-slice_fusion.4
  28.2 0.7 bitcast_dynamic-update-slice_fusion.3
  29.0 0.7 bitcast_dynamic-update-slice_fusion.2
  29.7 0.7 bitcast_dynamic-update-slice_fusion.1
  30.4 0.8 fusion.18
  31.3 0.7 bitcast_dynamic-update-slice_fusion
  32.0 1.5 %convolution_convert_fusion.3 = bf16[64,1024]{1,0:T(8,128)(2,1)S(1)} fusion(bf16[1024,1024]{1,0:T(8,128)(2,1)S(1)} %copy-done, bf16[8,128,1024]{2,1,0:T(8,128)(2,1)} %bitcast_dynamic-update-slice_fusion, s32[]{:T(128)S(6)} %select_n.98), kind=kOutput, calls=%fused_computation.33 | convolution fusion | flops 134283264 | bytes 2359300 | tf_op jit(solution)/shard_map/sum_layers/dot_general | solution.py:196
  33.5 3.2 %collective-permute-start.10 = (bf16[64,1024]{1,0:T(8,128)(2,1)S(1)}, bf16[64,1024]{1,0:T(8,128)(2,1)S(1)}, u32[]{:S(2)}, u32[]{:S(2)}) collective-permute-start(bf16[64,1024]{1,0:T(8,128)(2,1)S(1)} %convolution_convert_fusion.3), channel_id=1, source_target_pairs={{0,2},{2,4},{4,6},{6,8},{8,10},{10,12},{12,14},{14,0},{1,3},{3,5},... | collective-permute-start | bytes 393224 | tf_op jit(solution)/shard_map/sum_layers/ppermute | solution.py:25
  36.7 0.5 convolution_convert_fusion.2
  37.3 0.5 convolution_convert_fusion.1
  37.8 3.3 %collective-permute-start.18 = (bf16[64,1024]{1,0:T(8,128)(2,1)S(1)}, bf16[64,1024]{1,0:T(8,128)(2,1)S(1)}, u32[]{:S(2)}, u32[]{:S(2)}) collective-permute-start(bf16[64,1024]{1,0:T(8,128)(2,1)S(1)} %convolution_convert_fusion.1), channel_id=1, source_target_pairs={{0,2},{2,4},{4,6},{6,8},{8,10},{10,12},{12,14},{14,0},{1,3},{3,5},... | collective-permute-start | bytes 393224 | tf_op jit(solution)/shard_map/sum_layers/ppermute | solution.py:25
  41.1 0.5 convolution_convert_fusion
  41.9 0.4 fusion.6
  42.3 3.3 %collective-permute-start.11 = (bf16[128,1024]{1,0:T(8,128)(2,1)S(1)}, bf16[128,1024]{1,0:T(8,128)(2,1)S(1)}, u32[]{:S(2)}, u32[]{:S(2)}) collective-permute-start(bf16[128,1024]{1,0:T(8,128)(2,1)S(1)} %fusion.6), channel_id=1, source_target_pairs={{0,2},{2,4},{4,6},{6,8},{8,10},{10,12},{12,14},{14,0},{1,3},{3,5},... | collective-permute-start | bytes 786440 | tf_op jit(solution)/shard_map/sum_layers/ppermute | solution.py:25
  45.6 0.4 fusion.9
  46.2 0.4 fusion.12
  46.6 3.3 %collective-permute-start.19 = (bf16[128,1024]{1,0:T(8,128)(2,1)S(1)}, bf16[128,1024]{1,0:T(8,128)(2,1)S(1)}, u32[]{:S(2)}, u32[]{:S(2)}) collective-permute-start(bf16[128,1024]{1,0:T(8,128)(2,1)S(1)} %fusion.12), channel_id=1, source_target_pairs={{0,2},{2,4},{4,6},{6,8},{8,10},{10,12},{12,14},{14,0},{1,3},{3,5},... | collective-permute-start | bytes 786440 | tf_op jit(solution)/shard_map/sum_layers/ppermute | solution.py:25
  50.5 1.7 %collective-permute-done.11 = bf16[128,1024]{1,0:T(8,128)(2,1)S(1)} collective-permute-done((bf16[128,1024]{1,0:T(8,128)(2,1)S(1)}, bf16[128,1024]{1,0:T(8,128)(2,1)S(1)}, u32[]{:S(2)}, u32[]{:S(2)}) %collective-permute-start.11) | collective-permute-done | bytes 262176 | tf_op jit(solution)/shard_map/sum_layers/ppermute | solution.py:25
  52.2 0.4 fusion.5
  52.7 3.8 %collective-permute-start.12 = (bf16[128,1024]{1,0:T(8,128)(2,1)S(1)}, bf16[128,1024]{1,0:T(8,128)(2,1)S(1)}, u32[]{:S(2)}, u32[]{:S(2)}) collective-permute-start(bf16[128,1024]{1,0:T(8,128)(2,1)S(1)} %fusion.5), channel_id=1, source_target_pairs={{0,2},{2,4},{4,6},{6,8},{8,10},{10,12},{12,14},{14,0},{1,3},{3,5},... | collective-permute-start | bytes 786440 | tf_op jit(solution)/shard_map/sum_layers/ppermute | solution.py:25
  56.6 0.4 fusion.8
  57.2 0.7 collective-permute-done.19
  57.8 0.4 fusion.11
  58.3 3.8 %collective-permute-start.20 = (bf16[128,1024]{1,0:T(8,128)(2,1)S(1)}, bf16[128,1024]{1,0:T(8,128)(2,1)S(1)}, u32[]{:S(2)}, u32[]{:S(2)}) collective-permute-start(bf16[128,1024]{1,0:T(8,128)(2,1)S(1)} %fusion.11), channel_id=1, source_target_pairs={{0,2},{2,4},{4,6},{6,8},{8,10},{10,12},{12,14},{14,0},{1,3},{3,5},... | collective-permute-start | bytes 786440 | tf_op jit(solution)/shard_map/sum_layers/ppermute | solution.py:25
  62.2 0.4 fusion.14
  62.8 0.7 collective-permute-done.12
  63.5 0.4 fusion.4
  63.9 3.8 %collective-permute-start.13 = (bf16[128,1024]{1,0:T(8,128)(2,1)S(1)}, bf16[128,1024]{1,0:T(8,128)(2,1)S(1)}, u32[]{:S(2)}, u32[]{:S(2)}) collective-permute-start(bf16[128,1024]{1,0:T(8,128)(2,1)S(1)} %fusion.4), channel_id=1, source_target_pairs={{0,2},{2,4},{4,6},{6,8},{8,10},{10,12},{12,14},{14,0},{1,3},{3,5},... | collective-permute-start | bytes 786440 | tf_op jit(solution)/shard_map/sum_layers/ppermute | solution.py:25
  67.9 0.4 fusion.7
  68.4 0.7 collective-permute-done.20
  69.1 0.4 fusion.10
  69.5 4.0 %collective-permute-start.21 = (bf16[128,1024]{1,0:T(8,128)(2,1)S(1)}, bf16[128,1024]{1,0:T(8,128)(2,1)S(1)}, u32[]{:S(2)}, u32[]{:S(2)}) collective-permute-start(bf16[128,1024]{1,0:T(8,128)(2,1)S(1)} %fusion.10), channel_id=1, source_target_pairs={{0,2},{2,4},{4,6},{6,8},{8,10},{10,12},{12,14},{14,0},{1,3},{3,5},... | collective-permute-start | bytes 786440 | tf_op jit(solution)/shard_map/sum_layers/ppermute | solution.py:25
  73.5 0.4 fusion.13
  74.1 0.6 collective-permute-done.13
  74.7 4.2 %collective-permute-done.17 = bf16[128,1024]{1,0:T(8,128)(2,1)S(1)} collective-permute-done((bf16[128,1024]{1,0:T(8,128)(2,1)S(1)}, bf16[128,1024]{1,0:T(8,128)(2,1)S(1)}, u32[]{:S(2)}, u32[]{:S(2)}) %collective-permute-start.17) | collective-permute-done | bytes 262176 | tf_op jit(solution)/shard_map/sum_layers/ppermute | solution.py:25
  78.9 0.5 fusion.2
  79.4 2.3 %collective-permute-done.25 = bf16[128,1024]{1,0:T(8,128)(2,1)S(1)} collective-permute-done((bf16[128,1024]{1,0:T(8,128)(2,1)S(1)}, bf16[128,1024]{1,0:T(8,128)(2,1)S(1)}, u32[]{:S(2)}, u32[]{:S(2)}) %collective-permute-start.25) | collective-permute-done | bytes 262176 | tf_op jit(solution)/shard_map/sum_layers/ppermute | solution.py:25
  81.7 0.5 fusion.3
  82.2 0.8 maximum_bitcast_fusion
  83.1 6.7 %all-to-all-start = ((bf16[16,8,2048]{2,1,0:T(8,128)(2,1)}), bf16[16,8,2048]{2,1,0:T(8,128)(2,1)S(1)}, u32[]{:S(2)}, u32[]{:S(2)}) async-start(bf16[16,8,2048]{2,1,0:T(8,128)(2,1)} %maximum_bitcast_fusion), calls=%async_computation | async-start | bytes 1048576 | tf_op jit(solution)/shard_map/to_components/all_to_all | solution.py:229
  90.6 9.3 %all-to-all-done = bf16[16,8,2048]{2,1,0:T(8,128)(2,1)S(1)} async-done(((bf16[16,8,2048]{2,1,0:T(8,128)(2,1)}), bf16[16,8,2048]{2,1,0:T(8,128)(2,1)S(1)}, u32[]{:S(2)}, u32[]{:S(2)}) %all-to-all-start) | async-done | bytes 524320 | tf_op jit(solution)/shard_map/to_components/all_to_all | solution.py:229
  99.9 2.2 %fit.1 = f32[32,1,256]{2,1,0:T(1,128)} custom-call(s32[1]{0:T(128)} %bitcast.slot_ref, bf16[128,2048]{1,0:T(8,128)(2,1)S(1)} %bitcast.87, f32[32,2048]{1,0:T(8,128)S(1)} %reshape.26.values_ref), custom_call_target="tpu_custom_call" | custom-call | tf_op jit(solution)/shard_map/fit/pallas_call | solution.py:119
  102.1 3.8 %all-to-all-start.2 = ((f32[32,1,256]{2,1,0:T(1,128)}), f32[32,1,256]{2,1,0:T(1,128)S(1)}, u32[]{:S(2)}, u32[]{:S(2)}) async-start(f32[32,1,256]{2,1,0:T(1,128)} %fit.1), calls=%async_computation.2 | async-start | bytes 65536 | tf_op jit(solution)/shard_map/gather_scores/all_to_all | solution.py:234
  106.0 7.3 %all-to-all-done.2 = f32[32,1,256]{2,1,0:T(1,128)S(1)} async-done(((f32[32,1,256]{2,1,0:T(1,128)}), f32[32,1,256]{2,1,0:T(1,128)S(1)}, u32[]{:S(2)}, u32[]{:S(2)}) %all-to-all-start.2) | async-done | bytes 32800 | tf_op jit(solution)/shard_map/gather_scores/all_to_all | solution.py:234
  113.4 1.9 %collective-permute-start.26 = (f32[256]{0:T(256)S(1)}, f32[256]{0:T(256)S(1)}, u32[]{:S(2)}, u32[]{:S(2)}) collective-permute-start(f32[256]{0:T(256)S(1)} %reduce_sum.9), channel_id=1, source_target_pairs={{0,2},{2,4},{4,6},{6,8},{8,10},{10,12},{12,14},{3,1},{5,3},{7,5},{... | collective-permute-start | bytes 3080 | tf_op jit(solution)/shard_map/gather_scores/ppermute | solution.py:237
  115.3 0.6 dynamic_slice.54
  115.9 2.9 %collective-permute-done.26 = f32[256]{0:T(256)S(1)} collective-permute-done((f32[256]{0:T(256)S(1)}, f32[256]{0:T(256)S(1)}, u32[]{:S(2)}, u32[]{:S(2)}) %collective-permute-start.26) | collective-permute-done | bytes 1056 | tf_op jit(solution)/shard_map/gather_scores/ppermute | solution.py:237
  119.1 0.6 add_divide_fusion
  (54 shorter events, 3.1 us)
Async XLA Ops:
  0.6 29.8 %collective-permute-start.9 = (bf16[1024,1024]{1,0:T(8,128)(2,1)}, bf16[1024,1024]{1,0:T(8,128)(2,1)S(1)}, u32[]{:S(2)}, u32[]{:S(2)}) collective-permute-start(bf16[1024,1024]{1,0:T(8,128)(2,1)} %param.10), channel_id=1, source_target_pairs={{0,16},{16,0},{1,17},{17,1},{2,18},{18,2},{3,19},{19,3},{4,20},{20... | collective-permute-start | bytes 6291464 | tf_op jit(solution)/shard_map/swap_eigvecs/ppermute | solution.py:25
  2.6 10.1 %collective-permute-start.1 = (bf16[128,1024]{1,0:T(8,128)(2,1)}, bf16[128,1024]{1,0:T(8,128)(2,1)S(1)}, u32[]{:S(2)}, u32[]{:S(2)}) collective-permute-start(bf16[128,1024]{1,0:T(8,128)(2,1)} %weigh.1), channel_id=1, source_target_pairs={{0,32},{32,64},{64,96},{96,0},{1,33},{33,65},{65,97},{97,1},{2,34}... | collective-permute-start | bytes 786440 | tf_op jit(solution)/shard_map/gather_rows/ppermute | solution.py:25
  4.1 11.6 %collective-permute-start.3 = (bf16[128,1024]{1,0:T(8,128)(2,1)}, bf16[128,1024]{1,0:T(8,128)(2,1)S(1)}, u32[]{:S(2)}, u32[]{:S(2)}) collective-permute-start(bf16[128,1024]{1,0:T(8,128)(2,1)} %weigh.1), channel_id=1, source_target_pairs={{0,128},{128,0},{1,129},{129,1},{2,130},{130,2},{3,131},{131,3},{4... | collective-permute-start | bytes 786440 | tf_op jit(solution)/shard_map/gather_rows/ppermute | solution.py:25
  5.6 13.5 %collective-permute-start = (bf16[128,1024]{1,0:T(8,128)(2,1)}, bf16[128,1024]{1,0:T(8,128)(2,1)}, u32[]{:S(2)}, u32[]{:S(2)}) collective-permute-start(bf16[128,1024]{1,0:T(8,128)(2,1)} %weigh.1), channel_id=1, source_target_pairs={{0,96},{32,0},{64,32},{96,64},{1,97},{33,1},{65,33},{97,65},{2,98}... | collective-permute-start | bytes 786440 | tf_op jit(solution)/shard_map/gather_rows/ppermute | solution.py:25
  8.7 74.3 %all-to-all-start.1 = ((f32[16,1,1024]{2,1,0:T(1,128)}), f32[16,1,1024]{2,1,0:T(1,128)S(1)}, u32[]{:S(2)}, u32[]{:S(2)}) async-start(f32[16,1,1024]{2,1,0:T(1,128)} %broadcast_in_dim.17), calls=%async_computation.1 | async-start | bytes 131072 | tf_op jit(solution)/shard_map/gather_values/all_to_all | solution.py:170
  12.7 11.3 %collective-permute-start.2 = (bf16[128,1024]{1,0:T(8,128)(2,1)S(1)}, bf16[128,1024]{1,0:T(8,128)(2,1)S(1)}, u32[]{:S(2)}, u32[]{:S(2)}) collective-permute-start(bf16[128,1024]{1,0:T(8,128)(2,1)S(1)} %collective-permute-done.1), channel_id=1, source_target_pairs={{0,32},{32,64},{64,96},{96,0},{1,33},{33,65},{65,97},{97,1},{2,34}... | collective-permute-start | bytes 786440 | tf_op jit(solution)/shard_map/gather_rows/ppermute | solution.py:25
  14.1 8.5 %collective-permute-start.5 = (bf16[128,1024]{1,0:T(8,128)(2,1)S(1)}, bf16[128,1024]{1,0:T(8,128)(2,1)S(1)}, u32[]{:S(2)}, u32[]{:S(2)}) collective-permute-start(bf16[128,1024]{1,0:T(8,128)(2,1)S(1)} %collective-permute-done.1), channel_id=1, source_target_pairs={{0,128},{128,0},{1,129},{129,1},{2,130},{130,2},{3,131},{131,3},{4... | collective-permute-start | bytes 786440 | tf_op jit(solution)/shard_map/gather_rows/ppermute | solution.py:25
  15.6 9.7 %collective-permute-start.4 = (bf16[128,1024]{1,0:T(8,128)(2,1)S(1)}, bf16[128,1024]{1,0:T(8,128)(2,1)S(1)}, u32[]{:S(2)}, u32[]{:S(2)}) collective-permute-start(bf16[128,1024]{1,0:T(8,128)(2,1)S(1)} %collective-permute-done.3), channel_id=1, source_target_pairs={{0,96},{32,0},{64,32},{96,64},{1,97},{33,1},{65,33},{97,65},{2,98}... | collective-permute-start | bytes 786440 | tf_op jit(solution)/shard_map/gather_rows/ppermute | solution.py:25
  20.8 11.2 %copy-start = (bf16[1024,1024]{1,0:T(8,128)(2,1)S(1)}, bf16[1024,1024]{1,0:T(8,128)(2,1)}, u32[]{:S(2)}) copy-start(bf16[1024,1024]{1,0:T(8,128)(2,1)} %param.10) | copy-start | bytes 6291460
  22.6 7.8 %collective-permute-start.6 = (bf16[48,1024]{1,0:T(8,128)(2,1)S(1)}, bf16[48,1024]{1,0:T(8,128)(2,1)S(1)}, u32[]{:S(2)}, u32[]{:S(2)}) collective-permute-start(bf16[48,1024]{1,0:T(8,128)(2,1)S(1)} %slice.255), channel_id=1, source_target_pairs={{0,32},{32,64},{64,96},{96,0},{1,33},{33,65},{65,97},{97,1},{2,34}... | collective-permute-start | bytes 294920 | tf_op jit(solution)/shard_map/gather_rows/ppermute | solution.py:25
  24.0 6.4 %collective-permute-start.8 = (bf16[32,1024]{1,0:T(8,128)(2,1)S(1)}, bf16[32,1024]{1,0:T(8,128)(2,1)S(1)}, u32[]{:S(2)}, u32[]{:S(2)}) collective-permute-start(bf16[32,1024]{1,0:T(8,128)(2,1)S(1)} %slice.257), channel_id=1, source_target_pairs={{0,128},{128,0},{1,129},{129,1},{2,130},{130,2},{3,131},{131,3},{4... | collective-permute-start | bytes 196616 | tf_op jit(solution)/shard_map/gather_rows/ppermute | solution.py:25
  25.4 5.0 %collective-permute-start.7 = (bf16[48,1024]{1,0:T(8,128)(2,1)S(1)}, bf16[48,1024]{1,0:T(8,128)(2,1)S(1)}, u32[]{:S(2)}, u32[]{:S(2)}) collective-permute-start(bf16[48,1024]{1,0:T(8,128)(2,1)S(1)} %slice.256), channel_id=1, source_target_pairs={{0,96},{32,0},{64,32},{96,64},{1,97},{33,1},{65,33},{97,65},{2,98}... | collective-permute-start | bytes 294920 | tf_op jit(solution)/shard_map/gather_rows/ppermute | solution.py:25
  32.0 4.8 %copy-start.1 = (bf16[8,128,1024]{2,1,0:T(8,128)(2,1)S(1)}, bf16[8,128,1024]{2,1,0:T(8,128)(2,1)}, u32[]{:S(2)}) copy-start(bf16[8,128,1024]{2,1,0:T(8,128)(2,1)} %bitcast_dynamic-update-slice_fusion) | copy-start | bytes 6291460
  33.5 8.3 %collective-permute-start.10 = (bf16[64,1024]{1,0:T(8,128)(2,1)S(1)}, bf16[64,1024]{1,0:T(8,128)(2,1)S(1)}, u32[]{:S(2)}, u32[]{:S(2)}) collective-permute-start(bf16[64,1024]{1,0:T(8,128)(2,1)S(1)} %convolution_convert_fusion.3), channel_id=1, source_target_pairs={{0,2},{2,4},{4,6},{6,8},{8,10},{10,12},{12,14},{14,0},{1,3},{3,5},... | collective-permute-start | bytes 393224 | tf_op jit(solution)/shard_map/sum_layers/ppermute | solution.py:25
  37.2 8.4 %collective-permute-start.14 = (bf16[64,1024]{1,0:T(8,128)(2,1)S(1)}, bf16[64,1024]{1,0:T(8,128)(2,1)S(1)}, u32[]{:S(2)}, u32[]{:S(2)}) collective-permute-start(bf16[64,1024]{1,0:T(8,128)(2,1)S(1)} %convolution_convert_fusion.2), channel_id=1, source_target_pairs={{0,14},{2,0},{4,2},{6,4},{8,6},{10,8},{12,10},{14,12},{1,15},{3,1}... | collective-permute-start | bytes 393224 | tf_op jit(solution)/shard_map/sum_layers/ppermute | solution.py:25
  37.8 8.4 %collective-permute-start.18 = (bf16[64,1024]{1,0:T(8,128)(2,1)S(1)}, bf16[64,1024]{1,0:T(8,128)(2,1)S(1)}, u32[]{:S(2)}, u32[]{:S(2)}) collective-permute-start(bf16[64,1024]{1,0:T(8,128)(2,1)S(1)} %convolution_convert_fusion.1), channel_id=1, source_target_pairs={{0,2},{2,4},{4,6},{6,8},{8,10},{10,12},{12,14},{14,0},{1,3},{3,5},... | collective-permute-start | bytes 393224 | tf_op jit(solution)/shard_map/sum_layers/ppermute | solution.py:25
  41.6 8.3 %collective-permute-start.22 = (bf16[64,1024]{1,0:T(8,128)(2,1)S(1)}, bf16[64,1024]{1,0:T(8,128)(2,1)S(1)}, u32[]{:S(2)}, u32[]{:S(2)}) collective-permute-start(bf16[64,1024]{1,0:T(8,128)(2,1)S(1)} %convolution_convert_fusion), channel_id=1, source_target_pairs={{0,14},{2,0},{4,2},{6,4},{8,6},{10,8},{12,10},{14,12},{1,15},{3,1}... | collective-permute-start | bytes 393224 | tf_op jit(solution)/shard_map/sum_layers/ppermute | solution.py:25
  42.3 9.9 %collective-permute-start.11 = (bf16[128,1024]{1,0:T(8,128)(2,1)S(1)}, bf16[128,1024]{1,0:T(8,128)(2,1)S(1)}, u32[]{:S(2)}, u32[]{:S(2)}) collective-permute-start(bf16[128,1024]{1,0:T(8,128)(2,1)S(1)} %fusion.6), channel_id=1, source_target_pairs={{0,2},{2,4},{4,6},{6,8},{8,10},{10,12},{12,14},{14,0},{1,3},{3,5},... | collective-permute-start | bytes 786440 | tf_op jit(solution)/shard_map/sum_layers/ppermute | solution.py:25
  46.1 10.5 %collective-permute-start.15 = (bf16[128,1024]{1,0:T(8,128)(2,1)S(1)}, bf16[128,1024]{1,0:T(8,128)(2,1)S(1)}, u32[]{:S(2)}, u32[]{:S(2)}) collective-permute-start(bf16[128,1024]{1,0:T(8,128)(2,1)S(1)} %fusion.9), channel_id=1, source_target_pairs={{0,14},{2,0},{4,2},{6,4},{8,6},{10,8},{12,10},{14,12},{1,15},{3,1}... | collective-permute-start | bytes 786440 | tf_op jit(solution)/shard_map/sum_layers/ppermute | solution.py:25
  46.6 11.2 %collective-permute-start.19 = (bf16[128,1024]{1,0:T(8,128)(2,1)S(1)}, bf16[128,1024]{1,0:T(8,128)(2,1)S(1)}, u32[]{:S(2)}, u32[]{:S(2)}) collective-permute-start(bf16[128,1024]{1,0:T(8,128)(2,1)S(1)} %fusion.12), channel_id=1, source_target_pairs={{0,2},{2,4},{4,6},{6,8},{8,10},{10,12},{12,14},{14,0},{1,3},{3,5},... | collective-permute-start | bytes 786440 | tf_op jit(solution)/shard_map/sum_layers/ppermute | solution.py:25
  50.4 11.8 %collective-permute-start.23 = (bf16[128,1024]{1,0:T(8,128)(2,1)S(1)}, bf16[128,1024]{1,0:T(8,128)(2,1)S(1)}, u32[]{:S(2)}, u32[]{:S(2)}) collective-permute-start(bf16[128,1024]{1,0:T(8,128)(2,1)S(1)} %fusion.15), channel_id=1, source_target_pairs={{0,14},{2,0},{4,2},{6,4},{8,6},{10,8},{12,10},{14,12},{1,15},{3,1}... | collective-permute-start | bytes 786440 | tf_op jit(solution)/shard_map/sum_layers/ppermute | solution.py:25
  52.7 10.8 %collective-permute-start.12 = (bf16[128,1024]{1,0:T(8,128)(2,1)S(1)}, bf16[128,1024]{1,0:T(8,128)(2,1)S(1)}, u32[]{:S(2)}, u32[]{:S(2)}) collective-permute-start(bf16[128,1024]{1,0:T(8,128)(2,1)S(1)} %fusion.5), channel_id=1, source_target_pairs={{0,2},{2,4},{4,6},{6,8},{8,10},{10,12},{12,14},{14,0},{1,3},{3,5},... | collective-permute-start | bytes 786440 | tf_op jit(solution)/shard_map/sum_layers/ppermute | solution.py:25
  57.1 10.8 %collective-permute-start.16 = (bf16[128,1024]{1,0:T(8,128)(2,1)S(1)}, bf16[128,1024]{1,0:T(8,128)(2,1)S(1)}, u32[]{:S(2)}, u32[]{:S(2)}) collective-permute-start(bf16[128,1024]{1,0:T(8,128)(2,1)S(1)} %fusion.8), channel_id=1, source_target_pairs={{0,14},{2,0},{4,2},{6,4},{8,6},{10,8},{12,10},{14,12},{1,15},{3,1}... | collective-permute-start | bytes 786440 | tf_op jit(solution)/shard_map/sum_layers/ppermute | solution.py:25
  58.3 10.8 %collective-permute-start.20 = (bf16[128,1024]{1,0:T(8,128)(2,1)S(1)}, bf16[128,1024]{1,0:T(8,128)(2,1)S(1)}, u32[]{:S(2)}, u32[]{:S(2)}) collective-permute-start(bf16[128,1024]{1,0:T(8,128)(2,1)S(1)} %fusion.11), channel_id=1, source_target_pairs={{0,2},{2,4},{4,6},{6,8},{8,10},{10,12},{12,14},{14,0},{1,3},{3,5},... | collective-permute-start | bytes 786440 | tf_op jit(solution)/shard_map/sum_layers/ppermute | solution.py:25
  62.7 10.8 %collective-permute-start.24 = (bf16[128,1024]{1,0:T(8,128)(2,1)S(1)}, bf16[128,1024]{1,0:T(8,128)(2,1)S(1)}, u32[]{:S(2)}, u32[]{:S(2)}) collective-permute-start(bf16[128,1024]{1,0:T(8,128)(2,1)S(1)} %fusion.14), channel_id=1, source_target_pairs={{0,14},{2,0},{4,2},{6,4},{8,6},{10,8},{12,10},{14,12},{1,15},{3,1}... | collective-permute-start | bytes 786440 | tf_op jit(solution)/shard_map/sum_layers/ppermute | solution.py:25
  63.9 10.8 %collective-permute-start.13 = (bf16[128,1024]{1,0:T(8,128)(2,1)S(1)}, bf16[128,1024]{1,0:T(8,128)(2,1)S(1)}, u32[]{:S(2)}, u32[]{:S(2)}) collective-permute-start(bf16[128,1024]{1,0:T(8,128)(2,1)S(1)} %fusion.4), channel_id=1, source_target_pairs={{0,2},{2,4},{4,6},{6,8},{8,10},{10,12},{12,14},{14,0},{1,3},{3,5},... | collective-permute-start | bytes 786440 | tf_op jit(solution)/shard_map/sum_layers/ppermute | solution.py:25
  68.3 10.6 %collective-permute-start.17 = (bf16[128,1024]{1,0:T(8,128)(2,1)S(1)}, bf16[128,1024]{1,0:T(8,128)(2,1)S(1)}, u32[]{:S(2)}, u32[]{:S(2)}) collective-permute-start(bf16[128,1024]{1,0:T(8,128)(2,1)S(1)} %fusion.7), channel_id=1, source_target_pairs={{0,14},{2,0},{4,2},{6,4},{8,6},{10,8},{12,10},{14,12},{1,15},{3,1}... | collective-permute-start | bytes 786440 | tf_op jit(solution)/shard_map/sum_layers/ppermute | solution.py:25
  69.5 9.9 %collective-permute-start.21 = (bf16[128,1024]{1,0:T(8,128)(2,1)S(1)}, bf16[128,1024]{1,0:T(8,128)(2,1)S(1)}, u32[]{:S(2)}, u32[]{:S(2)}) collective-permute-start(bf16[128,1024]{1,0:T(8,128)(2,1)S(1)} %fusion.10), channel_id=1, source_target_pairs={{0,2},{2,4},{4,6},{6,8},{8,10},{10,12},{12,14},{14,0},{1,3},{3,5},... | collective-permute-start | bytes 786440 | tf_op jit(solution)/shard_map/sum_layers/ppermute | solution.py:25
  74.0 7.8 %collective-permute-start.25 = (bf16[128,1024]{1,0:T(8,128)(2,1)S(1)}, bf16[128,1024]{1,0:T(8,128)(2,1)S(1)}, u32[]{:S(2)}, u32[]{:S(2)}) collective-permute-start(bf16[128,1024]{1,0:T(8,128)(2,1)S(1)} %fusion.13), channel_id=1, source_target_pairs={{0,14},{2,0},{4,2},{6,4},{8,6},{10,8},{12,10},{14,12},{1,15},{3,1}... | collective-permute-start | bytes 786440 | tf_op jit(solution)/shard_map/sum_layers/ppermute | solution.py:25
  79.4 10.4 %copy-start.2 = (s32[1024]{0:T(1024)S(1)}, s32[1024]{0:T(1024)}, u32[]{:S(2)}) copy-start(s32[1024]{0:T(1024)} %param.12) | copy-start | bytes 12292
  82.2 36.9 %copy-start.3 = (s32[64]{0:T(128)S(1)}, s32[64]{0:T(128)}, u32[]{:S(2)}) copy-start(s32[64]{0:T(128)} %param.13) | copy-start | bytes 772
  83.1 16.8 %all-to-all-start = ((bf16[16,8,2048]{2,1,0:T(8,128)(2,1)}), bf16[16,8,2048]{2,1,0:T(8,128)(2,1)S(1)}, u32[]{:S(2)}, u32[]{:S(2)}) async-start(bf16[16,8,2048]{2,1,0:T(8,128)(2,1)} %maximum_bitcast_fusion), calls=%async_computation | async-start | bytes 1048576 | tf_op jit(solution)/shard_map/to_components/all_to_all | solution.py:229
  102.1 11.3 %all-to-all-start.2 = ((f32[32,1,256]{2,1,0:T(1,128)}), f32[32,1,256]{2,1,0:T(1,128)S(1)}, u32[]{:S(2)}, u32[]{:S(2)}) async-start(f32[32,1,256]{2,1,0:T(1,128)} %fit.1), calls=%async_computation.2 | async-start | bytes 65536 | tf_op jit(solution)/shard_map/gather_scores/all_to_all | solution.py:234
  113.4 5.5 %collective-permute-start.26 = (f32[256]{0:T(256)S(1)}, f32[256]{0:T(256)S(1)}, u32[]{:S(2)}, u32[]{:S(2)}) collective-permute-start(f32[256]{0:T(256)S(1)} %reduce_sum.9), channel_id=1, source_target_pairs={{0,2},{2,4},{4,6},{6,8},{8,10},{10,12},{12,14},{3,1},{5,3},{7,5},{... | collective-permute-start | bytes 3080 | tf_op jit(solution)/shard_map/gather_scores/ppermute | solution.py:237

commit v9 on v8

--- a/solution.py
+++ b/solution.py
@@ -25,28 +25,101 @@
     return lax.ppermute(value, axis, [(i, (i + by) % peers) for i in range(peers)])
 
 
-def weigh_kernel(resp_ref, weight_ref, trait_ref, out_ref):
-    rows = resp_ref.shape[0]
+CUT = 64
+EXTRA = 16
+
+
+def weigh_kernel(resp_ref, weight_ref, trait_ref, values_ref, first_ref, second_ref):
     trait = trait_ref[...]
-    for at in range(0, rows, 16):
+    width = trait.shape[1]
+    upper = lax.broadcasted_iota(jnp.int32, (8, width), 0) < 4
+    for at in range(0, resp_ref.shape[0], 16):
         root = jnp.sqrt(weight_ref[at : at + 16, :].astype(jnp.float32))
         weighted = root * resp_ref[at : at + 16, :].astype(jnp.float32)
         design = root * trait
-        upper = lax.broadcasted_iota(jnp.int32, (8, root.shape[1]), 0) < 4
         tiles = []
         for half in (0, 8):
             a, b = weighted[half : half + 8], design[half : half + 8]
             tiles.append(jnp.where(upper, a, pltpu.roll(b, 4, 0)))
             tiles.append(jnp.where(upper, pltpu.roll(a, 4, 0), b))
-        out_ref[2 * at : 2 * at + 32, :] = jnp.concatenate(tiles, axis=0).astype(jnp.bfloat16)
-
-
-def weigh(responses, weights, phenotype):
+        out_ref, base = (first_ref, 0) if 2 * at < CUT else (second_ref, CUT)
+        out_ref[2 * at - base : 2 * at - base + 32, :] = jnp.concatenate(tiles, axis=0).astype(
+            jnp.bfloat16
+        )
+    rest = values_ref[...]
+    row = lax.broadcasted_iota(jnp.int32, (EXTRA, width), 0)
+    parts = jnp.zeros((EXTRA, width), jnp.float32)
+    for k in range(3):
+        part = rest.astype(jnp.bfloat16).astype(jnp.float32)
+        parts = jnp.where(row == k, part, parts)
+        rest = rest - part
+    bottom = second_ref.shape[0] - EXTRA
+    second_ref[bottom:, :] = parts.astype(jnp.bfloat16)
+
+
+def weigh(responses, weights, phenotype, eigvals):
     rows, width = responses.shape
     return pl.pallas_call(
         weigh_kernel,
-        out_shape=jax.ShapeDtypeStruct((2 * rows, width), jnp.bfloat16),
-    )(responses, weights, phenotype[None, :])
+        out_shape=[
+            jax.ShapeDtypeStruct((CUT, width), jnp.bfloat16),
+            jax.ShapeDtypeStruct((2 * rows - CUT + EXTRA, width), jnp.bfloat16),
+        ],
+    )(responses, weights, phenotype[None, :], eigvals[None, :])
+
+
+def stack_kernel(ahead_ref, chip_ref, *refs):
+    *pieces, _, blocks_ref, values_ref, parts_ref, sems = refs
+    rows = blocks_ref.shape[1]
+    copies = []
+    for place in range(8):
+        at, given = 0, pieces[place * 2 : place * 2 + 2] if place < 7 else pieces[14:]
+        for piece in given:
+            count = min(piece.shape[0], rows - at)
+            sem = sems.at[len(copies)]
+            copies.append(
+                pltpu.make_async_copy(
+                    piece.at[pl.ds(0, count)],
+                    blocks_ref.at[ahead_ref[place], pl.ds(at, count)],
+                    sem,
+                )
+            )
+            at += count
+        sem = sems.at[len(copies)]
+        copies.append(
+            pltpu.make_async_copy(
+                given[-1].at[pl.ds(given[-1].shape[0] - EXTRA, EXTRA)],
+                parts_ref.at[chip_ref[place]],
+                sem,
+            )
+        )
+    for copy in copies:
+        copy.start()
+    for copy in copies:
+        copy.wait()
+    for chip in range(8):
+        parts = parts_ref[chip].astype(jnp.float32)
+        values_ref[chip : chip + 1, :] = parts[0:1] + parts[1:2] + parts[2:3]
+
+
+def stack(ahead, chip, pieces, last, rows):
+    width = pieces[0].shape[1]
+    smem = pl.BlockSpec(memory_space=pltpu.SMEM)
+    anywhere = pl.BlockSpec(memory_space=pl.ANY)
+    return pl.pallas_call(
+        stack_kernel,
+        out_shape=[
+            jax.ShapeDtypeStruct((8, rows, width), jnp.bfloat16),
+            jax.ShapeDtypeStruct((8, width), jnp.float32),
+        ],
+        in_specs=[smem, smem] + [anywhere] * (len(pieces) + 1),
+        out_specs=[anywhere, pl.BlockSpec(memory_space=pltpu.VMEM)],
+        scratch_shapes=[
+            pltpu.VMEM((8, EXTRA, width), jnp.bfloat16),
+            pltpu.SemaphoreType.DMA((len(pieces) + 8,)),
+        ],
+        compiler_params=pltpu.CompilerParams(vmem_limit_bytes=4 * 1024 * 1024),
+    )(ahead, chip, *pieces, last)
 
 
 def fit_kernel(slot_ref, sums_ref, values_ref, out_ref, r_ref, d_ref, w_ref):
@@ -126,24 +199,26 @@
     )(slot, sums, values)
 
 
-def gather_plane(own, other):
+def gather_plane(halves):
     x, y = "samp_1", "samp_0"
-    left = shifted(own, x, 1)
-    right = shifted(own, x, -1)
-    over = shifted(own, y, 1)
-    far = shifted(left, x, 1)
-    over_right = shifted(over, x, -1)
-    over_left = shifted(left, y, 1)
-    over_far = jnp.concatenate(
-        [
-            shifted(over_left[:48], x, 1),
-            shifted(over_right[48:96], x, -1),
-            shifted(far[96:], y, 1),
-        ],
-        axis=0,
-    )
-    over_far = over_far + 0 * other[: own.shape[0]]
-    return jnp.stack([own, right, far, left, over, over_right, over_far, over_left])
+    got = []
+    for own in halves:
+        left = shifted(own, x, 1)
+        right = shifted(own, x, -1)
+        over = shifted(own, y, 1)
+        got.append([own, right, None, left, over, None, None])
+    for each in got:
+        _, _, _, left, over, _, _ = each
+        each[2] = shifted(left, x, 1)
+        each[5] = shifted(over, x, -1)
+        each[6] = shifted(left, y, 1)
+    first, second = got
+    farthest = [
+        shifted(first[6], x, 1),
+        shifted(second[5][:48], x, -1),
+        shifted(second[2][48:], y, 1),
+    ]
+    return [piece for place in zip(first, second) for piece in place] + farthest
 
 
 def smooth_block(widened, places, present, reaches):
@@ -179,20 +254,19 @@
         other = shifted(eigvecs, "samp_2", 1)
         vecs = (eigvecs, other)
     with jax.named_scope("weigh"):
-        own = weigh(responses, weights, phenotype)
+        halves = weigh(responses, weights, phenotype, eigvals)
+    rows = 2 * responses.shape[0]
     with jax.named_scope("gather_rows"):
-        blocks = gather_plane(own, other)
+        place = jnp.array([0, 1, 2, 3, 4, 5, 7, 6], jnp.int32)
+        chip = (4 * (y ^ (place // 4)) + (x + place) % 4).astype(jnp.int32)
+        ahead = ((chip - z) % layers).astype(jnp.int32)
+        blocks, values = stack(ahead, chip, gather_plane(halves), other, rows)
     with jax.named_scope("gather_values"):
-        everywhere = copies(eigvals, SAMP).reshape(-1, 2, eigvals.shape[0])
-        everywhere = jnp.where(lax.axis_index("samp_2") == 0, everywhere, everywhere[:, ::-1])
-        everywhere = jnp.repeat(everywhere.reshape(everywhere.shape[0], -1), 4, axis=0)
-    rows = own.shape[0]
+        values = jnp.concatenate([values, shifted(values, "samp_2", 1)], axis=1)
+        everywhere = jnp.repeat(values, 4, axis=0)
 
     def term(q, ahead, lo, hi):
-        dest = lax.rem(z + ahead + layers, layers)
-        across, along = dest // 4, lax.rem(dest, 4)
-        place = 4 * (across ^ y) + lax.rem(along - x + 4, 4)
-        block = lax.dynamic_index_in_dim(blocks, place, 0, keepdims=False)[lo:hi]
+        block = blocks[ahead % layers, lo:hi]
         return jnp.dot(block, vecs[q], preferred_element_type=jnp.float32)
 
     far = layers // 2

time: 120 us -> 126 us (1.050)
  the two profiles are of different devices: /device:TPU:96 before, /device:TPU:24 now
where the time goes in v9:
time: 126 us; the launch traced here: 125 us
  starting transfers between devices  61.9 us (49%)
  waiting for transfers between devices  41 us (33%)
  matrix products  8.2 us (7%)
  Pallas kernels  7.99 us (6%)
  local copies, waits for them, and re-layouts  2.81 us (2%)
  other arithmetic  2.3 us (2%)
    ppermute x33, starting transfers between devices, shifted(): lax.ppermute(value, axis, [(i, (i + by) % peers) for i in range(peers)])  48.2 us
    ppermute x33, waiting for transfers between devices, shifted(): lax.ppermute(value, axis, [(i, (i + by) % peers) for i in range(peers)])  25.6 us
    dot_general x18, matrix products, term(): return jnp.dot(block, vecs[q], preferred_element_type=jnp.float32)  8.2 us
    all_to_all x1, waiting for transfers between devices, shards(): sums = lax.all_to_all(whole, PLANE, 0, 0, tiled=True)  6.49 us
    all_to_all x1, starting transfers between devices, shards(): sums = lax.all_to_all(whole, PLANE, 0, 0, tiled=True)  6.4 us
    all_to_all x1, starting transfers between devices, shards(): lax.all_to_all(fitted, LAYER, 0, 0, tiled=True)  6.02 us
    all_to_all x1, waiting for transfers between devices, shards(): lax.all_to_all(fitted, LAYER, 0, 0, tiled=True)  5.39 us
    pallas_call x1, Pallas kernels, stack(): pl.pallas_call(stack_kernel, out_shape=[jax.ShapeDtypeStruct((8, rows, wi...  4 us
  transfers between devices with their start and end apart: 36, of which 16 were waited for; matrix products, arithmetic and copies ran while one was open for 6% of the time, Pallas kernels for 1%

profile of v9, /device:TPU:24, one launch (start us, length us, event | category | flops | bytes accessed | tf_op | source)
XLA Modules:
  0.0 125.3 jit_solution(2437956531366899412)
XLA Ops:
  0.7 1.8 %weigh.1 = (bf16[64,1024]{1,0:T(8,128)(2,1)}, bf16[80,1024]{1,0:T(8,128)(2,1)}) custom-call(bf16[64,1024]{1,0:T(8,128)(2,1)} %resp_ref.1, bf16[64,1024]{1,0:T(8,128)(2,1)} %weight_ref.1, f32[1,1024]{1,0:T(1,128)} %bitcast.70, f32[1,1024]{1,0:T(1,128)} %bitcast.71), custom_call_target="tpu_custom_call" | custom-call | tf_op jit(solution)/shard_map/weigh/pallas_call | solution.py:62
  2.5 1.5 %collective-permute-start.4 = (bf16[80,1024]{1,0:T(8,128)(2,1)}, bf16[80,1024]{1,0:T(8,128)(2,1)S(1)}, u32[]{:S(2)}, u32[]{:S(2)}) collective-permute-start(bf16[80,1024]{1,0:T(8,128)(2,1)} %get-tuple-element.7.refs_1_), channel_id=1, source_target_pairs={{0,32},{32,64},{64,96},{96,0},{1,33},{33,65},{65,97},{97,1},{2,34}... | collective-permute-start | bytes 491528 | tf_op jit(solution)/shard_map/gather_rows/ppermute | solution.py:25
  4.0 0.7 collective-permute-start.7
  4.8 1.7 %collective-permute-start = (bf16[64,1024]{1,0:T(8,128)(2,1)}, bf16[64,1024]{1,0:T(8,128)(2,1)S(1)}, u32[]{:S(2)}, u32[]{:S(2)}) collective-permute-start(bf16[64,1024]{1,0:T(8,128)(2,1)} %get-tuple-element.6.refs_0_), channel_id=1, source_target_pairs={{0,96},{32,0},{64,32},{96,64},{1,97},{33,1},{65,33},{97,65},{2,98}... | collective-permute-start | bytes 393224 | tf_op jit(solution)/shard_map/gather_rows/ppermute | solution.py:25
  6.8 4.1 %collective-permute-done.4.refs_7_ = bf16[80,1024]{1,0:T(8,128)(2,1)S(1)} collective-permute-done((bf16[80,1024]{1,0:T(8,128)(2,1)}, bf16[80,1024]{1,0:T(8,128)(2,1)S(1)}, u32[]{:S(2)}, u32[]{:S(2)}) %collective-permute-start.4) | collective-permute-done | bytes 163872 | tf_op jit(solution)/shard_map/gather_rows/ppermute | solution.py:25
  11.2 2.9 %collective-permute-start.9 = (bf16[80,1024]{1,0:T(8,128)(2,1)S(1)}, bf16[80,1024]{1,0:T(8,128)(2,1)S(1)}, u32[]{:S(2)}, u32[]{:S(2)}) collective-permute-start(bf16[80,1024]{1,0:T(8,128)(2,1)S(1)} %collective-permute-done.7.refs_9_), channel_id=1, source_target_pairs={{0,96},{32,0},{64,32},{96,64},{1,97},{33,1},{65,33},{97,65},{2,98}... | collective-permute-start | bytes 491528 | tf_op jit(solution)/shard_map/gather_rows/ppermute | solution.py:25
  14.1 0.4 collective-permute-start.6
  14.5 0.8 collective-permute-start.1
  15.3 4.0 %collective-permute-done.6.refs_8_ = bf16[64,1024]{1,0:T(8,128)(2,1)S(1)} collective-permute-done((bf16[64,1024]{1,0:T(8,128)(2,1)}, bf16[64,1024]{1,0:T(8,128)(2,1)S(1)}, u32[]{:S(2)}, u32[]{:S(2)}) %collective-permute-start.6) | collective-permute-done | bytes 131104 | tf_op jit(solution)/shard_map/gather_rows/ppermute | solution.py:25
  19.3 0.4 collective-permute-start.10
  19.7 3.2 %collective-permute-start.8 = (bf16[64,1024]{1,0:T(8,128)(2,1)S(1)}, bf16[64,1024]{1,0:T(8,128)(2,1)}, u32[]{:S(2)}, u32[]{:S(2)}) collective-permute-start(bf16[64,1024]{1,0:T(8,128)(2,1)S(1)} %collective-permute-done.6.refs_8_), channel_id=1, source_target_pairs={{0,96},{32,0},{64,32},{96,64},{1,97},{33,1},{65,33},{97,65},{2,98}... | collective-permute-start | bytes 393224 | tf_op jit(solution)/shard_map/gather_rows/ppermute | solution.py:25
  23.0 1.7 %collective-permute-start.11 = (bf16[80,1024]{1,0:T(8,128)(2,1)S(1)}, bf16[80,1024]{1,0:T(8,128)(2,1)S(1)}, u32[]{:S(2)}, u32[]{:S(2)}) collective-permute-start(bf16[80,1024]{1,0:T(8,128)(2,1)S(1)} %collective-permute-done.4.refs_7_), channel_id=1, source_target_pairs={{0,128},{128,0},{1,129},{129,1},{2,130},{130,2},{3,131},{131,3},{4... | collective-permute-start | bytes 491528 | tf_op jit(solution)/shard_map/gather_rows/ppermute | solution.py:25
  24.7 0.7 collective-permute-done.10.refs_12_
  25.4 1.2 collective-permute-done.3.refs_4_
  26.6 2.0 %collective-permute-start.13 = (bf16[48,1024]{1,0:T(8,128)(2,1)S(1)}, bf16[48,1024]{1,0:T(8,128)(2,1)S(1)}, u32[]{:S(2)}, u32[]{:S(2)}) collective-permute-start(bf16[48,1024]{1,0:T(8,128)(2,1)S(1)} %slice.274), channel_id=1, source_target_pairs={{0,96},{32,0},{64,32},{96,64},{1,97},{33,1},{65,33},{97,65},{2,98}... | collective-permute-start | bytes 294920 | tf_op jit(solution)/shard_map/gather_rows/ppermute | solution.py:25
  29.0 0.7 and_select_fusion
  29.7 1.8 %collective-permute-done.12.refs_14_ = bf16[64,1024]{1,0:T(8,128)(2,1)S(1)} collective-permute-done((bf16[64,1024]{1,0:T(8,128)(2,1)S(1)}, bf16[64,1024]{1,0:T(8,128)(2,1)S(1)}, u32[]{:S(2)}, u32[]{:S(2)}) %collective-permute-start.12) | collective-permute-done | bytes 131104 | tf_op jit(solution)/shard_map/gather_rows/ppermute | solution.py:25
  31.5 1.3 %collective-permute-done.14.refs_16_ = bf16[32,1024]{1,0:T(8,128)(2,1)S(1)} collective-permute-done((bf16[32,1024]{1,0:T(8,128)(2,1)S(1)}, bf16[32,1024]{1,0:T(8,128)(2,1)S(1)}, u32[]{:S(2)}, u32[]{:S(2)}) %collective-permute-start.14) | collective-permute-done | bytes 65568 | tf_op jit(solution)/shard_map/gather_rows/ppermute | solution.py:25
  32.9 0.9 copy-done
  33.8 0.9 copy-done.1
  34.7 4.0 %gather_rows.1 = (bf16[8,128,1024]{2,1,0:T(8,128)(2,1)S(1)}, f32[8,1024]{1,0:T(8,128)S(1)}) custom-call(s32[8]{0:T(128)S(1)} %get-tuple-element.10.ahead_ref, s32[8]{0:T(128)S(1)} %get-tuple-element.11.chip_ref, bf16[64,1024]{1,0:T(8,128)(2,1)S(1)} %copy-done.1, bf16[80,1024]{1,0:T(8,128)(2,1)S(1)} %copy-done, ...), custom_call_target="tpu_custom_call" | custom-call | tf_op jit(solution)/shard_map/gather_rows/pallas_call | solution.py:109
  38.7 0.5 convolution_convert_fusion.2
  39.2 0.5 convolution_convert_fusion.3
  39.7 0.5 convolution_convert_fusion
  40.2 5.9 %collective-permute-start.28 = (bf16[64,1024]{1,0:T(8,128)(2,1)S(1)}, bf16[64,1024]{1,0:T(8,128)(2,1)S(1)}, u32[]{:S(2)}, u32[]{:S(2)}) collective-permute-start(bf16[64,1024]{1,0:T(8,128)(2,1)S(1)} %convolution_convert_fusion), channel_id=1, source_target_pairs={{0,14},{2,0},{4,2},{6,4},{8,6},{10,8},{12,10},{14,12},{1,15},{3,1}... | collective-permute-start | bytes 393224 | tf_op jit(solution)/shard_map/sum_layers/ppermute | solution.py:25
  46.1 0.5 convolution_convert_fusion.1
  46.7 3.2 %collective-permute-start.20 = (bf16[64,1024]{1,0:T(8,128)(2,1)S(1)}, bf16[64,1024]{1,0:T(8,128)(2,1)S(1)}, u32[]{:S(2)}, u32[]{:S(2)}) collective-permute-start(bf16[64,1024]{1,0:T(8,128)(2,1)S(1)} %convolution_convert_fusion.2), channel_id=1, source_target_pairs={{0,14},{2,0},{4,2},{6,4},{8,6},{10,8},{12,10},{14,12},{1,15},{3,1}... | collective-permute-start | bytes 393224 | tf_op jit(solution)/shard_map/sum_layers/ppermute | solution.py:25
  49.9 0.4 fusion.15
  50.4 3.3 %collective-permute-start.29 = (bf16[128,1024]{1,0:T(8,128)(2,1)S(1)}, bf16[128,1024]{1,0:T(8,128)(2,1)S(1)}, u32[]{:S(2)}, u32[]{:S(2)}) collective-permute-start(bf16[128,1024]{1,0:T(8,128)(2,1)S(1)} %fusion.15), channel_id=1, source_target_pairs={{0,14},{2,0},{4,2},{6,4},{8,6},{10,8},{12,10},{14,12},{1,15},{3,1}... | collective-permute-start | bytes 786440 | tf_op jit(solution)/shard_map/sum_layers/ppermute | solution.py:25
  53.7 0.4 fusion.12
  54.3 0.4 fusion.9
  54.7 3.3 %collective-permute-start.21 = (bf16[128,1024]{1,0:T(8,128)(2,1)S(1)}, bf16[128,1024]{1,0:T(8,128)(2,1)S(1)}, u32[]{:S(2)}, u32[]{:S(2)}) collective-permute-start(bf16[128,1024]{1,0:T(8,128)(2,1)S(1)} %fusion.9), channel_id=1, source_target_pairs={{0,14},{2,0},{4,2},{6,4},{8,6},{10,8},{12,10},{14,12},{1,15},{3,1}... | collective-permute-start | bytes 786440 | tf_op jit(solution)/shard_map/sum_layers/ppermute | solution.py:25
  58.0 0.4 fusion.6
  58.5 1.9 %collective-permute-done.29 = bf16[128,1024]{1,0:T(8,128)(2,1)S(1)} collective-permute-done((bf16[128,1024]{1,0:T(8,128)(2,1)S(1)}, bf16[128,1024]{1,0:T(8,128)(2,1)S(1)}, u32[]{:S(2)}, u32[]{:S(2)}) %collective-permute-start.29) | collective-permute-done | bytes 262176 | tf_op jit(solution)/shard_map/sum_layers/ppermute | solution.py:25
  60.5 0.4 fusion.14
  60.9 3.8 %collective-permute-start.30 = (bf16[128,1024]{1,0:T(8,128)(2,1)S(1)}, bf16[128,1024]{1,0:T(8,128)(2,1)S(1)}, u32[]{:S(2)}, u32[]{:S(2)}) collective-permute-start(bf16[128,1024]{1,0:T(8,128)(2,1)S(1)} %fusion.14), channel_id=1, source_target_pairs={{0,14},{2,0},{4,2},{6,4},{8,6},{10,8},{12,10},{14,12},{1,15},{3,1}... | collective-permute-start | bytes 786440 | tf_op jit(solution)/shard_map/sum_layers/ppermute | solution.py:25
  64.7 0.4 fusion.11
  65.2 0.8 collective-permute-done.21
  66.1 0.4 fusion.8
  66.5 4.0 %collective-permute-start.22 = (bf16[128,1024]{1,0:T(8,128)(2,1)S(1)}, bf16[128,1024]{1,0:T(8,128)(2,1)S(1)}, u32[]{:S(2)}, u32[]{:S(2)}) collective-permute-start(bf16[128,1024]{1,0:T(8,128)(2,1)S(1)} %fusion.8), channel_id=1, source_target_pairs={{0,14},{2,0},{4,2},{6,4},{8,6},{10,8},{12,10},{14,12},{1,15},{3,1}... | collective-permute-start | bytes 786440 | tf_op jit(solution)/shard_map/sum_layers/ppermute | solution.py:25
  70.5 0.4 fusion.5
  71.1 0.6 collective-permute-done.30
  71.7 0.4 fusion.13
  72.1 3.8 %collective-permute-start.31 = (bf16[128,1024]{1,0:T(8,128)(2,1)S(1)}, bf16[128,1024]{1,0:T(8,128)(2,1)S(1)}, u32[]{:S(2)}, u32[]{:S(2)}) collective-permute-start(bf16[128,1024]{1,0:T(8,128)(2,1)S(1)} %fusion.13), channel_id=1, source_target_pairs={{0,14},{2,0},{4,2},{6,4},{8,6},{10,8},{12,10},{14,12},{1,15},{3,1}... | collective-permute-start | bytes 786440 | tf_op jit(solution)/shard_map/sum_layers/ppermute | solution.py:25
  75.9 0.4 fusion.10
  76.5 0.8 collective-permute-done.22
  77.3 0.4 fusion.7
  77.8 3.8 %collective-permute-start.23 = (bf16[128,1024]{1,0:T(8,128)(2,1)S(1)}, bf16[128,1024]{1,0:T(8,128)(2,1)S(1)}, u32[]{:S(2)}, u32[]{:S(2)}) collective-permute-start(bf16[128,1024]{1,0:T(8,128)(2,1)S(1)} %fusion.7), channel_id=1, source_target_pairs={{0,14},{2,0},{4,2},{6,4},{8,6},{10,8},{12,10},{14,12},{1,15},{3,1}... | collective-permute-start | bytes 786440 | tf_op jit(solution)/shard_map/sum_layers/ppermute | solution.py:25
  81.5 0.4 fusion.4
  82.1 3.1 %collective-permute-done.27 = bf16[128,1024]{1,0:T(8,128)(2,1)S(1)} collective-permute-done((bf16[128,1024]{1,0:T(8,128)(2,1)S(1)}, bf16[128,1024]{1,0:T(8,128)(2,1)S(1)}, u32[]{:S(2)}, u32[]{:S(2)}) %collective-permute-start.27) | collective-permute-done | bytes 262176 | tf_op jit(solution)/shard_map/sum_layers/ppermute | solution.py:25
  85.2 0.5 fusion.3
  85.7 4.0 %collective-permute-done.19 = bf16[128,1024]{1,0:T(8,128)(2,1)S(1)} collective-permute-done((bf16[128,1024]{1,0:T(8,128)(2,1)S(1)}, bf16[128,1024]{1,0:T(8,128)(2,1)S(1)}, u32[]{:S(2)}, u32[]{:S(2)}) %collective-permute-start.19) | collective-permute-done | bytes 262176 | tf_op jit(solution)/shard_map/sum_layers/ppermute | solution.py:25
  89.7 0.5 fusion.2
  90.1 0.8 maximum_bitcast_fusion
  91.0 6.4 %all-to-all-start = ((bf16[16,8,2048]{2,1,0:T(8,128)(2,1)}), bf16[16,8,2048]{2,1,0:T(8,128)(2,1)S(1)}, u32[]{:S(2)}, u32[]{:S(2)}) async-start(bf16[16,8,2048]{2,1,0:T(8,128)(2,1)} %maximum_bitcast_fusion), calls=%async_computation | async-start | bytes 1048576 | tf_op jit(solution)/shard_map/to_components/all_to_all | solution.py:303
  97.4 1.1 collective-permute-done.32
  98.7 6.5 %all-to-all-done = bf16[16,8,2048]{2,1,0:T(8,128)(2,1)S(1)} async-done(((bf16[16,8,2048]{2,1,0:T(8,128)(2,1)}), bf16[16,8,2048]{2,1,0:T(8,128)(2,1)S(1)}, u32[]{:S(2)}, u32[]{:S(2)}) %all-to-all-start) | async-done | bytes 524320 | tf_op jit(solution)/shard_map/to_components/all_to_all | solution.py:303
  105.2 2.2 %fit.1 = f32[32,1,256]{2,1,0:T(1,128)} custom-call(s32[1]{0:T(128)} %bitcast.slot_ref, bf16[128,2048]{1,0:T(8,128)(2,1)S(1)} %bitcast.69, f32[32,2048]{1,0:T(8,128)S(1)} %reshape.9.values_ref), custom_call_target="tpu_custom_call" | custom-call | tf_op jit(solution)/shard_map/fit/pallas_call | solution.py:192
  107.4 6.0 %all-to-all-start.1 = ((f32[32,1,256]{2,1,0:T(1,128)}), f32[32,1,256]{2,1,0:T(1,128)S(1)}, u32[]{:S(2)}, u32[]{:S(2)}) async-start(f32[32,1,256]{2,1,0:T(1,128)} %fit.1), calls=%async_computation.1 | async-start | bytes 65536 | tf_op jit(solution)/shard_map/gather_scores/all_to_all | solution.py:308
  113.5 5.4 %all-to-all-done.1 = f32[32,1,256]{2,1,0:T(1,128)S(1)} async-done(((f32[32,1,256]{2,1,0:T(1,128)}), f32[32,1,256]{2,1,0:T(1,128)S(1)}, u32[]{:S(2)}, u32[]{:S(2)}) %all-to-all-start.1) | async-done | bytes 32800 | tf_op jit(solution)/shard_map/gather_scores/all_to_all | solution.py:308
  119.0 1.3 %collective-permute-start.33 = (f32[256]{0:T(256)S(1)}, f32[256]{0:T(256)S(1)}, u32[]{:S(2)}, u32[]{:S(2)}) collective-permute-start(f32[256]{0:T(256)S(1)} %reduce_sum.9), channel_id=1, source_target_pairs={{0,2},{2,4},{4,6},{6,8},{8,10},{10,12},{12,14},{3,1},{5,3},{7,5},{... | collective-permute-start | bytes 3080 | tf_op jit(solution)/shard_map/gather_scores/ppermute | solution.py:311
  120.3 0.6 dynamic_slice.11
  120.9 3.6 %collective-permute-done.33 = f32[256]{0:T(256)S(1)} collective-permute-done((f32[256]{0:T(256)S(1)}, f32[256]{0:T(256)S(1)}, u32[]{:S(2)}, u32[]{:S(2)}) %collective-permute-start.33) | collective-permute-done | bytes 1056 | tf_op jit(solution)/shard_map/gather_scores/ppermute | solution.py:311
  124.7 0.6 add_divide_fusion
  (56 shorter events, 2.3 us)
Async XLA Ops:
  0.6 32.2 %collective-permute-start.15 = (bf16[1024,1024]{1,0:T(8,128)(2,1)}, bf16[1024,1024]{1,0:T(8,128)(2,1)S(1)}, u32[]{:S(2)}, u32[]{:S(2)}) collective-permute-start(bf16[1024,1024]{1,0:T(8,128)(2,1)} %param.11), channel_id=1, source_target_pairs={{0,16},{16,0},{1,17},{17,1},{2,18},{18,2},{3,19},{19,3},{4,20},{20... | collective-permute-start | bytes 6291464 | tf_op jit(solution)/shard_map/swap_eigvecs/ppermute | solution.py:25
  2.5 8.3 %collective-permute-start.4 = (bf16[80,1024]{1,0:T(8,128)(2,1)}, bf16[80,1024]{1,0:T(8,128)(2,1)S(1)}, u32[]{:S(2)}, u32[]{:S(2)}) collective-permute-start(bf16[80,1024]{1,0:T(8,128)(2,1)} %get-tuple-element.7.refs_1_), channel_id=1, source_target_pairs={{0,32},{32,64},{64,96},{96,0},{1,33},{33,65},{65,97},{97,1},{2,34}... | collective-permute-start | bytes 491528 | tf_op jit(solution)/shard_map/gather_rows/ppermute | solution.py:25
  4.0 7.2 %collective-permute-start.7 = (bf16[80,1024]{1,0:T(8,128)(2,1)}, bf16[80,1024]{1,0:T(8,128)(2,1)S(1)}, u32[]{:S(2)}, u32[]{:S(2)}) collective-permute-start(bf16[80,1024]{1,0:T(8,128)(2,1)} %get-tuple-element.7.refs_1_), channel_id=1, source_target_pairs={{0,128},{128,0},{1,129},{129,1},{2,130},{130,2},{3,131},{131,3},{4... | collective-permute-start | bytes 491528 | tf_op jit(solution)/shard_map/gather_rows/ppermute | solution.py:25
  4.8 9.3 %collective-permute-start = (bf16[64,1024]{1,0:T(8,128)(2,1)}, bf16[64,1024]{1,0:T(8,128)(2,1)S(1)}, u32[]{:S(2)}, u32[]{:S(2)}) collective-permute-start(bf16[64,1024]{1,0:T(8,128)(2,1)} %get-tuple-element.6.refs_0_), channel_id=1, source_target_pairs={{0,96},{32,0},{64,32},{96,64},{1,97},{33,1},{65,33},{97,65},{2,98}... | collective-permute-start | bytes 393224 | tf_op jit(solution)/shard_map/gather_rows/ppermute | solution.py:25
  6.5 8.0 %collective-permute-start.2 = (bf16[64,1024]{1,0:T(8,128)(2,1)}, bf16[64,1024]{1,0:T(8,128)(2,1)S(1)}, u32[]{:S(2)}, u32[]{:S(2)}) collective-permute-start(bf16[64,1024]{1,0:T(8,128)(2,1)} %get-tuple-element.6.refs_0_), channel_id=1, source_target_pairs={{0,32},{32,64},{64,96},{96,0},{1,33},{33,65},{65,97},{97,1},{2,34}... | collective-permute-start | bytes 393224 | tf_op jit(solution)/shard_map/gather_rows/ppermute | solution.py:25
  10.9 8.9 %collective-permute-start.5 = (bf16[80,1024]{1,0:T(8,128)(2,1)S(1)}, bf16[80,1024]{1,0:T(8,128)(2,1)S(1)}, u32[]{:S(2)}, u32[]{:S(2)}) collective-permute-start(bf16[80,1024]{1,0:T(8,128)(2,1)S(1)} %collective-permute-done.4.refs_7_), channel_id=1, source_target_pairs={{0,32},{32,64},{64,96},{96,0},{1,33},{33,65},{65,97},{97,1},{2,34}... | collective-permute-start | bytes 491528 | tf_op jit(solution)/shard_map/gather_rows/ppermute | solution.py:25
  11.2 8.5 %collective-permute-start.9 = (bf16[80,1024]{1,0:T(8,128)(2,1)S(1)}, bf16[80,1024]{1,0:T(8,128)(2,1)S(1)}, u32[]{:S(2)}, u32[]{:S(2)}) collective-permute-start(bf16[80,1024]{1,0:T(8,128)(2,1)S(1)} %collective-permute-done.7.refs_9_), channel_id=1, source_target_pairs={{0,96},{32,0},{64,32},{96,64},{1,97},{33,1},{65,33},{97,65},{2,98}... | collective-permute-start | bytes 491528 | tf_op jit(solution)/shard_map/gather_rows/ppermute | solution.py:25
  14.1 5.2 %collective-permute-start.6 = (bf16[64,1024]{1,0:T(8,128)(2,1)}, bf16[64,1024]{1,0:T(8,128)(2,1)S(1)}, u32[]{:S(2)}, u32[]{:S(2)}) collective-permute-start(bf16[64,1024]{1,0:T(8,128)(2,1)} %get-tuple-element.6.refs_0_), channel_id=1, source_target_pairs={{0,128},{128,0},{1,129},{129,1},{2,130},{130,2},{3,131},{131,3},{4... | collective-permute-start | bytes 393224 | tf_op jit(solution)/shard_map/gather_rows/ppermute | solution.py:25
  14.5 8.4 %collective-permute-start.1 = (bf16[80,1024]{1,0:T(8,128)(2,1)}, bf16[80,1024]{1,0:T(8,128)(2,1)S(1)}, u32[]{:S(2)}, u32[]{:S(2)}) collective-permute-start(bf16[80,1024]{1,0:T(8,128)(2,1)} %get-tuple-element.7.refs_1_), channel_id=1, source_target_pairs={{0,96},{32,0},{64,32},{96,64},{1,97},{33,1},{65,33},{97,65},{2,98}... | collective-permute-start | bytes 491528 | tf_op jit(solution)/shard_map/gather_rows/ppermute | solution.py:25
  19.3 6.1 %collective-permute-start.10 = (bf16[64,1024]{1,0:T(8,128)(2,1)S(1)}, bf16[64,1024]{1,0:T(8,128)(2,1)S(1)}, u32[]{:S(2)}, u32[]{:S(2)}) collective-permute-start(bf16[64,1024]{1,0:T(8,128)(2,1)S(1)} %collective-permute-done.2.refs_6_), channel_id=1, source_target_pairs={{0,128},{128,0},{1,129},{129,1},{2,130},{130,2},{3,131},{131,3},{4... | collective-permute-start | bytes 393224 | tf_op jit(solution)/shard_map/gather_rows/ppermute | solution.py:25
  19.7 6.9 %collective-permute-start.3 = (bf16[64,1024]{1,0:T(8,128)(2,1)S(1)}, bf16[64,1024]{1,0:T(8,128)(2,1)}, u32[]{:S(2)}, u32[]{:S(2)}) collective-permute-start(bf16[64,1024]{1,0:T(8,128)(2,1)S(1)} %collective-permute-done.2.refs_6_), channel_id=1, source_target_pairs={{0,32},{32,64},{64,96},{96,0},{1,33},{33,65},{65,97},{97,1},{2,34}... | collective-permute-start | bytes 393224 | tf_op jit(solution)/shard_map/gather_rows/ppermute | solution.py:25
  19.7 8.9 %collective-permute-start.8 = (bf16[64,1024]{1,0:T(8,128)(2,1)S(1)}, bf16[64,1024]{1,0:T(8,128)(2,1)}, u32[]{:S(2)}, u32[]{:S(2)}) collective-permute-start(bf16[64,1024]{1,0:T(8,128)(2,1)S(1)} %collective-permute-done.6.refs_8_), channel_id=1, source_target_pairs={{0,96},{32,0},{64,32},{96,64},{1,97},{33,1},{65,33},{97,65},{2,98}... | collective-permute-start | bytes 393224 | tf_op jit(solution)/shard_map/gather_rows/ppermute | solution.py:25
  23.0 6.7 %collective-permute-start.11 = (bf16[80,1024]{1,0:T(8,128)(2,1)S(1)}, bf16[80,1024]{1,0:T(8,128)(2,1)S(1)}, u32[]{:S(2)}, u32[]{:S(2)}) collective-permute-start(bf16[80,1024]{1,0:T(8,128)(2,1)S(1)} %collective-permute-done.4.refs_7_), channel_id=1, source_target_pairs={{0,128},{128,0},{1,129},{129,1},{2,130},{130,2},{3,131},{131,3},{4... | collective-permute-start | bytes 491528 | tf_op jit(solution)/shard_map/gather_rows/ppermute | solution.py:25
  25.4 6.2 %collective-permute-start.12 = (bf16[64,1024]{1,0:T(8,128)(2,1)S(1)}, bf16[64,1024]{1,0:T(8,128)(2,1)S(1)}, u32[]{:S(2)}, u32[]{:S(2)}) collective-permute-start(bf16[64,1024]{1,0:T(8,128)(2,1)S(1)} %collective-permute-done.10.refs_12_), channel_id=1, source_target_pairs={{0,32},{32,64},{64,96},{96,0},{1,33},{33,65},{65,97},{97,1},{2,34}... | collective-permute-start | bytes 393224 | tf_op jit(solution)/shard_map/gather_rows/ppermute | solution.py:25
  26.6 6.3 %collective-permute-start.13 = (bf16[48,1024]{1,0:T(8,128)(2,1)S(1)}, bf16[48,1024]{1,0:T(8,128)(2,1)S(1)}, u32[]{:S(2)}, u32[]{:S(2)}) collective-permute-start(bf16[48,1024]{1,0:T(8,128)(2,1)S(1)} %slice.274), channel_id=1, source_target_pairs={{0,96},{32,0},{64,32},{96,64},{1,97},{33,1},{65,33},{97,65},{2,98}... | collective-permute-start | bytes 294920 | tf_op jit(solution)/shard_map/gather_rows/ppermute | solution.py:25
  28.6 4.3 %collective-permute-start.14 = (bf16[32,1024]{1,0:T(8,128)(2,1)S(1)}, bf16[32,1024]{1,0:T(8,128)(2,1)S(1)}, u32[]{:S(2)}, u32[]{:S(2)}) collective-permute-start(bf16[32,1024]{1,0:T(8,128)(2,1)S(1)} %slice.275), channel_id=1, source_target_pairs={{0,128},{128,0},{1,129},{129,1},{2,130},{130,2},{3,131},{131,3},{4... | collective-permute-start | bytes 196616 | tf_op jit(solution)/shard_map/gather_rows/ppermute | solution.py:25
  32.9 0.9 copy-start
  33.8 0.9 copy-start.1
  34.7 4.0 %copy-start.2 = (bf16[1024,1024]{1,0:T(8,128)(2,1)S(1)}, bf16[1024,1024]{1,0:T(8,128)(2,1)}, u32[]{:S(2)}) copy-start(bf16[1024,1024]{1,0:T(8,128)(2,1)} %param.11) | copy-start | bytes 6291460
  40.2 9.7 %collective-permute-start.28 = (bf16[64,1024]{1,0:T(8,128)(2,1)S(1)}, bf16[64,1024]{1,0:T(8,128)(2,1)S(1)}, u32[]{:S(2)}, u32[]{:S(2)}) collective-permute-start(bf16[64,1024]{1,0:T(8,128)(2,1)S(1)} %convolution_convert_fusion), channel_id=1, source_target_pairs={{0,14},{2,0},{4,2},{6,4},{8,6},{10,8},{12,10},{14,12},{1,15},{3,1}... | collective-permute-start | bytes 393224 | tf_op jit(solution)/shard_map/sum_layers/ppermute | solution.py:25
  46.6 7.1 %collective-permute-start.24 = (bf16[64,1024]{1,0:T(8,128)(2,1)S(1)}, bf16[64,1024]{1,0:T(8,128)(2,1)S(1)}, u32[]{:S(2)}, u32[]{:S(2)}) collective-permute-start(bf16[64,1024]{1,0:T(8,128)(2,1)S(1)} %convolution_convert_fusion.1), channel_id=1, source_target_pairs={{0,2},{2,4},{4,6},{6,8},{8,10},{10,12},{12,14},{14,0},{1,3},{3,5},... | collective-permute-start | bytes 393224 | tf_op jit(solution)/shard_map/sum_layers/ppermute | solution.py:25
  46.7 7.5 %collective-permute-start.20 = (bf16[64,1024]{1,0:T(8,128)(2,1)S(1)}, bf16[64,1024]{1,0:T(8,128)(2,1)S(1)}, u32[]{:S(2)}, u32[]{:S(2)}) collective-permute-start(bf16[64,1024]{1,0:T(8,128)(2,1)S(1)} %convolution_convert_fusion.2), channel_id=1, source_target_pairs={{0,14},{2,0},{4,2},{6,4},{8,6},{10,8},{12,10},{14,12},{1,15},{3,1}... | collective-permute-start | bytes 393224 | tf_op jit(solution)/shard_map/sum_layers/ppermute | solution.py:25
  49.9 8.1 %collective-permute-start.16 = (bf16[64,1024]{1,0:T(8,128)(2,1)S(1)}, bf16[64,1024]{1,0:T(8,128)(2,1)S(1)}, u32[]{:S(2)}, u32[]{:S(2)}) collective-permute-start(bf16[64,1024]{1,0:T(8,128)(2,1)S(1)} %convolution_convert_fusion.3), channel_id=1, source_target_pairs={{0,2},{2,4},{4,6},{6,8},{8,10},{10,12},{12,14},{14,0},{1,3},{3,5},... | collective-permute-start | bytes 393224 | tf_op jit(solution)/shard_map/sum_layers/ppermute | solution.py:25
  50.4 10.1 %collective-permute-start.29 = (bf16[128,1024]{1,0:T(8,128)(2,1)S(1)}, bf16[128,1024]{1,0:T(8,128)(2,1)S(1)}, u32[]{:S(2)}, u32[]{:S(2)}) collective-permute-start(bf16[128,1024]{1,0:T(8,128)(2,1)S(1)} %fusion.15), channel_id=1, source_target_pairs={{0,14},{2,0},{4,2},{6,4},{8,6},{10,8},{12,10},{14,12},{1,15},{3,1}... | collective-permute-start | bytes 786440 | tf_op jit(solution)/shard_map/sum_layers/ppermute | solution.py:25
  54.2 10.5 %collective-permute-start.25 = (bf16[128,1024]{1,0:T(8,128)(2,1)S(1)}, bf16[128,1024]{1,0:T(8,128)(2,1)S(1)}, u32[]{:S(2)}, u32[]{:S(2)}) collective-permute-start(bf16[128,1024]{1,0:T(8,128)(2,1)S(1)} %fusion.12), channel_id=1, source_target_pairs={{0,2},{2,4},{4,6},{6,8},{8,10},{10,12},{12,14},{14,0},{1,3},{3,5},... | collective-permute-start | bytes 786440 | tf_op jit(solution)/shard_map/sum_layers/ppermute | solution.py:25
  54.7 11.4 %collective-permute-start.21 = (bf16[128,1024]{1,0:T(8,128)(2,1)S(1)}, bf16[128,1024]{1,0:T(8,128)(2,1)S(1)}, u32[]{:S(2)}, u32[]{:S(2)}) collective-permute-start(bf16[128,1024]{1,0:T(8,128)(2,1)S(1)} %fusion.9), channel_id=1, source_target_pairs={{0,14},{2,0},{4,2},{6,4},{8,6},{10,8},{12,10},{14,12},{1,15},{3,1}... | collective-permute-start | bytes 786440 | tf_op jit(solution)/shard_map/sum_layers/ppermute | solution.py:25
  58.5 12.1 %collective-permute-start.17 = (bf16[128,1024]{1,0:T(8,128)(2,1)S(1)}, bf16[128,1024]{1,0:T(8,128)(2,1)S(1)}, u32[]{:S(2)}, u32[]{:S(2)}) collective-permute-start(bf16[128,1024]{1,0:T(8,128)(2,1)S(1)} %fusion.6), channel_id=1, source_target_pairs={{0,2},{2,4},{4,6},{6,8},{8,10},{10,12},{12,14},{14,0},{1,3},{3,5},... | collective-permute-start | bytes 786440 | tf_op jit(solution)/shard_map/sum_layers/ppermute | solution.py:25
  60.9 10.8 %collective-permute-start.30 = (bf16[128,1024]{1,0:T(8,128)(2,1)S(1)}, bf16[128,1024]{1,0:T(8,128)(2,1)S(1)}, u32[]{:S(2)}, u32[]{:S(2)}) collective-permute-start(bf16[128,1024]{1,0:T(8,128)(2,1)S(1)} %fusion.14), channel_id=1, source_target_pairs={{0,14},{2,0},{4,2},{6,4},{8,6},{10,8},{12,10},{14,12},{1,15},{3,1}... | collective-permute-start | bytes 786440 | tf_op jit(solution)/shard_map/sum_layers/ppermute | solution.py:25
  65.1 10.8 %collective-permute-start.26 = (bf16[128,1024]{1,0:T(8,128)(2,1)S(1)}, bf16[128,1024]{1,0:T(8,128)(2,1)S(1)}, u32[]{:S(2)}, u32[]{:S(2)}) collective-permute-start(bf16[128,1024]{1,0:T(8,128)(2,1)S(1)} %fusion.11), channel_id=1, source_target_pairs={{0,2},{2,4},{4,6},{6,8},{8,10},{10,12},{12,14},{14,0},{1,3},{3,5},... | collective-permute-start | bytes 786440 | tf_op jit(solution)/shard_map/sum_layers/ppermute | solution.py:25
  66.5 10.8 %collective-permute-start.22 = (bf16[128,1024]{1,0:T(8,128)(2,1)S(1)}, bf16[128,1024]{1,0:T(8,128)(2,1)S(1)}, u32[]{:S(2)}, u32[]{:S(2)}) collective-permute-start(bf16[128,1024]{1,0:T(8,128)(2,1)S(1)} %fusion.8), channel_id=1, source_target_pairs={{0,14},{2,0},{4,2},{6,4},{8,6},{10,8},{12,10},{14,12},{1,15},{3,1}... | collective-permute-start | bytes 786440 | tf_op jit(solution)/shard_map/sum_layers/ppermute | solution.py:25
  71.0 10.6 %collective-permute-start.18 = (bf16[128,1024]{1,0:T(8,128)(2,1)S(1)}, bf16[128,1024]{1,0:T(8,128)(2,1)S(1)}, u32[]{:S(2)}, u32[]{:S(2)}) collective-permute-start(bf16[128,1024]{1,0:T(8,128)(2,1)S(1)} %fusion.5), channel_id=1, source_target_pairs={{0,2},{2,4},{4,6},{6,8},{8,10},{10,12},{12,14},{14,0},{1,3},{3,5},... | collective-permute-start | bytes 786440 | tf_op jit(solution)/shard_map/sum_layers/ppermute | solution.py:25
  72.1 9.9 %collective-permute-start.31 = (bf16[128,1024]{1,0:T(8,128)(2,1)S(1)}, bf16[128,1024]{1,0:T(8,128)(2,1)S(1)}, u32[]{:S(2)}, u32[]{:S(2)}) collective-permute-start(bf16[128,1024]{1,0:T(8,128)(2,1)S(1)} %fusion.13), channel_id=1, source_target_pairs={{0,14},{2,0},{4,2},{6,4},{8,6},{10,8},{12,10},{14,12},{1,15},{3,1}... | collective-permute-start | bytes 786440 | tf_op jit(solution)/shard_map/sum_layers/ppermute | solution.py:25
  76.4 8.8 %collective-permute-start.27 = (bf16[128,1024]{1,0:T(8,128)(2,1)S(1)}, bf16[128,1024]{1,0:T(8,128)(2,1)S(1)}, u32[]{:S(2)}, u32[]{:S(2)}) collective-permute-start(bf16[128,1024]{1,0:T(8,128)(2,1)S(1)} %fusion.10), channel_id=1, source_target_pairs={{0,2},{2,4},{4,6},{6,8},{8,10},{10,12},{12,14},{14,0},{1,3},{3,5},... | collective-permute-start | bytes 786440 | tf_op jit(solution)/shard_map/sum_layers/ppermute | solution.py:25
  77.8 7.9 %collective-permute-start.23 = (bf16[128,1024]{1,0:T(8,128)(2,1)S(1)}, bf16[128,1024]{1,0:T(8,128)(2,1)S(1)}, u32[]{:S(2)}, u32[]{:S(2)}) collective-permute-start(bf16[128,1024]{1,0:T(8,128)(2,1)S(1)} %fusion.7), channel_id=1, source_target_pairs={{0,14},{2,0},{4,2},{6,4},{8,6},{10,8},{12,10},{14,12},{1,15},{3,1}... | collective-permute-start | bytes 786440 | tf_op jit(solution)/shard_map/sum_layers/ppermute | solution.py:25
  82.0 7.7 %collective-permute-start.19 = (bf16[128,1024]{1,0:T(8,128)(2,1)S(1)}, bf16[128,1024]{1,0:T(8,128)(2,1)S(1)}, u32[]{:S(2)}, u32[]{:S(2)}) collective-permute-start(bf16[128,1024]{1,0:T(8,128)(2,1)S(1)} %fusion.4), channel_id=1, source_target_pairs={{0,2},{2,4},{4,6},{6,8},{8,10},{10,12},{12,14},{14,0},{1,3},{3,5},... | collective-permute-start | bytes 786440 | tf_op jit(solution)/shard_map/sum_layers/ppermute | solution.py:25
  85.6 11.8 %copy-start.3 = (s32[1024]{0:T(1024)S(1)}, s32[1024]{0:T(1024)}, u32[]{:S(2)}) copy-start(s32[1024]{0:T(1024)} %param.13) | copy-start | bytes 12292
  90.1 34.5 %copy-start.4 = (s32[64]{0:T(128)S(1)}, s32[64]{0:T(128)}, u32[]{:S(2)}) copy-start(s32[64]{0:T(128)} %param.14) | copy-start | bytes 772
  91.0 14.2 %all-to-all-start = ((bf16[16,8,2048]{2,1,0:T(8,128)(2,1)}), bf16[16,8,2048]{2,1,0:T(8,128)(2,1)S(1)}, u32[]{:S(2)}, u32[]{:S(2)}) async-start(bf16[16,8,2048]{2,1,0:T(8,128)(2,1)} %maximum_bitcast_fusion), calls=%async_computation | async-start | bytes 1048576 | tf_op jit(solution)/shard_map/to_components/all_to_all | solution.py:303
  97.4 1.2 collective-permute-start.32
  107.4 11.5 %all-to-all-start.1 = ((f32[32,1,256]{2,1,0:T(1,128)}), f32[32,1,256]{2,1,0:T(1,128)S(1)}, u32[]{:S(2)}, u32[]{:S(2)}) async-start(f32[32,1,256]{2,1,0:T(1,128)} %fit.1), calls=%async_computation.1 | async-start | bytes 65536 | tf_op jit(solution)/shard_map/gather_scores/all_to_all | solution.py:308
  119.0 5.5 %collective-permute-start.33 = (f32[256]{0:T(256)S(1)}, f32[256]{0:T(256)S(1)}, u32[]{:S(2)}, u32[]{:S(2)}) collective-permute-start(f32[256]{0:T(256)S(1)} %reduce_sum.9), channel_id=1, source_target_pairs={{0,2},{2,4},{4,6},{6,8},{8,10},{10,12},{12,14},{3,1},{5,3},{7,5},{... | collective-permute-start | bytes 3080 | tf_op jit(solution)/shard_map/gather_scores/ppermute | solution.py:311

commit v10 on v8

--- a/solution.py
+++ b/solution.py
@@ -131,19 +131,20 @@
     left = shifted(own, x, 1)
     right = shifted(own, x, -1)
     over = shifted(own, y, 1)
+    floor = lax.axis_size(x)
+
+    def across(value, by):
+        pairs = [
+            (floor * v + u, floor * (1 - v) + (u + by) % floor) for v in (0, 1) for u in range(floor)
+        ]
+        return lax.ppermute(value, (y, x), pairs)
+
+    over_left = shifted(left, y, 1)
+    over_far = across(right, -1)
+    over_right = shifted(over, x, -1)
     far = shifted(left, x, 1)
-    over_right = shifted(over, x, -1)
-    over_left = shifted(left, y, 1)
-    over_far = jnp.concatenate(
-        [
-            shifted(over_left[:48], x, 1),
-            shifted(over_right[48:96], x, -1),
-            shifted(far[96:], y, 1),
-        ],
-        axis=0,
-    )
     over_far = over_far + 0 * other[: own.shape[0]]
-    return jnp.stack([own, right, far, left, over, over_right, over_far, over_left])
+    return jnp.stack([over_left, own, right, far, left, over, over_right, over_far])
 
 
 def smooth_block(widened, places, present, reaches):
@@ -191,7 +192,7 @@
     def term(q, ahead, lo, hi):
         dest = lax.rem(z + ahead + layers, layers)
         across, along = dest // 4, lax.rem(dest, 4)
-        place = 4 * (across ^ y) + lax.rem(along - x + 4, 4)
+        place = (4 * (across ^ y) + lax.rem(along - x + 4, 4) + 1) & 7
         block = lax.dynamic_index_in_dim(blocks, place, 0, keepdims=False)[lo:hi]
         return jnp.dot(block, vecs[q], preferred_element_type=jnp.float32)
 

time: 120 us -> 122 us (1.017)
  waiting for transfers between devices: 33.3 us -> 44.9 us
  local copies, waits for them, and re-layouts: 9.74 us -> 3.99 us
  starting transfers between devices: 59.7 us -> 57.3 us
    ppermute x26 -> x23, waiting for transfers between devices: 13.8 us -> 19.9 us  [shifted(): lax.ppermute(value, axis, [(i, (i + by) % peers) for i in range(peers)])]
    ppermute x0 -> x1, waiting for transfers between devices: none -> 5.44 us  [across(): return lax.ppermute(value, (y, x), pairs)]
    unnamed x15 -> x14, local copies, waits for them, and re-layouts: 6.27 us -> 1.27 us
    ppermute x26 -> x23, starting transfers between devices: 43.8 us -> 38.9 us  [shifted(): lax.ppermute(value, axis, [(i, (i + by) % peers) for i in range(peers)])]
    ppermute x0 -> x1, starting transfers between devices: none -> 2.45 us  [across(): return lax.ppermute(value, (y, x), pairs)]
  transfers between devices with their start and end apart: 30 -> 28, of which waited for: 15 -> 18; matrix products, arithmetic and copies ran while one was open for 17% -> 11% of each run, Pallas kernels for 2% -> 0%
where the time goes in v10:
time: 122 us
  starting transfers between devices  57.3 us (47%)
  waiting for transfers between devices  44.9 us (37%)
  matrix products  8.21 us (7%)
  Pallas kernels  4.01 us (3%)
  local copies, waits for them, and re-layouts  3.99 us (3%)
  other arithmetic  1.92 us (2%)
  between operations  1.38 us (1%)
    ppermute x23, starting transfers between devices, shifted(): lax.ppermute(value, axis, [(i, (i + by) % peers) for i in range(peers)])  38.9 us
    ppermute x23, waiting for transfers between devices, shifted(): lax.ppermute(value, axis, [(i, (i + by) % peers) for i in range(peers)])  19.9 us
    all_to_all x1, waiting for transfers between devices, shards(): sums = lax.all_to_all(whole, PLANE, 0, 0, tiled=True)  9.25 us
    dot_general x18, matrix products, term(): return jnp.dot(block, vecs[q], preferred_element_type=jnp.float32)  8.21 us
    all_to_all x1, waiting for transfers between devices, shards(): lax.all_to_all(fitted, LAYER, 0, 0, tiled=True)  7.32 us
    all_to_all x1, starting transfers between devices, shards(): sums = lax.all_to_all(whole, PLANE, 0, 0, tiled=True)  6.69 us
    ppermute x1, waiting for transfers between devices, across(): return lax.ppermute(value, (y, x), pairs)  5.44 us
    all_to_all x1, starting transfers between devices, shards(): lax.all_to_all(fitted, LAYER, 0, 0, tiled=True)  3.81 us
  transfers between devices with their start and end apart: 28, of which 18 were waited for; matrix products, arithmetic and copies ran while one was open for 11% of the time, Pallas kernels for 0%

profile of v10, /device:TPU:96, one launch (start us, length us, event | category | flops | bytes accessed | tf_op | source)
XLA Modules:
  0.0 121.7 jit_solution(8563086767804277979)
XLA Ops:
  0.6 1.8 %weigh.1 = bf16[128,1024]{1,0:T(8,128)(2,1)} custom-call(bf16[64,1024]{1,0:T(8,128)(2,1)} %resp_ref.1, bf16[64,1024]{1,0:T(8,128)(2,1)} %weight_ref.1, f32[1,1024]{1,0:T(1,128)} %bitcast.103), custom_call_target="tpu_custom_call" | custom-call | tf_op jit(solution)/shard_map/weigh/pallas_call | solution.py:46
  2.4 1.5 %collective-permute-start = (bf16[128,1024]{1,0:T(8,128)(2,1)}, bf16[128,1024]{1,0:T(8,128)(2,1)S(1)}, u32[]{:S(2)}, u32[]{:S(2)}) collective-permute-start(bf16[128,1024]{1,0:T(8,128)(2,1)} %weigh.1), channel_id=1, source_target_pairs={{0,32},{32,64},{64,96},{96,0},{1,33},{33,65},{65,97},{97,1},{2,34}... | collective-permute-start | bytes 786440 | tf_op jit(solution)/shard_map/gather_rows/ppermute | solution.py:25
  3.9 1.6 %collective-permute-start.4 = (bf16[128,1024]{1,0:T(8,128)(2,1)}, bf16[128,1024]{1,0:T(8,128)(2,1)S(1)}, u32[]{:S(2)}, u32[]{:S(2)}) collective-permute-start(bf16[128,1024]{1,0:T(8,128)(2,1)} %weigh.1), channel_id=1, source_target_pairs={{0,128},{128,0},{1,129},{129,1},{2,130},{130,2},{3,131},{131,3},{4... | collective-permute-start | bytes 786440 | tf_op jit(solution)/shard_map/gather_rows/ppermute | solution.py:25
  5.5 1.7 %collective-permute-start.2 = (bf16[128,1024]{1,0:T(8,128)(2,1)}, bf16[128,1024]{1,0:T(8,128)(2,1)S(1)}, u32[]{:S(2)}, u32[]{:S(2)}) collective-permute-start(bf16[128,1024]{1,0:T(8,128)(2,1)} %weigh.1), channel_id=1, source_target_pairs={{0,96},{32,0},{64,32},{96,64},{1,97},{33,1},{65,33},{97,65},{2,98}... | collective-permute-start | bytes 786440 | tf_op jit(solution)/shard_map/gather_rows/ppermute | solution.py:25
  7.3 4.6 %collective-permute-done = bf16[128,1024]{1,0:T(8,128)(2,1)S(1)} collective-permute-done((bf16[128,1024]{1,0:T(8,128)(2,1)}, bf16[128,1024]{1,0:T(8,128)(2,1)S(1)}, u32[]{:S(2)}, u32[]{:S(2)}) %collective-permute-start) | collective-permute-done | bytes 262176 | tf_op jit(solution)/shard_map/gather_rows/ppermute | solution.py:25
  11.9 1.6 %collective-permute-start.1 = (bf16[128,1024]{1,0:T(8,128)(2,1)S(1)}, bf16[128,1024]{1,0:T(8,128)(2,1)S(1)}, u32[]{:S(2)}, u32[]{:S(2)}) collective-permute-start(bf16[128,1024]{1,0:T(8,128)(2,1)S(1)} %collective-permute-done), channel_id=1, source_target_pairs={{0,128},{128,0},{1,129},{129,1},{2,130},{130,2},{3,131},{131,3},{4... | collective-permute-start | bytes 786440 | tf_op jit(solution)/shard_map/gather_rows/ppermute | solution.py:25
  13.5 1.3 %broadcast_in_dim.17 = f32[16,1,1024]{2,1,0:T(1,128)} broadcast(f32[1024]{0:T(1024)} %param.11), dimensions={2} | broadcast | bytes 69632 | tf_op jit(solution)/shard_map/gather_values/broadcast_in_dim | solution.py:172
  14.8 3.5 %all-to-all-start.1 = ((f32[16,1,1024]{2,1,0:T(1,128)}), f32[16,1,1024]{2,1,0:T(1,128)S(1)}, u32[]{:S(2)}, u32[]{:S(2)}) async-start(f32[16,1,1024]{2,1,0:T(1,128)} %broadcast_in_dim.17), calls=%async_computation.1 | async-start | bytes 131072 | tf_op jit(solution)/shard_map/gather_values/all_to_all | solution.py:171
  18.6 1.5 %collective-permute-start.3 = (bf16[128,1024]{1,0:T(8,128)(2,1)S(1)}, bf16[128,1024]{1,0:T(8,128)(2,1)S(1)}, u32[]{:S(2)}, u32[]{:S(2)}) collective-permute-start(bf16[128,1024]{1,0:T(8,128)(2,1)S(1)} %collective-permute-done), channel_id=1, source_target_pairs={{0,32},{32,64},{64,96},{96,0},{1,33},{33,65},{65,97},{97,1},{2,34}... | collective-permute-start | bytes 786440 | tf_op jit(solution)/shard_map/gather_rows/ppermute | solution.py:25
  20.1 1.8 %collective-permute-start.5 = (bf16[128,1024]{1,0:T(8,128)(2,1)S(1)}, bf16[128,1024]{1,0:T(8,128)(2,1)S(1)}, u32[]{:S(2)}, u32[]{:S(2)}) collective-permute-start(bf16[128,1024]{1,0:T(8,128)(2,1)S(1)} %collective-permute-done.4), channel_id=1, source_target_pairs={{0,96},{32,0},{64,32},{96,64},{1,97},{33,1},{65,33},{97,65},{2,98}... | collective-permute-start | bytes 786440 | tf_op jit(solution)/shard_map/gather_rows/ppermute | solution.py:25
  21.9 2.4 %collective-permute-start.6 = (bf16[128,1024]{1,0:T(8,128)(2,1)S(1)}, bf16[128,1024]{1,0:T(8,128)(2,1)S(1)}, u32[]{:S(2)}, u32[]{:S(2)}) collective-permute-start(bf16[128,1024]{1,0:T(8,128)(2,1)S(1)} %collective-permute-done.2), channel_id=1, source_target_pairs={{0,224},{32,128},{64,160},{96,192},{128,96},{160,0},{192,32},{224,... | collective-permute-start | bytes 786440 | tf_op jit(solution)/shard_map/gather_rows/ppermute | solution.py:140
  24.4 1.1 bitcast_dynamic-update-slice_fusion.5
  25.5 3.3 %collective-permute-done.3 = bf16[128,1024]{1,0:T(8,128)(2,1)S(1)} collective-permute-done((bf16[128,1024]{1,0:T(8,128)(2,1)S(1)}, bf16[128,1024]{1,0:T(8,128)(2,1)S(1)}, u32[]{:S(2)}, u32[]{:S(2)}) %collective-permute-start.3) | collective-permute-done | bytes 262176 | tf_op jit(solution)/shard_map/gather_rows/ppermute | solution.py:25
  29.0 0.4 collective-permute-done.5
  29.4 5.4 %collective-permute-done.6 = bf16[128,1024]{1,0:T(8,128)(2,1)S(1)} collective-permute-done((bf16[128,1024]{1,0:T(8,128)(2,1)S(1)}, bf16[128,1024]{1,0:T(8,128)(2,1)S(1)}, u32[]{:S(2)}, u32[]{:S(2)}) %collective-permute-start.6) | collective-permute-done | bytes 262176 | tf_op jit(solution)/shard_map/gather_rows/ppermute | solution.py:140
  34.9 0.5 convolution_convert_fusion.3
  35.4 3.2 %collective-permute-start.8 = (bf16[64,1024]{1,0:T(8,128)(2,1)S(1)}, bf16[64,1024]{1,0:T(8,128)(2,1)S(1)}, u32[]{:S(2)}, u32[]{:S(2)}) collective-permute-start(bf16[64,1024]{1,0:T(8,128)(2,1)S(1)} %convolution_convert_fusion.3), channel_id=1, source_target_pairs={{0,2},{2,4},{4,6},{6,8},{8,10},{10,12},{12,14},{14,0},{1,3},{3,5},... | collective-permute-start | bytes 393224 | tf_op jit(solution)/shard_map/sum_layers/ppermute | solution.py:25
  38.6 0.5 convolution_convert_fusion.2
  39.2 0.5 convolution_convert_fusion.1
  39.7 3.3 %collective-permute-start.16 = (bf16[64,1024]{1,0:T(8,128)(2,1)S(1)}, bf16[64,1024]{1,0:T(8,128)(2,1)S(1)}, u32[]{:S(2)}, u32[]{:S(2)}) collective-permute-start(bf16[64,1024]{1,0:T(8,128)(2,1)S(1)} %convolution_convert_fusion.1), channel_id=1, source_target_pairs={{0,2},{2,4},{4,6},{6,8},{8,10},{10,12},{12,14},{14,0},{1,3},{3,5},... | collective-permute-start | bytes 393224 | tf_op jit(solution)/shard_map/sum_layers/ppermute | solution.py:25
  43.0 0.5 convolution_convert_fusion
  43.5 0.5 add_convert_fusion.6
  44.0 3.5 %collective-permute-start.9 = (bf16[128,1024]{1,0:T(8,128)(2,1)S(1)}, bf16[128,1024]{1,0:T(8,128)(2,1)S(1)}, u32[]{:S(2)}, u32[]{:S(2)}) collective-permute-start(bf16[128,1024]{1,0:T(8,128)(2,1)S(1)} %add_convert_fusion.6), channel_id=1, source_target_pairs={{0,2},{2,4},{4,6},{6,8},{8,10},{10,12},{12,14},{14,0},{1,3},{3,5},... | collective-permute-start | bytes 786440 | tf_op jit(solution)/shard_map/sum_layers/ppermute | solution.py:25
  47.5 0.4 add_convert_fusion.3
  48.0 0.5 fusion.4
  48.5 3.3 %collective-permute-start.17 = (bf16[128,1024]{1,0:T(8,128)(2,1)S(1)}, bf16[128,1024]{1,0:T(8,128)(2,1)S(1)}, u32[]{:S(2)}, u32[]{:S(2)}) collective-permute-start(bf16[128,1024]{1,0:T(8,128)(2,1)S(1)} %fusion.4), channel_id=1, source_target_pairs={{0,2},{2,4},{4,6},{6,8},{8,10},{10,12},{12,14},{14,0},{1,3},{3,5},... | collective-permute-start | bytes 786440 | tf_op jit(solution)/shard_map/sum_layers/ppermute | solution.py:25
  51.8 0.4 fusion.7
  52.3 1.2 %collective-permute-done.9 = bf16[128,1024]{1,0:T(8,128)(2,1)S(1)} collective-permute-done((bf16[128,1024]{1,0:T(8,128)(2,1)S(1)}, bf16[128,1024]{1,0:T(8,128)(2,1)S(1)}, u32[]{:S(2)}, u32[]{:S(2)}) %collective-permute-start.9) | collective-permute-done | bytes 262176 | tf_op jit(solution)/shard_map/sum_layers/ppermute | solution.py:25
  53.6 0.4 add_convert_fusion.5
  54.0 3.8 %collective-permute-start.10 = (bf16[128,1024]{1,0:T(8,128)(2,1)S(1)}, bf16[128,1024]{1,0:T(8,128)(2,1)S(1)}, u32[]{:S(2)}, u32[]{:S(2)}) collective-permute-start(bf16[128,1024]{1,0:T(8,128)(2,1)S(1)} %add_convert_fusion.5), channel_id=1, source_target_pairs={{0,2},{2,4},{4,6},{6,8},{8,10},{10,12},{12,14},{14,0},{1,3},{3,5},... | collective-permute-start | bytes 786440 | tf_op jit(solution)/shard_map/sum_layers/ppermute | solution.py:25
  57.8 0.3 collective-permute-done.13
  58.1 0.4 add_convert_fusion.2
  58.7 0.5 collective-permute-done.17
  59.2 0.4 fusion.3
  59.6 3.8 %collective-permute-start.18 = (bf16[128,1024]{1,0:T(8,128)(2,1)S(1)}, bf16[128,1024]{1,0:T(8,128)(2,1)S(1)}, u32[]{:S(2)}, u32[]{:S(2)}) collective-permute-start(bf16[128,1024]{1,0:T(8,128)(2,1)S(1)} %fusion.3), channel_id=1, source_target_pairs={{0,2},{2,4},{4,6},{6,8},{8,10},{10,12},{12,14},{14,0},{1,3},{3,5},... | collective-permute-start | bytes 786440 | tf_op jit(solution)/shard_map/sum_layers/ppermute | solution.py:25
  63.4 0.3 collective-permute-done.21
  63.7 0.4 fusion.6
  64.3 0.5 collective-permute-done.10
  64.8 0.4 add_convert_fusion.4
  65.3 3.8 %collective-permute-start.11 = (bf16[128,1024]{1,0:T(8,128)(2,1)S(1)}, bf16[128,1024]{1,0:T(8,128)(2,1)S(1)}, u32[]{:S(2)}, u32[]{:S(2)}) collective-permute-start(bf16[128,1024]{1,0:T(8,128)(2,1)S(1)} %add_convert_fusion.4), channel_id=1, source_target_pairs={{0,2},{2,4},{4,6},{6,8},{8,10},{10,12},{12,14},{14,0},{1,3},{3,5},... | collective-permute-start | bytes 786440 | tf_op jit(solution)/shard_map/sum_layers/ppermute | solution.py:25
  69.0 0.3 collective-permute-done.14
  69.3 0.4 add_convert_fusion.1
  69.9 0.5 collective-permute-done.18
  70.4 0.4 fusion.2
  70.9 3.8 %collective-permute-start.19 = (bf16[128,1024]{1,0:T(8,128)(2,1)S(1)}, bf16[128,1024]{1,0:T(8,128)(2,1)S(1)}, u32[]{:S(2)}, u32[]{:S(2)}) collective-permute-start(bf16[128,1024]{1,0:T(8,128)(2,1)S(1)} %fusion.2), channel_id=1, source_target_pairs={{0,2},{2,4},{4,6},{6,8},{8,10},{10,12},{12,14},{14,0},{1,3},{3,5},... | collective-permute-start | bytes 786440 | tf_op jit(solution)/shard_map/sum_layers/ppermute | solution.py:25
  74.6 0.3 collective-permute-done.22
  75.0 0.4 fusion.5
  75.4 0.3 collective-permute-start.23
  75.7 0.3 collective-permute-done.11
  76.0 4.5 %collective-permute-done.15 = bf16[128,1024]{1,0:T(8,128)(2,1)S(1)} collective-permute-done((bf16[128,1024]{1,0:T(8,128)(2,1)S(1)}, bf16[128,1024]{1,0:T(8,128)(2,1)S(1)}, u32[]{:S(2)}, u32[]{:S(2)}) %collective-permute-start.15) | collective-permute-done | bytes 262176 | tf_op jit(solution)/shard_map/sum_layers/ppermute | solution.py:25
  80.6 0.5 add_convert_fusion
  81.1 2.6 %collective-permute-done.23 = bf16[128,1024]{1,0:T(8,128)(2,1)S(1)} collective-permute-done((bf16[128,1024]{1,0:T(8,128)(2,1)S(1)}, bf16[128,1024]{1,0:T(8,128)(2,1)S(1)}, u32[]{:S(2)}, u32[]{:S(2)}) %collective-permute-start.23) | collective-permute-done | bytes 262176 | tf_op jit(solution)/shard_map/sum_layers/ppermute | solution.py:25
  83.7 0.5 fusion.1
  84.2 0.9 maximum_bitcast_fusion
  85.0 6.7 %all-to-all-start = ((bf16[16,8,2048]{2,1,0:T(8,128)(2,1)}), bf16[16,8,2048]{2,1,0:T(8,128)(2,1)S(1)}, u32[]{:S(2)}, u32[]{:S(2)}) async-start(bf16[16,8,2048]{2,1,0:T(8,128)(2,1)} %maximum_bitcast_fusion), calls=%async_computation | async-start | bytes 1048576 | tf_op jit(solution)/shard_map/to_components/all_to_all | solution.py:230
  92.0 0.4 rev.3
  92.6 9.3 %all-to-all-done = bf16[16,8,2048]{2,1,0:T(8,128)(2,1)S(1)} async-done(((bf16[16,8,2048]{2,1,0:T(8,128)(2,1)}), bf16[16,8,2048]{2,1,0:T(8,128)(2,1)S(1)}, u32[]{:S(2)}, u32[]{:S(2)}) %all-to-all-start) | async-done | bytes 524320 | tf_op jit(solution)/shard_map/to_components/all_to_all | solution.py:230
  101.9 2.2 %fit.1 = f32[32,1,256]{2,1,0:T(1,128)} custom-call(s32[1]{0:T(128)} %bitcast.slot_ref, bf16[128,2048]{1,0:T(8,128)(2,1)S(1)} %bitcast.101, f32[32,2048]{1,0:T(8,128)S(1)} %reshape.26.values_ref), custom_call_target="tpu_custom_call" | custom-call | tf_op jit(solution)/shard_map/fit/pallas_call | solution.py:119
  104.1 3.8 %all-to-all-start.2 = ((f32[32,1,256]{2,1,0:T(1,128)}), f32[32,1,256]{2,1,0:T(1,128)S(1)}, u32[]{:S(2)}, u32[]{:S(2)}) async-start(f32[32,1,256]{2,1,0:T(1,128)} %fit.1), calls=%async_computation.2 | async-start | bytes 65536 | tf_op jit(solution)/shard_map/gather_scores/all_to_all | solution.py:235
  108.0 7.3 %all-to-all-done.2 = f32[32,1,256]{2,1,0:T(1,128)S(1)} async-done(((f32[32,1,256]{2,1,0:T(1,128)}), f32[32,1,256]{2,1,0:T(1,128)S(1)}, u32[]{:S(2)}, u32[]{:S(2)}) %all-to-all-start.2) | async-done | bytes 32800 | tf_op jit(solution)/shard_map/gather_scores/all_to_all | solution.py:235
  115.3 1.9 %collective-permute-start.24 = (f32[256]{0:T(256)S(1)}, f32[256]{0:T(256)S(1)}, u32[]{:S(2)}, u32[]{:S(2)}) collective-permute-start(f32[256]{0:T(256)S(1)} %reduce_sum.9), channel_id=1, source_target_pairs={{0,2},{2,4},{4,6},{6,8},{8,10},{10,12},{12,14},{3,1},{5,3},{7,5},{... | collective-permute-start | bytes 3080 | tf_op jit(solution)/shard_map/gather_scores/ppermute | solution.py:238
  117.3 0.6 dynamic_slice.54
  117.9 2.9 %collective-permute-done.24 = f32[256]{0:T(256)S(1)} collective-permute-done((f32[256]{0:T(256)S(1)}, f32[256]{0:T(256)S(1)}, u32[]{:S(2)}, u32[]{:S(2)}) %collective-permute-start.24) | collective-permute-done | bytes 1056 | tf_op jit(solution)/shard_map/gather_scores/ppermute | solution.py:238
  121.0 0.6 add_divide_fusion
  (45 shorter events, 1.6 us)
Async XLA Ops:
  2.4 9.5 %collective-permute-start = (bf16[128,1024]{1,0:T(8,128)(2,1)}, bf16[128,1024]{1,0:T(8,128)(2,1)S(1)}, u32[]{:S(2)}, u32[]{:S(2)}) collective-permute-start(bf16[128,1024]{1,0:T(8,128)(2,1)} %weigh.1), channel_id=1, source_target_pairs={{0,32},{32,64},{64,96},{96,0},{1,33},{33,65},{65,97},{97,1},{2,34}... | collective-permute-start | bytes 786440 | tf_op jit(solution)/shard_map/gather_rows/ppermute | solution.py:25
  3.9 30.9 %collective-permute-start.7 = (bf16[1024,1024]{1,0:T(8,128)(2,1)}, bf16[1024,1024]{1,0:T(8,128)(2,1)S(1)}, u32[]{:S(2)}, u32[]{:S(2)}) collective-permute-start(bf16[1024,1024]{1,0:T(8,128)(2,1)} %param.10), channel_id=1, source_target_pairs={{0,16},{16,0},{1,17},{17,1},{2,18},{18,2},{3,19},{19,3},{4,20},{20... | collective-permute-start | bytes 6291464 | tf_op jit(solution)/shard_map/swap_eigvecs/ppermute | solution.py:25
  3.9 16.2 %collective-permute-start.4 = (bf16[128,1024]{1,0:T(8,128)(2,1)}, bf16[128,1024]{1,0:T(8,128)(2,1)S(1)}, u32[]{:S(2)}, u32[]{:S(2)}) collective-permute-start(bf16[128,1024]{1,0:T(8,128)(2,1)} %weigh.1), channel_id=1, source_target_pairs={{0,128},{128,0},{1,129},{129,1},{2,130},{130,2},{3,131},{131,3},{4... | collective-permute-start | bytes 786440 | tf_op jit(solution)/shard_map/gather_rows/ppermute | solution.py:25
  5.5 16.4 %collective-permute-start.2 = (bf16[128,1024]{1,0:T(8,128)(2,1)}, bf16[128,1024]{1,0:T(8,128)(2,1)S(1)}, u32[]{:S(2)}, u32[]{:S(2)}) collective-permute-start(bf16[128,1024]{1,0:T(8,128)(2,1)} %weigh.1), channel_id=1, source_target_pairs={{0,96},{32,0},{64,32},{96,64},{1,97},{33,1},{65,33},{97,65},{2,98}... | collective-permute-start | bytes 786440 | tf_op jit(solution)/shard_map/gather_rows/ppermute | solution.py:25
  11.9 12.5 %collective-permute-start.1 = (bf16[128,1024]{1,0:T(8,128)(2,1)S(1)}, bf16[128,1024]{1,0:T(8,128)(2,1)S(1)}, u32[]{:S(2)}, u32[]{:S(2)}) collective-permute-start(bf16[128,1024]{1,0:T(8,128)(2,1)S(1)} %collective-permute-done), channel_id=1, source_target_pairs={{0,128},{128,0},{1,129},{129,1},{2,130},{130,2},{3,131},{131,3},{4... | collective-permute-start | bytes 786440 | tf_op jit(solution)/shard_map/gather_rows/ppermute | solution.py:25
  14.8 70.2 %all-to-all-start.1 = ((f32[16,1,1024]{2,1,0:T(1,128)}), f32[16,1,1024]{2,1,0:T(1,128)S(1)}, u32[]{:S(2)}, u32[]{:S(2)}) async-start(f32[16,1,1024]{2,1,0:T(1,128)} %broadcast_in_dim.17), calls=%async_computation.1 | async-start | bytes 131072 | tf_op jit(solution)/shard_map/gather_values/all_to_all | solution.py:171
  18.6 10.3 %collective-permute-start.3 = (bf16[128,1024]{1,0:T(8,128)(2,1)S(1)}, bf16[128,1024]{1,0:T(8,128)(2,1)S(1)}, u32[]{:S(2)}, u32[]{:S(2)}) collective-permute-start(bf16[128,1024]{1,0:T(8,128)(2,1)S(1)} %collective-permute-done), channel_id=1, source_target_pairs={{0,32},{32,64},{64,96},{96,0},{1,33},{33,65},{65,97},{97,1},{2,34}... | collective-permute-start | bytes 786440 | tf_op jit(solution)/shard_map/gather_rows/ppermute | solution.py:25
  20.1 9.2 %collective-permute-start.5 = (bf16[128,1024]{1,0:T(8,128)(2,1)S(1)}, bf16[128,1024]{1,0:T(8,128)(2,1)S(1)}, u32[]{:S(2)}, u32[]{:S(2)}) collective-permute-start(bf16[128,1024]{1,0:T(8,128)(2,1)S(1)} %collective-permute-done.4), channel_id=1, source_target_pairs={{0,96},{32,0},{64,32},{96,64},{1,97},{33,1},{65,33},{97,65},{2,98}... | collective-permute-start | bytes 786440 | tf_op jit(solution)/shard_map/gather_rows/ppermute | solution.py:25
  21.9 12.9 %collective-permute-start.6 = (bf16[128,1024]{1,0:T(8,128)(2,1)S(1)}, bf16[128,1024]{1,0:T(8,128)(2,1)S(1)}, u32[]{:S(2)}, u32[]{:S(2)}) collective-permute-start(bf16[128,1024]{1,0:T(8,128)(2,1)S(1)} %collective-permute-done.2), channel_id=1, source_target_pairs={{0,224},{32,128},{64,160},{96,192},{128,96},{160,0},{192,32},{224,... | collective-permute-start | bytes 786440 | tf_op jit(solution)/shard_map/gather_rows/ppermute | solution.py:140
  24.4 10.5 %copy-start = (bf16[1024,1024]{1,0:T(8,128)(2,1)S(1)}, bf16[1024,1024]{1,0:T(8,128)(2,1)}, u32[]{:S(2)}) copy-start(bf16[1024,1024]{1,0:T(8,128)(2,1)} %param.10) | copy-start | bytes 6291460
  35.4 8.2 %collective-permute-start.8 = (bf16[64,1024]{1,0:T(8,128)(2,1)S(1)}, bf16[64,1024]{1,0:T(8,128)(2,1)S(1)}, u32[]{:S(2)}, u32[]{:S(2)}) collective-permute-start(bf16[64,1024]{1,0:T(8,128)(2,1)S(1)} %convolution_convert_fusion.3), channel_id=1, source_target_pairs={{0,2},{2,4},{4,6},{6,8},{8,10},{10,12},{12,14},{14,0},{1,3},{3,5},... | collective-permute-start | bytes 393224 | tf_op jit(solution)/shard_map/sum_layers/ppermute | solution.py:25
  39.1 8.4 %collective-permute-start.12 = (bf16[64,1024]{1,0:T(8,128)(2,1)S(1)}, bf16[64,1024]{1,0:T(8,128)(2,1)S(1)}, u32[]{:S(2)}, u32[]{:S(2)}) collective-permute-start(bf16[64,1024]{1,0:T(8,128)(2,1)S(1)} %convolution_convert_fusion.2), channel_id=1, source_target_pairs={{0,14},{2,0},{4,2},{6,4},{8,6},{10,8},{12,10},{14,12},{1,15},{3,1}... | collective-permute-start | bytes 393224 | tf_op jit(solution)/shard_map/sum_layers/ppermute | solution.py:25
  39.7 8.4 %collective-permute-start.16 = (bf16[64,1024]{1,0:T(8,128)(2,1)S(1)}, bf16[64,1024]{1,0:T(8,128)(2,1)S(1)}, u32[]{:S(2)}, u32[]{:S(2)}) collective-permute-start(bf16[64,1024]{1,0:T(8,128)(2,1)S(1)} %convolution_convert_fusion.1), channel_id=1, source_target_pairs={{0,2},{2,4},{4,6},{6,8},{8,10},{10,12},{12,14},{14,0},{1,3},{3,5},... | collective-permute-start | bytes 393224 | tf_op jit(solution)/shard_map/sum_layers/ppermute | solution.py:25
  43.4 8.3 %collective-permute-start.20 = (bf16[64,1024]{1,0:T(8,128)(2,1)S(1)}, bf16[64,1024]{1,0:T(8,128)(2,1)S(1)}, u32[]{:S(2)}, u32[]{:S(2)}) collective-permute-start(bf16[64,1024]{1,0:T(8,128)(2,1)S(1)} %convolution_convert_fusion), channel_id=1, source_target_pairs={{0,14},{2,0},{4,2},{6,4},{8,6},{10,8},{12,10},{14,12},{1,15},{3,1}... | collective-permute-start | bytes 393224 | tf_op jit(solution)/shard_map/sum_layers/ppermute | solution.py:25
  44.0 9.6 %collective-permute-start.9 = (bf16[128,1024]{1,0:T(8,128)(2,1)S(1)}, bf16[128,1024]{1,0:T(8,128)(2,1)S(1)}, u32[]{:S(2)}, u32[]{:S(2)}) collective-permute-start(bf16[128,1024]{1,0:T(8,128)(2,1)S(1)} %add_convert_fusion.6), channel_id=1, source_target_pairs={{0,2},{2,4},{4,6},{6,8},{8,10},{10,12},{12,14},{14,0},{1,3},{3,5},... | collective-permute-start | bytes 786440 | tf_op jit(solution)/shard_map/sum_layers/ppermute | solution.py:25
  47.9 10.2 %collective-permute-start.13 = (bf16[128,1024]{1,0:T(8,128)(2,1)S(1)}, bf16[128,1024]{1,0:T(8,128)(2,1)S(1)}, u32[]{:S(2)}, u32[]{:S(2)}) collective-permute-start(bf16[128,1024]{1,0:T(8,128)(2,1)S(1)} %add_convert_fusion.3), channel_id=1, source_target_pairs={{0,14},{2,0},{4,2},{6,4},{8,6},{10,8},{12,10},{14,12},{1,15},{3,1}... | collective-permute-start | bytes 786440 | tf_op jit(solution)/shard_map/sum_layers/ppermute | solution.py:25
  48.5 10.7 %collective-permute-start.17 = (bf16[128,1024]{1,0:T(8,128)(2,1)S(1)}, bf16[128,1024]{1,0:T(8,128)(2,1)S(1)}, u32[]{:S(2)}, u32[]{:S(2)}) collective-permute-start(bf16[128,1024]{1,0:T(8,128)(2,1)S(1)} %fusion.4), channel_id=1, source_target_pairs={{0,2},{2,4},{4,6},{6,8},{8,10},{10,12},{12,14},{14,0},{1,3},{3,5},... | collective-permute-start | bytes 786440 | tf_op jit(solution)/shard_map/sum_layers/ppermute | solution.py:25
  52.2 11.5 %collective-permute-start.21 = (bf16[128,1024]{1,0:T(8,128)(2,1)S(1)}, bf16[128,1024]{1,0:T(8,128)(2,1)S(1)}, u32[]{:S(2)}, u32[]{:S(2)}) collective-permute-start(bf16[128,1024]{1,0:T(8,128)(2,1)S(1)} %fusion.7), channel_id=1, source_target_pairs={{0,14},{2,0},{4,2},{6,4},{8,6},{10,8},{12,10},{14,12},{1,15},{3,1}... | collective-permute-start | bytes 786440 | tf_op jit(solution)/shard_map/sum_layers/ppermute | solution.py:25
  54.0 10.8 %collective-permute-start.10 = (bf16[128,1024]{1,0:T(8,128)(2,1)S(1)}, bf16[128,1024]{1,0:T(8,128)(2,1)S(1)}, u32[]{:S(2)}, u32[]{:S(2)}) collective-permute-start(bf16[128,1024]{1,0:T(8,128)(2,1)S(1)} %add_convert_fusion.5), channel_id=1, source_target_pairs={{0,2},{2,4},{4,6},{6,8},{8,10},{10,12},{12,14},{14,0},{1,3},{3,5},... | collective-permute-start | bytes 786440 | tf_op jit(solution)/shard_map/sum_layers/ppermute | solution.py:25
  58.6 10.8 %collective-permute-start.14 = (bf16[128,1024]{1,0:T(8,128)(2,1)S(1)}, bf16[128,1024]{1,0:T(8,128)(2,1)S(1)}, u32[]{:S(2)}, u32[]{:S(2)}) collective-permute-start(bf16[128,1024]{1,0:T(8,128)(2,1)S(1)} %add_convert_fusion.2), channel_id=1, source_target_pairs={{0,14},{2,0},{4,2},{6,4},{8,6},{10,8},{12,10},{14,12},{1,15},{3,1}... | collective-permute-start | bytes 786440 | tf_op jit(solution)/shard_map/sum_layers/ppermute | solution.py:25
  59.6 10.8 %collective-permute-start.18 = (bf16[128,1024]{1,0:T(8,128)(2,1)S(1)}, bf16[128,1024]{1,0:T(8,128)(2,1)S(1)}, u32[]{:S(2)}, u32[]{:S(2)}) collective-permute-start(bf16[128,1024]{1,0:T(8,128)(2,1)S(1)} %fusion.3), channel_id=1, source_target_pairs={{0,2},{2,4},{4,6},{6,8},{8,10},{10,12},{12,14},{14,0},{1,3},{3,5},... | collective-permute-start | bytes 786440 | tf_op jit(solution)/shard_map/sum_layers/ppermute | solution.py:25
  64.2 10.8 %collective-permute-start.22 = (bf16[128,1024]{1,0:T(8,128)(2,1)S(1)}, bf16[128,1024]{1,0:T(8,128)(2,1)S(1)}, u32[]{:S(2)}, u32[]{:S(2)}) collective-permute-start(bf16[128,1024]{1,0:T(8,128)(2,1)S(1)} %fusion.6), channel_id=1, source_target_pairs={{0,14},{2,0},{4,2},{6,4},{8,6},{10,8},{12,10},{14,12},{1,15},{3,1}... | collective-permute-start | bytes 786440 | tf_op jit(solution)/shard_map/sum_layers/ppermute | solution.py:25
  65.3 10.8 %collective-permute-start.11 = (bf16[128,1024]{1,0:T(8,128)(2,1)S(1)}, bf16[128,1024]{1,0:T(8,128)(2,1)S(1)}, u32[]{:S(2)}, u32[]{:S(2)}) collective-permute-start(bf16[128,1024]{1,0:T(8,128)(2,1)S(1)} %add_convert_fusion.4), channel_id=1, source_target_pairs={{0,2},{2,4},{4,6},{6,8},{8,10},{10,12},{12,14},{14,0},{1,3},{3,5},... | collective-permute-start | bytes 786440 | tf_op jit(solution)/shard_map/sum_layers/ppermute | solution.py:25
  69.8 10.8 %collective-permute-start.15 = (bf16[128,1024]{1,0:T(8,128)(2,1)S(1)}, bf16[128,1024]{1,0:T(8,128)(2,1)S(1)}, u32[]{:S(2)}, u32[]{:S(2)}) collective-permute-start(bf16[128,1024]{1,0:T(8,128)(2,1)S(1)} %add_convert_fusion.1), channel_id=1, source_target_pairs={{0,14},{2,0},{4,2},{6,4},{8,6},{10,8},{12,10},{14,12},{1,15},{3,1}... | collective-permute-start | bytes 786440 | tf_op jit(solution)/shard_map/sum_layers/ppermute | solution.py:25
  70.9 10.2 %collective-permute-start.19 = (bf16[128,1024]{1,0:T(8,128)(2,1)S(1)}, bf16[128,1024]{1,0:T(8,128)(2,1)S(1)}, u32[]{:S(2)}, u32[]{:S(2)}) collective-permute-start(bf16[128,1024]{1,0:T(8,128)(2,1)S(1)} %fusion.2), channel_id=1, source_target_pairs={{0,2},{2,4},{4,6},{6,8},{8,10},{10,12},{12,14},{14,0},{1,3},{3,5},... | collective-permute-start | bytes 786440 | tf_op jit(solution)/shard_map/sum_layers/ppermute | solution.py:25
  75.4 8.3 %collective-permute-start.23 = (bf16[128,1024]{1,0:T(8,128)(2,1)S(1)}, bf16[128,1024]{1,0:T(8,128)(2,1)S(1)}, u32[]{:S(2)}, u32[]{:S(2)}) collective-permute-start(bf16[128,1024]{1,0:T(8,128)(2,1)S(1)} %fusion.5), channel_id=1, source_target_pairs={{0,14},{2,0},{4,2},{6,4},{8,6},{10,8},{12,10},{14,12},{1,15},{3,1}... | collective-permute-start | bytes 786440 | tf_op jit(solution)/shard_map/sum_layers/ppermute | solution.py:25
  81.1 10.7 %copy-start.1 = (s32[1024]{0:T(1024)S(1)}, s32[1024]{0:T(1024)}, u32[]{:S(2)}) copy-start(s32[1024]{0:T(1024)} %param.12) | copy-start | bytes 12292
  84.2 36.9 %copy-start.2 = (s32[64]{0:T(128)S(1)}, s32[64]{0:T(128)}, u32[]{:S(2)}) copy-start(s32[64]{0:T(128)} %param.13) | copy-start | bytes 772
  85.0 16.8 %all-to-all-start = ((bf16[16,8,2048]{2,1,0:T(8,128)(2,1)}), bf16[16,8,2048]{2,1,0:T(8,128)(2,1)S(1)}, u32[]{:S(2)}, u32[]{:S(2)}) async-start(bf16[16,8,2048]{2,1,0:T(8,128)(2,1)} %maximum_bitcast_fusion), calls=%async_computation | async-start | bytes 1048576 | tf_op jit(solution)/shard_map/to_components/all_to_all | solution.py:230
  104.1 11.2 %all-to-all-start.2 = ((f32[32,1,256]{2,1,0:T(1,128)}), f32[32,1,256]{2,1,0:T(1,128)S(1)}, u32[]{:S(2)}, u32[]{:S(2)}) async-start(f32[32,1,256]{2,1,0:T(1,128)} %fit.1), calls=%async_computation.2 | async-start | bytes 65536 | tf_op jit(solution)/shard_map/gather_scores/all_to_all | solution.py:235
  115.3 5.5 %collective-permute-start.24 = (f32[256]{0:T(256)S(1)}, f32[256]{0:T(256)S(1)}, u32[]{:S(2)}, u32[]{:S(2)}) collective-permute-start(f32[256]{0:T(256)S(1)} %reduce_sum.9), channel_id=1, source_target_pairs={{0,2},{2,4},{4,6},{6,8},{8,10},{10,12},{12,14},{3,1},{5,3},{7,5},{... | collective-permute-start | bytes 3080 | tf_op jit(solution)/shard_map/gather_scores/ppermute | solution.py:238

commit v11 on v10

--- a/solution.py
+++ b/solution.py
@@ -25,28 +25,39 @@
     return lax.ppermute(value, axis, [(i, (i + by) % peers) for i in range(peers)])
 
 
-def weigh_kernel(resp_ref, weight_ref, trait_ref, out_ref):
-    rows = resp_ref.shape[0]
+EXTRA = 16
+
+
+def weigh_kernel(resp_ref, weight_ref, trait_ref, values_ref, out_ref):
     trait = trait_ref[...]
-    for at in range(0, rows, 16):
+    width = trait.shape[1]
+    upper = lax.broadcasted_iota(jnp.int32, (8, width), 0) < 4
+    for at in range(0, resp_ref.shape[0], 16):
         root = jnp.sqrt(weight_ref[at : at + 16, :].astype(jnp.float32))
         weighted = root * resp_ref[at : at + 16, :].astype(jnp.float32)
         design = root * trait
-        upper = lax.broadcasted_iota(jnp.int32, (8, root.shape[1]), 0) < 4
         tiles = []
         for half in (0, 8):
             a, b = weighted[half : half + 8], design[half : half + 8]
             tiles.append(jnp.where(upper, a, pltpu.roll(b, 4, 0)))
             tiles.append(jnp.where(upper, pltpu.roll(a, 4, 0), b))
         out_ref[2 * at : 2 * at + 32, :] = jnp.concatenate(tiles, axis=0).astype(jnp.bfloat16)
-
-
-def weigh(responses, weights, phenotype):
+    rest = values_ref[...]
+    row = lax.broadcasted_iota(jnp.int32, (EXTRA, width), 0)
+    parts = jnp.zeros((EXTRA, width), jnp.float32)
+    for k in range(3):
+        part = rest.astype(jnp.bfloat16).astype(jnp.float32)
+        parts = jnp.where(row == k, part, parts)
+        rest = rest - part
+    out_ref[out_ref.shape[0] - EXTRA :, :] = parts.astype(jnp.bfloat16)
+
+
+def weigh(responses, weights, phenotype, eigvals):
     rows, width = responses.shape
     return pl.pallas_call(
         weigh_kernel,
-        out_shape=jax.ShapeDtypeStruct((2 * rows, width), jnp.bfloat16),
-    )(responses, weights, phenotype[None, :])
+        out_shape=jax.ShapeDtypeStruct((2 * rows + EXTRA, width), jnp.bfloat16),
+    )(responses, weights, phenotype[None, :], eigvals[None, :])
 
 
 def fit_kernel(slot_ref, sums_ref, values_ref, out_ref, r_ref, d_ref, w_ref):
@@ -180,20 +191,27 @@
         other = shifted(eigvecs, "samp_2", 1)
         vecs = (eigvecs, other)
     with jax.named_scope("weigh"):
-        own = weigh(responses, weights, phenotype)
+        own = weigh(responses, weights, phenotype, eigvals)
     with jax.named_scope("gather_rows"):
         blocks = gather_plane(own, other)
+    rows = own.shape[0] - EXTRA
+
+    def place(across, along):
+        return (4 * (across ^ y) + (along - x) % 4 + 1) % 8
+
     with jax.named_scope("gather_values"):
-        everywhere = copies(eigvals, SAMP).reshape(-1, 2, eigvals.shape[0])
-        everywhere = jnp.where(lax.axis_index("samp_2") == 0, everywhere, everywhere[:, ::-1])
-        everywhere = jnp.repeat(everywhere.reshape(everywhere.shape[0], -1), 4, axis=0)
-    rows = own.shape[0]
+        here = jnp.arange(8, dtype=jnp.int32)
+        kept = place(here // 4, here % 4)[:, None] == here[None, :]
+        parts = blocks[:, rows : rows + 3].astype(jnp.float32)
+        parts = parts[:, 0] + parts[:, 1] + parts[:, 2]
+        values = jnp.sum(jnp.where(kept[:, :, None], parts[None], 0.0), axis=1)
+        values = jnp.concatenate([values, shifted(values, "samp_2", 1)], axis=1)
+        everywhere = jnp.repeat(values, 4, axis=0)
 
     def term(q, ahead, lo, hi):
         dest = lax.rem(z + ahead + layers, layers)
-        across, along = dest // 4, lax.rem(dest, 4)
-        place = (4 * (across ^ y) + lax.rem(along - x + 4, 4) + 1) & 7
-        block = lax.dynamic_index_in_dim(blocks, place, 0, keepdims=False)[lo:hi]
+        at = place(dest // 4, lax.rem(dest, 4))
+        block = lax.dynamic_index_in_dim(blocks, at, 0, keepdims=False)[lo:hi]
         return jnp.dot(block, vecs[q], preferred_element_type=jnp.float32)
 
     far = layers // 2

time: 122 us -> 118 us (0.967)
  starting transfers between devices: 57.3 us -> 51.6 us
  waiting for transfers between devices: 44.9 us -> 48.2 us
  local copies, waits for them, and re-layouts: 3.99 us -> 2.25 us
    ppermute x23 -> x24, waiting for transfers between devices: 19.9 us -> 24.5 us  [shifted(): lax.ppermute(value, axis, [(i, (i + by) % peers) for i in range(peers)])]
    all_to_all x1 -> x0, starting transfers between devices: 3.49 us -> none  [copies(): lax.all_to_all(jnp.broadcast_to(value[None], (peers, *value.shape)), axes...]
    broadcast_in_dim x2 -> x1, local copies, waits for them, and re-layouts: 1.39 us -> 0.05 us  [shards(): everywhere = jnp.repeat(values, 4, axis=0)]
    ppermute x23 -> x24, starting transfers between devices: 38.9 us -> 37.8 us  [shifted(): lax.ppermute(value, axis, [(i, (i + by) % peers) for i in range(peers)])]
  transfers between devices with their start and end apart: 28 -> 28, of which waited for: 18 -> 17; matrix products, arithmetic and copies ran while one was open for 11% -> 8% of each run, Pallas kernels for 0% -> 0%
where the time goes in v11:
time: 118 us; the launch traced here: 117 us
  starting transfers between devices  51.6 us (44%)
  waiting for transfers between devices  48.2 us (41%)
  matrix products  8.2 us (7%)
  Pallas kernels  4.05 us (3%)
  local copies, waits for them, and re-layouts  2.25 us (2%)
  other arithmetic  2.04 us (2%)
    ppermute x24, starting transfers between devices, shifted(): lax.ppermute(value, axis, [(i, (i + by) % peers) for i in range(peers)])  37.8 us
    ppermute x24, waiting for transfers between devices, shifted(): lax.ppermute(value, axis, [(i, (i + by) % peers) for i in range(peers)])  24.5 us
    all_to_all x1, waiting for transfers between devices, shards(): sums = lax.all_to_all(whole, PLANE, 0, 0, tiled=True)  8.45 us
    dot_general x18, matrix products, term(): return jnp.dot(block, vecs[q], preferred_element_type=jnp.float32)  8.2 us
    all_to_all x1, waiting for transfers between devices, shards(): lax.all_to_all(fitted, LAYER, 0, 0, tiled=True)  7.32 us
    all_to_all x1, starting transfers between devices, shards(): sums = lax.all_to_all(whole, PLANE, 0, 0, tiled=True)  6.47 us
    ppermute x1, waiting for transfers between devices, across(): return lax.ppermute(value, (y, x), pairs)  4.98 us
    all_to_all x1, starting transfers between devices, shards(): lax.all_to_all(fitted, LAYER, 0, 0, tiled=True)  3.83 us
  transfers between devices with their start and end apart: 28, of which 17 were waited for; matrix products, arithmetic and copies ran while one was open for 8% of the time, Pallas kernels for 0%

profile of v11, /device:TPU:96, one launch (start us, length us, event | category | flops | bytes accessed | tf_op | source)
XLA Modules:
  0.0 117.4 jit_solution(1471790051429635239)
XLA Ops:
  0.6 1.9 %weigh.1 = bf16[144,1024]{1,0:T(8,128)(2,1)} custom-call(bf16[64,1024]{1,0:T(8,128)(2,1)} %resp_ref.1, bf16[64,1024]{1,0:T(8,128)(2,1)} %weight_ref.1, f32[1,1024]{1,0:T(1,128)} %bitcast.97, f32[1,1024]{1,0:T(1,128)} %bitcast.98), custom_call_target="tpu_custom_call" | custom-call | tf_op jit(solution)/shard_map/weigh/pallas_call | solution.py:57
  2.5 1.5 %collective-permute-start = (bf16[144,1024]{1,0:T(8,128)(2,1)}, bf16[144,1024]{1,0:T(8,128)(2,1)S(1)}, u32[]{:S(2)}, u32[]{:S(2)}) collective-permute-start(bf16[144,1024]{1,0:T(8,128)(2,1)} %weigh.1), channel_id=1, source_target_pairs={{0,32},{32,64},{64,96},{96,0},{1,33},{33,65},{65,97},{97,1},{2,34}... | collective-permute-start | bytes 884744 | tf_op jit(solution)/shard_map/gather_rows/ppermute | solution.py:25
  4.0 1.7 %collective-permute-start.2 = (bf16[144,1024]{1,0:T(8,128)(2,1)}, bf16[144,1024]{1,0:T(8,128)(2,1)S(1)}, u32[]{:S(2)}, u32[]{:S(2)}) collective-permute-start(bf16[144,1024]{1,0:T(8,128)(2,1)} %weigh.1), channel_id=1, source_target_pairs={{0,96},{32,0},{64,32},{96,64},{1,97},{33,1},{65,33},{97,65},{2,98}... | collective-permute-start | bytes 884744 | tf_op jit(solution)/shard_map/gather_rows/ppermute | solution.py:25
  5.7 1.6 %collective-permute-start.4 = (bf16[144,1024]{1,0:T(8,128)(2,1)}, bf16[144,1024]{1,0:T(8,128)(2,1)S(1)}, u32[]{:S(2)}, u32[]{:S(2)}) collective-permute-start(bf16[144,1024]{1,0:T(8,128)(2,1)} %weigh.1), channel_id=1, source_target_pairs={{0,128},{128,0},{1,129},{129,1},{2,130},{130,2},{3,131},{131,3},{4... | collective-permute-start | bytes 884744 | tf_op jit(solution)/shard_map/gather_rows/ppermute | solution.py:25
  7.3 5.4 %collective-permute-done = bf16[144,1024]{1,0:T(8,128)(2,1)S(1)} collective-permute-done((bf16[144,1024]{1,0:T(8,128)(2,1)}, bf16[144,1024]{1,0:T(8,128)(2,1)S(1)}, u32[]{:S(2)}, u32[]{:S(2)}) %collective-permute-start) | collective-permute-done | bytes 294944 | tf_op jit(solution)/shard_map/gather_rows/ppermute | solution.py:25
  12.7 1.6 %collective-permute-start.1 = (bf16[144,1024]{1,0:T(8,128)(2,1)S(1)}, bf16[144,1024]{1,0:T(8,128)(2,1)S(1)}, u32[]{:S(2)}, u32[]{:S(2)}) collective-permute-start(bf16[144,1024]{1,0:T(8,128)(2,1)S(1)} %collective-permute-done), channel_id=1, source_target_pairs={{0,128},{128,0},{1,129},{129,1},{2,130},{130,2},{3,131},{131,3},{4... | collective-permute-start | bytes 884744 | tf_op jit(solution)/shard_map/gather_rows/ppermute | solution.py:25
  14.3 0.3 collective-permute-start.3
  14.6 1.2 collective-permute-done.4
  15.8 1.8 %collective-permute-start.5 = (bf16[144,1024]{1,0:T(8,128)(2,1)S(1)}, bf16[144,1024]{1,0:T(8,128)(2,1)S(1)}, u32[]{:S(2)}, u32[]{:S(2)}) collective-permute-start(bf16[144,1024]{1,0:T(8,128)(2,1)S(1)} %collective-permute-done.4), channel_id=1, source_target_pairs={{0,96},{32,0},{64,32},{96,64},{1,97},{33,1},{65,33},{97,65},{2,98}... | collective-permute-start | bytes 884744 | tf_op jit(solution)/shard_map/gather_rows/ppermute | solution.py:25
  17.6 1.6 %collective-permute-start.6 = (bf16[144,1024]{1,0:T(8,128)(2,1)S(1)}, bf16[144,1024]{1,0:T(8,128)(2,1)S(1)}, u32[]{:S(2)}, u32[]{:S(2)}) collective-permute-start(bf16[144,1024]{1,0:T(8,128)(2,1)S(1)} %collective-permute-done.2), channel_id=1, source_target_pairs={{0,224},{32,128},{64,160},{96,192},{128,96},{160,0},{192,32},{224,... | collective-permute-start | bytes 884744 | tf_op jit(solution)/shard_map/gather_rows/ppermute | solution.py:151
  19.2 2.2 %collective-permute-done.1 = bf16[144,1024]{1,0:T(8,128)(2,1)S(1)} collective-permute-done((bf16[144,1024]{1,0:T(8,128)(2,1)S(1)}, bf16[144,1024]{1,0:T(8,128)(2,1)S(1)}, u32[]{:S(2)}, u32[]{:S(2)}) %collective-permute-start.1) | collective-permute-done | bytes 294944 | tf_op jit(solution)/shard_map/gather_rows/ppermute | solution.py:25
  21.4 1.1 bitcast_dynamic-update-slice_fusion.5
  22.6 0.5 collective-permute-done.3
  23.2 2.5 %collective-permute-done.5 = bf16[144,1024]{1,0:T(8,128)(2,1)S(1)} collective-permute-done((bf16[144,1024]{1,0:T(8,128)(2,1)S(1)}, bf16[144,1024]{1,0:T(8,128)(2,1)S(1)}, u32[]{:S(2)}, u32[]{:S(2)}) %collective-permute-start.5) | collective-permute-done | bytes 294944 | tf_op jit(solution)/shard_map/gather_rows/ppermute | solution.py:25
  25.8 5.0 %collective-permute-done.6 = bf16[144,1024]{1,0:T(8,128)(2,1)S(1)} collective-permute-done((bf16[144,1024]{1,0:T(8,128)(2,1)S(1)}, bf16[144,1024]{1,0:T(8,128)(2,1)S(1)}, u32[]{:S(2)}, u32[]{:S(2)}) %collective-permute-start.6) | collective-permute-done | bytes 294944 | tf_op jit(solution)/shard_map/gather_rows/ppermute | solution.py:151
  30.7 0.1 fusion.10
  30.8 0.5 convolution_convert_fusion.3
  31.3 3.2 %collective-permute-start.8 = (bf16[64,1024]{1,0:T(8,128)(2,1)S(1)}, bf16[64,1024]{1,0:T(8,128)(2,1)S(1)}, u32[]{:S(2)}, u32[]{:S(2)}) collective-permute-start(bf16[64,1024]{1,0:T(8,128)(2,1)S(1)} %convolution_convert_fusion.3), channel_id=1, source_target_pairs={{0,2},{2,4},{4,6},{6,8},{8,10},{10,12},{12,14},{14,0},{1,3},{3,5},... | collective-permute-start | bytes 393224 | tf_op jit(solution)/shard_map/sum_layers/ppermute | solution.py:25
  34.5 0.5 convolution_convert_fusion.2
  35.1 0.5 convolution_convert_fusion.1
  35.6 3.3 %collective-permute-start.16 = (bf16[64,1024]{1,0:T(8,128)(2,1)S(1)}, bf16[64,1024]{1,0:T(8,128)(2,1)S(1)}, u32[]{:S(2)}, u32[]{:S(2)}) collective-permute-start(bf16[64,1024]{1,0:T(8,128)(2,1)S(1)} %convolution_convert_fusion.1), channel_id=1, source_target_pairs={{0,2},{2,4},{4,6},{6,8},{8,10},{10,12},{12,14},{14,0},{1,3},{3,5},... | collective-permute-start | bytes 393224 | tf_op jit(solution)/shard_map/sum_layers/ppermute | solution.py:25
  38.9 0.5 convolution_convert_fusion
  39.5 0.4 add_convert_fusion.6
  40.0 3.5 %collective-permute-start.9 = (bf16[128,1024]{1,0:T(8,128)(2,1)S(1)}, bf16[128,1024]{1,0:T(8,128)(2,1)S(1)}, u32[]{:S(2)}, u32[]{:S(2)}) collective-permute-start(bf16[128,1024]{1,0:T(8,128)(2,1)S(1)} %add_convert_fusion.6), channel_id=1, source_target_pairs={{0,2},{2,4},{4,6},{6,8},{8,10},{10,12},{12,14},{14,0},{1,3},{3,5},... | collective-permute-start | bytes 786440 | tf_op jit(solution)/shard_map/sum_layers/ppermute | solution.py:25
  43.5 0.4 add_convert_fusion.3
  44.0 0.4 fusion.4
  44.5 3.3 %collective-permute-start.17 = (bf16[128,1024]{1,0:T(8,128)(2,1)S(1)}, bf16[128,1024]{1,0:T(8,128)(2,1)S(1)}, u32[]{:S(2)}, u32[]{:S(2)}) collective-permute-start(bf16[128,1024]{1,0:T(8,128)(2,1)S(1)} %fusion.4), channel_id=1, source_target_pairs={{0,2},{2,4},{4,6},{6,8},{8,10},{10,12},{12,14},{14,0},{1,3},{3,5},... | collective-permute-start | bytes 786440 | tf_op jit(solution)/shard_map/sum_layers/ppermute | solution.py:25
  47.8 0.4 fusion.7
  48.3 1.9 %collective-permute-done.9 = bf16[128,1024]{1,0:T(8,128)(2,1)S(1)} collective-permute-done((bf16[128,1024]{1,0:T(8,128)(2,1)S(1)}, bf16[128,1024]{1,0:T(8,128)(2,1)S(1)}, u32[]{:S(2)}, u32[]{:S(2)}) %collective-permute-start.9) | collective-permute-done | bytes 262176 | tf_op jit(solution)/shard_map/sum_layers/ppermute | solution.py:25
  50.2 0.4 add_convert_fusion.5
  50.7 3.8 %collective-permute-start.10 = (bf16[128,1024]{1,0:T(8,128)(2,1)S(1)}, bf16[128,1024]{1,0:T(8,128)(2,1)S(1)}, u32[]{:S(2)}, u32[]{:S(2)}) collective-permute-start(bf16[128,1024]{1,0:T(8,128)(2,1)S(1)} %add_convert_fusion.5), channel_id=1, source_target_pairs={{0,2},{2,4},{4,6},{6,8},{8,10},{10,12},{12,14},{14,0},{1,3},{3,5},... | collective-permute-start | bytes 786440 | tf_op jit(solution)/shard_map/sum_layers/ppermute | solution.py:25
  54.4 0.4 add_convert_fusion.2
  55.0 0.8 collective-permute-done.17
  55.8 0.4 fusion.3
  56.3 3.8 %collective-permute-start.18 = (bf16[128,1024]{1,0:T(8,128)(2,1)S(1)}, bf16[128,1024]{1,0:T(8,128)(2,1)S(1)}, u32[]{:S(2)}, u32[]{:S(2)}) collective-permute-start(bf16[128,1024]{1,0:T(8,128)(2,1)S(1)} %fusion.3), channel_id=1, source_target_pairs={{0,2},{2,4},{4,6},{6,8},{8,10},{10,12},{12,14},{14,0},{1,3},{3,5},... | collective-permute-start | bytes 786440 | tf_op jit(solution)/shard_map/sum_layers/ppermute | solution.py:25
  60.1 0.4 fusion.6
  60.6 0.8 collective-permute-done.10
  61.5 0.4 add_convert_fusion.4
  61.9 3.8 %collective-permute-start.11 = (bf16[128,1024]{1,0:T(8,128)(2,1)S(1)}, bf16[128,1024]{1,0:T(8,128)(2,1)S(1)}, u32[]{:S(2)}, u32[]{:S(2)}) collective-permute-start(bf16[128,1024]{1,0:T(8,128)(2,1)S(1)} %add_convert_fusion.4), channel_id=1, source_target_pairs={{0,2},{2,4},{4,6},{6,8},{8,10},{10,12},{12,14},{14,0},{1,3},{3,5},... | collective-permute-start | bytes 786440 | tf_op jit(solution)/shard_map/sum_layers/ppermute | solution.py:25
  65.7 0.4 add_convert_fusion.1
  66.2 0.8 collective-permute-done.18
  67.1 0.4 fusion.2
  67.5 3.8 %collective-permute-start.19 = (bf16[128,1024]{1,0:T(8,128)(2,1)S(1)}, bf16[128,1024]{1,0:T(8,128)(2,1)S(1)}, u32[]{:S(2)}, u32[]{:S(2)}) collective-permute-start(bf16[128,1024]{1,0:T(8,128)(2,1)S(1)} %fusion.2), channel_id=1, source_target_pairs={{0,2},{2,4},{4,6},{6,8},{8,10},{10,12},{12,14},{14,0},{1,3},{3,5},... | collective-permute-start | bytes 786440 | tf_op jit(solution)/shard_map/sum_layers/ppermute | solution.py:25
  71.3 0.4 fusion.5
  71.8 0.3 collective-permute-start.23
  72.1 0.2 collective-permute-done.11
  72.3 4.2 %collective-permute-done.15 = bf16[128,1024]{1,0:T(8,128)(2,1)S(1)} collective-permute-done((bf16[128,1024]{1,0:T(8,128)(2,1)S(1)}, bf16[128,1024]{1,0:T(8,128)(2,1)S(1)}, u32[]{:S(2)}, u32[]{:S(2)}) %collective-permute-start.15) | collective-permute-done | bytes 262176 | tf_op jit(solution)/shard_map/sum_layers/ppermute | solution.py:25
  76.5 0.5 add_convert_fusion
  77.0 2.7 %collective-permute-done.23 = bf16[128,1024]{1,0:T(8,128)(2,1)S(1)} collective-permute-done((bf16[128,1024]{1,0:T(8,128)(2,1)S(1)}, bf16[128,1024]{1,0:T(8,128)(2,1)S(1)}, u32[]{:S(2)}, u32[]{:S(2)}) %collective-permute-start.23) | collective-permute-done | bytes 262176 | tf_op jit(solution)/shard_map/sum_layers/ppermute | solution.py:25
  79.6 0.5 fusion.1
  80.1 0.8 maximum_bitcast_fusion
  81.0 6.5 %all-to-all-start = ((bf16[16,8,2048]{2,1,0:T(8,128)(2,1)}), bf16[16,8,2048]{2,1,0:T(8,128)(2,1)S(1)}, u32[]{:S(2)}, u32[]{:S(2)}) async-start(bf16[16,8,2048]{2,1,0:T(8,128)(2,1)} %maximum_bitcast_fusion), calls=%async_computation | async-start | bytes 1048576 | tf_op jit(solution)/shard_map/to_components/all_to_all | solution.py:248
  87.5 0.1 select_reduce_fusion
  87.7 0.1 collective-permute-start.24
  87.8 1.1 collective-permute-done.24
  89.0 0.1 reshape.101.values_ref
  89.1 8.5 %all-to-all-done = bf16[16,8,2048]{2,1,0:T(8,128)(2,1)S(1)} async-done(((bf16[16,8,2048]{2,1,0:T(8,128)(2,1)}), bf16[16,8,2048]{2,1,0:T(8,128)(2,1)S(1)}, u32[]{:S(2)}, u32[]{:S(2)}) %all-to-all-start) | async-done | bytes 524320 | tf_op jit(solution)/shard_map/to_components/all_to_all | solution.py:248
  97.6 2.2 %fit.1 = f32[32,1,256]{2,1,0:T(1,128)} custom-call(s32[1]{0:T(128)} %bitcast.slot_ref, bf16[128,2048]{1,0:T(8,128)(2,1)S(1)} %bitcast.95, f32[32,2048]{1,0:T(8,128)S(1)} %reshape.101.values_ref), custom_call_target="tpu_custom_call" | custom-call | tf_op jit(solution)/shard_map/fit/pallas_call | solution.py:130
  99.8 3.8 %all-to-all-start.1 = ((f32[32,1,256]{2,1,0:T(1,128)}), f32[32,1,256]{2,1,0:T(1,128)S(1)}, u32[]{:S(2)}, u32[]{:S(2)}) async-start(f32[32,1,256]{2,1,0:T(1,128)} %fit.1), calls=%async_computation.1 | async-start | bytes 65536 | tf_op jit(solution)/shard_map/gather_scores/all_to_all | solution.py:253
  103.7 7.3 %all-to-all-done.1 = f32[32,1,256]{2,1,0:T(1,128)S(1)} async-done(((f32[32,1,256]{2,1,0:T(1,128)}), f32[32,1,256]{2,1,0:T(1,128)S(1)}, u32[]{:S(2)}, u32[]{:S(2)}) %all-to-all-start.1) | async-done | bytes 32800 | tf_op jit(solution)/shard_map/gather_scores/all_to_all | solution.py:253
  111.1 1.9 %collective-permute-start.25 = (f32[256]{0:T(256)S(1)}, f32[256]{0:T(256)S(1)}, u32[]{:S(2)}, u32[]{:S(2)}) collective-permute-start(f32[256]{0:T(256)S(1)} %reduce_sum.19), channel_id=1, source_target_pairs={{0,2},{2,4},{4,6},{6,8},{8,10},{10,12},{12,14},{3,1},{5,3},{7,5},{... | collective-permute-start | bytes 3080 | tf_op jit(solution)/shard_map/gather_scores/ppermute | solution.py:256
  113.0 0.6 dynamic_slice.54
  113.6 2.9 %collective-permute-done.25 = f32[256]{0:T(256)S(1)} collective-permute-done((f32[256]{0:T(256)S(1)}, f32[256]{0:T(256)S(1)}, u32[]{:S(2)}, u32[]{:S(2)}) %collective-permute-start.25) | collective-permute-done | bytes 1056 | tf_op jit(solution)/shard_map/gather_scores/ppermute | solution.py:256
  116.8 0.6 add_divide_fusion
  (46 shorter events, 1.4 us)
Async XLA Ops:
  2.5 10.2 %collective-permute-start = (bf16[144,1024]{1,0:T(8,128)(2,1)}, bf16[144,1024]{1,0:T(8,128)(2,1)S(1)}, u32[]{:S(2)}, u32[]{:S(2)}) collective-permute-start(bf16[144,1024]{1,0:T(8,128)(2,1)} %weigh.1), channel_id=1, source_target_pairs={{0,32},{32,64},{64,96},{96,0},{1,33},{33,65},{65,97},{97,1},{2,34}... | collective-permute-start | bytes 884744 | tf_op jit(solution)/shard_map/gather_rows/ppermute | solution.py:25
  4.0 26.8 %collective-permute-start.7 = (bf16[1024,1024]{1,0:T(8,128)(2,1)}, bf16[1024,1024]{1,0:T(8,128)(2,1)S(1)}, u32[]{:S(2)}, u32[]{:S(2)}) collective-permute-start(bf16[1024,1024]{1,0:T(8,128)(2,1)} %param.10), channel_id=1, source_target_pairs={{0,16},{16,0},{1,17},{17,1},{2,18},{18,2},{3,19},{19,3},{4,20},{20... | collective-permute-start | bytes 6291464 | tf_op jit(solution)/shard_map/swap_eigvecs/ppermute | solution.py:25
  4.0 13.6 %collective-permute-start.2 = (bf16[144,1024]{1,0:T(8,128)(2,1)}, bf16[144,1024]{1,0:T(8,128)(2,1)S(1)}, u32[]{:S(2)}, u32[]{:S(2)}) collective-permute-start(bf16[144,1024]{1,0:T(8,128)(2,1)} %weigh.1), channel_id=1, source_target_pairs={{0,96},{32,0},{64,32},{96,64},{1,97},{33,1},{65,33},{97,65},{2,98}... | collective-permute-start | bytes 884744 | tf_op jit(solution)/shard_map/gather_rows/ppermute | solution.py:25
  5.7 10.1 %collective-permute-start.4 = (bf16[144,1024]{1,0:T(8,128)(2,1)}, bf16[144,1024]{1,0:T(8,128)(2,1)S(1)}, u32[]{:S(2)}, u32[]{:S(2)}) collective-permute-start(bf16[144,1024]{1,0:T(8,128)(2,1)} %weigh.1), channel_id=1, source_target_pairs={{0,128},{128,0},{1,129},{129,1},{2,130},{130,2},{3,131},{131,3},{4... | collective-permute-start | bytes 884744 | tf_op jit(solution)/shard_map/gather_rows/ppermute | solution.py:25
  12.7 8.7 %collective-permute-start.1 = (bf16[144,1024]{1,0:T(8,128)(2,1)S(1)}, bf16[144,1024]{1,0:T(8,128)(2,1)S(1)}, u32[]{:S(2)}, u32[]{:S(2)}) collective-permute-start(bf16[144,1024]{1,0:T(8,128)(2,1)S(1)} %collective-permute-done), channel_id=1, source_target_pairs={{0,128},{128,0},{1,129},{129,1},{2,130},{130,2},{3,131},{131,3},{4... | collective-permute-start | bytes 884744 | tf_op jit(solution)/shard_map/gather_rows/ppermute | solution.py:25
  14.3 8.8 %collective-permute-start.3 = (bf16[144,1024]{1,0:T(8,128)(2,1)S(1)}, bf16[144,1024]{1,0:T(8,128)(2,1)S(1)}, u32[]{:S(2)}, u32[]{:S(2)}) collective-permute-start(bf16[144,1024]{1,0:T(8,128)(2,1)S(1)} %collective-permute-done), channel_id=1, source_target_pairs={{0,32},{32,64},{64,96},{96,0},{1,33},{33,65},{65,97},{97,1},{2,34}... | collective-permute-start | bytes 884744 | tf_op jit(solution)/shard_map/gather_rows/ppermute | solution.py:25
  15.8 9.9 %collective-permute-start.5 = (bf16[144,1024]{1,0:T(8,128)(2,1)S(1)}, bf16[144,1024]{1,0:T(8,128)(2,1)S(1)}, u32[]{:S(2)}, u32[]{:S(2)}) collective-permute-start(bf16[144,1024]{1,0:T(8,128)(2,1)S(1)} %collective-permute-done.4), channel_id=1, source_target_pairs={{0,96},{32,0},{64,32},{96,64},{1,97},{33,1},{65,33},{97,65},{2,98}... | collective-permute-start | bytes 884744 | tf_op jit(solution)/shard_map/gather_rows/ppermute | solution.py:25
  17.6 13.1 %collective-permute-start.6 = (bf16[144,1024]{1,0:T(8,128)(2,1)S(1)}, bf16[144,1024]{1,0:T(8,128)(2,1)S(1)}, u32[]{:S(2)}, u32[]{:S(2)}) collective-permute-start(bf16[144,1024]{1,0:T(8,128)(2,1)S(1)} %collective-permute-done.2), channel_id=1, source_target_pairs={{0,224},{32,128},{64,160},{96,192},{128,96},{160,0},{192,32},{224,... | collective-permute-start | bytes 884744 | tf_op jit(solution)/shard_map/gather_rows/ppermute | solution.py:151
  21.4 9.4 %copy-start = (bf16[1024,1024]{1,0:T(8,128)(2,1)S(1)}, bf16[1024,1024]{1,0:T(8,128)(2,1)}, u32[]{:S(2)}) copy-start(bf16[1024,1024]{1,0:T(8,128)(2,1)} %param.10) | copy-start | bytes 6291460
  31.3 8.2 %collective-permute-start.8 = (bf16[64,1024]{1,0:T(8,128)(2,1)S(1)}, bf16[64,1024]{1,0:T(8,128)(2,1)S(1)}, u32[]{:S(2)}, u32[]{:S(2)}) collective-permute-start(bf16[64,1024]{1,0:T(8,128)(2,1)S(1)} %convolution_convert_fusion.3), channel_id=1, source_target_pairs={{0,2},{2,4},{4,6},{6,8},{8,10},{10,12},{12,14},{14,0},{1,3},{3,5},... | collective-permute-start | bytes 393224 | tf_op jit(solution)/shard_map/sum_layers/ppermute | solution.py:25
  35.0 8.4 %collective-permute-start.12 = (bf16[64,1024]{1,0:T(8,128)(2,1)S(1)}, bf16[64,1024]{1,0:T(8,128)(2,1)S(1)}, u32[]{:S(2)}, u32[]{:S(2)}) collective-permute-start(bf16[64,1024]{1,0:T(8,128)(2,1)S(1)} %convolution_convert_fusion.2), channel_id=1, source_target_pairs={{0,14},{2,0},{4,2},{6,4},{8,6},{10,8},{12,10},{14,12},{1,15},{3,1}... | collective-permute-start | bytes 393224 | tf_op jit(solution)/shard_map/sum_layers/ppermute | solution.py:25
  35.6 8.4 %collective-permute-start.16 = (bf16[64,1024]{1,0:T(8,128)(2,1)S(1)}, bf16[64,1024]{1,0:T(8,128)(2,1)S(1)}, u32[]{:S(2)}, u32[]{:S(2)}) collective-permute-start(bf16[64,1024]{1,0:T(8,128)(2,1)S(1)} %convolution_convert_fusion.1), channel_id=1, source_target_pairs={{0,2},{2,4},{4,6},{6,8},{8,10},{10,12},{12,14},{14,0},{1,3},{3,5},... | collective-permute-start | bytes 393224 | tf_op jit(solution)/shard_map/sum_layers/ppermute | solution.py:25
  39.4 8.4 %collective-permute-start.20 = (bf16[64,1024]{1,0:T(8,128)(2,1)S(1)}, bf16[64,1024]{1,0:T(8,128)(2,1)S(1)}, u32[]{:S(2)}, u32[]{:S(2)}) collective-permute-start(bf16[64,1024]{1,0:T(8,128)(2,1)S(1)} %convolution_convert_fusion), channel_id=1, source_target_pairs={{0,14},{2,0},{4,2},{6,4},{8,6},{10,8},{12,10},{14,12},{1,15},{3,1}... | collective-permute-start | bytes 393224 | tf_op jit(solution)/shard_map/sum_layers/ppermute | solution.py:25
  40.0 10.2 %collective-permute-start.9 = (bf16[128,1024]{1,0:T(8,128)(2,1)S(1)}, bf16[128,1024]{1,0:T(8,128)(2,1)S(1)}, u32[]{:S(2)}, u32[]{:S(2)}) collective-permute-start(bf16[128,1024]{1,0:T(8,128)(2,1)S(1)} %add_convert_fusion.6), channel_id=1, source_target_pairs={{0,2},{2,4},{4,6},{6,8},{8,10},{10,12},{12,14},{14,0},{1,3},{3,5},... | collective-permute-start | bytes 786440 | tf_op jit(solution)/shard_map/sum_layers/ppermute | solution.py:25
  43.9 10.5 %collective-permute-start.13 = (bf16[128,1024]{1,0:T(8,128)(2,1)S(1)}, bf16[128,1024]{1,0:T(8,128)(2,1)S(1)}, u32[]{:S(2)}, u32[]{:S(2)}) collective-permute-start(bf16[128,1024]{1,0:T(8,128)(2,1)S(1)} %add_convert_fusion.3), channel_id=1, source_target_pairs={{0,14},{2,0},{4,2},{6,4},{8,6},{10,8},{12,10},{14,12},{1,15},{3,1}... | collective-permute-start | bytes 786440 | tf_op jit(solution)/shard_map/sum_layers/ppermute | solution.py:25
  44.5 11.4 %collective-permute-start.17 = (bf16[128,1024]{1,0:T(8,128)(2,1)S(1)}, bf16[128,1024]{1,0:T(8,128)(2,1)S(1)}, u32[]{:S(2)}, u32[]{:S(2)}) collective-permute-start(bf16[128,1024]{1,0:T(8,128)(2,1)S(1)} %fusion.4), channel_id=1, source_target_pairs={{0,2},{2,4},{4,6},{6,8},{8,10},{10,12},{12,14},{14,0},{1,3},{3,5},... | collective-permute-start | bytes 786440 | tf_op jit(solution)/shard_map/sum_layers/ppermute | solution.py:25
  48.2 11.8 %collective-permute-start.21 = (bf16[128,1024]{1,0:T(8,128)(2,1)S(1)}, bf16[128,1024]{1,0:T(8,128)(2,1)S(1)}, u32[]{:S(2)}, u32[]{:S(2)}) collective-permute-start(bf16[128,1024]{1,0:T(8,128)(2,1)S(1)} %fusion.7), channel_id=1, source_target_pairs={{0,14},{2,0},{4,2},{6,4},{8,6},{10,8},{12,10},{14,12},{1,15},{3,1}... | collective-permute-start | bytes 786440 | tf_op jit(solution)/shard_map/sum_layers/ppermute | solution.py:25
  50.7 10.8 %collective-permute-start.10 = (bf16[128,1024]{1,0:T(8,128)(2,1)S(1)}, bf16[128,1024]{1,0:T(8,128)(2,1)S(1)}, u32[]{:S(2)}, u32[]{:S(2)}) collective-permute-start(bf16[128,1024]{1,0:T(8,128)(2,1)S(1)} %add_convert_fusion.5), channel_id=1, source_target_pairs={{0,2},{2,4},{4,6},{6,8},{8,10},{10,12},{12,14},{14,0},{1,3},{3,5},... | collective-permute-start | bytes 786440 | tf_op jit(solution)/shard_map/sum_layers/ppermute | solution.py:25
  54.9 10.8 %collective-permute-start.14 = (bf16[128,1024]{1,0:T(8,128)(2,1)S(1)}, bf16[128,1024]{1,0:T(8,128)(2,1)S(1)}, u32[]{:S(2)}, u32[]{:S(2)}) collective-permute-start(bf16[128,1024]{1,0:T(8,128)(2,1)S(1)} %add_convert_fusion.2), channel_id=1, source_target_pairs={{0,14},{2,0},{4,2},{6,4},{8,6},{10,8},{12,10},{14,12},{1,15},{3,1}... | collective-permute-start | bytes 786440 | tf_op jit(solution)/shard_map/sum_layers/ppermute | solution.py:25
  56.3 10.8 %collective-permute-start.18 = (bf16[128,1024]{1,0:T(8,128)(2,1)S(1)}, bf16[128,1024]{1,0:T(8,128)(2,1)S(1)}, u32[]{:S(2)}, u32[]{:S(2)}) collective-permute-start(bf16[128,1024]{1,0:T(8,128)(2,1)S(1)} %fusion.3), channel_id=1, source_target_pairs={{0,2},{2,4},{4,6},{6,8},{8,10},{10,12},{12,14},{14,0},{1,3},{3,5},... | collective-permute-start | bytes 786440 | tf_op jit(solution)/shard_map/sum_layers/ppermute | solution.py:25
  60.5 10.8 %collective-permute-start.22 = (bf16[128,1024]{1,0:T(8,128)(2,1)S(1)}, bf16[128,1024]{1,0:T(8,128)(2,1)S(1)}, u32[]{:S(2)}, u32[]{:S(2)}) collective-permute-start(bf16[128,1024]{1,0:T(8,128)(2,1)S(1)} %fusion.6), channel_id=1, source_target_pairs={{0,14},{2,0},{4,2},{6,4},{8,6},{10,8},{12,10},{14,12},{1,15},{3,1}... | collective-permute-start | bytes 786440 | tf_op jit(solution)/shard_map/sum_layers/ppermute | solution.py:25
  61.9 10.4 %collective-permute-start.11 = (bf16[128,1024]{1,0:T(8,128)(2,1)S(1)}, bf16[128,1024]{1,0:T(8,128)(2,1)S(1)}, u32[]{:S(2)}, u32[]{:S(2)}) collective-permute-start(bf16[128,1024]{1,0:T(8,128)(2,1)S(1)} %add_convert_fusion.4), channel_id=1, source_target_pairs={{0,2},{2,4},{4,6},{6,8},{8,10},{10,12},{12,14},{14,0},{1,3},{3,5},... | collective-permute-start | bytes 786440 | tf_op jit(solution)/shard_map/sum_layers/ppermute | solution.py:25
  66.1 10.3 %collective-permute-start.15 = (bf16[128,1024]{1,0:T(8,128)(2,1)S(1)}, bf16[128,1024]{1,0:T(8,128)(2,1)S(1)}, u32[]{:S(2)}, u32[]{:S(2)}) collective-permute-start(bf16[128,1024]{1,0:T(8,128)(2,1)S(1)} %add_convert_fusion.1), channel_id=1, source_target_pairs={{0,14},{2,0},{4,2},{6,4},{8,6},{10,8},{12,10},{14,12},{1,15},{3,1}... | collective-permute-start | bytes 786440 | tf_op jit(solution)/shard_map/sum_layers/ppermute | solution.py:25
  67.5 9.4 %collective-permute-start.19 = (bf16[128,1024]{1,0:T(8,128)(2,1)S(1)}, bf16[128,1024]{1,0:T(8,128)(2,1)S(1)}, u32[]{:S(2)}, u32[]{:S(2)}) collective-permute-start(bf16[128,1024]{1,0:T(8,128)(2,1)S(1)} %fusion.2), channel_id=1, source_target_pairs={{0,2},{2,4},{4,6},{6,8},{8,10},{10,12},{12,14},{14,0},{1,3},{3,5},... | collective-permute-start | bytes 786440 | tf_op jit(solution)/shard_map/sum_layers/ppermute | solution.py:25
  71.8 7.9 %collective-permute-start.23 = (bf16[128,1024]{1,0:T(8,128)(2,1)S(1)}, bf16[128,1024]{1,0:T(8,128)(2,1)S(1)}, u32[]{:S(2)}, u32[]{:S(2)}) collective-permute-start(bf16[128,1024]{1,0:T(8,128)(2,1)S(1)} %fusion.5), channel_id=1, source_target_pairs={{0,14},{2,0},{4,2},{6,4},{8,6},{10,8},{12,10},{14,12},{1,15},{3,1}... | collective-permute-start | bytes 786440 | tf_op jit(solution)/shard_map/sum_layers/ppermute | solution.py:25
  77.0 10.9 %copy-start.1 = (s32[1024]{0:T(1024)S(1)}, s32[1024]{0:T(1024)}, u32[]{:S(2)}) copy-start(s32[1024]{0:T(1024)} %param.12) | copy-start | bytes 12292
  80.1 36.7 %copy-start.2 = (s32[64]{0:T(128)S(1)}, s32[64]{0:T(128)}, u32[]{:S(2)}) copy-start(s32[64]{0:T(128)} %param.13) | copy-start | bytes 772
  81.0 16.6 %all-to-all-start = ((bf16[16,8,2048]{2,1,0:T(8,128)(2,1)}), bf16[16,8,2048]{2,1,0:T(8,128)(2,1)S(1)}, u32[]{:S(2)}, u32[]{:S(2)}) async-start(bf16[16,8,2048]{2,1,0:T(8,128)(2,1)} %maximum_bitcast_fusion), calls=%async_computation | async-start | bytes 1048576 | tf_op jit(solution)/shard_map/to_components/all_to_all | solution.py:248
  87.7 1.3 %collective-permute-start.24 = (f32[8,1024]{1,0:T(8,128)S(1)}, f32[8,1024]{1,0:T(8,128)S(1)}, u32[]{:S(2)}, u32[]{:S(2)}) collective-permute-start(f32[8,1024]{1,0:T(8,128)S(1)} %select_reduce_fusion), channel_id=1, source_target_pairs={{0,16},{16,0},{1,17},{17,1},{2,18},{18,2},{3,19},{19,3},{4,20},{20... | collective-permute-start | bytes 98312 | tf_op jit(solution)/shard_map/gather_values/ppermute | solution.py:25
  99.8 11.2 %all-to-all-start.1 = ((f32[32,1,256]{2,1,0:T(1,128)}), f32[32,1,256]{2,1,0:T(1,128)S(1)}, u32[]{:S(2)}, u32[]{:S(2)}) async-start(f32[32,1,256]{2,1,0:T(1,128)} %fit.1), calls=%async_computation.1 | async-start | bytes 65536 | tf_op jit(solution)/shard_map/gather_scores/all_to_all | solution.py:253
  111.1 5.5 %collective-permute-start.25 = (f32[256]{0:T(256)S(1)}, f32[256]{0:T(256)S(1)}, u32[]{:S(2)}, u32[]{:S(2)}) collective-permute-start(f32[256]{0:T(256)S(1)} %reduce_sum.19), channel_id=1, source_target_pairs={{0,2},{2,4},{4,6},{6,8},{8,10},{10,12},{12,14},{3,1},{5,3},{7,5},{... | collective-permute-start | bytes 3080 | tf_op jit(solution)/shard_map/gather_scores/ppermute | solution.py:256

commit v12 on v11

--- a/solution.py
+++ b/solution.py
@@ -154,8 +154,8 @@
     over_far = across(right, -1)
     over_right = shifted(over, x, -1)
     far = shifted(left, x, 1)
-    over_far = over_far + 0 * other[: own.shape[0]]
-    return jnp.stack([over_left, own, right, far, left, over, over_right, over_far])
+    over_right = over_right + 0 * other[: own.shape[0]]
+    return jnp.stack([over_far, over_left, own, right, far, left, over, over_right])
 
 
 def smooth_block(widened, places, present, reaches):
@@ -197,7 +197,7 @@
     rows = own.shape[0] - EXTRA
 
     def place(across, along):
-        return (4 * (across ^ y) + (along - x) % 4 + 1) % 8
+        return (4 * (across ^ y) + (along - x) % 4 + 2) % 8
 
     with jax.named_scope("gather_values"):
         here = jnp.arange(8, dtype=jnp.int32)
@@ -208,41 +208,34 @@
         values = jnp.concatenate([values, shifted(values, "samp_2", 1)], axis=1)
         everywhere = jnp.repeat(values, 4, axis=0)
 
-    def term(q, ahead, lo, hi):
+    def term(q, ahead):
         dest = lax.rem(z + ahead + layers, layers)
         at = place(dest // 4, lax.rem(dest, 4))
-        block = lax.dynamic_index_in_dim(blocks, at, 0, keepdims=False)[lo:hi]
+        block = lax.dynamic_index_in_dim(blocks, at, 0, keepdims=False)[:rows]
         return jnp.dot(block, vecs[q], preferred_element_type=jnp.float32)
 
     far = layers // 2
-    cut = rows // 2
     sent = {}
 
-    def first(q):
-        sent[q, 1] = shifted(term(q, far, 0, cut).astype(jnp.bfloat16), "cpg_0", 1)
-        sent[q, -1] = shifted(term(q, far, cut, rows).astype(jnp.bfloat16), "cpg_0", -1)
-
-    def onward(q, ahead):
-        for way in (1, -1):
-            got = sent[q, way].astype(jnp.float32)
-            if got.shape[0] < rows:
-                rest = jnp.zeros_like(got)
-                got = jnp.concatenate([got, rest] if way == 1 else [rest, got], axis=0)
-            total = (term(q, way * ahead, 0, rows) + got).astype(jnp.bfloat16)
-            sent[q, way] = shifted(total, "cpg_0", way)
+    def onward(q, way, ahead):
+        total = term(q, way * ahead)
+        if (q, way) in sent:
+            total = total + sent[q, way].astype(jnp.float32)
+        sent[q, way] = shifted(total.astype(jnp.bfloat16), "cpg_0", way)
 
     def summed(q):
-        total = term(q, 0, 0, rows)
+        total = term(q, 0)
         for way in (1, -1):
             total = total + sent[q, way].astype(jnp.float32)
         return total.astype(jnp.bfloat16)
 
     with jax.named_scope("sum_layers"):
-        first(0)
-        first(1)
-        for ahead in range(far - 1, 0, -1):
-            onward(0, ahead)
-            onward(1, ahead)
+        for ahead in range(far, 0, -1):
+            onward(0, 1, ahead)
+            onward(1, -1, ahead)
+            if ahead > 1:
+                onward(0, -1, ahead - 1)
+                onward(1, 1, ahead - 1)
         whole = jnp.concatenate([summed(0), summed(1)], axis=1)
     with jax.named_scope("to_components"):
         sums = lax.all_to_all(whole, PLANE, 0, 0, tiled=True)

time: 118 us -> 118 us (level)
  starting transfers between devices: 51.6 us -> 48 us
  waiting for transfers between devices: 48.2 us -> 51.7 us
    ppermute x24 -> x22, waiting for transfers between devices: 24.5 us -> 32.3 us  [shifted(): lax.ppermute(value, axis, [(i, (i + by) % peers) for i in range(peers)])]
    ppermute x24 -> x22, starting transfers between devices: 37.8 us -> 31.2 us  [shifted(): lax.ppermute(value, axis, [(i, (i + by) % peers) for i in range(peers)])]
    ppermute x1, waiting for transfers between devices: 4.98 us -> 0.75 us  [across(): return lax.ppermute(value, (y, x), pairs)]
    ppermute x1, starting transfers between devices: 1.59 us -> 4.6 us  [across(): return lax.ppermute(value, (y, x), pairs)]
    dot_general x18 -> x16, matrix products: 8.2 us -> 7.16 us  [term(): return jnp.dot(block, vecs[q], preferred_element_type=jnp.float32)]
  transfers between devices with their start and end apart: 28 -> 26, of which waited for: 17 -> 17; matrix products, arithmetic and copies ran while one was open for 8% -> 8% of each run, Pallas kernels for 0% -> 0%
where the time goes in v12:
time: 118 us; the launch traced here: 117 us
  waiting for transfers between devices  51.7 us (44%)
  starting transfers between devices  48 us (41%)
  matrix products  7.16 us (6%)
  Pallas kernels  4.04 us (3%)
  local copies, waits for them, and re-layouts  3.06 us (3%)
  other arithmetic  2.04 us (2%)
    ppermute x22, waiting for transfers between devices, shifted(): lax.ppermute(value, axis, [(i, (i + by) % peers) for i in range(peers)])  32.3 us
    ppermute x22, starting transfers between devices, shifted(): lax.ppermute(value, axis, [(i, (i + by) % peers) for i in range(peers)])  31.2 us
    all_to_all x1, waiting for transfers between devices, shards(): sums = lax.all_to_all(whole, PLANE, 0, 0, tiled=True)  8.45 us
    all_to_all x1, waiting for transfers between devices, shards(): lax.all_to_all(fitted, LAYER, 0, 0, tiled=True)  7.32 us
    dot_general x16, matrix products, term(): return jnp.dot(block, vecs[q], preferred_element_type=jnp.float32)  7.16 us
    all_to_all x1, starting transfers between devices, shards(): sums = lax.all_to_all(whole, PLANE, 0, 0, tiled=True)  6.48 us
    ppermute x1, starting transfers between devices, across(): return lax.ppermute(value, (y, x), pairs)  4.6 us
    all_to_all x1, starting transfers between devices, shards(): lax.all_to_all(fitted, LAYER, 0, 0, tiled=True)  3.85 us
  transfers between devices with their start and end apart: 26, of which 17 were waited for; matrix products, arithmetic and copies ran while one was open for 8% of the time, Pallas kernels for 0%

profile of v12, /device:TPU:96, one launch (start us, length us, event | category | flops | bytes accessed | tf_op | source)
XLA Modules:
  0.0 117.2 jit_solution(17977457858864244090)
XLA Ops:
  0.6 1.8 %weigh.1 = bf16[144,1024]{1,0:T(8,128)(2,1)} custom-call(bf16[64,1024]{1,0:T(8,128)(2,1)} %resp_ref.1, bf16[64,1024]{1,0:T(8,128)(2,1)} %weight_ref.1, f32[1,1024]{1,0:T(1,128)} %bitcast.91, f32[1,1024]{1,0:T(1,128)} %bitcast.92), custom_call_target="tpu_custom_call" | custom-call | tf_op jit(solution)/shard_map/weigh/pallas_call | solution.py:57
  2.5 2.8 %collective-permute-start = (bf16[144,1024]{1,0:T(8,128)(2,1)}, bf16[144,1024]{1,0:T(8,128)(2,1)S(1)}, u32[]{:S(2)}, u32[]{:S(2)}) collective-permute-start(bf16[144,1024]{1,0:T(8,128)(2,1)} %weigh.1), channel_id=1, source_target_pairs={{0,96},{32,0},{64,32},{96,64},{1,97},{33,1},{65,33},{97,65},{2,98}... | collective-permute-start | bytes 884744 | tf_op jit(solution)/shard_map/gather_rows/ppermute | solution.py:25
  5.2 1.6 %collective-permute-start.5 = (bf16[144,1024]{1,0:T(8,128)(2,1)}, bf16[144,1024]{1,0:T(8,128)(2,1)S(1)}, u32[]{:S(2)}, u32[]{:S(2)}) collective-permute-start(bf16[144,1024]{1,0:T(8,128)(2,1)} %weigh.1), channel_id=1, source_target_pairs={{0,128},{128,0},{1,129},{129,1},{2,130},{130,2},{3,131},{131,3},{4... | collective-permute-start | bytes 884744 | tf_op jit(solution)/shard_map/gather_rows/ppermute | solution.py:25
  6.8 5.0 %collective-permute-done = bf16[144,1024]{1,0:T(8,128)(2,1)S(1)} collective-permute-done((bf16[144,1024]{1,0:T(8,128)(2,1)}, bf16[144,1024]{1,0:T(8,128)(2,1)S(1)}, u32[]{:S(2)}, u32[]{:S(2)}) %collective-permute-start) | collective-permute-done | bytes 294944 | tf_op jit(solution)/shard_map/gather_rows/ppermute | solution.py:25
  11.8 4.6 %collective-permute-start.1 = (bf16[144,1024]{1,0:T(8,128)(2,1)S(1)}, bf16[144,1024]{1,0:T(8,128)(2,1)S(1)}, u32[]{:S(2)}, u32[]{:S(2)}) collective-permute-start(bf16[144,1024]{1,0:T(8,128)(2,1)S(1)} %collective-permute-done), channel_id=1, source_target_pairs={{0,224},{32,128},{64,160},{96,192},{128,96},{160,0},{192,32},{224,... | collective-permute-start | bytes 884744 | tf_op jit(solution)/shard_map/gather_rows/ppermute | solution.py:151
  16.4 0.5 collective-permute-start.3
  17.1 0.1 collective-permute-start.4
  17.2 4.4 %collective-permute-done.5 = bf16[144,1024]{1,0:T(8,128)(2,1)S(1)} collective-permute-done((bf16[144,1024]{1,0:T(8,128)(2,1)}, bf16[144,1024]{1,0:T(8,128)(2,1)S(1)}, u32[]{:S(2)}, u32[]{:S(2)}) %collective-permute-start.5) | collective-permute-done | bytes 294944 | tf_op jit(solution)/shard_map/gather_rows/ppermute | solution.py:25
  21.6 0.7 collective-permute-done.1
  22.4 5.3 %collective-permute-done.3 = bf16[144,1024]{1,0:T(8,128)(2,1)} collective-permute-done((bf16[144,1024]{1,0:T(8,128)(2,1)S(1)}, bf16[144,1024]{1,0:T(8,128)(2,1)}, u32[]{:S(2)}, u32[]{:S(2)}) %collective-permute-start.3) | collective-permute-done | bytes 294944 | tf_op jit(solution)/shard_map/gather_rows/ppermute | solution.py:25
  27.6 1.0 bitcast_dynamic-update-slice_fusion.5
  28.6 1.0 bitcast_dynamic-update-slice_fusion.4
  29.7 0.1 collective-permute-done.6
  29.8 0.1 fusion.9
  29.9 0.4 convolution_convert_fusion.3
  30.4 3.2 %collective-permute-start.8 = (bf16[128,1024]{1,0:T(8,128)(2,1)S(1)}, bf16[128,1024]{1,0:T(8,128)(2,1)S(1)}, u32[]{:S(2)}, u32[]{:S(2)}) collective-permute-start(bf16[128,1024]{1,0:T(8,128)(2,1)S(1)} %convolution_convert_fusion.3), channel_id=1, source_target_pairs={{0,2},{2,4},{4,6},{6,8},{8,10},{10,12},{12,14},{14,0},{1,3},{3,5},... | collective-permute-start | bytes 786440 | tf_op jit(solution)/shard_map/sum_layers/ppermute | solution.py:25
  33.6 0.4 convolution_convert_fusion.2
  34.1 0.1 collective-permute-start.12
  34.1 0.4 convolution_convert_fusion.1
  34.6 3.3 %collective-permute-start.15 = (bf16[128,1024]{1,0:T(8,128)(2,1)S(1)}, bf16[128,1024]{1,0:T(8,128)(2,1)S(1)}, u32[]{:S(2)}, u32[]{:S(2)}) collective-permute-start(bf16[128,1024]{1,0:T(8,128)(2,1)S(1)} %convolution_convert_fusion.1), channel_id=1, source_target_pairs={{0,2},{2,4},{4,6},{6,8},{8,10},{10,12},{12,14},{14,0},{1,3},{3,5},... | collective-permute-start | bytes 786440 | tf_op jit(solution)/shard_map/sum_layers/ppermute | solution.py:25
  37.9 0.4 convolution_convert_fusion
  38.4 0.1 collective-permute-start.18
  38.5 1.9 %collective-permute-done.8 = bf16[128,1024]{1,0:T(8,128)(2,1)S(1)} collective-permute-done((bf16[128,1024]{1,0:T(8,128)(2,1)S(1)}, bf16[128,1024]{1,0:T(8,128)(2,1)S(1)}, u32[]{:S(2)}, u32[]{:S(2)}) %collective-permute-start.8) | collective-permute-done | bytes 262176 | tf_op jit(solution)/shard_map/sum_layers/ppermute | solution.py:25
  40.4 0.4 add_convert_fusion.5
  40.8 3.9 %collective-permute-start.9 = (bf16[128,1024]{1,0:T(8,128)(2,1)S(1)}, bf16[128,1024]{1,0:T(8,128)(2,1)S(1)}, u32[]{:S(2)}, u32[]{:S(2)}) collective-permute-start(bf16[128,1024]{1,0:T(8,128)(2,1)S(1)} %add_convert_fusion.5), channel_id=1, source_target_pairs={{0,2},{2,4},{4,6},{6,8},{8,10},{10,12},{12,14},{14,0},{1,3},{3,5},... | collective-permute-start | bytes 786440 | tf_op jit(solution)/shard_map/sum_layers/ppermute | solution.py:25
  44.8 0.4 add_convert_fusion.2
  45.3 0.7 collective-permute-done.15
  46.0 0.4 fusion.3
  46.4 3.8 %collective-permute-start.16 = (bf16[128,1024]{1,0:T(8,128)(2,1)S(1)}, bf16[128,1024]{1,0:T(8,128)(2,1)S(1)}, u32[]{:S(2)}, u32[]{:S(2)}) collective-permute-start(bf16[128,1024]{1,0:T(8,128)(2,1)S(1)} %fusion.3), channel_id=1, source_target_pairs={{0,2},{2,4},{4,6},{6,8},{8,10},{10,12},{12,14},{14,0},{1,3},{3,5},... | collective-permute-start | bytes 786440 | tf_op jit(solution)/shard_map/sum_layers/ppermute | solution.py:25
  50.2 0.4 fusion.6
  50.8 0.8 collective-permute-done.9
  51.6 0.4 add_convert_fusion.4
  52.0 3.8 %collective-permute-start.10 = (bf16[128,1024]{1,0:T(8,128)(2,1)S(1)}, bf16[128,1024]{1,0:T(8,128)(2,1)S(1)}, u32[]{:S(2)}, u32[]{:S(2)}) collective-permute-start(bf16[128,1024]{1,0:T(8,128)(2,1)S(1)} %add_convert_fusion.4), channel_id=1, source_target_pairs={{0,2},{2,4},{4,6},{6,8},{8,10},{10,12},{12,14},{14,0},{1,3},{3,5},... | collective-permute-start | bytes 786440 | tf_op jit(solution)/shard_map/sum_layers/ppermute | solution.py:25
  55.8 0.4 add_convert_fusion.1
  56.3 0.1 collective-permute-start.14
  56.4 0.8 collective-permute-done.16
  57.2 0.4 fusion.2
  57.7 3.8 %collective-permute-start.17 = (bf16[128,1024]{1,0:T(8,128)(2,1)S(1)}, bf16[128,1024]{1,0:T(8,128)(2,1)S(1)}, u32[]{:S(2)}, u32[]{:S(2)}) collective-permute-start(bf16[128,1024]{1,0:T(8,128)(2,1)S(1)} %fusion.2), channel_id=1, source_target_pairs={{0,2},{2,4},{4,6},{6,8},{8,10},{10,12},{12,14},{14,0},{1,3},{3,5},... | collective-permute-start | bytes 786440 | tf_op jit(solution)/shard_map/sum_layers/ppermute | solution.py:25
  61.4 0.4 fusion.5
  62.0 0.8 collective-permute-done.10
  62.8 0.4 add_convert_fusion.3
  63.3 3.8 %collective-permute-start.11 = (bf16[128,1024]{1,0:T(8,128)(2,1)S(1)}, bf16[128,1024]{1,0:T(8,128)(2,1)S(1)}, u32[]{:S(2)}, u32[]{:S(2)}) collective-permute-start(bf16[128,1024]{1,0:T(8,128)(2,1)S(1)} %add_convert_fusion.3), channel_id=1, source_target_pairs={{0,2},{2,4},{4,6},{6,8},{8,10},{10,12},{12,14},{14,0},{1,3},{3,5},... | collective-permute-start | bytes 786440 | tf_op jit(solution)/shard_map/sum_layers/ppermute | solution.py:25
  67.0 4.0 %collective-permute-done.20 = bf16[128,1024]{1,0:T(8,128)(2,1)S(1)} collective-permute-done((bf16[128,1024]{1,0:T(8,128)(2,1)S(1)}, bf16[128,1024]{1,0:T(8,128)(2,1)S(1)}, u32[]{:S(2)}, u32[]{:S(2)}) %collective-permute-start.20) | collective-permute-done | bytes 262176 | tf_op jit(solution)/shard_map/sum_layers/ppermute | solution.py:25
  71.0 0.4 fusion.4
  71.5 0.1 collective-permute-start.21
  71.6 1.1 collective-permute-done.11
  72.7 0.5 add_convert_fusion
  73.2 6.2 %collective-permute-done.21 = bf16[128,1024]{1,0:T(8,128)(2,1)S(1)} collective-permute-done((bf16[128,1024]{1,0:T(8,128)(2,1)S(1)}, bf16[128,1024]{1,0:T(8,128)(2,1)S(1)}, u32[]{:S(2)}, u32[]{:S(2)}) %collective-permute-start.21) | collective-permute-done | bytes 262176 | tf_op jit(solution)/shard_map/sum_layers/ppermute | solution.py:25
  79.4 0.5 fusion.1
  79.9 0.8 maximum_bitcast_fusion
  80.7 6.5 %all-to-all-start = ((bf16[16,8,2048]{2,1,0:T(8,128)(2,1)}), bf16[16,8,2048]{2,1,0:T(8,128)(2,1)S(1)}, u32[]{:S(2)}, u32[]{:S(2)}) async-start(bf16[16,8,2048]{2,1,0:T(8,128)(2,1)} %maximum_bitcast_fusion), calls=%async_computation | async-start | bytes 1048576 | tf_op jit(solution)/shard_map/to_components/all_to_all | solution.py:241
  87.3 0.1 select_reduce_fusion
  87.4 0.1 collective-permute-start.22
  87.6 1.1 collective-permute-done.22
  88.8 0.1 reshape.101.values_ref
  88.9 8.5 %all-to-all-done = bf16[16,8,2048]{2,1,0:T(8,128)(2,1)S(1)} async-done(((bf16[16,8,2048]{2,1,0:T(8,128)(2,1)}), bf16[16,8,2048]{2,1,0:T(8,128)(2,1)S(1)}, u32[]{:S(2)}, u32[]{:S(2)}) %all-to-all-start) | async-done | bytes 524320 | tf_op jit(solution)/shard_map/to_components/all_to_all | solution.py:241
  97.3 2.2 %fit.1 = f32[32,1,256]{2,1,0:T(1,128)} custom-call(s32[1]{0:T(128)} %bitcast.slot_ref, bf16[128,2048]{1,0:T(8,128)(2,1)S(1)} %bitcast.89, f32[32,2048]{1,0:T(8,128)S(1)} %reshape.101.values_ref), custom_call_target="tpu_custom_call" | custom-call | tf_op jit(solution)/shard_map/fit/pallas_call | solution.py:130
  99.5 3.8 %all-to-all-start.1 = ((f32[32,1,256]{2,1,0:T(1,128)}), f32[32,1,256]{2,1,0:T(1,128)S(1)}, u32[]{:S(2)}, u32[]{:S(2)}) async-start(f32[32,1,256]{2,1,0:T(1,128)} %fit.1), calls=%async_computation.1 | async-start | bytes 65536 | tf_op jit(solution)/shard_map/gather_scores/all_to_all | solution.py:246
  103.4 0.1 pad_dynamic-slice_fusion
  103.5 7.3 %all-to-all-done.1 = f32[32,1,256]{2,1,0:T(1,128)S(1)} async-done(((f32[32,1,256]{2,1,0:T(1,128)}), f32[32,1,256]{2,1,0:T(1,128)S(1)}, u32[]{:S(2)}, u32[]{:S(2)}) %all-to-all-start.1) | async-done | bytes 32800 | tf_op jit(solution)/shard_map/gather_scores/all_to_all | solution.py:246
  110.9 1.9 %collective-permute-start.23 = (f32[256]{0:T(256)S(1)}, f32[256]{0:T(256)S(1)}, u32[]{:S(2)}, u32[]{:S(2)}) collective-permute-start(f32[256]{0:T(256)S(1)} %reduce_sum.19), channel_id=1, source_target_pairs={{0,2},{2,4},{4,6},{6,8},{8,10},{10,12},{12,14},{3,1},{5,3},{7,5},{... | collective-permute-start | bytes 3080 | tf_op jit(solution)/shard_map/gather_scores/ppermute | solution.py:249
  112.8 0.6 dynamic_slice.55
  113.4 2.9 %collective-permute-done.23 = f32[256]{0:T(256)S(1)} collective-permute-done((f32[256]{0:T(256)S(1)}, f32[256]{0:T(256)S(1)}, u32[]{:S(2)}, u32[]{:S(2)}) %collective-permute-start.23) | collective-permute-done | bytes 1056 | tf_op jit(solution)/shard_map/gather_scores/ppermute | solution.py:249
  116.5 0.6 add_divide_fusion
  (40 shorter events, 1.0 us)
Async XLA Ops:
  2.5 9.3 %collective-permute-start = (bf16[144,1024]{1,0:T(8,128)(2,1)}, bf16[144,1024]{1,0:T(8,128)(2,1)S(1)}, u32[]{:S(2)}, u32[]{:S(2)}) collective-permute-start(bf16[144,1024]{1,0:T(8,128)(2,1)} %weigh.1), channel_id=1, source_target_pairs={{0,96},{32,0},{64,32},{96,64},{1,97},{33,1},{65,33},{97,65},{2,98}... | collective-permute-start | bytes 884744 | tf_op jit(solution)/shard_map/gather_rows/ppermute | solution.py:25
  5.2 11.2 %collective-permute-start.2 = (bf16[144,1024]{1,0:T(8,128)(2,1)}, bf16[144,1024]{1,0:T(8,128)(2,1)S(1)}, u32[]{:S(2)}, u32[]{:S(2)}) collective-permute-start(bf16[144,1024]{1,0:T(8,128)(2,1)} %weigh.1), channel_id=1, source_target_pairs={{0,32},{32,64},{64,96},{96,0},{1,33},{33,65},{65,97},{97,1},{2,34}... | collective-permute-start | bytes 884744 | tf_op jit(solution)/shard_map/gather_rows/ppermute | solution.py:25
  5.2 24.6 %collective-permute-start.7 = (bf16[1024,1024]{1,0:T(8,128)(2,1)}, bf16[1024,1024]{1,0:T(8,128)(2,1)S(1)}, u32[]{:S(2)}, u32[]{:S(2)}) collective-permute-start(bf16[1024,1024]{1,0:T(8,128)(2,1)} %param.10), channel_id=1, source_target_pairs={{0,16},{16,0},{1,17},{17,1},{2,18},{18,2},{3,19},{19,3},{4,20},{20... | collective-permute-start | bytes 6291464 | tf_op jit(solution)/shard_map/swap_eigvecs/ppermute | solution.py:25
  5.2 16.3 %collective-permute-start.5 = (bf16[144,1024]{1,0:T(8,128)(2,1)}, bf16[144,1024]{1,0:T(8,128)(2,1)S(1)}, u32[]{:S(2)}, u32[]{:S(2)}) collective-permute-start(bf16[144,1024]{1,0:T(8,128)(2,1)} %weigh.1), channel_id=1, source_target_pairs={{0,128},{128,0},{1,129},{129,1},{2,130},{130,2},{3,131},{131,3},{4... | collective-permute-start | bytes 884744 | tf_op jit(solution)/shard_map/gather_rows/ppermute | solution.py:25
  11.8 10.5 %collective-permute-start.1 = (bf16[144,1024]{1,0:T(8,128)(2,1)S(1)}, bf16[144,1024]{1,0:T(8,128)(2,1)S(1)}, u32[]{:S(2)}, u32[]{:S(2)}) collective-permute-start(bf16[144,1024]{1,0:T(8,128)(2,1)S(1)} %collective-permute-done), channel_id=1, source_target_pairs={{0,224},{32,128},{64,160},{96,192},{128,96},{160,0},{192,32},{224,... | collective-permute-start | bytes 884744 | tf_op jit(solution)/shard_map/gather_rows/ppermute | solution.py:151
  16.4 11.2 %collective-permute-start.3 = (bf16[144,1024]{1,0:T(8,128)(2,1)S(1)}, bf16[144,1024]{1,0:T(8,128)(2,1)}, u32[]{:S(2)}, u32[]{:S(2)}) collective-permute-start(bf16[144,1024]{1,0:T(8,128)(2,1)S(1)} %collective-permute-done.2), channel_id=1, source_target_pairs={{0,128},{128,0},{1,129},{129,1},{2,130},{130,2},{3,131},{131,3},{4... | collective-permute-start | bytes 884744 | tf_op jit(solution)/shard_map/gather_rows/ppermute | solution.py:25
  17.1 12.5 %collective-permute-start.4 = (bf16[144,1024]{1,0:T(8,128)(2,1)S(1)}, bf16[144,1024]{1,0:T(8,128)(2,1)S(1)}, u32[]{:S(2)}, u32[]{:S(2)}) collective-permute-start(bf16[144,1024]{1,0:T(8,128)(2,1)S(1)} %collective-permute-done.2), channel_id=1, source_target_pairs={{0,32},{32,64},{64,96},{96,0},{1,33},{33,65},{65,97},{97,1},{2,34}... | collective-permute-start | bytes 884744 | tf_op jit(solution)/shard_map/gather_rows/ppermute | solution.py:25
  21.6 8.3 %collective-permute-start.6 = (bf16[144,1024]{1,0:T(8,128)(2,1)S(1)}, bf16[144,1024]{1,0:T(8,128)(2,1)S(1)}, u32[]{:S(2)}, u32[]{:S(2)}) collective-permute-start(bf16[144,1024]{1,0:T(8,128)(2,1)S(1)} %collective-permute-done.5), channel_id=1, source_target_pairs={{0,96},{32,0},{64,32},{96,64},{1,97},{33,1},{65,33},{97,65},{2,98}... | collective-permute-start | bytes 884744 | tf_op jit(solution)/shard_map/gather_rows/ppermute | solution.py:25
  22.4 7.6 %copy-start = (bf16[1024,1024]{1,0:T(8,128)(2,1)S(1)}, bf16[1024,1024]{1,0:T(8,128)(2,1)}, u32[]{:S(2)}) copy-start(bf16[1024,1024]{1,0:T(8,128)(2,1)} %param.10) | copy-start | bytes 6291460
  30.4 10.0 %collective-permute-start.8 = (bf16[128,1024]{1,0:T(8,128)(2,1)S(1)}, bf16[128,1024]{1,0:T(8,128)(2,1)S(1)}, u32[]{:S(2)}, u32[]{:S(2)}) collective-permute-start(bf16[128,1024]{1,0:T(8,128)(2,1)S(1)} %convolution_convert_fusion.3), channel_id=1, source_target_pairs={{0,2},{2,4},{4,6},{6,8},{8,10},{10,12},{12,14},{14,0},{1,3},{3,5},... | collective-permute-start | bytes 786440 | tf_op jit(solution)/shard_map/sum_layers/ppermute | solution.py:25
  34.1 10.7 %collective-permute-start.12 = (bf16[128,1024]{1,0:T(8,128)(2,1)S(1)}, bf16[128,1024]{1,0:T(8,128)(2,1)S(1)}, u32[]{:S(2)}, u32[]{:S(2)}) collective-permute-start(bf16[128,1024]{1,0:T(8,128)(2,1)S(1)} %convolution_convert_fusion.2), channel_id=1, source_target_pairs={{0,14},{2,0},{4,2},{6,4},{8,6},{10,8},{12,10},{14,12},{1,15},{3,1}... | collective-permute-start | bytes 786440 | tf_op jit(solution)/shard_map/sum_layers/ppermute | solution.py:25
  34.6 11.4 %collective-permute-start.15 = (bf16[128,1024]{1,0:T(8,128)(2,1)S(1)}, bf16[128,1024]{1,0:T(8,128)(2,1)S(1)}, u32[]{:S(2)}, u32[]{:S(2)}) collective-permute-start(bf16[128,1024]{1,0:T(8,128)(2,1)S(1)} %convolution_convert_fusion.1), channel_id=1, source_target_pairs={{0,2},{2,4},{4,6},{6,8},{8,10},{10,12},{12,14},{14,0},{1,3},{3,5},... | collective-permute-start | bytes 786440 | tf_op jit(solution)/shard_map/sum_layers/ppermute | solution.py:25
  38.4 11.9 %collective-permute-start.18 = (bf16[128,1024]{1,0:T(8,128)(2,1)S(1)}, bf16[128,1024]{1,0:T(8,128)(2,1)S(1)}, u32[]{:S(2)}, u32[]{:S(2)}) collective-permute-start(bf16[128,1024]{1,0:T(8,128)(2,1)S(1)} %convolution_convert_fusion), channel_id=1, source_target_pairs={{0,14},{2,0},{4,2},{6,4},{8,6},{10,8},{12,10},{14,12},{1,15},{3,1}... | collective-permute-start | bytes 786440 | tf_op jit(solution)/shard_map/sum_layers/ppermute | solution.py:25
  40.8 10.8 %collective-permute-start.9 = (bf16[128,1024]{1,0:T(8,128)(2,1)S(1)}, bf16[128,1024]{1,0:T(8,128)(2,1)S(1)}, u32[]{:S(2)}, u32[]{:S(2)}) collective-permute-start(bf16[128,1024]{1,0:T(8,128)(2,1)S(1)} %add_convert_fusion.5), channel_id=1, source_target_pairs={{0,2},{2,4},{4,6},{6,8},{8,10},{10,12},{12,14},{14,0},{1,3},{3,5},... | collective-permute-start | bytes 786440 | tf_op jit(solution)/shard_map/sum_layers/ppermute | solution.py:25
  45.2 10.6 %collective-permute-start.13 = (bf16[128,1024]{1,0:T(8,128)(2,1)S(1)}, bf16[128,1024]{1,0:T(8,128)(2,1)S(1)}, u32[]{:S(2)}, u32[]{:S(2)}) collective-permute-start(bf16[128,1024]{1,0:T(8,128)(2,1)S(1)} %add_convert_fusion.2), channel_id=1, source_target_pairs={{0,14},{2,0},{4,2},{6,4},{8,6},{10,8},{12,10},{14,12},{1,15},{3,1}... | collective-permute-start | bytes 786440 | tf_op jit(solution)/shard_map/sum_layers/ppermute | solution.py:25
  46.4 10.8 %collective-permute-start.16 = (bf16[128,1024]{1,0:T(8,128)(2,1)S(1)}, bf16[128,1024]{1,0:T(8,128)(2,1)S(1)}, u32[]{:S(2)}, u32[]{:S(2)}) collective-permute-start(bf16[128,1024]{1,0:T(8,128)(2,1)S(1)} %fusion.3), channel_id=1, source_target_pairs={{0,2},{2,4},{4,6},{6,8},{8,10},{10,12},{12,14},{14,0},{1,3},{3,5},... | collective-permute-start | bytes 786440 | tf_op jit(solution)/shard_map/sum_layers/ppermute | solution.py:25
  50.7 10.8 %collective-permute-start.19 = (bf16[128,1024]{1,0:T(8,128)(2,1)S(1)}, bf16[128,1024]{1,0:T(8,128)(2,1)S(1)}, u32[]{:S(2)}, u32[]{:S(2)}) collective-permute-start(bf16[128,1024]{1,0:T(8,128)(2,1)S(1)} %fusion.6), channel_id=1, source_target_pairs={{0,14},{2,0},{4,2},{6,4},{8,6},{10,8},{12,10},{14,12},{1,15},{3,1}... | collective-permute-start | bytes 786440 | tf_op jit(solution)/shard_map/sum_layers/ppermute | solution.py:25
  52.0 10.8 %collective-permute-start.10 = (bf16[128,1024]{1,0:T(8,128)(2,1)S(1)}, bf16[128,1024]{1,0:T(8,128)(2,1)S(1)}, u32[]{:S(2)}, u32[]{:S(2)}) collective-permute-start(bf16[128,1024]{1,0:T(8,128)(2,1)S(1)} %add_convert_fusion.4), channel_id=1, source_target_pairs={{0,2},{2,4},{4,6},{6,8},{8,10},{10,12},{12,14},{14,0},{1,3},{3,5},... | collective-permute-start | bytes 786440 | tf_op jit(solution)/shard_map/sum_layers/ppermute | solution.py:25
  56.3 15.3 %collective-permute-start.14 = (bf16[128,1024]{1,0:T(8,128)(2,1)S(1)}, bf16[128,1024]{1,0:T(8,128)(2,1)S(1)}, u32[]{:S(2)}, u32[]{:S(2)}) collective-permute-start(bf16[128,1024]{1,0:T(8,128)(2,1)S(1)} %add_convert_fusion.1), channel_id=1, source_target_pairs={{0,14},{2,0},{4,2},{6,4},{8,6},{10,8},{12,10},{14,12},{1,15},{3,1}... | collective-permute-start | bytes 786440 | tf_op jit(solution)/shard_map/sum_layers/ppermute | solution.py:25
  57.7 15.5 %collective-permute-start.17 = (bf16[128,1024]{1,0:T(8,128)(2,1)S(1)}, bf16[128,1024]{1,0:T(8,128)(2,1)S(1)}, u32[]{:S(2)}, u32[]{:S(2)}) collective-permute-start(bf16[128,1024]{1,0:T(8,128)(2,1)S(1)} %fusion.2), channel_id=1, source_target_pairs={{0,2},{2,4},{4,6},{6,8},{8,10},{10,12},{12,14},{14,0},{1,3},{3,5},... | collective-permute-start | bytes 786440 | tf_op jit(solution)/shard_map/sum_layers/ppermute | solution.py:25
  61.9 9.1 %collective-permute-start.20 = (bf16[128,1024]{1,0:T(8,128)(2,1)S(1)}, bf16[128,1024]{1,0:T(8,128)(2,1)S(1)}, u32[]{:S(2)}, u32[]{:S(2)}) collective-permute-start(bf16[128,1024]{1,0:T(8,128)(2,1)S(1)} %fusion.5), channel_id=1, source_target_pairs={{0,14},{2,0},{4,2},{6,4},{8,6},{10,8},{12,10},{14,12},{1,15},{3,1}... | collective-permute-start | bytes 786440 | tf_op jit(solution)/shard_map/sum_layers/ppermute | solution.py:25
  63.3 9.4 %collective-permute-start.11 = (bf16[128,1024]{1,0:T(8,128)(2,1)S(1)}, bf16[128,1024]{1,0:T(8,128)(2,1)S(1)}, u32[]{:S(2)}, u32[]{:S(2)}) collective-permute-start(bf16[128,1024]{1,0:T(8,128)(2,1)S(1)} %add_convert_fusion.3), channel_id=1, source_target_pairs={{0,2},{2,4},{4,6},{6,8},{8,10},{10,12},{12,14},{14,0},{1,3},{3,5},... | collective-permute-start | bytes 786440 | tf_op jit(solution)/shard_map/sum_layers/ppermute | solution.py:25
  71.5 7.9 %collective-permute-start.21 = (bf16[128,1024]{1,0:T(8,128)(2,1)S(1)}, bf16[128,1024]{1,0:T(8,128)(2,1)S(1)}, u32[]{:S(2)}, u32[]{:S(2)}) collective-permute-start(bf16[128,1024]{1,0:T(8,128)(2,1)S(1)} %fusion.4), channel_id=1, source_target_pairs={{0,14},{2,0},{4,2},{6,4},{8,6},{10,8},{12,10},{14,12},{1,15},{3,1}... | collective-permute-start | bytes 786440 | tf_op jit(solution)/shard_map/sum_layers/ppermute | solution.py:25
  73.1 14.4 %copy-start.1 = (s32[1024]{0:T(1024)S(1)}, s32[1024]{0:T(1024)}, u32[]{:S(2)}) copy-start(s32[1024]{0:T(1024)} %param.12) | copy-start | bytes 12292
  79.9 36.7 %copy-start.2 = (s32[64]{0:T(128)S(1)}, s32[64]{0:T(128)}, u32[]{:S(2)}) copy-start(s32[64]{0:T(128)} %param.13) | copy-start | bytes 772
  80.7 16.6 %all-to-all-start = ((bf16[16,8,2048]{2,1,0:T(8,128)(2,1)}), bf16[16,8,2048]{2,1,0:T(8,128)(2,1)S(1)}, u32[]{:S(2)}, u32[]{:S(2)}) async-start(bf16[16,8,2048]{2,1,0:T(8,128)(2,1)} %maximum_bitcast_fusion), calls=%async_computation | async-start | bytes 1048576 | tf_op jit(solution)/shard_map/to_components/all_to_all | solution.py:241
  87.4 1.3 %collective-permute-start.22 = (f32[8,1024]{1,0:T(8,128)S(1)}, f32[8,1024]{1,0:T(8,128)S(1)}, u32[]{:S(2)}, u32[]{:S(2)}) collective-permute-start(f32[8,1024]{1,0:T(8,128)S(1)} %select_reduce_fusion), channel_id=1, source_target_pairs={{0,16},{16,0},{1,17},{17,1},{2,18},{18,2},{3,19},{19,3},{4,20},{20... | collective-permute-start | bytes 98312 | tf_op jit(solution)/shard_map/gather_values/ppermute | solution.py:25
  99.5 11.3 %all-to-all-start.1 = ((f32[32,1,256]{2,1,0:T(1,128)}), f32[32,1,256]{2,1,0:T(1,128)S(1)}, u32[]{:S(2)}, u32[]{:S(2)}) async-start(f32[32,1,256]{2,1,0:T(1,128)} %fit.1), calls=%async_computation.1 | async-start | bytes 65536 | tf_op jit(solution)/shard_map/gather_scores/all_to_all | solution.py:246
  110.9 5.5 %collective-permute-start.23 = (f32[256]{0:T(256)S(1)}, f32[256]{0:T(256)S(1)}, u32[]{:S(2)}, u32[]{:S(2)}) collective-permute-start(f32[256]{0:T(256)S(1)} %reduce_sum.19), channel_id=1, source_target_pairs={{0,2},{2,4},{4,6},{6,8},{8,10},{10,12},{12,14},{3,1},{5,3},{7,5},{... | collective-permute-start | bytes 3080 | tf_op jit(solution)/shard_map/gather_scores/ppermute | solution.py:249

commit v13 on v12

--- a/solution.py
+++ b/solution.py
@@ -154,8 +154,8 @@
     over_far = across(right, -1)
     over_right = shifted(over, x, -1)
     far = shifted(left, x, 1)
-    over_right = over_right + 0 * other[: own.shape[0]]
-    return jnp.stack([over_far, over_left, own, right, far, left, over, over_right])
+    over_left = over_left + 0 * other[: own.shape[0]]
+    return jnp.stack([over_far, over_right, over, left, far, right, own, over_left])
 
 
 def smooth_block(widened, places, present, reaches):
@@ -197,7 +197,7 @@
     rows = own.shape[0] - EXTRA
 
     def place(across, along):
-        return (4 * (across ^ y) + (along - x) % 4 + 2) % 8
+        return (6 - 4 * (across ^ y) - (along - x) % 4) % 8
 
     with jax.named_scope("gather_values"):
         here = jnp.arange(8, dtype=jnp.int32)
@@ -217,11 +217,15 @@
     far = layers // 2
     sent = {}
 
-    def onward(q, way, ahead):
+    def onward(q, way, ahead, behind=None):
         total = term(q, way * ahead)
         if (q, way) in sent:
             total = total + sent[q, way].astype(jnp.float32)
-        sent[q, way] = shifted(total.astype(jnp.bfloat16), "cpg_0", way)
+        if behind is not None:
+            total = total + 0.0 * behind.astype(jnp.float32)
+        total = total.astype(jnp.bfloat16)
+        sent[q, way] = shifted(total, "cpg_0", way)
+        return total
 
     def summed(q):
         total = term(q, 0)
@@ -232,10 +236,10 @@
     with jax.named_scope("sum_layers"):
         for ahead in range(far, 0, -1):
             onward(0, 1, ahead)
-            onward(1, -1, ahead)
+            behind = onward(1, -1, ahead)
             if ahead > 1:
-                onward(0, -1, ahead - 1)
-                onward(1, 1, ahead - 1)
+                onward(0, -1, ahead - 1, behind)
+                onward(1, 1, ahead - 1, behind)
         whole = jnp.concatenate([summed(0), summed(1)], axis=1)
     with jax.named_scope("to_components"):
         sums = lax.all_to_all(whole, PLANE, 0, 0, tiled=True)

time: 118 us -> 114 us (0.966)
  waiting for transfers between devices: 51.7 us -> 49.7 us
  starting transfers between devices: 48 us -> 46.3 us
    ppermute x22, waiting for transfers between devices: 32.3 us -> 27.3 us  [shifted(): lax.ppermute(value, axis, [(i, (i + by) % peers) for i in range(peers)])]
    ppermute x1, waiting for transfers between devices: 0.75 us -> 4.79 us  [across(): return lax.ppermute(value, (y, x), pairs)]
    ppermute x22, starting transfers between devices: 31.2 us -> 27.3 us  [shifted(): lax.ppermute(value, axis, [(i, (i + by) % peers) for i in range(peers)])]
  transfers between devices with their start and end apart: 26 -> 26, of which waited for: 17 -> 16; matrix products, arithmetic and copies ran while one was open for 8% -> 8% of each run, Pallas kernels for 0% -> 0%
where the time goes in v13:
time: 114 us
  waiting for transfers between devices  49.7 us (44%)
  starting transfers between devices  46.3 us (41%)
  matrix products  7.3 us (6%)
  Pallas kernels  4.06 us (4%)
  local copies, waits for them, and re-layouts  3.07 us (3%)
  other arithmetic  2.04 us (2%)
  between operations  1.57 us (1%)
    ppermute x22, waiting for transfers between devices, shifted(): lax.ppermute(value, axis, [(i, (i + by) % peers) for i in range(peers)])  27.3 us
    ppermute x22, starting transfers between devices, shifted(): lax.ppermute(value, axis, [(i, (i + by) % peers) for i in range(peers)])  27.3 us
    all_to_all x1, waiting for transfers between devices, shards(): sums = lax.all_to_all(whole, PLANE, 0, 0, tiled=True)  8.41 us
    all_to_all x1, starting transfers between devices, shards(): sums = lax.all_to_all(whole, PLANE, 0, 0, tiled=True)  7.58 us
    all_to_all x1, waiting for transfers between devices, shards(): lax.all_to_all(fitted, LAYER, 0, 0, tiled=True)  7.32 us
    dot_general x16, matrix products, term(): return jnp.dot(block, vecs[q], preferred_element_type=jnp.float32)  7.3 us
    ppermute x1, waiting for transfers between devices, across(): return lax.ppermute(value, (y, x), pairs)  4.79 us
    ppermute x1, starting transfers between devices, across(): return lax.ppermute(value, (y, x), pairs)  4.6 us
  transfers between devices with their start and end apart: 26, of which 16 were waited for; matrix products, arithmetic and copies ran while one was open for 8% of the time, Pallas kernels for 0%

profile of v13, /device:TPU:96, one launch (start us, length us, event | category | flops | bytes accessed | tf_op | source)
XLA Modules:
  0.0 114.0 jit_solution(8407261140242218143)
XLA Ops:
  0.6 1.9 %weigh.1 = bf16[144,1024]{1,0:T(8,128)(2,1)} custom-call(bf16[64,1024]{1,0:T(8,128)(2,1)} %resp_ref.1, bf16[64,1024]{1,0:T(8,128)(2,1)} %weight_ref.1, f32[1,1024]{1,0:T(1,128)} %bitcast.91, f32[1,1024]{1,0:T(1,128)} %bitcast.92), custom_call_target="tpu_custom_call" | custom-call | tf_op jit(solution)/shard_map/weigh/pallas_call | solution.py:57
  2.5 2.8 %collective-permute-start = (bf16[144,1024]{1,0:T(8,128)(2,1)}, bf16[144,1024]{1,0:T(8,128)(2,1)S(1)}, u32[]{:S(2)}, u32[]{:S(2)}) collective-permute-start(bf16[144,1024]{1,0:T(8,128)(2,1)} %weigh.1), channel_id=1, source_target_pairs={{0,96},{32,0},{64,32},{96,64},{1,97},{33,1},{65,33},{97,65},{2,98}... | collective-permute-start | bytes 884744 | tf_op jit(solution)/shard_map/gather_rows/ppermute | solution.py:25
  5.3 1.6 %collective-permute-start.2 = (bf16[144,1024]{1,0:T(8,128)(2,1)}, bf16[144,1024]{1,0:T(8,128)(2,1)S(1)}, u32[]{:S(2)}, u32[]{:S(2)}) collective-permute-start(bf16[144,1024]{1,0:T(8,128)(2,1)} %weigh.1), channel_id=1, source_target_pairs={{0,128},{128,0},{1,129},{129,1},{2,130},{130,2},{3,131},{131,3},{4... | collective-permute-start | bytes 884744 | tf_op jit(solution)/shard_map/gather_rows/ppermute | solution.py:25
  6.8 5.0 %collective-permute-done = bf16[144,1024]{1,0:T(8,128)(2,1)S(1)} collective-permute-done((bf16[144,1024]{1,0:T(8,128)(2,1)}, bf16[144,1024]{1,0:T(8,128)(2,1)S(1)}, u32[]{:S(2)}, u32[]{:S(2)}) %collective-permute-start) | collective-permute-done | bytes 294944 | tf_op jit(solution)/shard_map/gather_rows/ppermute | solution.py:25
  11.8 4.6 %collective-permute-start.1 = (bf16[144,1024]{1,0:T(8,128)(2,1)S(1)}, bf16[144,1024]{1,0:T(8,128)(2,1)}, u32[]{:S(2)}, u32[]{:S(2)}) collective-permute-start(bf16[144,1024]{1,0:T(8,128)(2,1)S(1)} %collective-permute-done), channel_id=1, source_target_pairs={{0,224},{32,128},{64,160},{96,192},{128,96},{160,0},{192,32},{224,... | collective-permute-start | bytes 884744 | tf_op jit(solution)/shard_map/gather_rows/ppermute | solution.py:151
  16.5 0.1 collective-permute-start.3
  17.1 0.6 collective-permute-done.4
  17.7 1.0 collective-permute-start.5
  18.7 0.4 collective-permute-start.6
  19.1 4.8 %collective-permute-done.1 = bf16[144,1024]{1,0:T(8,128)(2,1)} collective-permute-done((bf16[144,1024]{1,0:T(8,128)(2,1)S(1)}, bf16[144,1024]{1,0:T(8,128)(2,1)}, u32[]{:S(2)}, u32[]{:S(2)}) %collective-permute-start.1) | collective-permute-done | bytes 294944 | tf_op jit(solution)/shard_map/gather_rows/ppermute | solution.py:151
  23.9 1.0 bitcast_dynamic-update-slice_fusion.6
  24.9 3.3 %collective-permute-done.3 = bf16[144,1024]{1,0:T(8,128)(2,1)} collective-permute-done((bf16[144,1024]{1,0:T(8,128)(2,1)S(1)}, bf16[144,1024]{1,0:T(8,128)(2,1)}, u32[]{:S(2)}, u32[]{:S(2)}) %collective-permute-start.3) | collective-permute-done | bytes 294944 | tf_op jit(solution)/shard_map/gather_rows/ppermute | solution.py:25
  28.1 1.0 bitcast_dynamic-update-slice_fusion.5
  29.3 0.1 fusion.13
  29.4 0.4 convolution_convert_fusion.1
  29.9 3.2 %collective-permute-start.8 = (bf16[128,1024]{1,0:T(8,128)(2,1)S(1)}, bf16[128,1024]{1,0:T(8,128)(2,1)S(1)}, u32[]{:S(2)}, u32[]{:S(2)}) collective-permute-start(bf16[128,1024]{1,0:T(8,128)(2,1)S(1)} %convolution_convert_fusion.1), channel_id=1, source_target_pairs={{0,2},{2,4},{4,6},{6,8},{8,10},{10,12},{12,14},{14,0},{1,3},{3,5},... | collective-permute-start | bytes 786440 | tf_op jit(solution)/shard_map/sum_layers/ppermute | solution.py:25
  33.1 0.4 convolution_convert_fusion
  33.5 0.1 collective-permute-start.13
  33.6 0.5 fusion.6
  34.1 0.1 collective-permute-start.12
  34.2 0.5 fusion.9
  34.6 3.3 %collective-permute-start.17 = (bf16[128,1024]{1,0:T(8,128)(2,1)S(1)}, bf16[128,1024]{1,0:T(8,128)(2,1)S(1)}, u32[]{:S(2)}, u32[]{:S(2)}) collective-permute-start(bf16[128,1024]{1,0:T(8,128)(2,1)S(1)} %fusion.9), channel_id=1, source_target_pairs={{0,2},{2,4},{4,6},{6,8},{8,10},{10,12},{12,14},{14,0},{1,3},{3,5},... | collective-permute-start | bytes 786440 | tf_op jit(solution)/shard_map/sum_layers/ppermute | solution.py:25
  38.0 0.4 collective-permute-done.8
  38.4 0.4 add_convert_fusion.5
  38.8 4.0 %collective-permute-start.9 = (bf16[128,1024]{1,0:T(8,128)(2,1)S(1)}, bf16[128,1024]{1,0:T(8,128)(2,1)S(1)}, u32[]{:S(2)}, u32[]{:S(2)}) collective-permute-start(bf16[128,1024]{1,0:T(8,128)(2,1)S(1)} %add_convert_fusion.5), channel_id=1, source_target_pairs={{0,2},{2,4},{4,6},{6,8},{8,10},{10,12},{12,14},{14,0},{1,3},{3,5},... | collective-permute-start | bytes 786440 | tf_op jit(solution)/shard_map/sum_layers/ppermute | solution.py:25
  42.8 1.3 %collective-permute-done.13 = bf16[128,1024]{1,0:T(8,128)(2,1)S(1)} collective-permute-done((bf16[128,1024]{1,0:T(8,128)(2,1)S(1)}, bf16[128,1024]{1,0:T(8,128)(2,1)S(1)}, u32[]{:S(2)}, u32[]{:S(2)}) %collective-permute-start.13) | collective-permute-done | bytes 262176 | tf_op jit(solution)/shard_map/sum_layers/ppermute | solution.py:25
  44.1 0.4 fusion.7
  44.6 5.1 %collective-permute-done.12 = bf16[128,1024]{1,0:T(8,128)(2,1)S(1)} collective-permute-done((bf16[128,1024]{1,0:T(8,128)(2,1)S(1)}, bf16[128,1024]{1,0:T(8,128)(2,1)S(1)}, u32[]{:S(2)}, u32[]{:S(2)}) %collective-permute-start.12) | collective-permute-done | bytes 262176 | tf_op jit(solution)/shard_map/sum_layers/ppermute | solution.py:25
  49.7 0.5 add_convert_fusion.2
  50.3 0.5 fusion.5
  50.8 3.3 %collective-permute-start.18 = (bf16[128,1024]{1,0:T(8,128)(2,1)S(1)}, bf16[128,1024]{1,0:T(8,128)(2,1)S(1)}, u32[]{:S(2)}, u32[]{:S(2)}) collective-permute-start(bf16[128,1024]{1,0:T(8,128)(2,1)S(1)} %fusion.5), channel_id=1, source_target_pairs={{0,2},{2,4},{4,6},{6,8},{8,10},{10,12},{12,14},{14,0},{1,3},{3,5},... | collective-permute-start | bytes 786440 | tf_op jit(solution)/shard_map/sum_layers/ppermute | solution.py:25
  54.1 0.4 add_convert_fusion.4
  54.5 0.1 collective-permute-start.10
  54.6 0.5 collective-permute-done.15
  55.1 0.4 fusion.8
  55.6 1.6 %collective-permute-start.20 = (bf16[128,1024]{1,0:T(8,128)(2,1)S(1)}, bf16[128,1024]{1,0:T(8,128)(2,1)S(1)}, u32[]{:S(2)}, u32[]{:S(2)}) collective-permute-start(bf16[128,1024]{1,0:T(8,128)(2,1)S(1)} %fusion.8), channel_id=1, source_target_pairs={{0,14},{2,0},{4,2},{6,4},{8,6},{10,8},{12,10},{14,12},{1,15},{3,1}... | collective-permute-start | bytes 786440 | tf_op jit(solution)/shard_map/sum_layers/ppermute | solution.py:25
  57.2 3.6 %collective-permute-done.14 = bf16[128,1024]{1,0:T(8,128)(2,1)S(1)} collective-permute-done((bf16[128,1024]{1,0:T(8,128)(2,1)S(1)}, bf16[128,1024]{1,0:T(8,128)(2,1)S(1)}, u32[]{:S(2)}, u32[]{:S(2)}) %collective-permute-start.14) | collective-permute-done | bytes 262176 | tf_op jit(solution)/shard_map/sum_layers/ppermute | solution.py:25
  60.7 0.5 add_convert_fusion.1
  61.3 0.5 fusion.4
  61.8 3.3 %collective-permute-start.19 = (bf16[128,1024]{1,0:T(8,128)(2,1)S(1)}, bf16[128,1024]{1,0:T(8,128)(2,1)S(1)}, u32[]{:S(2)}, u32[]{:S(2)}) collective-permute-start(bf16[128,1024]{1,0:T(8,128)(2,1)S(1)} %fusion.4), channel_id=1, source_target_pairs={{0,2},{2,4},{4,6},{6,8},{8,10},{10,12},{12,14},{14,0},{1,3},{3,5},... | collective-permute-start | bytes 786440 | tf_op jit(solution)/shard_map/sum_layers/ppermute | solution.py:25
  65.1 0.4 add_convert_fusion.3
  65.6 1.4 %collective-permute-start.11 = (bf16[128,1024]{1,0:T(8,128)(2,1)S(1)}, bf16[128,1024]{1,0:T(8,128)(2,1)S(1)}, u32[]{:S(2)}, u32[]{:S(2)}) collective-permute-start(bf16[128,1024]{1,0:T(8,128)(2,1)S(1)} %add_convert_fusion.3), channel_id=1, source_target_pairs={{0,2},{2,4},{4,6},{6,8},{8,10},{10,12},{12,14},{14,0},{1,3},{3,5},... | collective-permute-start | bytes 786440 | tf_op jit(solution)/shard_map/sum_layers/ppermute | solution.py:25
  67.0 0.4 fusion.10
  67.4 0.8 collective-permute-start.21
  68.2 3.5 %collective-permute-done.16 = bf16[128,1024]{1,0:T(8,128)(2,1)S(1)} collective-permute-done((bf16[128,1024]{1,0:T(8,128)(2,1)S(1)}, bf16[128,1024]{1,0:T(8,128)(2,1)S(1)}, u32[]{:S(2)}, u32[]{:S(2)}) %collective-permute-start.16) | collective-permute-done | bytes 262176 | tf_op jit(solution)/shard_map/sum_layers/ppermute | solution.py:25
  71.7 0.5 collective-permute-done.11
  72.2 0.5 add_convert_fusion
  72.7 2.4 %collective-permute-done.21 = bf16[128,1024]{1,0:T(8,128)(2,1)S(1)} collective-permute-done((bf16[128,1024]{1,0:T(8,128)(2,1)S(1)}, bf16[128,1024]{1,0:T(8,128)(2,1)S(1)}, u32[]{:S(2)}, u32[]{:S(2)}) %collective-permute-start.21) | collective-permute-done | bytes 262176 | tf_op jit(solution)/shard_map/sum_layers/ppermute | solution.py:25
  75.1 0.5 fusion.3
  75.6 0.8 maximum_bitcast_fusion
  76.4 7.6 %all-to-all-start = ((bf16[16,8,2048]{2,1,0:T(8,128)(2,1)}), bf16[16,8,2048]{2,1,0:T(8,128)(2,1)S(1)}, u32[]{:S(2)}, u32[]{:S(2)}) async-start(bf16[16,8,2048]{2,1,0:T(8,128)(2,1)} %maximum_bitcast_fusion), calls=%async_computation | async-start | bytes 1048576 | tf_op jit(solution)/shard_map/to_components/all_to_all | solution.py:245
  84.1 0.1 select_reduce_fusion
  84.2 0.1 collective-permute-start.22
  84.4 1.1 collective-permute-done.22
  85.6 0.1 reshape.101.values_ref
  85.7 8.4 %all-to-all-done = bf16[16,8,2048]{2,1,0:T(8,128)(2,1)S(1)} async-done(((bf16[16,8,2048]{2,1,0:T(8,128)(2,1)}), bf16[16,8,2048]{2,1,0:T(8,128)(2,1)S(1)}, u32[]{:S(2)}, u32[]{:S(2)}) %all-to-all-start) | async-done | bytes 524320 | tf_op jit(solution)/shard_map/to_components/all_to_all | solution.py:245
  94.1 2.2 %fit.1 = f32[32,1,256]{2,1,0:T(1,128)} custom-call(s32[1]{0:T(128)} %bitcast.slot_ref, bf16[128,2048]{1,0:T(8,128)(2,1)S(1)} %bitcast.89, f32[32,2048]{1,0:T(8,128)S(1)} %reshape.101.values_ref), custom_call_target="tpu_custom_call" | custom-call | tf_op jit(solution)/shard_map/fit/pallas_call | solution.py:130
  96.3 3.9 %all-to-all-start.1 = ((f32[32,1,256]{2,1,0:T(1,128)}), f32[32,1,256]{2,1,0:T(1,128)S(1)}, u32[]{:S(2)}, u32[]{:S(2)}) async-start(f32[32,1,256]{2,1,0:T(1,128)} %fit.1), calls=%async_computation.1 | async-start | bytes 65536 | tf_op jit(solution)/shard_map/gather_scores/all_to_all | solution.py:250
  100.2 0.1 pad_dynamic-slice_fusion
  100.3 7.3 %all-to-all-done.1 = f32[32,1,256]{2,1,0:T(1,128)S(1)} async-done(((f32[32,1,256]{2,1,0:T(1,128)}), f32[32,1,256]{2,1,0:T(1,128)S(1)}, u32[]{:S(2)}, u32[]{:S(2)}) %all-to-all-start.1) | async-done | bytes 32800 | tf_op jit(solution)/shard_map/gather_scores/all_to_all | solution.py:250
  107.6 3.0 %collective-permute-start.23 = (f32[256]{0:T(256)S(1)}, f32[256]{0:T(256)S(1)}, u32[]{:S(2)}, u32[]{:S(2)}) collective-permute-start(f32[256]{0:T(256)S(1)} %reduce_sum.19), channel_id=1, source_target_pairs={{0,2},{2,4},{4,6},{6,8},{8,10},{10,12},{12,14},{3,1},{5,3},{7,5},{... | collective-permute-start | bytes 3080 | tf_op jit(solution)/shard_map/gather_scores/ppermute | solution.py:253
  110.6 0.6 dynamic_slice.55
  111.2 1.9 %collective-permute-done.23 = f32[256]{0:T(256)S(1)} collective-permute-done((f32[256]{0:T(256)S(1)}, f32[256]{0:T(256)S(1)}, u32[]{:S(2)}, u32[]{:S(2)}) %collective-permute-start.23) | collective-permute-done | bytes 1056 | tf_op jit(solution)/shard_map/gather_scores/ppermute | solution.py:253
  113.3 0.6 add_divide_fusion
  (42 shorter events, 0.9 us)
Async XLA Ops:
  2.5 26.8 %copy-start.1 = (bf16[144,1024]{1,0:T(8,128)(2,1)S(1)}, bf16[144,1024]{1,0:T(8,128)(2,1)}, u32[]{:S(2)}) copy-start(bf16[144,1024]{1,0:T(8,128)(2,1)} %weigh.1) | copy-start | bytes 884740
  2.5 9.3 %collective-permute-start = (bf16[144,1024]{1,0:T(8,128)(2,1)}, bf16[144,1024]{1,0:T(8,128)(2,1)S(1)}, u32[]{:S(2)}, u32[]{:S(2)}) collective-permute-start(bf16[144,1024]{1,0:T(8,128)(2,1)} %weigh.1), channel_id=1, source_target_pairs={{0,96},{32,0},{64,32},{96,64},{1,97},{33,1},{65,33},{97,65},{2,98}... | collective-permute-start | bytes 884744 | tf_op jit(solution)/shard_map/gather_rows/ppermute | solution.py:25
  5.3 11.2 %collective-permute-start.2 = (bf16[144,1024]{1,0:T(8,128)(2,1)}, bf16[144,1024]{1,0:T(8,128)(2,1)S(1)}, u32[]{:S(2)}, u32[]{:S(2)}) collective-permute-start(bf16[144,1024]{1,0:T(8,128)(2,1)} %weigh.1), channel_id=1, source_target_pairs={{0,128},{128,0},{1,129},{129,1},{2,130},{130,2},{3,131},{131,3},{4... | collective-permute-start | bytes 884744 | tf_op jit(solution)/shard_map/gather_rows/ppermute | solution.py:25
  6.8 22.5 %collective-permute-start.7 = (bf16[1024,1024]{1,0:T(8,128)(2,1)}, bf16[1024,1024]{1,0:T(8,128)(2,1)S(1)}, u32[]{:S(2)}, u32[]{:S(2)}) collective-permute-start(bf16[1024,1024]{1,0:T(8,128)(2,1)} %param.10), channel_id=1, source_target_pairs={{0,16},{16,0},{1,17},{17,1},{2,18},{18,2},{3,19},{19,3},{4,20},{20... | collective-permute-start | bytes 6291464 | tf_op jit(solution)/shard_map/swap_eigvecs/ppermute | solution.py:25
  6.8 10.8 %collective-permute-start.4 = (bf16[144,1024]{1,0:T(8,128)(2,1)}, bf16[144,1024]{1,0:T(8,128)(2,1)S(1)}, u32[]{:S(2)}, u32[]{:S(2)}) collective-permute-start(bf16[144,1024]{1,0:T(8,128)(2,1)} %weigh.1), channel_id=1, source_target_pairs={{0,32},{32,64},{64,96},{96,0},{1,33},{33,65},{65,97},{97,1},{2,34}... | collective-permute-start | bytes 884744 | tf_op jit(solution)/shard_map/gather_rows/ppermute | solution.py:25
  11.8 12.1 %collective-permute-start.1 = (bf16[144,1024]{1,0:T(8,128)(2,1)S(1)}, bf16[144,1024]{1,0:T(8,128)(2,1)}, u32[]{:S(2)}, u32[]{:S(2)}) collective-permute-start(bf16[144,1024]{1,0:T(8,128)(2,1)S(1)} %collective-permute-done), channel_id=1, source_target_pairs={{0,224},{32,128},{64,160},{96,192},{128,96},{160,0},{192,32},{224,... | collective-permute-start | bytes 884744 | tf_op jit(solution)/shard_map/gather_rows/ppermute | solution.py:151
  16.5 11.7 %collective-permute-start.3 = (bf16[144,1024]{1,0:T(8,128)(2,1)S(1)}, bf16[144,1024]{1,0:T(8,128)(2,1)}, u32[]{:S(2)}, u32[]{:S(2)}) collective-permute-start(bf16[144,1024]{1,0:T(8,128)(2,1)S(1)} %collective-permute-done.2), channel_id=1, source_target_pairs={{0,96},{32,0},{64,32},{96,64},{1,97},{33,1},{65,33},{97,65},{2,98}... | collective-permute-start | bytes 884744 | tf_op jit(solution)/shard_map/gather_rows/ppermute | solution.py:25
  17.7 11.5 %collective-permute-start.5 = (bf16[144,1024]{1,0:T(8,128)(2,1)S(1)}, bf16[144,1024]{1,0:T(8,128)(2,1)S(1)}, u32[]{:S(2)}, u32[]{:S(2)}) collective-permute-start(bf16[144,1024]{1,0:T(8,128)(2,1)S(1)} %collective-permute-done.4), channel_id=1, source_target_pairs={{0,32},{32,64},{64,96},{96,0},{1,33},{33,65},{65,97},{97,1},{2,34}... | collective-permute-start | bytes 884744 | tf_op jit(solution)/shard_map/gather_rows/ppermute | solution.py:25
  18.7 10.7 %collective-permute-start.6 = (bf16[144,1024]{1,0:T(8,128)(2,1)S(1)}, bf16[144,1024]{1,0:T(8,128)(2,1)S(1)}, u32[]{:S(2)}, u32[]{:S(2)}) collective-permute-start(bf16[144,1024]{1,0:T(8,128)(2,1)S(1)} %collective-permute-done.4), channel_id=1, source_target_pairs={{0,128},{128,0},{1,129},{129,1},{2,130},{130,2},{3,131},{131,3},{4... | collective-permute-start | bytes 884744 | tf_op jit(solution)/shard_map/gather_rows/ppermute | solution.py:25
  24.9 4.5 %copy-start = (bf16[1024,1024]{1,0:T(8,128)(2,1)S(1)}, bf16[1024,1024]{1,0:T(8,128)(2,1)}, u32[]{:S(2)}) copy-start(bf16[1024,1024]{1,0:T(8,128)(2,1)} %param.10) | copy-start | bytes 6291460
  29.9 8.5 %collective-permute-start.8 = (bf16[128,1024]{1,0:T(8,128)(2,1)S(1)}, bf16[128,1024]{1,0:T(8,128)(2,1)S(1)}, u32[]{:S(2)}, u32[]{:S(2)}) collective-permute-start(bf16[128,1024]{1,0:T(8,128)(2,1)S(1)} %convolution_convert_fusion.1), channel_id=1, source_target_pairs={{0,2},{2,4},{4,6},{6,8},{8,10},{10,12},{12,14},{14,0},{1,3},{3,5},... | collective-permute-start | bytes 786440 | tf_op jit(solution)/shard_map/sum_layers/ppermute | solution.py:25
  33.5 10.5 %collective-permute-start.13 = (bf16[128,1024]{1,0:T(8,128)(2,1)S(1)}, bf16[128,1024]{1,0:T(8,128)(2,1)S(1)}, u32[]{:S(2)}, u32[]{:S(2)}) collective-permute-start(bf16[128,1024]{1,0:T(8,128)(2,1)S(1)} %convolution_convert_fusion), channel_id=1, source_target_pairs={{0,14},{2,0},{4,2},{6,4},{8,6},{10,8},{12,10},{14,12},{1,15},{3,1}... | collective-permute-start | bytes 786440 | tf_op jit(solution)/shard_map/sum_layers/ppermute | solution.py:25
  34.1 15.6 %collective-permute-start.12 = (bf16[128,1024]{1,0:T(8,128)(2,1)S(1)}, bf16[128,1024]{1,0:T(8,128)(2,1)S(1)}, u32[]{:S(2)}, u32[]{:S(2)}) collective-permute-start(bf16[128,1024]{1,0:T(8,128)(2,1)S(1)} %fusion.6), channel_id=1, source_target_pairs={{0,14},{2,0},{4,2},{6,4},{8,6},{10,8},{12,10},{14,12},{1,15},{3,1}... | collective-permute-start | bytes 786440 | tf_op jit(solution)/shard_map/sum_layers/ppermute | solution.py:25
  34.6 15.6 %collective-permute-start.17 = (bf16[128,1024]{1,0:T(8,128)(2,1)S(1)}, bf16[128,1024]{1,0:T(8,128)(2,1)S(1)}, u32[]{:S(2)}, u32[]{:S(2)}) collective-permute-start(bf16[128,1024]{1,0:T(8,128)(2,1)S(1)} %fusion.9), channel_id=1, source_target_pairs={{0,2},{2,4},{4,6},{6,8},{8,10},{10,12},{12,14},{14,0},{1,3},{3,5},... | collective-permute-start | bytes 786440 | tf_op jit(solution)/shard_map/sum_layers/ppermute | solution.py:25
  38.8 15.2 %collective-permute-start.9 = (bf16[128,1024]{1,0:T(8,128)(2,1)S(1)}, bf16[128,1024]{1,0:T(8,128)(2,1)S(1)}, u32[]{:S(2)}, u32[]{:S(2)}) collective-permute-start(bf16[128,1024]{1,0:T(8,128)(2,1)S(1)} %add_convert_fusion.5), channel_id=1, source_target_pairs={{0,2},{2,4},{4,6},{6,8},{8,10},{10,12},{12,14},{14,0},{1,3},{3,5},... | collective-permute-start | bytes 786440 | tf_op jit(solution)/shard_map/sum_layers/ppermute | solution.py:25
  44.5 10.6 %collective-permute-start.15 = (bf16[128,1024]{1,0:T(8,128)(2,1)S(1)}, bf16[128,1024]{1,0:T(8,128)(2,1)S(1)}, u32[]{:S(2)}, u32[]{:S(2)}) collective-permute-start(bf16[128,1024]{1,0:T(8,128)(2,1)S(1)} %fusion.7), channel_id=1, source_target_pairs={{0,14},{2,0},{4,2},{6,4},{8,6},{10,8},{12,10},{14,12},{1,15},{3,1}... | collective-permute-start | bytes 786440 | tf_op jit(solution)/shard_map/sum_layers/ppermute | solution.py:25
  50.2 10.6 %collective-permute-start.14 = (bf16[128,1024]{1,0:T(8,128)(2,1)S(1)}, bf16[128,1024]{1,0:T(8,128)(2,1)S(1)}, u32[]{:S(2)}, u32[]{:S(2)}) collective-permute-start(bf16[128,1024]{1,0:T(8,128)(2,1)S(1)} %add_convert_fusion.2), channel_id=1, source_target_pairs={{0,14},{2,0},{4,2},{6,4},{8,6},{10,8},{12,10},{14,12},{1,15},{3,1}... | collective-permute-start | bytes 786440 | tf_op jit(solution)/shard_map/sum_layers/ppermute | solution.py:25
  50.8 10.5 %collective-permute-start.18 = (bf16[128,1024]{1,0:T(8,128)(2,1)S(1)}, bf16[128,1024]{1,0:T(8,128)(2,1)S(1)}, u32[]{:S(2)}, u32[]{:S(2)}) collective-permute-start(bf16[128,1024]{1,0:T(8,128)(2,1)S(1)} %fusion.5), channel_id=1, source_target_pairs={{0,2},{2,4},{4,6},{6,8},{8,10},{10,12},{12,14},{14,0},{1,3},{3,5},... | collective-permute-start | bytes 786440 | tf_op jit(solution)/shard_map/sum_layers/ppermute | solution.py:25
  54.5 10.6 %collective-permute-start.10 = (bf16[128,1024]{1,0:T(8,128)(2,1)S(1)}, bf16[128,1024]{1,0:T(8,128)(2,1)S(1)}, u32[]{:S(2)}, u32[]{:S(2)}) collective-permute-start(bf16[128,1024]{1,0:T(8,128)(2,1)S(1)} %add_convert_fusion.4), channel_id=1, source_target_pairs={{0,2},{2,4},{4,6},{6,8},{8,10},{10,12},{12,14},{14,0},{1,3},{3,5},... | collective-permute-start | bytes 786440 | tf_op jit(solution)/shard_map/sum_layers/ppermute | solution.py:25
  55.6 11.4 %collective-permute-start.20 = (bf16[128,1024]{1,0:T(8,128)(2,1)S(1)}, bf16[128,1024]{1,0:T(8,128)(2,1)S(1)}, u32[]{:S(2)}, u32[]{:S(2)}) collective-permute-start(bf16[128,1024]{1,0:T(8,128)(2,1)S(1)} %fusion.8), channel_id=1, source_target_pairs={{0,14},{2,0},{4,2},{6,4},{8,6},{10,8},{12,10},{14,12},{1,15},{3,1}... | collective-permute-start | bytes 786440 | tf_op jit(solution)/shard_map/sum_layers/ppermute | solution.py:25
  61.2 10.5 %collective-permute-start.16 = (bf16[128,1024]{1,0:T(8,128)(2,1)S(1)}, bf16[128,1024]{1,0:T(8,128)(2,1)S(1)}, u32[]{:S(2)}, u32[]{:S(2)}) collective-permute-start(bf16[128,1024]{1,0:T(8,128)(2,1)S(1)} %add_convert_fusion.1), channel_id=1, source_target_pairs={{0,14},{2,0},{4,2},{6,4},{8,6},{10,8},{12,10},{14,12},{1,15},{3,1}... | collective-permute-start | bytes 786440 | tf_op jit(solution)/shard_map/sum_layers/ppermute | solution.py:25
  61.8 10.9 %collective-permute-start.19 = (bf16[128,1024]{1,0:T(8,128)(2,1)S(1)}, bf16[128,1024]{1,0:T(8,128)(2,1)S(1)}, u32[]{:S(2)}, u32[]{:S(2)}) collective-permute-start(bf16[128,1024]{1,0:T(8,128)(2,1)S(1)} %fusion.4), channel_id=1, source_target_pairs={{0,2},{2,4},{4,6},{6,8},{8,10},{10,12},{12,14},{14,0},{1,3},{3,5},... | collective-permute-start | bytes 786440 | tf_op jit(solution)/shard_map/sum_layers/ppermute | solution.py:25
  65.6 6.6 %collective-permute-start.11 = (bf16[128,1024]{1,0:T(8,128)(2,1)S(1)}, bf16[128,1024]{1,0:T(8,128)(2,1)S(1)}, u32[]{:S(2)}, u32[]{:S(2)}) collective-permute-start(bf16[128,1024]{1,0:T(8,128)(2,1)S(1)} %add_convert_fusion.3), channel_id=1, source_target_pairs={{0,2},{2,4},{4,6},{6,8},{8,10},{10,12},{12,14},{14,0},{1,3},{3,5},... | collective-permute-start | bytes 786440 | tf_op jit(solution)/shard_map/sum_layers/ppermute | solution.py:25
  67.4 7.7 %collective-permute-start.21 = (bf16[128,1024]{1,0:T(8,128)(2,1)S(1)}, bf16[128,1024]{1,0:T(8,128)(2,1)S(1)}, u32[]{:S(2)}, u32[]{:S(2)}) collective-permute-start(bf16[128,1024]{1,0:T(8,128)(2,1)S(1)} %fusion.10), channel_id=1, source_target_pairs={{0,14},{2,0},{4,2},{6,4},{8,6},{10,8},{12,10},{14,12},{1,15},{3,1}... | collective-permute-start | bytes 786440 | tf_op jit(solution)/shard_map/sum_layers/ppermute | solution.py:25
  72.7 11.7 %copy-start.2 = (s32[1024]{0:T(1024)S(1)}, s32[1024]{0:T(1024)}, u32[]{:S(2)}) copy-start(s32[1024]{0:T(1024)} %param.12) | copy-start | bytes 12292
  75.6 37.8 %copy-start.3 = (s32[64]{0:T(128)S(1)}, s32[64]{0:T(128)}, u32[]{:S(2)}) copy-start(s32[64]{0:T(128)} %param.13) | copy-start | bytes 772
  76.4 17.7 %all-to-all-start = ((bf16[16,8,2048]{2,1,0:T(8,128)(2,1)}), bf16[16,8,2048]{2,1,0:T(8,128)(2,1)S(1)}, u32[]{:S(2)}, u32[]{:S(2)}) async-start(bf16[16,8,2048]{2,1,0:T(8,128)(2,1)} %maximum_bitcast_fusion), calls=%async_computation | async-start | bytes 1048576 | tf_op jit(solution)/shard_map/to_components/all_to_all | solution.py:245
  84.2 1.3 %collective-permute-start.22 = (f32[8,1024]{1,0:T(8,128)S(1)}, f32[8,1024]{1,0:T(8,128)S(1)}, u32[]{:S(2)}, u32[]{:S(2)}) collective-permute-start(f32[8,1024]{1,0:T(8,128)S(1)} %select_reduce_fusion), channel_id=1, source_target_pairs={{0,16},{16,0},{1,17},{17,1},{2,18},{18,2},{3,19},{19,3},{4,20},{20... | collective-permute-start | bytes 98312 | tf_op jit(solution)/shard_map/gather_values/ppermute | solution.py:25
  96.3 11.3 %all-to-all-start.1 = ((f32[32,1,256]{2,1,0:T(1,128)}), f32[32,1,256]{2,1,0:T(1,128)S(1)}, u32[]{:S(2)}, u32[]{:S(2)}) async-start(f32[32,1,256]{2,1,0:T(1,128)} %fit.1), calls=%async_computation.1 | async-start | bytes 65536 | tf_op jit(solution)/shard_map/gather_scores/all_to_all | solution.py:250
  107.6 5.5 %collective-permute-start.23 = (f32[256]{0:T(256)S(1)}, f32[256]{0:T(256)S(1)}, u32[]{:S(2)}, u32[]{:S(2)}) collective-permute-start(f32[256]{0:T(256)S(1)} %reduce_sum.19), channel_id=1, source_target_pairs={{0,2},{2,4},{4,6},{6,8},{8,10},{10,12},{12,14},{3,1},{5,3},{7,5},{... | collective-permute-start | bytes 3080 | tf_op jit(solution)/shard_map/gather_scores/ppermute | solution.py:253

commit v14 on v13

--- a/solution.py
+++ b/solution.py
@@ -56,7 +56,7 @@
     rows, width = responses.shape
     return pl.pallas_call(
         weigh_kernel,
-        out_shape=jax.ShapeDtypeStruct((2 * rows + EXTRA, width), jnp.bfloat16),
+        out_shape=pltpu.VMEM((2 * rows + EXTRA, width), jnp.bfloat16),
     )(responses, weights, phenotype[None, :], eigvals[None, :])
 
 

time: 114 us -> 113 us (level)
  no operation moved by 1% of the time
where the time goes in v14:
time: 113 us
  waiting for transfers between devices  49.4 us (44%)
  starting transfers between devices  46.4 us (41%)
  matrix products  7.3 us (6%)
  Pallas kernels  3.33 us (3%)
  local copies, waits for them, and re-layouts  3.06 us (3%)
  other arithmetic  2.04 us (2%)
  between operations  1.56 us (1%)
    ppermute x22, starting transfers between devices, shifted(): lax.ppermute(value, axis, [(i, (i + by) % peers) for i in range(peers)])  27.3 us
    ppermute x22, waiting for transfers between devices, shifted(): lax.ppermute(value, axis, [(i, (i + by) % peers) for i in range(peers)])  27 us
    all_to_all x1, waiting for transfers between devices, shards(): sums = lax.all_to_all(whole, PLANE, 0, 0, tiled=True)  8.41 us
    all_to_all x1, starting transfers between devices, shards(): sums = lax.all_to_all(whole, PLANE, 0, 0, tiled=True)  7.57 us
    all_to_all x1, waiting for transfers between devices, shards(): lax.all_to_all(fitted, LAYER, 0, 0, tiled=True)  7.32 us
    dot_general x16, matrix products, term(): return jnp.dot(block, vecs[q], preferred_element_type=jnp.float32)  7.3 us
    ppermute x1, waiting for transfers between devices, across(): return lax.ppermute(value, (y, x), pairs)  4.79 us
    ppermute x1, starting transfers between devices, across(): return lax.ppermute(value, (y, x), pairs)  4.7 us
  transfers between devices with their start and end apart: 26, of which 16 were waited for; matrix products, arithmetic and copies ran while one was open for 8% of the time, Pallas kernels for 0%

profile of v14, /device:TPU:96, one launch (start us, length us, event | category | flops | bytes accessed | tf_op | source)
XLA Modules:
  0.0 113.1 jit_solution(7001785867903163494)
XLA Ops:
  0.6 1.1 %weigh.1 = bf16[144,1024]{1,0:T(8,128)(2,1)S(1)} custom-call(bf16[64,1024]{1,0:T(8,128)(2,1)} %resp_ref.1, bf16[64,1024]{1,0:T(8,128)(2,1)} %weight_ref.1, f32[1,1024]{1,0:T(1,128)} %bitcast.91, f32[1,1024]{1,0:T(1,128)} %bitcast.92), custom_call_target="tpu_custom_call" | custom-call | tf_op jit(solution)/shard_map/weigh/pallas_call | solution.py:57
  1.8 2.8 %collective-permute-start = (bf16[144,1024]{1,0:T(8,128)(2,1)S(1)}, bf16[144,1024]{1,0:T(8,128)(2,1)S(1)}, u32[]{:S(2)}, u32[]{:S(2)}) collective-permute-start(bf16[144,1024]{1,0:T(8,128)(2,1)S(1)} %weigh.1), channel_id=1, source_target_pairs={{0,96},{32,0},{64,32},{96,64},{1,97},{33,1},{65,33},{97,65},{2,98}... | collective-permute-start | bytes 884744 | tf_op jit(solution)/shard_map/gather_rows/ppermute | solution.py:25
  4.6 1.6 %collective-permute-start.2 = (bf16[144,1024]{1,0:T(8,128)(2,1)S(1)}, bf16[144,1024]{1,0:T(8,128)(2,1)S(1)}, u32[]{:S(2)}, u32[]{:S(2)}) collective-permute-start(bf16[144,1024]{1,0:T(8,128)(2,1)S(1)} %weigh.1), channel_id=1, source_target_pairs={{0,128},{128,0},{1,129},{129,1},{2,130},{130,2},{3,131},{131,3},{4... | collective-permute-start | bytes 884744 | tf_op jit(solution)/shard_map/gather_rows/ppermute | solution.py:25
  6.2 4.7 %collective-permute-done = bf16[144,1024]{1,0:T(8,128)(2,1)S(1)} collective-permute-done((bf16[144,1024]{1,0:T(8,128)(2,1)S(1)}, bf16[144,1024]{1,0:T(8,128)(2,1)S(1)}, u32[]{:S(2)}, u32[]{:S(2)}) %collective-permute-start) | collective-permute-done | bytes 294944 | tf_op jit(solution)/shard_map/gather_rows/ppermute | solution.py:25
  10.9 4.7 %collective-permute-start.1 = (bf16[144,1024]{1,0:T(8,128)(2,1)S(1)}, bf16[144,1024]{1,0:T(8,128)(2,1)}, u32[]{:S(2)}, u32[]{:S(2)}) collective-permute-start(bf16[144,1024]{1,0:T(8,128)(2,1)S(1)} %collective-permute-done), channel_id=1, source_target_pairs={{0,224},{32,128},{64,160},{96,192},{128,96},{160,0},{192,32},{224,... | collective-permute-start | bytes 884744 | tf_op jit(solution)/shard_map/gather_rows/ppermute | solution.py:151
  15.6 0.1 collective-permute-start.3
  16.2 0.6 collective-permute-done.4
  16.8 1.0 collective-permute-start.5
  17.8 0.4 collective-permute-start.6
  18.2 4.8 %collective-permute-done.1 = bf16[144,1024]{1,0:T(8,128)(2,1)} collective-permute-done((bf16[144,1024]{1,0:T(8,128)(2,1)S(1)}, bf16[144,1024]{1,0:T(8,128)(2,1)}, u32[]{:S(2)}, u32[]{:S(2)}) %collective-permute-start.1) | collective-permute-done | bytes 294944 | tf_op jit(solution)/shard_map/gather_rows/ppermute | solution.py:151
  23.0 1.0 bitcast_dynamic-update-slice_fusion.6
  24.0 3.3 %collective-permute-done.3 = bf16[144,1024]{1,0:T(8,128)(2,1)} collective-permute-done((bf16[144,1024]{1,0:T(8,128)(2,1)S(1)}, bf16[144,1024]{1,0:T(8,128)(2,1)}, u32[]{:S(2)}, u32[]{:S(2)}) %collective-permute-start.3) | collective-permute-done | bytes 294944 | tf_op jit(solution)/shard_map/gather_rows/ppermute | solution.py:25
  27.3 1.0 bitcast_dynamic-update-slice_fusion.5
  28.5 0.1 fusion.13
  28.6 0.4 convolution_convert_fusion.1
  29.0 3.2 %collective-permute-start.8 = (bf16[128,1024]{1,0:T(8,128)(2,1)S(1)}, bf16[128,1024]{1,0:T(8,128)(2,1)S(1)}, u32[]{:S(2)}, u32[]{:S(2)}) collective-permute-start(bf16[128,1024]{1,0:T(8,128)(2,1)S(1)} %convolution_convert_fusion.1), channel_id=1, source_target_pairs={{0,2},{2,4},{4,6},{6,8},{8,10},{10,12},{12,14},{14,0},{1,3},{3,5},... | collective-permute-start | bytes 786440 | tf_op jit(solution)/shard_map/sum_layers/ppermute | solution.py:25
  32.2 0.4 convolution_convert_fusion
  32.7 0.1 collective-permute-start.13
  32.8 0.4 fusion.6
  33.3 0.5 fusion.9
  33.8 3.3 %collective-permute-start.17 = (bf16[128,1024]{1,0:T(8,128)(2,1)S(1)}, bf16[128,1024]{1,0:T(8,128)(2,1)S(1)}, u32[]{:S(2)}, u32[]{:S(2)}) collective-permute-start(bf16[128,1024]{1,0:T(8,128)(2,1)S(1)} %fusion.9), channel_id=1, source_target_pairs={{0,2},{2,4},{4,6},{6,8},{8,10},{10,12},{12,14},{14,0},{1,3},{3,5},... | collective-permute-start | bytes 786440 | tf_op jit(solution)/shard_map/sum_layers/ppermute | solution.py:25
  37.1 0.4 collective-permute-done.8
  37.5 0.4 add_convert_fusion.5
  38.0 3.9 %collective-permute-start.9 = (bf16[128,1024]{1,0:T(8,128)(2,1)S(1)}, bf16[128,1024]{1,0:T(8,128)(2,1)S(1)}, u32[]{:S(2)}, u32[]{:S(2)}) collective-permute-start(bf16[128,1024]{1,0:T(8,128)(2,1)S(1)} %add_convert_fusion.5), channel_id=1, source_target_pairs={{0,2},{2,4},{4,6},{6,8},{8,10},{10,12},{12,14},{14,0},{1,3},{3,5},... | collective-permute-start | bytes 786440 | tf_op jit(solution)/shard_map/sum_layers/ppermute | solution.py:25
  41.9 1.3 %collective-permute-done.13 = bf16[128,1024]{1,0:T(8,128)(2,1)S(1)} collective-permute-done((bf16[128,1024]{1,0:T(8,128)(2,1)S(1)}, bf16[128,1024]{1,0:T(8,128)(2,1)S(1)}, u32[]{:S(2)}, u32[]{:S(2)}) %collective-permute-start.13) | collective-permute-done | bytes 262176 | tf_op jit(solution)/shard_map/sum_layers/ppermute | solution.py:25
  43.2 0.4 fusion.7
  43.7 0.1 collective-permute-start.15
  43.8 5.1 %collective-permute-done.12 = bf16[128,1024]{1,0:T(8,128)(2,1)S(1)} collective-permute-done((bf16[128,1024]{1,0:T(8,128)(2,1)S(1)}, bf16[128,1024]{1,0:T(8,128)(2,1)S(1)}, u32[]{:S(2)}, u32[]{:S(2)}) %collective-permute-start.12) | collective-permute-done | bytes 262176 | tf_op jit(solution)/shard_map/sum_layers/ppermute | solution.py:25
  48.8 0.5 add_convert_fusion.2
  49.4 0.5 fusion.5
  49.9 3.3 %collective-permute-start.18 = (bf16[128,1024]{1,0:T(8,128)(2,1)S(1)}, bf16[128,1024]{1,0:T(8,128)(2,1)S(1)}, u32[]{:S(2)}, u32[]{:S(2)}) collective-permute-start(bf16[128,1024]{1,0:T(8,128)(2,1)S(1)} %fusion.5), channel_id=1, source_target_pairs={{0,2},{2,4},{4,6},{6,8},{8,10},{10,12},{12,14},{14,0},{1,3},{3,5},... | collective-permute-start | bytes 786440 | tf_op jit(solution)/shard_map/sum_layers/ppermute | solution.py:25
  53.2 0.4 add_convert_fusion.4
  53.7 0.1 collective-permute-start.10
  53.8 0.5 collective-permute-done.15
  54.3 0.4 fusion.8
  54.7 1.6 %collective-permute-start.20 = (bf16[128,1024]{1,0:T(8,128)(2,1)S(1)}, bf16[128,1024]{1,0:T(8,128)(2,1)S(1)}, u32[]{:S(2)}, u32[]{:S(2)}) collective-permute-start(bf16[128,1024]{1,0:T(8,128)(2,1)S(1)} %fusion.8), channel_id=1, source_target_pairs={{0,14},{2,0},{4,2},{6,4},{8,6},{10,8},{12,10},{14,12},{1,15},{3,1}... | collective-permute-start | bytes 786440 | tf_op jit(solution)/shard_map/sum_layers/ppermute | solution.py:25
  56.3 3.6 %collective-permute-done.14 = bf16[128,1024]{1,0:T(8,128)(2,1)S(1)} collective-permute-done((bf16[128,1024]{1,0:T(8,128)(2,1)S(1)}, bf16[128,1024]{1,0:T(8,128)(2,1)S(1)}, u32[]{:S(2)}, u32[]{:S(2)}) %collective-permute-start.14) | collective-permute-done | bytes 262176 | tf_op jit(solution)/shard_map/sum_layers/ppermute | solution.py:25
  59.9 0.5 add_convert_fusion.1
  60.5 0.5 fusion.4
  60.9 3.3 %collective-permute-start.19 = (bf16[128,1024]{1,0:T(8,128)(2,1)S(1)}, bf16[128,1024]{1,0:T(8,128)(2,1)S(1)}, u32[]{:S(2)}, u32[]{:S(2)}) collective-permute-start(bf16[128,1024]{1,0:T(8,128)(2,1)S(1)} %fusion.4), channel_id=1, source_target_pairs={{0,2},{2,4},{4,6},{6,8},{8,10},{10,12},{12,14},{14,0},{1,3},{3,5},... | collective-permute-start | bytes 786440 | tf_op jit(solution)/shard_map/sum_layers/ppermute | solution.py:25
  64.2 0.4 add_convert_fusion.3
  64.7 1.4 %collective-permute-start.11 = (bf16[128,1024]{1,0:T(8,128)(2,1)S(1)}, bf16[128,1024]{1,0:T(8,128)(2,1)S(1)}, u32[]{:S(2)}, u32[]{:S(2)}) collective-permute-start(bf16[128,1024]{1,0:T(8,128)(2,1)S(1)} %add_convert_fusion.3), channel_id=1, source_target_pairs={{0,2},{2,4},{4,6},{6,8},{8,10},{10,12},{12,14},{14,0},{1,3},{3,5},... | collective-permute-start | bytes 786440 | tf_op jit(solution)/shard_map/sum_layers/ppermute | solution.py:25
  66.1 0.4 fusion.10
  66.6 0.7 collective-permute-start.21
  67.3 3.5 %collective-permute-done.16 = bf16[128,1024]{1,0:T(8,128)(2,1)S(1)} collective-permute-done((bf16[128,1024]{1,0:T(8,128)(2,1)S(1)}, bf16[128,1024]{1,0:T(8,128)(2,1)S(1)}, u32[]{:S(2)}, u32[]{:S(2)}) %collective-permute-start.16) | collective-permute-done | bytes 262176 | tf_op jit(solution)/shard_map/sum_layers/ppermute | solution.py:25
  70.8 0.5 collective-permute-done.11
  71.3 0.5 add_convert_fusion
  71.8 2.4 %collective-permute-done.21 = bf16[128,1024]{1,0:T(8,128)(2,1)S(1)} collective-permute-done((bf16[128,1024]{1,0:T(8,128)(2,1)S(1)}, bf16[128,1024]{1,0:T(8,128)(2,1)S(1)}, u32[]{:S(2)}, u32[]{:S(2)}) %collective-permute-start.21) | collective-permute-done | bytes 262176 | tf_op jit(solution)/shard_map/sum_layers/ppermute | solution.py:25
  74.2 0.5 fusion.3
  74.7 0.8 maximum_bitcast_fusion
  75.6 7.6 %all-to-all-start = ((bf16[16,8,2048]{2,1,0:T(8,128)(2,1)}), bf16[16,8,2048]{2,1,0:T(8,128)(2,1)S(1)}, u32[]{:S(2)}, u32[]{:S(2)}) async-start(bf16[16,8,2048]{2,1,0:T(8,128)(2,1)} %maximum_bitcast_fusion), calls=%async_computation | async-start | bytes 1048576 | tf_op jit(solution)/shard_map/to_components/all_to_all | solution.py:245
  83.2 0.1 select_reduce_fusion
  83.4 0.1 collective-permute-start.22
  83.5 1.1 %collective-permute-done.22 = f32[8,1024]{1,0:T(8,128)S(1)} collective-permute-done((f32[8,1024]{1,0:T(8,128)S(1)}, f32[8,1024]{1,0:T(8,128)S(1)}, u32[]{:S(2)}, u32[]{:S(2)}) %collective-permute-start.22) | collective-permute-done | bytes 32800 | tf_op jit(solution)/shard_map/gather_values/ppermute | solution.py:25
  84.7 0.1 reshape.101.values_ref
  84.8 8.4 %all-to-all-done = bf16[16,8,2048]{2,1,0:T(8,128)(2,1)S(1)} async-done(((bf16[16,8,2048]{2,1,0:T(8,128)(2,1)}), bf16[16,8,2048]{2,1,0:T(8,128)(2,1)S(1)}, u32[]{:S(2)}, u32[]{:S(2)}) %all-to-all-start) | async-done | bytes 524320 | tf_op jit(solution)/shard_map/to_components/all_to_all | solution.py:245
  93.3 2.2 %fit.1 = f32[32,1,256]{2,1,0:T(1,128)} custom-call(s32[1]{0:T(128)} %bitcast.slot_ref, bf16[128,2048]{1,0:T(8,128)(2,1)S(1)} %bitcast.89, f32[32,2048]{1,0:T(8,128)S(1)} %reshape.101.values_ref), custom_call_target="tpu_custom_call" | custom-call | tf_op jit(solution)/shard_map/fit/pallas_call | solution.py:130
  95.5 3.8 %all-to-all-start.1 = ((f32[32,1,256]{2,1,0:T(1,128)}), f32[32,1,256]{2,1,0:T(1,128)S(1)}, u32[]{:S(2)}, u32[]{:S(2)}) async-start(f32[32,1,256]{2,1,0:T(1,128)} %fit.1), calls=%async_computation.1 | async-start | bytes 65536 | tf_op jit(solution)/shard_map/gather_scores/all_to_all | solution.py:250
  99.3 0.1 pad_dynamic-slice_fusion
  99.4 7.3 %all-to-all-done.1 = f32[32,1,256]{2,1,0:T(1,128)S(1)} async-done(((f32[32,1,256]{2,1,0:T(1,128)}), f32[32,1,256]{2,1,0:T(1,128)S(1)}, u32[]{:S(2)}, u32[]{:S(2)}) %all-to-all-start.1) | async-done | bytes 32800 | tf_op jit(solution)/shard_map/gather_scores/all_to_all | solution.py:250
  106.8 3.0 %collective-permute-start.23 = (f32[256]{0:T(256)S(1)}, f32[256]{0:T(256)S(1)}, u32[]{:S(2)}, u32[]{:S(2)}) collective-permute-start(f32[256]{0:T(256)S(1)} %reduce_sum.19), channel_id=1, source_target_pairs={{0,2},{2,4},{4,6},{6,8},{8,10},{10,12},{12,14},{3,1},{5,3},{7,5},{... | collective-permute-start | bytes 3080 | tf_op jit(solution)/shard_map/gather_scores/ppermute | solution.py:253
  109.8 0.6 dynamic_slice.55
  110.4 1.9 %collective-permute-done.23 = f32[256]{0:T(256)S(1)} collective-permute-done((f32[256]{0:T(256)S(1)}, f32[256]{0:T(256)S(1)}, u32[]{:S(2)}, u32[]{:S(2)}) %collective-permute-start.23) | collective-permute-done | bytes 1056 | tf_op jit(solution)/shard_map/gather_scores/ppermute | solution.py:253
  112.5 0.6 add_divide_fusion
  (40 shorter events, 0.9 us)
Async XLA Ops:
  1.8 9.1 %collective-permute-start = (bf16[144,1024]{1,0:T(8,128)(2,1)S(1)}, bf16[144,1024]{1,0:T(8,128)(2,1)S(1)}, u32[]{:S(2)}, u32[]{:S(2)}) collective-permute-start(bf16[144,1024]{1,0:T(8,128)(2,1)S(1)} %weigh.1), channel_id=1, source_target_pairs={{0,96},{32,0},{64,32},{96,64},{1,97},{33,1},{65,33},{97,65},{2,98}... | collective-permute-start | bytes 884744 | tf_op jit(solution)/shard_map/gather_rows/ppermute | solution.py:25
  4.6 11.0 %collective-permute-start.2 = (bf16[144,1024]{1,0:T(8,128)(2,1)S(1)}, bf16[144,1024]{1,0:T(8,128)(2,1)S(1)}, u32[]{:S(2)}, u32[]{:S(2)}) collective-permute-start(bf16[144,1024]{1,0:T(8,128)(2,1)S(1)} %weigh.1), channel_id=1, source_target_pairs={{0,128},{128,0},{1,129},{129,1},{2,130},{130,2},{3,131},{131,3},{4... | collective-permute-start | bytes 884744 | tf_op jit(solution)/shard_map/gather_rows/ppermute | solution.py:25
  6.2 22.3 %collective-permute-start.7 = (bf16[1024,1024]{1,0:T(8,128)(2,1)}, bf16[1024,1024]{1,0:T(8,128)(2,1)S(1)}, u32[]{:S(2)}, u32[]{:S(2)}) collective-permute-start(bf16[1024,1024]{1,0:T(8,128)(2,1)} %param.10), channel_id=1, source_target_pairs={{0,16},{16,0},{1,17},{17,1},{2,18},{18,2},{3,19},{19,3},{4,20},{20... | collective-permute-start | bytes 6291464 | tf_op jit(solution)/shard_map/swap_eigvecs/ppermute | solution.py:25
  6.2 10.6 %collective-permute-start.4 = (bf16[144,1024]{1,0:T(8,128)(2,1)S(1)}, bf16[144,1024]{1,0:T(8,128)(2,1)S(1)}, u32[]{:S(2)}, u32[]{:S(2)}) collective-permute-start(bf16[144,1024]{1,0:T(8,128)(2,1)S(1)} %weigh.1), channel_id=1, source_target_pairs={{0,32},{32,64},{64,96},{96,0},{1,33},{33,65},{65,97},{97,1},{2,34}... | collective-permute-start | bytes 884744 | tf_op jit(solution)/shard_map/gather_rows/ppermute | solution.py:25
  10.9 12.2 %collective-permute-start.1 = (bf16[144,1024]{1,0:T(8,128)(2,1)S(1)}, bf16[144,1024]{1,0:T(8,128)(2,1)}, u32[]{:S(2)}, u32[]{:S(2)}) collective-permute-start(bf16[144,1024]{1,0:T(8,128)(2,1)S(1)} %collective-permute-done), channel_id=1, source_target_pairs={{0,224},{32,128},{64,160},{96,192},{128,96},{160,0},{192,32},{224,... | collective-permute-start | bytes 884744 | tf_op jit(solution)/shard_map/gather_rows/ppermute | solution.py:151
  15.6 11.7 %collective-permute-start.3 = (bf16[144,1024]{1,0:T(8,128)(2,1)S(1)}, bf16[144,1024]{1,0:T(8,128)(2,1)}, u32[]{:S(2)}, u32[]{:S(2)}) collective-permute-start(bf16[144,1024]{1,0:T(8,128)(2,1)S(1)} %collective-permute-done.2), channel_id=1, source_target_pairs={{0,96},{32,0},{64,32},{96,64},{1,97},{33,1},{65,33},{97,65},{2,98}... | collective-permute-start | bytes 884744 | tf_op jit(solution)/shard_map/gather_rows/ppermute | solution.py:25
  16.8 11.5 %collective-permute-start.5 = (bf16[144,1024]{1,0:T(8,128)(2,1)S(1)}, bf16[144,1024]{1,0:T(8,128)(2,1)S(1)}, u32[]{:S(2)}, u32[]{:S(2)}) collective-permute-start(bf16[144,1024]{1,0:T(8,128)(2,1)S(1)} %collective-permute-done.4), channel_id=1, source_target_pairs={{0,32},{32,64},{64,96},{96,0},{1,33},{33,65},{65,97},{97,1},{2,34}... | collective-permute-start | bytes 884744 | tf_op jit(solution)/shard_map/gather_rows/ppermute | solution.py:25
  17.8 10.6 %collective-permute-start.6 = (bf16[144,1024]{1,0:T(8,128)(2,1)S(1)}, bf16[144,1024]{1,0:T(8,128)(2,1)S(1)}, u32[]{:S(2)}, u32[]{:S(2)}) collective-permute-start(bf16[144,1024]{1,0:T(8,128)(2,1)S(1)} %collective-permute-done.4), channel_id=1, source_target_pairs={{0,128},{128,0},{1,129},{129,1},{2,130},{130,2},{3,131},{131,3},{4... | collective-permute-start | bytes 884744 | tf_op jit(solution)/shard_map/gather_rows/ppermute | solution.py:25
  24.0 4.5 %copy-start = (bf16[1024,1024]{1,0:T(8,128)(2,1)S(1)}, bf16[1024,1024]{1,0:T(8,128)(2,1)}, u32[]{:S(2)}) copy-start(bf16[1024,1024]{1,0:T(8,128)(2,1)} %param.10) | copy-start | bytes 6291460
  29.0 8.5 %collective-permute-start.8 = (bf16[128,1024]{1,0:T(8,128)(2,1)S(1)}, bf16[128,1024]{1,0:T(8,128)(2,1)S(1)}, u32[]{:S(2)}, u32[]{:S(2)}) collective-permute-start(bf16[128,1024]{1,0:T(8,128)(2,1)S(1)} %convolution_convert_fusion.1), channel_id=1, source_target_pairs={{0,2},{2,4},{4,6},{6,8},{8,10},{10,12},{12,14},{14,0},{1,3},{3,5},... | collective-permute-start | bytes 786440 | tf_op jit(solution)/shard_map/sum_layers/ppermute | solution.py:25
  32.7 10.5 %collective-permute-start.13 = (bf16[128,1024]{1,0:T(8,128)(2,1)S(1)}, bf16[128,1024]{1,0:T(8,128)(2,1)S(1)}, u32[]{:S(2)}, u32[]{:S(2)}) collective-permute-start(bf16[128,1024]{1,0:T(8,128)(2,1)S(1)} %convolution_convert_fusion), channel_id=1, source_target_pairs={{0,14},{2,0},{4,2},{6,4},{8,6},{10,8},{12,10},{14,12},{1,15},{3,1}... | collective-permute-start | bytes 786440 | tf_op jit(solution)/shard_map/sum_layers/ppermute | solution.py:25
  33.2 15.6 %collective-permute-start.12 = (bf16[128,1024]{1,0:T(8,128)(2,1)S(1)}, bf16[128,1024]{1,0:T(8,128)(2,1)S(1)}, u32[]{:S(2)}, u32[]{:S(2)}) collective-permute-start(bf16[128,1024]{1,0:T(8,128)(2,1)S(1)} %fusion.6), channel_id=1, source_target_pairs={{0,14},{2,0},{4,2},{6,4},{8,6},{10,8},{12,10},{14,12},{1,15},{3,1}... | collective-permute-start | bytes 786440 | tf_op jit(solution)/shard_map/sum_layers/ppermute | solution.py:25
  33.8 15.6 %collective-permute-start.17 = (bf16[128,1024]{1,0:T(8,128)(2,1)S(1)}, bf16[128,1024]{1,0:T(8,128)(2,1)S(1)}, u32[]{:S(2)}, u32[]{:S(2)}) collective-permute-start(bf16[128,1024]{1,0:T(8,128)(2,1)S(1)} %fusion.9), channel_id=1, source_target_pairs={{0,2},{2,4},{4,6},{6,8},{8,10},{10,12},{12,14},{14,0},{1,3},{3,5},... | collective-permute-start | bytes 786440 | tf_op jit(solution)/shard_map/sum_layers/ppermute | solution.py:25
  38.0 15.2 %collective-permute-start.9 = (bf16[128,1024]{1,0:T(8,128)(2,1)S(1)}, bf16[128,1024]{1,0:T(8,128)(2,1)S(1)}, u32[]{:S(2)}, u32[]{:S(2)}) collective-permute-start(bf16[128,1024]{1,0:T(8,128)(2,1)S(1)} %add_convert_fusion.5), channel_id=1, source_target_pairs={{0,2},{2,4},{4,6},{6,8},{8,10},{10,12},{12,14},{14,0},{1,3},{3,5},... | collective-permute-start | bytes 786440 | tf_op jit(solution)/shard_map/sum_layers/ppermute | solution.py:25
  43.7 10.6 %collective-permute-start.15 = (bf16[128,1024]{1,0:T(8,128)(2,1)S(1)}, bf16[128,1024]{1,0:T(8,128)(2,1)S(1)}, u32[]{:S(2)}, u32[]{:S(2)}) collective-permute-start(bf16[128,1024]{1,0:T(8,128)(2,1)S(1)} %fusion.7), channel_id=1, source_target_pairs={{0,14},{2,0},{4,2},{6,4},{8,6},{10,8},{12,10},{14,12},{1,15},{3,1}... | collective-permute-start | bytes 786440 | tf_op jit(solution)/shard_map/sum_layers/ppermute | solution.py:25
  49.3 10.6 %collective-permute-start.14 = (bf16[128,1024]{1,0:T(8,128)(2,1)S(1)}, bf16[128,1024]{1,0:T(8,128)(2,1)S(1)}, u32[]{:S(2)}, u32[]{:S(2)}) collective-permute-start(bf16[128,1024]{1,0:T(8,128)(2,1)S(1)} %add_convert_fusion.2), channel_id=1, source_target_pairs={{0,14},{2,0},{4,2},{6,4},{8,6},{10,8},{12,10},{14,12},{1,15},{3,1}... | collective-permute-start | bytes 786440 | tf_op jit(solution)/shard_map/sum_layers/ppermute | solution.py:25
  49.9 10.5 %collective-permute-start.18 = (bf16[128,1024]{1,0:T(8,128)(2,1)S(1)}, bf16[128,1024]{1,0:T(8,128)(2,1)S(1)}, u32[]{:S(2)}, u32[]{:S(2)}) collective-permute-start(bf16[128,1024]{1,0:T(8,128)(2,1)S(1)} %fusion.5), channel_id=1, source_target_pairs={{0,2},{2,4},{4,6},{6,8},{8,10},{10,12},{12,14},{14,0},{1,3},{3,5},... | collective-permute-start | bytes 786440 | tf_op jit(solution)/shard_map/sum_layers/ppermute | solution.py:25
  53.7 10.6 %collective-permute-start.10 = (bf16[128,1024]{1,0:T(8,128)(2,1)S(1)}, bf16[128,1024]{1,0:T(8,128)(2,1)S(1)}, u32[]{:S(2)}, u32[]{:S(2)}) collective-permute-start(bf16[128,1024]{1,0:T(8,128)(2,1)S(1)} %add_convert_fusion.4), channel_id=1, source_target_pairs={{0,2},{2,4},{4,6},{6,8},{8,10},{10,12},{12,14},{14,0},{1,3},{3,5},... | collective-permute-start | bytes 786440 | tf_op jit(solution)/shard_map/sum_layers/ppermute | solution.py:25
  54.7 11.4 %collective-permute-start.20 = (bf16[128,1024]{1,0:T(8,128)(2,1)S(1)}, bf16[128,1024]{1,0:T(8,128)(2,1)S(1)}, u32[]{:S(2)}, u32[]{:S(2)}) collective-permute-start(bf16[128,1024]{1,0:T(8,128)(2,1)S(1)} %fusion.8), channel_id=1, source_target_pairs={{0,14},{2,0},{4,2},{6,4},{8,6},{10,8},{12,10},{14,12},{1,15},{3,1}... | collective-permute-start | bytes 786440 | tf_op jit(solution)/shard_map/sum_layers/ppermute | solution.py:25
  60.4 10.5 %collective-permute-start.16 = (bf16[128,1024]{1,0:T(8,128)(2,1)S(1)}, bf16[128,1024]{1,0:T(8,128)(2,1)S(1)}, u32[]{:S(2)}, u32[]{:S(2)}) collective-permute-start(bf16[128,1024]{1,0:T(8,128)(2,1)S(1)} %add_convert_fusion.1), channel_id=1, source_target_pairs={{0,14},{2,0},{4,2},{6,4},{8,6},{10,8},{12,10},{14,12},{1,15},{3,1}... | collective-permute-start | bytes 786440 | tf_op jit(solution)/shard_map/sum_layers/ppermute | solution.py:25
  60.9 10.9 %collective-permute-start.19 = (bf16[128,1024]{1,0:T(8,128)(2,1)S(1)}, bf16[128,1024]{1,0:T(8,128)(2,1)S(1)}, u32[]{:S(2)}, u32[]{:S(2)}) collective-permute-start(bf16[128,1024]{1,0:T(8,128)(2,1)S(1)} %fusion.4), channel_id=1, source_target_pairs={{0,2},{2,4},{4,6},{6,8},{8,10},{10,12},{12,14},{14,0},{1,3},{3,5},... | collective-permute-start | bytes 786440 | tf_op jit(solution)/shard_map/sum_layers/ppermute | solution.py:25
  64.7 6.7 %collective-permute-start.11 = (bf16[128,1024]{1,0:T(8,128)(2,1)S(1)}, bf16[128,1024]{1,0:T(8,128)(2,1)S(1)}, u32[]{:S(2)}, u32[]{:S(2)}) collective-permute-start(bf16[128,1024]{1,0:T(8,128)(2,1)S(1)} %add_convert_fusion.3), channel_id=1, source_target_pairs={{0,2},{2,4},{4,6},{6,8},{8,10},{10,12},{12,14},{14,0},{1,3},{3,5},... | collective-permute-start | bytes 786440 | tf_op jit(solution)/shard_map/sum_layers/ppermute | solution.py:25
  66.6 7.7 %collective-permute-start.21 = (bf16[128,1024]{1,0:T(8,128)(2,1)S(1)}, bf16[128,1024]{1,0:T(8,128)(2,1)S(1)}, u32[]{:S(2)}, u32[]{:S(2)}) collective-permute-start(bf16[128,1024]{1,0:T(8,128)(2,1)S(1)} %fusion.10), channel_id=1, source_target_pairs={{0,14},{2,0},{4,2},{6,4},{8,6},{10,8},{12,10},{14,12},{1,15},{3,1}... | collective-permute-start | bytes 786440 | tf_op jit(solution)/shard_map/sum_layers/ppermute | solution.py:25
  71.8 11.7 %copy-start.1 = (s32[1024]{0:T(1024)S(1)}, s32[1024]{0:T(1024)}, u32[]{:S(2)}) copy-start(s32[1024]{0:T(1024)} %param.12) | copy-start | bytes 12292
  74.7 37.7 %copy-start.2 = (s32[64]{0:T(128)S(1)}, s32[64]{0:T(128)}, u32[]{:S(2)}) copy-start(s32[64]{0:T(128)} %param.13) | copy-start | bytes 772
  75.6 17.7 %all-to-all-start = ((bf16[16,8,2048]{2,1,0:T(8,128)(2,1)}), bf16[16,8,2048]{2,1,0:T(8,128)(2,1)S(1)}, u32[]{:S(2)}, u32[]{:S(2)}) async-start(bf16[16,8,2048]{2,1,0:T(8,128)(2,1)} %maximum_bitcast_fusion), calls=%async_computation | async-start | bytes 1048576 | tf_op jit(solution)/shard_map/to_components/all_to_all | solution.py:245
  83.4 1.3 %collective-permute-start.22 = (f32[8,1024]{1,0:T(8,128)S(1)}, f32[8,1024]{1,0:T(8,128)S(1)}, u32[]{:S(2)}, u32[]{:S(2)}) collective-permute-start(f32[8,1024]{1,0:T(8,128)S(1)} %select_reduce_fusion), channel_id=1, source_target_pairs={{0,16},{16,0},{1,17},{17,1},{2,18},{18,2},{3,19},{19,3},{4,20},{20... | collective-permute-start | bytes 98312 | tf_op jit(solution)/shard_map/gather_values/ppermute | solution.py:25
  95.5 11.3 %all-to-all-start.1 = ((f32[32,1,256]{2,1,0:T(1,128)}), f32[32,1,256]{2,1,0:T(1,128)S(1)}, u32[]{:S(2)}, u32[]{:S(2)}) async-start(f32[32,1,256]{2,1,0:T(1,128)} %fit.1), calls=%async_computation.1 | async-start | bytes 65536 | tf_op jit(solution)/shard_map/gather_scores/all_to_all | solution.py:250
  106.8 5.5 %collective-permute-start.23 = (f32[256]{0:T(256)S(1)}, f32[256]{0:T(256)S(1)}, u32[]{:S(2)}, u32[]{:S(2)}) collective-permute-start(f32[256]{0:T(256)S(1)} %reduce_sum.19), channel_id=1, source_target_pairs={{0,2},{2,4},{4,6},{6,8},{8,10},{10,12},{12,14},{3,1},{5,3},{7,5},{... | collective-permute-start | bytes 3080 | tf_op jit(solution)/shard_map/gather_scores/ppermute | solution.py:253

commit v15 on v14

--- a/solution.py
+++ b/solution.py
@@ -151,11 +151,11 @@
         return lax.ppermute(value, (y, x), pairs)
 
     over_left = shifted(left, y, 1)
-    over_far = across(right, -1)
+    over_far = across(left, 1)
     over_right = shifted(over, x, -1)
-    far = shifted(left, x, 1)
-    over_left = over_left + 0 * other[: own.shape[0]]
-    return jnp.stack([over_far, over_right, over, left, far, right, own, over_left])
+    far = shifted(right, x, -1)
+    over_right = over_right + 0 * other[: own.shape[0]]
+    return jnp.stack([over, left, far, right, own, over_left, over_far, over_right])
 
 
 def smooth_block(widened, places, present, reaches):
@@ -197,7 +197,7 @@
     rows = own.shape[0] - EXTRA
 
     def place(across, along):
-        return (6 - 4 * (across ^ y) - (along - x) % 4) % 8
+        return (4 - 4 * (across ^ y) - (along - x) % 4) % 8
 
     with jax.named_scope("gather_values"):
         here = jnp.arange(8, dtype=jnp.int32)

time: 113 us -> 114 us (level)
  waiting for transfers between devices: 49.4 us -> 52.5 us
  local copies, waits for them, and re-layouts: 3.06 us -> 1.14 us
    ppermute x22, waiting for transfers between devices: 27 us -> 35.2 us  [shifted(): lax.ppermute(value, axis, [(i, (i + by) % peers) for i in range(peers)])]
    ppermute x1, waiting for transfers between devices: 4.79 us -> 0.01 us  [across(): return lax.ppermute(value, (y, x), pairs)]
    ppermute x1, starting transfers between devices: 4.7 us -> 0.17 us  [across(): return lax.ppermute(value, (y, x), pairs)]
    ppermute x22, starting transfers between devices: 27.3 us -> 31.1 us  [shifted(): lax.ppermute(value, axis, [(i, (i + by) % peers) for i in range(peers)])]
    unnamed x14, local copies, waits for them, and re-layouts: 2.1 us -> 0.17 us
  transfers between devices with their start and end apart: 26 -> 26, of which waited for: 16 -> 16; matrix products, arithmetic and copies ran while one was open for 8% -> 7% of each run, Pallas kernels for 0% -> 1%
where the time goes in v15:
time: 114 us
  waiting for transfers between devices  52.5 us (46%)
  starting transfers between devices  46.2 us (41%)
  matrix products  7.3 us (6%)
  Pallas kernels  3.33 us (3%)
  other arithmetic  2.04 us (2%)
    ppermute x22, waiting for transfers between devices, shifted(): lax.ppermute(value, axis, [(i, (i + by) % peers) for i in range(peers)])  35.2 us
    ppermute x22, starting transfers between devices, shifted(): lax.ppermute(value, axis, [(i, (i + by) % peers) for i in range(peers)])  31.1 us
    all_to_all x1, waiting for transfers between devices, shards(): sums = lax.all_to_all(whole, PLANE, 0, 0, tiled=True)  8.45 us
    all_to_all x1, starting transfers between devices, shards(): sums = lax.all_to_all(whole, PLANE, 0, 0, tiled=True)  7.7 us
    all_to_all x1, waiting for transfers between devices, shards(): lax.all_to_all(fitted, LAYER, 0, 0, tiled=True)  7.32 us
    dot_general x16, matrix products, term(): return jnp.dot(block, vecs[q], preferred_element_type=jnp.float32)  7.3 us
    all_to_all x1, starting transfers between devices, shards(): lax.all_to_all(fitted, LAYER, 0, 0, tiled=True)  3.84 us
    ppermute x1, starting transfers between devices, shards(): other = lax.ppermute(layer, CPG, beside)  3.38 us
  transfers between devices with their start and end apart: 26, of which 16 were waited for; matrix products, arithmetic and copies ran while one was open for 7% of the time, Pallas kernels for 1%

profile of v15, /device:TPU:96, one launch (start us, length us, event | category | flops | bytes accessed | tf_op | source)
XLA Modules:
  0.0 113.6 jit_solution(4790533573112238854)
XLA Ops:
  0.6 0.1 collective-permute-start.7
  0.7 1.1 %weigh.1 = bf16[144,1024]{1,0:T(8,128)(2,1)S(1)} custom-call(bf16[64,1024]{1,0:T(8,128)(2,1)} %resp_ref.1, bf16[64,1024]{1,0:T(8,128)(2,1)} %weight_ref.1, f32[1,1024]{1,0:T(1,128)} %bitcast.91, f32[1,1024]{1,0:T(1,128)} %bitcast.92), custom_call_target="tpu_custom_call" | custom-call | tf_op jit(solution)/shard_map/weigh/pallas_call | solution.py:57
  1.9 1.6 %collective-permute-start.1 = (bf16[144,1024]{1,0:T(8,128)(2,1)S(1)}, bf16[144,1024]{1,0:T(8,128)(2,1)S(1)}, u32[]{:S(2)}, u32[]{:S(2)}) collective-permute-start(bf16[144,1024]{1,0:T(8,128)(2,1)S(1)} %weigh.1), channel_id=1, source_target_pairs={{0,32},{32,64},{64,96},{96,0},{1,33},{33,65},{65,97},{97,1},{2,34}... | collective-permute-start | bytes 884744 | tf_op jit(solution)/shard_map/gather_rows/ppermute | solution.py:25
  3.4 1.6 %collective-permute-start = (bf16[144,1024]{1,0:T(8,128)(2,1)S(1)}, bf16[144,1024]{1,0:T(8,128)(2,1)S(1)}, u32[]{:S(2)}, u32[]{:S(2)}) collective-permute-start(bf16[144,1024]{1,0:T(8,128)(2,1)S(1)} %weigh.1), channel_id=1, source_target_pairs={{0,128},{128,0},{1,129},{129,1},{2,130},{130,2},{3,131},{131,3},{4... | collective-permute-start | bytes 884744 | tf_op jit(solution)/shard_map/gather_rows/ppermute | solution.py:25
  5.0 1.7 %collective-permute-start.2 = (bf16[144,1024]{1,0:T(8,128)(2,1)S(1)}, bf16[144,1024]{1,0:T(8,128)(2,1)S(1)}, u32[]{:S(2)}, u32[]{:S(2)}) collective-permute-start(bf16[144,1024]{1,0:T(8,128)(2,1)S(1)} %weigh.1), channel_id=1, source_target_pairs={{0,96},{32,0},{64,32},{96,64},{1,97},{33,1},{65,33},{97,65},{2,98}... | collective-permute-start | bytes 884744 | tf_op jit(solution)/shard_map/gather_rows/ppermute | solution.py:25
  6.9 5.7 %collective-permute-done.1 = bf16[144,1024]{1,0:T(8,128)(2,1)S(1)} collective-permute-done((bf16[144,1024]{1,0:T(8,128)(2,1)S(1)}, bf16[144,1024]{1,0:T(8,128)(2,1)S(1)}, u32[]{:S(2)}, u32[]{:S(2)}) %collective-permute-start.1) | collective-permute-done | bytes 294944 | tf_op jit(solution)/shard_map/gather_rows/ppermute | solution.py:25
  12.6 1.6 %collective-permute-start.4 = (bf16[144,1024]{1,0:T(8,128)(2,1)S(1)}, bf16[144,1024]{1,0:T(8,128)(2,1)S(1)}, u32[]{:S(2)}, u32[]{:S(2)}) collective-permute-start(bf16[144,1024]{1,0:T(8,128)(2,1)S(1)} %collective-permute-done.1), channel_id=1, source_target_pairs={{0,128},{128,0},{1,129},{129,1},{2,130},{130,2},{3,131},{131,3},{4... | collective-permute-start | bytes 884744 | tf_op jit(solution)/shard_map/gather_rows/ppermute | solution.py:25
  14.1 0.2 collective-permute-start.5
  14.3 3.0 %collective-permute-start.3 = (bf16[144,1024]{1,0:T(8,128)(2,1)S(1)}, bf16[144,1024]{1,0:T(8,128)(2,1)S(1)}, u32[]{:S(2)}, u32[]{:S(2)}) collective-permute-start(bf16[144,1024]{1,0:T(8,128)(2,1)S(1)} %collective-permute-done.2), channel_id=1, source_target_pairs={{0,96},{32,0},{64,32},{96,64},{1,97},{33,1},{65,33},{97,65},{2,98}... | collective-permute-start | bytes 884744 | tf_op jit(solution)/shard_map/gather_rows/ppermute | solution.py:25
  17.3 0.4 collective-permute-start.6
  17.7 7.0 %collective-permute-done.3 = bf16[144,1024]{1,0:T(8,128)(2,1)S(1)} collective-permute-done((bf16[144,1024]{1,0:T(8,128)(2,1)S(1)}, bf16[144,1024]{1,0:T(8,128)(2,1)S(1)}, u32[]{:S(2)}, u32[]{:S(2)}) %collective-permute-start.3) | collective-permute-done | bytes 294944 | tf_op jit(solution)/shard_map/gather_rows/ppermute | solution.py:25
  24.8 2.7 %collective-permute-done.4 = bf16[144,1024]{1,0:T(8,128)(2,1)S(1)} collective-permute-done((bf16[144,1024]{1,0:T(8,128)(2,1)S(1)}, bf16[144,1024]{1,0:T(8,128)(2,1)S(1)}, u32[]{:S(2)}, u32[]{:S(2)}) %collective-permute-start.4) | collective-permute-done | bytes 294944 | tf_op jit(solution)/shard_map/gather_rows/ppermute | solution.py:25
  27.6 1.6 %collective-permute-done.6 = bf16[144,1024]{1,0:T(8,128)(2,1)S(1)} collective-permute-done((bf16[144,1024]{1,0:T(8,128)(2,1)S(1)}, bf16[144,1024]{1,0:T(8,128)(2,1)S(1)}, u32[]{:S(2)}, u32[]{:S(2)}) %collective-permute-start.6) | collective-permute-done | bytes 294944 | tf_op jit(solution)/shard_map/gather_rows/ppermute | solution.py:25
  29.2 0.1 fusion.13
  29.3 0.4 convolution_convert_fusion.1
  29.7 3.2 %collective-permute-start.8 = (bf16[128,1024]{1,0:T(8,128)(2,1)S(1)}, bf16[128,1024]{1,0:T(8,128)(2,1)S(1)}, u32[]{:S(2)}, u32[]{:S(2)}) collective-permute-start(bf16[128,1024]{1,0:T(8,128)(2,1)S(1)} %convolution_convert_fusion.1), channel_id=1, source_target_pairs={{0,2},{2,4},{4,6},{6,8},{8,10},{10,12},{12,14},{14,0},{1,3},{3,5},... | collective-permute-start | bytes 786440 | tf_op jit(solution)/shard_map/sum_layers/ppermute | solution.py:25
  32.9 0.4 convolution_convert_fusion
  33.4 0.1 collective-permute-start.13
  33.5 0.4 fusion.6
  33.9 0.1 collective-permute-start.12
  34.0 0.4 fusion.9
  34.5 3.3 %collective-permute-start.17 = (bf16[128,1024]{1,0:T(8,128)(2,1)S(1)}, bf16[128,1024]{1,0:T(8,128)(2,1)S(1)}, u32[]{:S(2)}, u32[]{:S(2)}) collective-permute-start(bf16[128,1024]{1,0:T(8,128)(2,1)S(1)} %fusion.9), channel_id=1, source_target_pairs={{0,2},{2,4},{4,6},{6,8},{8,10},{10,12},{12,14},{14,0},{1,3},{3,5},... | collective-permute-start | bytes 786440 | tf_op jit(solution)/shard_map/sum_layers/ppermute | solution.py:25
  37.8 0.4 collective-permute-done.8
  38.2 0.4 add_convert_fusion.5
  38.6 4.0 %collective-permute-start.9 = (bf16[128,1024]{1,0:T(8,128)(2,1)S(1)}, bf16[128,1024]{1,0:T(8,128)(2,1)S(1)}, u32[]{:S(2)}, u32[]{:S(2)}) collective-permute-start(bf16[128,1024]{1,0:T(8,128)(2,1)S(1)} %add_convert_fusion.5), channel_id=1, source_target_pairs={{0,2},{2,4},{4,6},{6,8},{8,10},{10,12},{12,14},{14,0},{1,3},{3,5},... | collective-permute-start | bytes 786440 | tf_op jit(solution)/shard_map/sum_layers/ppermute | solution.py:25
  42.6 1.4 %collective-permute-done.13 = bf16[128,1024]{1,0:T(8,128)(2,1)S(1)} collective-permute-done((bf16[128,1024]{1,0:T(8,128)(2,1)S(1)}, bf16[128,1024]{1,0:T(8,128)(2,1)S(1)}, u32[]{:S(2)}, u32[]{:S(2)}) %collective-permute-start.13) | collective-permute-done | bytes 262176 | tf_op jit(solution)/shard_map/sum_layers/ppermute | solution.py:25
  43.9 0.4 fusion.7
  44.5 5.1 %collective-permute-done.12 = bf16[128,1024]{1,0:T(8,128)(2,1)S(1)} collective-permute-done((bf16[128,1024]{1,0:T(8,128)(2,1)S(1)}, bf16[128,1024]{1,0:T(8,128)(2,1)S(1)}, u32[]{:S(2)}, u32[]{:S(2)}) %collective-permute-start.12) | collective-permute-done | bytes 262176 | tf_op jit(solution)/shard_map/sum_layers/ppermute | solution.py:25
  49.5 0.5 add_convert_fusion.2
  50.1 0.5 fusion.5
  50.6 3.3 %collective-permute-start.18 = (bf16[128,1024]{1,0:T(8,128)(2,1)S(1)}, bf16[128,1024]{1,0:T(8,128)(2,1)S(1)}, u32[]{:S(2)}, u32[]{:S(2)}) collective-permute-start(bf16[128,1024]{1,0:T(8,128)(2,1)S(1)} %fusion.5), channel_id=1, source_target_pairs={{0,2},{2,4},{4,6},{6,8},{8,10},{10,12},{12,14},{14,0},{1,3},{3,5},... | collective-permute-start | bytes 786440 | tf_op jit(solution)/shard_map/sum_layers/ppermute | solution.py:25
  53.9 0.4 add_convert_fusion.4
  54.4 0.1 collective-permute-start.10
  54.5 0.7 collective-permute-done.15
  55.2 0.4 fusion.8
  55.6 1.4 %collective-permute-start.20 = (bf16[128,1024]{1,0:T(8,128)(2,1)S(1)}, bf16[128,1024]{1,0:T(8,128)(2,1)S(1)}, u32[]{:S(2)}, u32[]{:S(2)}) collective-permute-start(bf16[128,1024]{1,0:T(8,128)(2,1)S(1)} %fusion.8), channel_id=1, source_target_pairs={{0,14},{2,0},{4,2},{6,4},{8,6},{10,8},{12,10},{14,12},{1,15},{3,1}... | collective-permute-start | bytes 786440 | tf_op jit(solution)/shard_map/sum_layers/ppermute | solution.py:25
  57.0 3.8 %collective-permute-done.14 = bf16[128,1024]{1,0:T(8,128)(2,1)S(1)} collective-permute-done((bf16[128,1024]{1,0:T(8,128)(2,1)S(1)}, bf16[128,1024]{1,0:T(8,128)(2,1)S(1)}, u32[]{:S(2)}, u32[]{:S(2)}) %collective-permute-start.14) | collective-permute-done | bytes 262176 | tf_op jit(solution)/shard_map/sum_layers/ppermute | solution.py:25
  60.8 0.5 add_convert_fusion.1
  61.4 0.5 fusion.4
  61.9 3.3 %collective-permute-start.19 = (bf16[128,1024]{1,0:T(8,128)(2,1)S(1)}, bf16[128,1024]{1,0:T(8,128)(2,1)S(1)}, u32[]{:S(2)}, u32[]{:S(2)}) collective-permute-start(bf16[128,1024]{1,0:T(8,128)(2,1)S(1)} %fusion.4), channel_id=1, source_target_pairs={{0,2},{2,4},{4,6},{6,8},{8,10},{10,12},{12,14},{14,0},{1,3},{3,5},... | collective-permute-start | bytes 786440 | tf_op jit(solution)/shard_map/sum_layers/ppermute | solution.py:25
  65.1 0.4 add_convert_fusion.3
  65.6 0.8 collective-permute-start.11
  66.5 0.4 fusion.10
  66.9 1.3 %collective-permute-start.21 = (bf16[128,1024]{1,0:T(8,128)(2,1)S(1)}, bf16[128,1024]{1,0:T(8,128)(2,1)S(1)}, u32[]{:S(2)}, u32[]{:S(2)}) collective-permute-start(bf16[128,1024]{1,0:T(8,128)(2,1)S(1)} %fusion.10), channel_id=1, source_target_pairs={{0,14},{2,0},{4,2},{6,4},{8,6},{10,8},{12,10},{14,12},{1,15},{3,1}... | collective-permute-start | bytes 786440 | tf_op jit(solution)/shard_map/sum_layers/ppermute | solution.py:25
  68.2 3.5 %collective-permute-done.16 = bf16[128,1024]{1,0:T(8,128)(2,1)S(1)} collective-permute-done((bf16[128,1024]{1,0:T(8,128)(2,1)S(1)}, bf16[128,1024]{1,0:T(8,128)(2,1)S(1)}, u32[]{:S(2)}, u32[]{:S(2)}) %collective-permute-start.16) | collective-permute-done | bytes 262176 | tf_op jit(solution)/shard_map/sum_layers/ppermute | solution.py:25
  71.7 0.3 collective-permute-done.11
  72.1 0.5 add_convert_fusion
  72.5 2.0 %collective-permute-done.21 = bf16[128,1024]{1,0:T(8,128)(2,1)S(1)} collective-permute-done((bf16[128,1024]{1,0:T(8,128)(2,1)S(1)}, bf16[128,1024]{1,0:T(8,128)(2,1)S(1)}, u32[]{:S(2)}, u32[]{:S(2)}) %collective-permute-start.21) | collective-permute-done | bytes 262176 | tf_op jit(solution)/shard_map/sum_layers/ppermute | solution.py:25
  74.6 0.5 fusion.3
  75.1 0.8 maximum_bitcast_fusion
  75.9 7.7 %all-to-all-start = ((bf16[16,8,2048]{2,1,0:T(8,128)(2,1)}), bf16[16,8,2048]{2,1,0:T(8,128)(2,1)S(1)}, u32[]{:S(2)}, u32[]{:S(2)}) async-start(bf16[16,8,2048]{2,1,0:T(8,128)(2,1)} %maximum_bitcast_fusion), calls=%async_computation | async-start | bytes 1048576 | tf_op jit(solution)/shard_map/to_components/all_to_all | solution.py:245
  83.7 0.1 select_reduce_fusion
  83.8 0.1 collective-permute-start.22
  84.0 1.1 %collective-permute-done.22 = f32[8,1024]{1,0:T(8,128)S(1)} collective-permute-done((f32[8,1024]{1,0:T(8,128)S(1)}, f32[8,1024]{1,0:T(8,128)S(1)}, u32[]{:S(2)}, u32[]{:S(2)}) %collective-permute-start.22) | collective-permute-done | bytes 32800 | tf_op jit(solution)/shard_map/gather_values/ppermute | solution.py:25
  85.2 0.1 reshape.101.values_ref
  85.3 8.5 %all-to-all-done = bf16[16,8,2048]{2,1,0:T(8,128)(2,1)S(1)} async-done(((bf16[16,8,2048]{2,1,0:T(8,128)(2,1)}), bf16[16,8,2048]{2,1,0:T(8,128)(2,1)S(1)}, u32[]{:S(2)}, u32[]{:S(2)}) %all-to-all-start) | async-done | bytes 524320 | tf_op jit(solution)/shard_map/to_components/all_to_all | solution.py:245
  93.8 2.2 %fit.1 = f32[32,1,256]{2,1,0:T(1,128)} custom-call(s32[1]{0:T(128)} %bitcast.slot_ref, bf16[128,2048]{1,0:T(8,128)(2,1)S(1)} %bitcast.89, f32[32,2048]{1,0:T(8,128)S(1)} %reshape.101.values_ref), custom_call_target="tpu_custom_call" | custom-call | tf_op jit(solution)/shard_map/fit/pallas_call | solution.py:130
  95.9 3.8 %all-to-all-start.1 = ((f32[32,1,256]{2,1,0:T(1,128)}), f32[32,1,256]{2,1,0:T(1,128)S(1)}, u32[]{:S(2)}, u32[]{:S(2)}) async-start(f32[32,1,256]{2,1,0:T(1,128)} %fit.1), calls=%async_computation.1 | async-start | bytes 65536 | tf_op jit(solution)/shard_map/gather_scores/all_to_all | solution.py:250
  99.8 0.1 pad_dynamic-slice_fusion
  99.9 7.3 %all-to-all-done.1 = f32[32,1,256]{2,1,0:T(1,128)S(1)} async-done(((f32[32,1,256]{2,1,0:T(1,128)}), f32[32,1,256]{2,1,0:T(1,128)S(1)}, u32[]{:S(2)}, u32[]{:S(2)}) %all-to-all-start.1) | async-done | bytes 32800 | tf_op jit(solution)/shard_map/gather_scores/all_to_all | solution.py:250
  107.3 3.4 %collective-permute-start.23 = (f32[256]{0:T(256)S(1)}, f32[256]{0:T(256)S(1)}, u32[]{:S(2)}, u32[]{:S(2)}) collective-permute-start(f32[256]{0:T(256)S(1)} %reduce_sum.19), channel_id=1, source_target_pairs={{0,2},{2,4},{4,6},{6,8},{8,10},{10,12},{12,14},{3,1},{5,3},{7,5},{... | collective-permute-start | bytes 3080 | tf_op jit(solution)/shard_map/gather_scores/ppermute | solution.py:253
  110.7 0.6 dynamic_slice.55
  111.3 1.5 %collective-permute-done.23 = f32[256]{0:T(256)S(1)} collective-permute-done((f32[256]{0:T(256)S(1)}, f32[256]{0:T(256)S(1)}, u32[]{:S(2)}, u32[]{:S(2)}) %collective-permute-start.23) | collective-permute-done | bytes 1056 | tf_op jit(solution)/shard_map/gather_scores/ppermute | solution.py:253
  113.0 0.6 add_divide_fusion
  (40 shorter events, 1.0 us)
Async XLA Ops:
  0.6 28.5 %collective-permute-start.7 = (bf16[1024,1024]{1,0:T(8,128)(2,1)}, bf16[1024,1024]{1,0:T(8,128)(2,1)S(1)}, u32[]{:S(2)}, u32[]{:S(2)}) collective-permute-start(bf16[1024,1024]{1,0:T(8,128)(2,1)} %param.10), channel_id=1, source_target_pairs={{0,16},{16,0},{1,17},{17,1},{2,18},{18,2},{3,19},{19,3},{4,20},{20... | collective-permute-start | bytes 6291464 | tf_op jit(solution)/shard_map/swap_eigvecs/ppermute | solution.py:25
  1.9 10.7 %collective-permute-start.1 = (bf16[144,1024]{1,0:T(8,128)(2,1)S(1)}, bf16[144,1024]{1,0:T(8,128)(2,1)S(1)}, u32[]{:S(2)}, u32[]{:S(2)}) collective-permute-start(bf16[144,1024]{1,0:T(8,128)(2,1)S(1)} %weigh.1), channel_id=1, source_target_pairs={{0,32},{32,64},{64,96},{96,0},{1,33},{33,65},{65,97},{97,1},{2,34}... | collective-permute-start | bytes 884744 | tf_op jit(solution)/shard_map/gather_rows/ppermute | solution.py:25
  3.4 13.8 %collective-permute-start = (bf16[144,1024]{1,0:T(8,128)(2,1)S(1)}, bf16[144,1024]{1,0:T(8,128)(2,1)S(1)}, u32[]{:S(2)}, u32[]{:S(2)}) collective-permute-start(bf16[144,1024]{1,0:T(8,128)(2,1)S(1)} %weigh.1), channel_id=1, source_target_pairs={{0,128},{128,0},{1,129},{129,1},{2,130},{130,2},{3,131},{131,3},{4... | collective-permute-start | bytes 884744 | tf_op jit(solution)/shard_map/gather_rows/ppermute | solution.py:25
  5.0 9.3 %collective-permute-start.2 = (bf16[144,1024]{1,0:T(8,128)(2,1)S(1)}, bf16[144,1024]{1,0:T(8,128)(2,1)S(1)}, u32[]{:S(2)}, u32[]{:S(2)}) collective-permute-start(bf16[144,1024]{1,0:T(8,128)(2,1)S(1)} %weigh.1), channel_id=1, source_target_pairs={{0,96},{32,0},{64,32},{96,64},{1,97},{33,1},{65,33},{97,65},{2,98}... | collective-permute-start | bytes 884744 | tf_op jit(solution)/shard_map/gather_rows/ppermute | solution.py:25
  12.6 14.9 %collective-permute-start.4 = (bf16[144,1024]{1,0:T(8,128)(2,1)S(1)}, bf16[144,1024]{1,0:T(8,128)(2,1)S(1)}, u32[]{:S(2)}, u32[]{:S(2)}) collective-permute-start(bf16[144,1024]{1,0:T(8,128)(2,1)S(1)} %collective-permute-done.1), channel_id=1, source_target_pairs={{0,128},{128,0},{1,129},{129,1},{2,130},{130,2},{3,131},{131,3},{4... | collective-permute-start | bytes 884744 | tf_op jit(solution)/shard_map/gather_rows/ppermute | solution.py:25
  14.1 13.4 %collective-permute-start.5 = (bf16[144,1024]{1,0:T(8,128)(2,1)S(1)}, bf16[144,1024]{1,0:T(8,128)(2,1)S(1)}, u32[]{:S(2)}, u32[]{:S(2)}) collective-permute-start(bf16[144,1024]{1,0:T(8,128)(2,1)S(1)} %collective-permute-done.1), channel_id=1, source_target_pairs={{0,160},{32,192},{64,224},{96,128},{128,32},{160,64},{192,96},{224... | collective-permute-start | bytes 884744 | tf_op jit(solution)/shard_map/gather_rows/ppermute | solution.py:151
  14.3 10.4 %collective-permute-start.3 = (bf16[144,1024]{1,0:T(8,128)(2,1)S(1)}, bf16[144,1024]{1,0:T(8,128)(2,1)S(1)}, u32[]{:S(2)}, u32[]{:S(2)}) collective-permute-start(bf16[144,1024]{1,0:T(8,128)(2,1)S(1)} %collective-permute-done.2), channel_id=1, source_target_pairs={{0,96},{32,0},{64,32},{96,64},{1,97},{33,1},{65,33},{97,65},{2,98}... | collective-permute-start | bytes 884744 | tf_op jit(solution)/shard_map/gather_rows/ppermute | solution.py:25
  17.3 12.0 %copy-start = (bf16[1024,1024]{1,0:T(8,128)(2,1)S(1)}, bf16[1024,1024]{1,0:T(8,128)(2,1)}, u32[]{:S(2)}) copy-start(bf16[1024,1024]{1,0:T(8,128)(2,1)} %param.10) | copy-start | bytes 6291460
  17.3 11.9 %collective-permute-start.6 = (bf16[144,1024]{1,0:T(8,128)(2,1)S(1)}, bf16[144,1024]{1,0:T(8,128)(2,1)S(1)}, u32[]{:S(2)}, u32[]{:S(2)}) collective-permute-start(bf16[144,1024]{1,0:T(8,128)(2,1)S(1)} %collective-permute-done), channel_id=1, source_target_pairs={{0,96},{32,0},{64,32},{96,64},{1,97},{33,1},{65,33},{97,65},{2,98}... | collective-permute-start | bytes 884744 | tf_op jit(solution)/shard_map/gather_rows/ppermute | solution.py:25
  29.7 8.4 %collective-permute-start.8 = (bf16[128,1024]{1,0:T(8,128)(2,1)S(1)}, bf16[128,1024]{1,0:T(8,128)(2,1)S(1)}, u32[]{:S(2)}, u32[]{:S(2)}) collective-permute-start(bf16[128,1024]{1,0:T(8,128)(2,1)S(1)} %convolution_convert_fusion.1), channel_id=1, source_target_pairs={{0,2},{2,4},{4,6},{6,8},{8,10},{10,12},{12,14},{14,0},{1,3},{3,5},... | collective-permute-start | bytes 786440 | tf_op jit(solution)/shard_map/sum_layers/ppermute | solution.py:25
  33.4 10.5 %collective-permute-start.13 = (bf16[128,1024]{1,0:T(8,128)(2,1)S(1)}, bf16[128,1024]{1,0:T(8,128)(2,1)S(1)}, u32[]{:S(2)}, u32[]{:S(2)}) collective-permute-start(bf16[128,1024]{1,0:T(8,128)(2,1)S(1)} %convolution_convert_fusion), channel_id=1, source_target_pairs={{0,14},{2,0},{4,2},{6,4},{8,6},{10,8},{12,10},{14,12},{1,15},{3,1}... | collective-permute-start | bytes 786440 | tf_op jit(solution)/shard_map/sum_layers/ppermute | solution.py:25
  33.9 15.6 %collective-permute-start.12 = (bf16[128,1024]{1,0:T(8,128)(2,1)S(1)}, bf16[128,1024]{1,0:T(8,128)(2,1)S(1)}, u32[]{:S(2)}, u32[]{:S(2)}) collective-permute-start(bf16[128,1024]{1,0:T(8,128)(2,1)S(1)} %fusion.6), channel_id=1, source_target_pairs={{0,14},{2,0},{4,2},{6,4},{8,6},{10,8},{12,10},{14,12},{1,15},{3,1}... | collective-permute-start | bytes 786440 | tf_op jit(solution)/shard_map/sum_layers/ppermute | solution.py:25
  34.5 15.6 %collective-permute-start.17 = (bf16[128,1024]{1,0:T(8,128)(2,1)S(1)}, bf16[128,1024]{1,0:T(8,128)(2,1)S(1)}, u32[]{:S(2)}, u32[]{:S(2)}) collective-permute-start(bf16[128,1024]{1,0:T(8,128)(2,1)S(1)} %fusion.9), channel_id=1, source_target_pairs={{0,2},{2,4},{4,6},{6,8},{8,10},{10,12},{12,14},{14,0},{1,3},{3,5},... | collective-permute-start | bytes 786440 | tf_op jit(solution)/shard_map/sum_layers/ppermute | solution.py:25
  38.6 15.3 %collective-permute-start.9 = (bf16[128,1024]{1,0:T(8,128)(2,1)S(1)}, bf16[128,1024]{1,0:T(8,128)(2,1)S(1)}, u32[]{:S(2)}, u32[]{:S(2)}) collective-permute-start(bf16[128,1024]{1,0:T(8,128)(2,1)S(1)} %add_convert_fusion.5), channel_id=1, source_target_pairs={{0,2},{2,4},{4,6},{6,8},{8,10},{10,12},{12,14},{14,0},{1,3},{3,5},... | collective-permute-start | bytes 786440 | tf_op jit(solution)/shard_map/sum_layers/ppermute | solution.py:25
  44.4 10.8 %collective-permute-start.15 = (bf16[128,1024]{1,0:T(8,128)(2,1)S(1)}, bf16[128,1024]{1,0:T(8,128)(2,1)S(1)}, u32[]{:S(2)}, u32[]{:S(2)}) collective-permute-start(bf16[128,1024]{1,0:T(8,128)(2,1)S(1)} %fusion.7), channel_id=1, source_target_pairs={{0,14},{2,0},{4,2},{6,4},{8,6},{10,8},{12,10},{14,12},{1,15},{3,1}... | collective-permute-start | bytes 786440 | tf_op jit(solution)/shard_map/sum_layers/ppermute | solution.py:25
  50.0 10.8 %collective-permute-start.14 = (bf16[128,1024]{1,0:T(8,128)(2,1)S(1)}, bf16[128,1024]{1,0:T(8,128)(2,1)S(1)}, u32[]{:S(2)}, u32[]{:S(2)}) collective-permute-start(bf16[128,1024]{1,0:T(8,128)(2,1)S(1)} %add_convert_fusion.2), channel_id=1, source_target_pairs={{0,14},{2,0},{4,2},{6,4},{8,6},{10,8},{12,10},{14,12},{1,15},{3,1}... | collective-permute-start | bytes 786440 | tf_op jit(solution)/shard_map/sum_layers/ppermute | solution.py:25
  50.6 10.7 %collective-permute-start.18 = (bf16[128,1024]{1,0:T(8,128)(2,1)S(1)}, bf16[128,1024]{1,0:T(8,128)(2,1)S(1)}, u32[]{:S(2)}, u32[]{:S(2)}) collective-permute-start(bf16[128,1024]{1,0:T(8,128)(2,1)S(1)} %fusion.5), channel_id=1, source_target_pairs={{0,2},{2,4},{4,6},{6,8},{8,10},{10,12},{12,14},{14,0},{1,3},{3,5},... | collective-permute-start | bytes 786440 | tf_op jit(solution)/shard_map/sum_layers/ppermute | solution.py:25
  54.4 10.8 %collective-permute-start.10 = (bf16[128,1024]{1,0:T(8,128)(2,1)S(1)}, bf16[128,1024]{1,0:T(8,128)(2,1)S(1)}, u32[]{:S(2)}, u32[]{:S(2)}) collective-permute-start(bf16[128,1024]{1,0:T(8,128)(2,1)S(1)} %add_convert_fusion.4), channel_id=1, source_target_pairs={{0,2},{2,4},{4,6},{6,8},{8,10},{10,12},{12,14},{14,0},{1,3},{3,5},... | collective-permute-start | bytes 786440 | tf_op jit(solution)/shard_map/sum_layers/ppermute | solution.py:25
  55.6 10.8 %collective-permute-start.20 = (bf16[128,1024]{1,0:T(8,128)(2,1)S(1)}, bf16[128,1024]{1,0:T(8,128)(2,1)S(1)}, u32[]{:S(2)}, u32[]{:S(2)}) collective-permute-start(bf16[128,1024]{1,0:T(8,128)(2,1)S(1)} %fusion.8), channel_id=1, source_target_pairs={{0,14},{2,0},{4,2},{6,4},{8,6},{10,8},{12,10},{14,12},{1,15},{3,1}... | collective-permute-start | bytes 786440 | tf_op jit(solution)/shard_map/sum_layers/ppermute | solution.py:25
  61.3 10.5 %collective-permute-start.16 = (bf16[128,1024]{1,0:T(8,128)(2,1)S(1)}, bf16[128,1024]{1,0:T(8,128)(2,1)S(1)}, u32[]{:S(2)}, u32[]{:S(2)}) collective-permute-start(bf16[128,1024]{1,0:T(8,128)(2,1)S(1)} %add_convert_fusion.1), channel_id=1, source_target_pairs={{0,14},{2,0},{4,2},{6,4},{8,6},{10,8},{12,10},{14,12},{1,15},{3,1}... | collective-permute-start | bytes 786440 | tf_op jit(solution)/shard_map/sum_layers/ppermute | solution.py:25
  61.9 10.7 %collective-permute-start.19 = (bf16[128,1024]{1,0:T(8,128)(2,1)S(1)}, bf16[128,1024]{1,0:T(8,128)(2,1)S(1)}, u32[]{:S(2)}, u32[]{:S(2)}) collective-permute-start(bf16[128,1024]{1,0:T(8,128)(2,1)S(1)} %fusion.4), channel_id=1, source_target_pairs={{0,2},{2,4},{4,6},{6,8},{8,10},{10,12},{12,14},{14,0},{1,3},{3,5},... | collective-permute-start | bytes 786440 | tf_op jit(solution)/shard_map/sum_layers/ppermute | solution.py:25
  65.6 6.4 %collective-permute-start.11 = (bf16[128,1024]{1,0:T(8,128)(2,1)S(1)}, bf16[128,1024]{1,0:T(8,128)(2,1)S(1)}, u32[]{:S(2)}, u32[]{:S(2)}) collective-permute-start(bf16[128,1024]{1,0:T(8,128)(2,1)S(1)} %add_convert_fusion.3), channel_id=1, source_target_pairs={{0,2},{2,4},{4,6},{6,8},{8,10},{10,12},{12,14},{14,0},{1,3},{3,5},... | collective-permute-start | bytes 786440 | tf_op jit(solution)/shard_map/sum_layers/ppermute | solution.py:25
  66.9 7.7 %collective-permute-start.21 = (bf16[128,1024]{1,0:T(8,128)(2,1)S(1)}, bf16[128,1024]{1,0:T(8,128)(2,1)S(1)}, u32[]{:S(2)}, u32[]{:S(2)}) collective-permute-start(bf16[128,1024]{1,0:T(8,128)(2,1)S(1)} %fusion.10), channel_id=1, source_target_pairs={{0,14},{2,0},{4,2},{6,4},{8,6},{10,8},{12,10},{14,12},{1,15},{3,1}... | collective-permute-start | bytes 786440 | tf_op jit(solution)/shard_map/sum_layers/ppermute | solution.py:25
  72.5 11.4 %copy-start.1 = (s32[1024]{0:T(1024)S(1)}, s32[1024]{0:T(1024)}, u32[]{:S(2)}) copy-start(s32[1024]{0:T(1024)} %param.12) | copy-start | bytes 12292
  75.0 37.9 %copy-start.2 = (s32[64]{0:T(128)S(1)}, s32[64]{0:T(128)}, u32[]{:S(2)}) copy-start(s32[64]{0:T(128)} %param.13) | copy-start | bytes 772
  75.9 17.8 %all-to-all-start = ((bf16[16,8,2048]{2,1,0:T(8,128)(2,1)}), bf16[16,8,2048]{2,1,0:T(8,128)(2,1)S(1)}, u32[]{:S(2)}, u32[]{:S(2)}) async-start(bf16[16,8,2048]{2,1,0:T(8,128)(2,1)} %maximum_bitcast_fusion), calls=%async_computation | async-start | bytes 1048576 | tf_op jit(solution)/shard_map/to_components/all_to_all | solution.py:245
  83.8 1.3 %collective-permute-start.22 = (f32[8,1024]{1,0:T(8,128)S(1)}, f32[8,1024]{1,0:T(8,128)S(1)}, u32[]{:S(2)}, u32[]{:S(2)}) collective-permute-start(f32[8,1024]{1,0:T(8,128)S(1)} %select_reduce_fusion), channel_id=1, source_target_pairs={{0,16},{16,0},{1,17},{17,1},{2,18},{18,2},{3,19},{19,3},{4,20},{20... | collective-permute-start | bytes 98312 | tf_op jit(solution)/shard_map/gather_values/ppermute | solution.py:25
  95.9 11.3 %all-to-all-start.1 = ((f32[32,1,256]{2,1,0:T(1,128)}), f32[32,1,256]{2,1,0:T(1,128)S(1)}, u32[]{:S(2)}, u32[]{:S(2)}) async-start(f32[32,1,256]{2,1,0:T(1,128)} %fit.1), calls=%async_computation.1 | async-start | bytes 65536 | tf_op jit(solution)/shard_map/gather_scores/all_to_all | solution.py:250
  107.3 5.5 %collective-permute-start.23 = (f32[256]{0:T(256)S(1)}, f32[256]{0:T(256)S(1)}, u32[]{:S(2)}, u32[]{:S(2)}) collective-permute-start(f32[256]{0:T(256)S(1)} %reduce_sum.19), channel_id=1, source_target_pairs={{0,2},{2,4},{4,6},{6,8},{8,10},{10,12},{12,14},{3,1},{5,3},{7,5},{... | collective-permute-start | bytes 3080 | tf_op jit(solution)/shard_map/gather_scores/ppermute | solution.py:253

commit v16 on v14

--- a/solution.py
+++ b/solution.py
@@ -227,12 +227,6 @@
         sent[q, way] = shifted(total, "cpg_0", way)
         return total
 
-    def summed(q):
-        total = term(q, 0)
-        for way in (1, -1):
-            total = total + sent[q, way].astype(jnp.float32)
-        return total.astype(jnp.bfloat16)
-
     with jax.named_scope("sum_layers"):
         for ahead in range(far, 0, -1):
             onward(0, 1, ahead)
@@ -240,7 +234,13 @@
             if ahead > 1:
                 onward(0, -1, ahead - 1, behind)
                 onward(1, 1, ahead - 1, behind)
-        whole = jnp.concatenate([summed(0), summed(1)], axis=1)
+        def joined(first, second):
+            return jnp.concatenate([first, second], axis=1).astype(jnp.float32)
+
+        whole = joined(term(0, 0), term(1, 0))
+        for way in (1, -1):
+            whole = whole + joined(sent[0, way], sent[1, way])
+        whole = whole.astype(jnp.bfloat16)
     with jax.named_scope("to_components"):
         sums = lax.all_to_all(whole, PLANE, 0, 0, tiled=True)
     with jax.named_scope("fit"):

time: 113 us -> 118 us (1.044)
  the two profiles are of different devices: /device:TPU:96 before, /device:TPU:24 now
where the time goes in v16:
time: 118 us
  starting transfers between devices  53.5 us (45%)
  waiting for transfers between devices  46.7 us (40%)
  matrix products  7.31 us (6%)
  Pallas kernels  3.33 us (3%)
  local copies, waits for them, and re-layouts  3.06 us (3%)
  other arithmetic  2.2 us (2%)
  between operations  1.54 us (1%)
    ppermute x22, starting transfers between devices, shifted(): lax.ppermute(value, axis, [(i, (i + by) % peers) for i in range(peers)])  33.3 us
    ppermute x22, waiting for transfers between devices, shifted(): lax.ppermute(value, axis, [(i, (i + by) % peers) for i in range(peers)])  27.6 us
    all_to_all x1, starting transfers between devices, shards(): sums = lax.all_to_all(whole, PLANE, 0, 0, tiled=True)  8.96 us
    dot_general x16, matrix products, term(): return jnp.dot(block, vecs[q], preferred_element_type=jnp.float32)  7.31 us
    all_to_all x1, waiting for transfers between devices, shards(): sums = lax.all_to_all(whole, PLANE, 0, 0, tiled=True)  6.17 us
    all_to_all x1, starting transfers between devices, shards(): lax.all_to_all(fitted, LAYER, 0, 0, tiled=True)  6.04 us
    all_to_all x1, waiting for transfers between devices, shards(): lax.all_to_all(fitted, LAYER, 0, 0, tiled=True)  5.39 us
    ppermute x1, waiting for transfers between devices, across(): return lax.ppermute(value, (y, x), pairs)  3.96 us
  transfers between devices with their start and end apart: 26, of which 16 were waited for; matrix products, arithmetic and copies ran while one was open for 9% of the time, Pallas kernels for 0%

profile of v16, /device:TPU:24, one launch (start us, length us, event | category | flops | bytes accessed | tf_op | source)
XLA Modules:
  0.0 117.6 jit_solution(13837607820436565427)
XLA Ops:
  0.6 1.1 weigh.1
  1.8 2.8 %collective-permute-start = (bf16[144,1024]{1,0:T(8,128)(2,1)S(1)}, bf16[144,1024]{1,0:T(8,128)(2,1)S(1)}, u32[]{:S(2)}, u32[]{:S(2)}) collective-permute-start(bf16[144,1024]{1,0:T(8,128)(2,1)S(1)} %weigh.1), channel_id=1, source_target_pairs={{0,96},{32,0},{64,32},{96,64},{1,97},{33,1},{65,33},{97,65},{2,98}... | collective-permute-start | bytes 884744 | tf_op jit(solution)/shard_map/gather_rows/ppermute | solution.py:25
  4.6 0.7 collective-permute-start.2
  5.4 5.5 %collective-permute-done = bf16[144,1024]{1,0:T(8,128)(2,1)S(1)} collective-permute-done((bf16[144,1024]{1,0:T(8,128)(2,1)S(1)}, bf16[144,1024]{1,0:T(8,128)(2,1)S(1)}, u32[]{:S(2)}, u32[]{:S(2)}) %collective-permute-start) | collective-permute-done | bytes 294944 | tf_op jit(solution)/shard_map/gather_rows/ppermute | solution.py:25
  10.9 3.9 %collective-permute-start.1 = (bf16[144,1024]{1,0:T(8,128)(2,1)S(1)}, bf16[144,1024]{1,0:T(8,128)(2,1)}, u32[]{:S(2)}, u32[]{:S(2)}) collective-permute-start(bf16[144,1024]{1,0:T(8,128)(2,1)S(1)} %collective-permute-done), channel_id=1, source_target_pairs={{0,224},{32,128},{64,160},{96,192},{128,96},{160,0},{192,32},{224,... | collective-permute-start | bytes 884744 | tf_op jit(solution)/shard_map/gather_rows/ppermute | solution.py:151
  14.8 0.1 collective-permute-start.3
  15.4 0.6 collective-permute-done.4
  16.0 1.0 collective-permute-start.5
  17.0 1.3 %collective-permute-start.6 = (bf16[144,1024]{1,0:T(8,128)(2,1)S(1)}, bf16[144,1024]{1,0:T(8,128)(2,1)S(1)}, u32[]{:S(2)}, u32[]{:S(2)}) collective-permute-start(bf16[144,1024]{1,0:T(8,128)(2,1)S(1)} %collective-permute-done.4), channel_id=1, source_target_pairs={{0,128},{128,0},{1,129},{129,1},{2,130},{130,2},{3,131},{131,3},{4... | collective-permute-start | bytes 884744 | tf_op jit(solution)/shard_map/gather_rows/ppermute | solution.py:25
  18.2 4.0 %collective-permute-done.1 = bf16[144,1024]{1,0:T(8,128)(2,1)} collective-permute-done((bf16[144,1024]{1,0:T(8,128)(2,1)S(1)}, bf16[144,1024]{1,0:T(8,128)(2,1)}, u32[]{:S(2)}, u32[]{:S(2)}) %collective-permute-start.1) | collective-permute-done | bytes 294944 | tf_op jit(solution)/shard_map/gather_rows/ppermute | solution.py:151
  22.2 1.0 bitcast_dynamic-update-slice_fusion.6
  23.2 3.3 %collective-permute-done.3 = bf16[144,1024]{1,0:T(8,128)(2,1)} collective-permute-done((bf16[144,1024]{1,0:T(8,128)(2,1)S(1)}, bf16[144,1024]{1,0:T(8,128)(2,1)}, u32[]{:S(2)}, u32[]{:S(2)}) %collective-permute-start.3) | collective-permute-done | bytes 294944 | tf_op jit(solution)/shard_map/gather_rows/ppermute | solution.py:25
  26.5 1.0 bitcast_dynamic-update-slice_fusion.5
  27.6 0.1 fusion.17
  27.8 0.4 convolution_convert_fusion
  28.2 5.9 %collective-permute-start.13 = (bf16[128,1024]{1,0:T(8,128)(2,1)S(1)}, bf16[128,1024]{1,0:T(8,128)(2,1)S(1)}, u32[]{:S(2)}, u32[]{:S(2)}) collective-permute-start(bf16[128,1024]{1,0:T(8,128)(2,1)S(1)} %convolution_convert_fusion), channel_id=1, source_target_pairs={{0,14},{2,0},{4,2},{6,4},{8,6},{10,8},{12,10},{14,12},{1,15},{3,1}... | collective-permute-start | bytes 786440 | tf_op jit(solution)/shard_map/sum_layers/ppermute | solution.py:25
  34.2 0.4 fusion.11
  34.6 1.1 collective-permute-start.17
  35.7 0.4 convolution_convert_fusion.1
  36.1 1.1 collective-permute-start.8
  37.2 0.4 fusion.8
  37.7 0.1 collective-permute-start.12
  37.8 0.4 fusion.2
  38.2 2.7 %collective-permute-done.13 = bf16[128,1024]{1,0:T(8,128)(2,1)S(1)} collective-permute-done((bf16[128,1024]{1,0:T(8,128)(2,1)S(1)}, bf16[128,1024]{1,0:T(8,128)(2,1)S(1)}, u32[]{:S(2)}, u32[]{:S(2)}) %collective-permute-start.13) | collective-permute-done | bytes 262176 | tf_op jit(solution)/shard_map/sum_layers/ppermute | solution.py:25
  40.9 0.5 fusion.9
  41.4 4.0 %collective-permute-start.15 = (bf16[128,1024]{1,0:T(8,128)(2,1)S(1)}, bf16[128,1024]{1,0:T(8,128)(2,1)S(1)}, u32[]{:S(2)}, u32[]{:S(2)}) collective-permute-start(bf16[128,1024]{1,0:T(8,128)(2,1)S(1)} %fusion.9), channel_id=1, source_target_pairs={{0,14},{2,0},{4,2},{6,4},{8,6},{10,8},{12,10},{14,12},{1,15},{3,1}... | collective-permute-start | bytes 786440 | tf_op jit(solution)/shard_map/sum_layers/ppermute | solution.py:25
  45.3 1.2 %collective-permute-done.17 = bf16[128,1024]{1,0:T(8,128)(2,1)S(1)} collective-permute-done((bf16[128,1024]{1,0:T(8,128)(2,1)S(1)}, bf16[128,1024]{1,0:T(8,128)(2,1)S(1)}, u32[]{:S(2)}, u32[]{:S(2)}) %collective-permute-start.17) | collective-permute-done | bytes 262176 | tf_op jit(solution)/shard_map/sum_layers/ppermute | solution.py:25
  46.5 0.5 add_convert_fusion.1
  47.0 3.8 %collective-permute-start.18 = (bf16[128,1024]{1,0:T(8,128)(2,1)S(1)}, bf16[128,1024]{1,0:T(8,128)(2,1)S(1)}, u32[]{:S(2)}, u32[]{:S(2)}) collective-permute-start(bf16[128,1024]{1,0:T(8,128)(2,1)S(1)} %add_convert_fusion.1), channel_id=1, source_target_pairs={{0,14},{2,0},{4,2},{6,4},{8,6},{10,8},{12,10},{14,12},{1,15},{3,1}... | collective-permute-start | bytes 786440 | tf_op jit(solution)/shard_map/sum_layers/ppermute | solution.py:25
  50.8 0.5 add_convert_fusion.4
  51.3 0.1 collective-permute-start.9
  51.4 0.5 fusion.7
  51.8 0.1 collective-permute-start.14
  51.9 0.2 collective-permute-done.15
  52.2 0.5 fusion.10
  52.6 3.8 %collective-permute-start.20 = (bf16[128,1024]{1,0:T(8,128)(2,1)S(1)}, bf16[128,1024]{1,0:T(8,128)(2,1)S(1)}, u32[]{:S(2)}, u32[]{:S(2)}) collective-permute-start(bf16[128,1024]{1,0:T(8,128)(2,1)S(1)} %fusion.10), channel_id=1, source_target_pairs={{0,14},{2,0},{4,2},{6,4},{8,6},{10,8},{12,10},{14,12},{1,15},{3,1}... | collective-permute-start | bytes 786440 | tf_op jit(solution)/shard_map/sum_layers/ppermute | solution.py:25
  56.4 1.4 %collective-permute-done.18 = bf16[128,1024]{1,0:T(8,128)(2,1)S(1)} collective-permute-done((bf16[128,1024]{1,0:T(8,128)(2,1)S(1)}, bf16[128,1024]{1,0:T(8,128)(2,1)S(1)}, u32[]{:S(2)}, u32[]{:S(2)}) %collective-permute-start.18) | collective-permute-done | bytes 262176 | tf_op jit(solution)/shard_map/sum_layers/ppermute | solution.py:25
  57.8 0.5 add_convert_fusion
  58.3 3.8 %collective-permute-start.19 = (bf16[128,1024]{1,0:T(8,128)(2,1)S(1)}, bf16[128,1024]{1,0:T(8,128)(2,1)S(1)}, u32[]{:S(2)}, u32[]{:S(2)}) collective-permute-start(bf16[128,1024]{1,0:T(8,128)(2,1)S(1)} %add_convert_fusion), channel_id=1, source_target_pairs={{0,14},{2,0},{4,2},{6,4},{8,6},{10,8},{12,10},{14,12},{1,15},{3,1}... | collective-permute-start | bytes 786440 | tf_op jit(solution)/shard_map/sum_layers/ppermute | solution.py:25
  62.0 0.5 add_convert_fusion.3
  62.6 0.6 collective-permute-done.14
  63.2 0.5 fusion.6
  63.7 0.5 fusion.12
  64.2 3.4 %collective-permute-start.21 = (bf16[128,1024]{1,0:T(8,128)(2,1)S(1)}, bf16[128,1024]{1,0:T(8,128)(2,1)S(1)}, u32[]{:S(2)}, u32[]{:S(2)}) collective-permute-start(bf16[128,1024]{1,0:T(8,128)(2,1)S(1)} %fusion.12), channel_id=1, source_target_pairs={{0,14},{2,0},{4,2},{6,4},{8,6},{10,8},{12,10},{14,12},{1,15},{3,1}... | collective-permute-start | bytes 786440 | tf_op jit(solution)/shard_map/sum_layers/ppermute | solution.py:25
  67.6 3.9 %collective-permute-done.10 = bf16[128,1024]{1,0:T(8,128)(2,1)S(1)} collective-permute-done((bf16[128,1024]{1,0:T(8,128)(2,1)S(1)}, bf16[128,1024]{1,0:T(8,128)(2,1)S(1)}, u32[]{:S(2)}, u32[]{:S(2)}) %collective-permute-start.10) | collective-permute-done | bytes 262176 | tf_op jit(solution)/shard_map/sum_layers/ppermute | solution.py:25
  71.6 0.5 add_convert_fusion.2
  72.1 0.4 fusion
  72.6 3.2 %collective-permute-done.16 = bf16[128,1024]{1,0:T(8,128)(2,1)S(1)} collective-permute-done((bf16[128,1024]{1,0:T(8,128)(2,1)S(1)}, bf16[128,1024]{1,0:T(8,128)(2,1)S(1)}, u32[]{:S(2)}, u32[]{:S(2)}) %collective-permute-start.16) | collective-permute-done | bytes 262176 | tf_op jit(solution)/shard_map/sum_layers/ppermute | solution.py:25
  75.8 3.9 %collective-permute-done.11 = bf16[128,1024]{1,0:T(8,128)(2,1)S(1)} collective-permute-done((bf16[128,1024]{1,0:T(8,128)(2,1)S(1)}, bf16[128,1024]{1,0:T(8,128)(2,1)S(1)}, u32[]{:S(2)}, u32[]{:S(2)}) %collective-permute-start.11) | collective-permute-done | bytes 262176 | tf_op jit(solution)/shard_map/sum_layers/ppermute | solution.py:25
  79.7 1.0 fusion.14
  80.7 9.0 %all-to-all-start = ((bf16[16,8,2048]{2,1,0:T(8,128)(2,1)}), bf16[16,8,2048]{2,1,0:T(8,128)(2,1)S(1)}, u32[]{:S(2)}, u32[]{:S(2)}) async-start(bf16[16,8,2048]{2,1,0:T(8,128)(2,1)} %fusion.14), calls=%async_computation | async-start | bytes 1048576 | tf_op jit(solution)/shard_map/to_components/all_to_all | solution.py:245
  89.7 0.1 select_reduce_fusion
  89.9 0.1 collective-permute-start.22
  90.0 1.1 collective-permute-done.22
  91.2 0.1 reshape.111.values_ref
  91.3 6.2 %all-to-all-done = bf16[16,8,2048]{2,1,0:T(8,128)(2,1)S(1)} async-done(((bf16[16,8,2048]{2,1,0:T(8,128)(2,1)}), bf16[16,8,2048]{2,1,0:T(8,128)(2,1)S(1)}, u32[]{:S(2)}, u32[]{:S(2)}) %all-to-all-start) | async-done | bytes 524320 | tf_op jit(solution)/shard_map/to_components/all_to_all | solution.py:245
  97.5 2.2 %fit.1 = f32[32,1,256]{2,1,0:T(1,128)} custom-call(s32[1]{0:T(128)} %bitcast.slot_ref, bf16[128,2048]{1,0:T(8,128)(2,1)S(1)} %bitcast.93, f32[32,2048]{1,0:T(8,128)S(1)} %reshape.111.values_ref), custom_call_target="tpu_custom_call" | custom-call | tf_op jit(solution)/shard_map/fit/pallas_call | solution.py:130
  99.7 6.0 %all-to-all-start.1 = ((f32[32,1,256]{2,1,0:T(1,128)}), f32[32,1,256]{2,1,0:T(1,128)S(1)}, u32[]{:S(2)}, u32[]{:S(2)}) async-start(f32[32,1,256]{2,1,0:T(1,128)} %fit.1), calls=%async_computation.1 | async-start | bytes 65536 | tf_op jit(solution)/shard_map/gather_scores/all_to_all | solution.py:250
  105.7 0.1 pad_dynamic-slice_fusion
  105.8 5.4 %all-to-all-done.1 = f32[32,1,256]{2,1,0:T(1,128)S(1)} async-done(((f32[32,1,256]{2,1,0:T(1,128)}), f32[32,1,256]{2,1,0:T(1,128)S(1)}, u32[]{:S(2)}, u32[]{:S(2)}) %all-to-all-start.1) | async-done | bytes 32800 | tf_op jit(solution)/shard_map/gather_scores/all_to_all | solution.py:250
  111.3 1.3 %collective-permute-start.23 = (f32[256]{0:T(256)S(1)}, f32[256]{0:T(256)S(1)}, u32[]{:S(2)}, u32[]{:S(2)}) collective-permute-start(f32[256]{0:T(256)S(1)} %reduce_sum.19), channel_id=1, source_target_pairs={{0,2},{2,4},{4,6},{6,8},{8,10},{10,12},{12,14},{3,1},{5,3},{7,5},{... | collective-permute-start | bytes 3080 | tf_op jit(solution)/shard_map/gather_scores/ppermute | solution.py:253
  112.6 0.6 dynamic_slice.55
  113.2 3.6 %collective-permute-done.23 = f32[256]{0:T(256)S(1)} collective-permute-done((f32[256]{0:T(256)S(1)}, f32[256]{0:T(256)S(1)}, u32[]{:S(2)}, u32[]{:S(2)}) %collective-permute-start.23) | collective-permute-done | bytes 1056 | tf_op jit(solution)/shard_map/gather_scores/ppermute | solution.py:253
  117.0 0.6 add_divide_fusion
  (40 shorter events, 0.9 us)
Async XLA Ops:
  1.8 9.1 %collective-permute-start = (bf16[144,1024]{1,0:T(8,128)(2,1)S(1)}, bf16[144,1024]{1,0:T(8,128)(2,1)S(1)}, u32[]{:S(2)}, u32[]{:S(2)}) collective-permute-start(bf16[144,1024]{1,0:T(8,128)(2,1)S(1)} %weigh.1), channel_id=1, source_target_pairs={{0,96},{32,0},{64,32},{96,64},{1,97},{33,1},{65,33},{97,65},{2,98}... | collective-permute-start | bytes 884744 | tf_op jit(solution)/shard_map/gather_rows/ppermute | solution.py:25
  4.6 10.2 %collective-permute-start.2 = (bf16[144,1024]{1,0:T(8,128)(2,1)S(1)}, bf16[144,1024]{1,0:T(8,128)(2,1)S(1)}, u32[]{:S(2)}, u32[]{:S(2)}) collective-permute-start(bf16[144,1024]{1,0:T(8,128)(2,1)S(1)} %weigh.1), channel_id=1, source_target_pairs={{0,128},{128,0},{1,129},{129,1},{2,130},{130,2},{3,131},{131,3},{4... | collective-permute-start | bytes 884744 | tf_op jit(solution)/shard_map/gather_rows/ppermute | solution.py:25
  5.4 22.3 %collective-permute-start.7 = (bf16[1024,1024]{1,0:T(8,128)(2,1)}, bf16[1024,1024]{1,0:T(8,128)(2,1)S(1)}, u32[]{:S(2)}, u32[]{:S(2)}) collective-permute-start(bf16[1024,1024]{1,0:T(8,128)(2,1)} %param.10), channel_id=1, source_target_pairs={{0,16},{16,0},{1,17},{17,1},{2,18},{18,2},{3,19},{19,3},{4,20},{20... | collective-permute-start | bytes 6291464 | tf_op jit(solution)/shard_map/swap_eigvecs/ppermute | solution.py:25
  5.4 10.6 %collective-permute-start.4 = (bf16[144,1024]{1,0:T(8,128)(2,1)S(1)}, bf16[144,1024]{1,0:T(8,128)(2,1)S(1)}, u32[]{:S(2)}, u32[]{:S(2)}) collective-permute-start(bf16[144,1024]{1,0:T(8,128)(2,1)S(1)} %weigh.1), channel_id=1, source_target_pairs={{0,32},{32,64},{64,96},{96,0},{1,33},{33,65},{65,97},{97,1},{2,34}... | collective-permute-start | bytes 884744 | tf_op jit(solution)/shard_map/gather_rows/ppermute | solution.py:25
  10.9 11.3 %collective-permute-start.1 = (bf16[144,1024]{1,0:T(8,128)(2,1)S(1)}, bf16[144,1024]{1,0:T(8,128)(2,1)}, u32[]{:S(2)}, u32[]{:S(2)}) collective-permute-start(bf16[144,1024]{1,0:T(8,128)(2,1)S(1)} %collective-permute-done), channel_id=1, source_target_pairs={{0,224},{32,128},{64,160},{96,192},{128,96},{160,0},{192,32},{224,... | collective-permute-start | bytes 884744 | tf_op jit(solution)/shard_map/gather_rows/ppermute | solution.py:151
  14.8 11.7 %collective-permute-start.3 = (bf16[144,1024]{1,0:T(8,128)(2,1)S(1)}, bf16[144,1024]{1,0:T(8,128)(2,1)}, u32[]{:S(2)}, u32[]{:S(2)}) collective-permute-start(bf16[144,1024]{1,0:T(8,128)(2,1)S(1)} %collective-permute-done.2), channel_id=1, source_target_pairs={{0,96},{32,0},{64,32},{96,64},{1,97},{33,1},{65,33},{97,65},{2,98}... | collective-permute-start | bytes 884744 | tf_op jit(solution)/shard_map/gather_rows/ppermute | solution.py:25
  16.0 11.5 %collective-permute-start.5 = (bf16[144,1024]{1,0:T(8,128)(2,1)S(1)}, bf16[144,1024]{1,0:T(8,128)(2,1)S(1)}, u32[]{:S(2)}, u32[]{:S(2)}) collective-permute-start(bf16[144,1024]{1,0:T(8,128)(2,1)S(1)} %collective-permute-done.4), channel_id=1, source_target_pairs={{0,32},{32,64},{64,96},{96,0},{1,33},{33,65},{65,97},{97,1},{2,34}... | collective-permute-start | bytes 884744 | tf_op jit(solution)/shard_map/gather_rows/ppermute | solution.py:25
  17.0 10.7 %collective-permute-start.6 = (bf16[144,1024]{1,0:T(8,128)(2,1)S(1)}, bf16[144,1024]{1,0:T(8,128)(2,1)S(1)}, u32[]{:S(2)}, u32[]{:S(2)}) collective-permute-start(bf16[144,1024]{1,0:T(8,128)(2,1)S(1)} %collective-permute-done.4), channel_id=1, source_target_pairs={{0,128},{128,0},{1,129},{129,1},{2,130},{130,2},{3,131},{131,3},{4... | collective-permute-start | bytes 884744 | tf_op jit(solution)/shard_map/gather_rows/ppermute | solution.py:25
  27.5 6.6 %copy-start = (bf16[1024,1024]{1,0:T(8,128)(2,1)S(1)}, bf16[1024,1024]{1,0:T(8,128)(2,1)}, u32[]{:S(2)}) copy-start(bf16[1024,1024]{1,0:T(8,128)(2,1)} %param.10) | copy-start | bytes 6291460
  28.2 12.7 %collective-permute-start.13 = (bf16[128,1024]{1,0:T(8,128)(2,1)S(1)}, bf16[128,1024]{1,0:T(8,128)(2,1)S(1)}, u32[]{:S(2)}, u32[]{:S(2)}) collective-permute-start(bf16[128,1024]{1,0:T(8,128)(2,1)S(1)} %convolution_convert_fusion), channel_id=1, source_target_pairs={{0,14},{2,0},{4,2},{6,4},{8,6},{10,8},{12,10},{14,12},{1,15},{3,1}... | collective-permute-start | bytes 786440 | tf_op jit(solution)/shard_map/sum_layers/ppermute | solution.py:25
  34.6 11.9 %collective-permute-start.17 = (bf16[128,1024]{1,0:T(8,128)(2,1)S(1)}, bf16[128,1024]{1,0:T(8,128)(2,1)S(1)}, u32[]{:S(2)}, u32[]{:S(2)}) collective-permute-start(bf16[128,1024]{1,0:T(8,128)(2,1)S(1)} %fusion.11), channel_id=1, source_target_pairs={{0,14},{2,0},{4,2},{6,4},{8,6},{10,8},{12,10},{14,12},{1,15},{3,1}... | collective-permute-start | bytes 786440 | tf_op jit(solution)/shard_map/sum_layers/ppermute | solution.py:25
  36.1 14.6 %collective-permute-start.8 = (bf16[128,1024]{1,0:T(8,128)(2,1)S(1)}, bf16[128,1024]{1,0:T(8,128)(2,1)S(1)}, u32[]{:S(2)}, u32[]{:S(2)}) collective-permute-start(bf16[128,1024]{1,0:T(8,128)(2,1)S(1)} %convolution_convert_fusion.1), channel_id=1, source_target_pairs={{0,2},{2,4},{4,6},{6,8},{8,10},{10,12},{12,14},{14,0},{1,3},{3,5},... | collective-permute-start | bytes 786440 | tf_op jit(solution)/shard_map/sum_layers/ppermute | solution.py:25
  37.7 13.7 %collective-permute-start.12 = (bf16[128,1024]{1,0:T(8,128)(2,1)S(1)}, bf16[128,1024]{1,0:T(8,128)(2,1)S(1)}, u32[]{:S(2)}, u32[]{:S(2)}) collective-permute-start(bf16[128,1024]{1,0:T(8,128)(2,1)S(1)} %fusion.8), channel_id=1, source_target_pairs={{0,2},{2,4},{4,6},{6,8},{8,10},{10,12},{12,14},{14,0},{1,3},{3,5},... | collective-permute-start | bytes 786440 | tf_op jit(solution)/shard_map/sum_layers/ppermute | solution.py:25
  41.4 10.8 %collective-permute-start.15 = (bf16[128,1024]{1,0:T(8,128)(2,1)S(1)}, bf16[128,1024]{1,0:T(8,128)(2,1)S(1)}, u32[]{:S(2)}, u32[]{:S(2)}) collective-permute-start(bf16[128,1024]{1,0:T(8,128)(2,1)S(1)} %fusion.9), channel_id=1, source_target_pairs={{0,14},{2,0},{4,2},{6,4},{8,6},{10,8},{12,10},{14,12},{1,15},{3,1}... | collective-permute-start | bytes 786440 | tf_op jit(solution)/shard_map/sum_layers/ppermute | solution.py:25
  47.0 10.7 %collective-permute-start.18 = (bf16[128,1024]{1,0:T(8,128)(2,1)S(1)}, bf16[128,1024]{1,0:T(8,128)(2,1)S(1)}, u32[]{:S(2)}, u32[]{:S(2)}) collective-permute-start(bf16[128,1024]{1,0:T(8,128)(2,1)S(1)} %add_convert_fusion.1), channel_id=1, source_target_pairs={{0,14},{2,0},{4,2},{6,4},{8,6},{10,8},{12,10},{14,12},{1,15},{3,1}... | collective-permute-start | bytes 786440 | tf_op jit(solution)/shard_map/sum_layers/ppermute | solution.py:25
  51.3 10.8 %collective-permute-start.9 = (bf16[128,1024]{1,0:T(8,128)(2,1)S(1)}, bf16[128,1024]{1,0:T(8,128)(2,1)S(1)}, u32[]{:S(2)}, u32[]{:S(2)}) collective-permute-start(bf16[128,1024]{1,0:T(8,128)(2,1)S(1)} %add_convert_fusion.4), channel_id=1, source_target_pairs={{0,2},{2,4},{4,6},{6,8},{8,10},{10,12},{12,14},{14,0},{1,3},{3,5},... | collective-permute-start | bytes 786440 | tf_op jit(solution)/shard_map/sum_layers/ppermute | solution.py:25
  51.8 11.3 %collective-permute-start.14 = (bf16[128,1024]{1,0:T(8,128)(2,1)S(1)}, bf16[128,1024]{1,0:T(8,128)(2,1)S(1)}, u32[]{:S(2)}, u32[]{:S(2)}) collective-permute-start(bf16[128,1024]{1,0:T(8,128)(2,1)S(1)} %fusion.7), channel_id=1, source_target_pairs={{0,2},{2,4},{4,6},{6,8},{8,10},{10,12},{12,14},{14,0},{1,3},{3,5},... | collective-permute-start | bytes 786440 | tf_op jit(solution)/shard_map/sum_layers/ppermute | solution.py:25
  52.6 11.1 %collective-permute-start.20 = (bf16[128,1024]{1,0:T(8,128)(2,1)S(1)}, bf16[128,1024]{1,0:T(8,128)(2,1)S(1)}, u32[]{:S(2)}, u32[]{:S(2)}) collective-permute-start(bf16[128,1024]{1,0:T(8,128)(2,1)S(1)} %fusion.10), channel_id=1, source_target_pairs={{0,14},{2,0},{4,2},{6,4},{8,6},{10,8},{12,10},{14,12},{1,15},{3,1}... | collective-permute-start | bytes 786440 | tf_op jit(solution)/shard_map/sum_layers/ppermute | solution.py:25
  58.3 14.3 %collective-permute-start.19 = (bf16[128,1024]{1,0:T(8,128)(2,1)S(1)}, bf16[128,1024]{1,0:T(8,128)(2,1)S(1)}, u32[]{:S(2)}, u32[]{:S(2)}) collective-permute-start(bf16[128,1024]{1,0:T(8,128)(2,1)S(1)} %add_convert_fusion), channel_id=1, source_target_pairs={{0,14},{2,0},{4,2},{6,4},{8,6},{10,8},{12,10},{14,12},{1,15},{3,1}... | collective-permute-start | bytes 786440 | tf_op jit(solution)/shard_map/sum_layers/ppermute | solution.py:25
  62.5 9.1 %collective-permute-start.10 = (bf16[128,1024]{1,0:T(8,128)(2,1)S(1)}, bf16[128,1024]{1,0:T(8,128)(2,1)S(1)}, u32[]{:S(2)}, u32[]{:S(2)}) collective-permute-start(bf16[128,1024]{1,0:T(8,128)(2,1)S(1)} %add_convert_fusion.3), channel_id=1, source_target_pairs={{0,2},{2,4},{4,6},{6,8},{8,10},{10,12},{12,14},{14,0},{1,3},{3,5},... | collective-permute-start | bytes 786440 | tf_op jit(solution)/shard_map/sum_layers/ppermute | solution.py:25
  63.6 12.1 %collective-permute-start.16 = (bf16[128,1024]{1,0:T(8,128)(2,1)S(1)}, bf16[128,1024]{1,0:T(8,128)(2,1)S(1)}, u32[]{:S(2)}, u32[]{:S(2)}) collective-permute-start(bf16[128,1024]{1,0:T(8,128)(2,1)S(1)} %fusion.6), channel_id=1, source_target_pairs={{0,2},{2,4},{4,6},{6,8},{8,10},{10,12},{12,14},{14,0},{1,3},{3,5},... | collective-permute-start | bytes 786440 | tf_op jit(solution)/shard_map/sum_layers/ppermute | solution.py:25
  64.2 11.6 %collective-permute-start.21 = (bf16[128,1024]{1,0:T(8,128)(2,1)S(1)}, bf16[128,1024]{1,0:T(8,128)(2,1)S(1)}, u32[]{:S(2)}, u32[]{:S(2)}) collective-permute-start(bf16[128,1024]{1,0:T(8,128)(2,1)S(1)} %fusion.12), channel_id=1, source_target_pairs={{0,14},{2,0},{4,2},{6,4},{8,6},{10,8},{12,10},{14,12},{1,15},{3,1}... | collective-permute-start | bytes 786440 | tf_op jit(solution)/shard_map/sum_layers/ppermute | solution.py:25
  72.0 7.7 %collective-permute-start.11 = (bf16[128,1024]{1,0:T(8,128)(2,1)S(1)}, bf16[128,1024]{1,0:T(8,128)(2,1)S(1)}, u32[]{:S(2)}, u32[]{:S(2)}) collective-permute-start(bf16[128,1024]{1,0:T(8,128)(2,1)S(1)} %add_convert_fusion.2), channel_id=1, source_target_pairs={{0,2},{2,4},{4,6},{6,8},{8,10},{10,12},{12,14},{14,0},{1,3},{3,5},... | collective-permute-start | bytes 786440 | tf_op jit(solution)/shard_map/sum_layers/ppermute | solution.py:25
  72.6 17.4 %copy-start.1 = (s32[1024]{0:T(1024)S(1)}, s32[1024]{0:T(1024)}, u32[]{:S(2)}) copy-start(s32[1024]{0:T(1024)} %param.12) | copy-start | bytes 12292
  79.7 37.3 %copy-start.2 = (s32[64]{0:T(128)S(1)}, s32[64]{0:T(128)}, u32[]{:S(2)}) copy-start(s32[64]{0:T(128)} %param.13) | copy-start | bytes 772
  80.7 16.8 %all-to-all-start = ((bf16[16,8,2048]{2,1,0:T(8,128)(2,1)}), bf16[16,8,2048]{2,1,0:T(8,128)(2,1)S(1)}, u32[]{:S(2)}, u32[]{:S(2)}) async-start(bf16[16,8,2048]{2,1,0:T(8,128)(2,1)} %fusion.14), calls=%async_computation | async-start | bytes 1048576 | tf_op jit(solution)/shard_map/to_components/all_to_all | solution.py:245
  89.9 1.3 %collective-permute-start.22 = (f32[8,1024]{1,0:T(8,128)S(1)}, f32[8,1024]{1,0:T(8,128)S(1)}, u32[]{:S(2)}, u32[]{:S(2)}) collective-permute-start(f32[8,1024]{1,0:T(8,128)S(1)} %select_reduce_fusion), channel_id=1, source_target_pairs={{0,16},{16,0},{1,17},{17,1},{2,18},{18,2},{3,19},{19,3},{4,20},{20... | collective-permute-start | bytes 98312 | tf_op jit(solution)/shard_map/gather_values/ppermute | solution.py:25
  99.7 11.5 %all-to-all-start.1 = ((f32[32,1,256]{2,1,0:T(1,128)}), f32[32,1,256]{2,1,0:T(1,128)S(1)}, u32[]{:S(2)}, u32[]{:S(2)}) async-start(f32[32,1,256]{2,1,0:T(1,128)} %fit.1), calls=%async_computation.1 | async-start | bytes 65536 | tf_op jit(solution)/shard_map/gather_scores/all_to_all | solution.py:250
  111.3 5.5 %collective-permute-start.23 = (f32[256]{0:T(256)S(1)}, f32[256]{0:T(256)S(1)}, u32[]{:S(2)}, u32[]{:S(2)}) collective-permute-start(f32[256]{0:T(256)S(1)} %reduce_sum.19), channel_id=1, source_target_pairs={{0,2},{2,4},{4,6},{6,8},{8,10},{10,12},{12,14},{3,1},{5,3},{7,5},{... | collective-permute-start | bytes 3080 | tf_op jit(solution)/shard_map/gather_scores/ppermute | solution.py:253
